TPU v7x, 512 devices: a whole 4x8x8 slice. The times are simulated.
512 devices in a mesh: region: 128 (over z, y, core), chan: 4 (over x).
Axes of the slice: x: 4, y: 8, z: 8, core: 2. Of those that a mesh axis runs over, the one named last changes fastest.
Arguments:
- grid_state: bfloat16 [131072, 1024], P('region', 'chan'), may hold values from -6 to 6
- mesh_state: bfloat16 [32768, 1024], P('region', 'chan'), may hold values from -6 to 6
- enc_send: bfloat16 [1024, 1024], P(None, 'chan'), may hold values from -0.1875 to 0.1875
- enc_out: bfloat16 [1024, 1024], P(None, 'chan'), may hold values from -0.1875 to 0.1875
- proc_send: bfloat16 [1024, 1024], P(None, 'chan'), may hold values from -0.1875 to 0.1875
- proc_out: bfloat16 [1024, 1024], P(None, 'chan'), may hold values from -0.1875 to 0.1875
- dec_send: bfloat16 [1024, 1024], P(None, 'chan'), may hold values from -0.1875 to 0.1875
- dec_out: bfloat16 [1024, 1024], P(None, 'chan'), may hold values from -0.1875 to 0.1875
- g2m_index: int32 [16, 32768], P(None, 'region'), may hold values from 0 to 131071, as said below
- g2m_weight: float32 [16, 32768], P(None, 'region'), may hold values from 0.25 to 4
- g2m_count: int32 [32768], P('region'), may hold values from 1 to 16
- m2m_index: int32 [8, 32768], P(None, 'region'), may hold values from 0 to 32767, as said below
- m2m_weight: float32 [8, 32768], P(None, 'region'), may hold values from 0.25 to 4
- m2m_count: int32 [32768], P('region'), may hold values from 1 to 8
- m2g_index: int32 [4, 131072], P(None, 'region'), may hold values from 0 to 32767, as said below
- m2g_weight: float32 [4, 131072], P(None, 'region'), may hold values from 0.25 to 4
- m2g_count: int32 [131072], P('region'), may hold values from 1 to 4
Outputs:
- grid_next: bfloat16 [131072, 1024], P('region', 'chan')
- mesh_next: bfloat16 [32768, 1024], P('region', 'chan')
Inputs may be any that keep to these rules, and one draw needn't show every extreme that they name: Column i of g2m_index belongs to mesh node i, of region i // 256; each entry names a grid node whose region (index // 1024) differs from it by at most 2. `m2m_index`: column i belongs to mesh node i, of region i // 256; each entry names a mesh node whose region (index // 256) differs from it by at most 2. `m2g_index`: column i belongs to grid node i, of region i // 1024; each entry names a mesh node whose region (index // 256) differs from it by at most 2.
All inputs are finite; a program needn't handle non-finite values.
Results may differ from a plain program's by a relative error of at most 0.017.
Values may be sent and summed in bfloat16 or wider, within the bound.
No kernel may reach another device: no remote copies, remote signals or barrier semaphores. Data moves between devices by JAX's collectives and lax.ppermute only.
A program may use at most 64 MiB of HBM per device.

v0:
```python
import jax
import jax.numpy as jnp
from jax import lax
from jax.sharding import PartitionSpec as P

SPAN = 2


def from_behind(shard, axis, by):
    devices = lax.axis_size(axis)
    pairs = [(i, i + by) for i in range(devices) if 0 <= i + by < devices]
    return lax.ppermute(shard, axis, pairs)


def project(values, weight):
    return jnp.dot(
        lax.all_gather(values, "chan", axis=1, tiled=True),
        weight,
        preferred_element_type=jnp.float32,
    )


def neighbourhood(projected):
    fetched = {}
    for offset in [o for o in range(1, SPAN + 1)] + [-o for o in range(1, SPAN + 1)]:
        fetched[offset] = from_behind(projected, "region", offset)
    ordered = (
        [fetched[o] for o in range(SPAN, 0, -1)]
        + [projected]
        + [fetched[-o] for o in range(1, SPAN + 1)]
    )
    return jnp.concatenate(ordered, axis=0)


def messages(projected, receivers, index_block, edge_weight, counts):
    slots = index_block.shape[0]
    fetched = jnp.take(projected, index_block, axis=0).astype(jnp.float32)
    message = jax.nn.silu(fetched + receivers.astype(jnp.float32)[None]) * edge_weight[:, :, None]
    valid = jnp.arange(slots, dtype=jnp.int32)[:, None] < counts[None, :]
    summed = jnp.sum(jnp.where(valid[:, :, None], message, 0.0), axis=0)
    return (summed / counts.astype(jnp.float32)[:, None]).astype(jnp.bfloat16)


def pulled_aggregate(projected, receivers, index_block, edge_weight, counts):
    window = neighbourhood(projected)
    first_row = (lax.axis_index("region") - SPAN) * projected.shape[0]
    local_index = index_block - first_row
    return messages(window, receivers, local_index, edge_weight, counts)


def finish(receivers, aggregate, w_out):
    return (receivers.astype(jnp.float32) + project(aggregate, w_out)).astype(jnp.bfloat16)


def layer(senders, receivers, w_send, w_out, index_block, edge_weight, counts):
    projected = project(senders, w_send).astype(jnp.bfloat16)
    aggregate = pulled_aggregate(projected, receivers, index_block, edge_weight, counts)
    return finish(receivers, aggregate, w_out)


def shards(
    grid_state,
    mesh_state,
    enc_send,
    enc_out,
    proc_send,
    proc_out,
    dec_send,
    dec_out,
    g2m_index,
    g2m_weight,
    g2m_count,
    m2m_index,
    m2m_weight,
    m2m_count,
    m2g_index,
    m2g_weight,
    m2g_count,
):
    mesh_one = layer(grid_state, mesh_state, enc_send, enc_out, g2m_index, g2m_weight, g2m_count)
    mesh_next = layer(mesh_one, mesh_one, proc_send, proc_out, m2m_index, m2m_weight, m2m_count)
    grid_next = layer(mesh_next, grid_state, dec_send, dec_out, m2g_index, m2g_weight, m2g_count)
    return (grid_next, mesh_next)


def solution(mesh):
    placed = (
        P("region", "chan"),
        P("region", "chan"),
        P(None, "chan"),
        P(None, "chan"),
        P(None, "chan"),
        P(None, "chan"),
        P(None, "chan"),
        P(None, "chan"),
        P(None, "region"),
        P(None, "region"),
        P("region"),
        P(None, "region"),
        P(None, "region"),
        P("region"),
        P(None, "region"),
        P(None, "region"),
        P("region"),
    )
    return jax.shard_map(
        shards,
        mesh=mesh,
        in_specs=placed,
        out_specs=(P("region", "chan"), P("region", "chan")),
        check_vma=False,
    )
```

profile of v0, /device:TPU:1, one launch (start us, length us, event | category | flops | bytes accessed | tf_op | source)
XLA Modules:
  0.0 280.1 jit_solution(15519909509398561267)
XLA Ops:
  7.2 0.7 all-gather.3.cloned.1.call-update
  8.0 0.7 fusion.3
  8.7 0.6 broadcast_clamp_fusion
  9.3 0.7 fusion.4
  10.1 44.5 %all-gather.3.cloned.1.call-done = bf16[1024,1024]{1,0:T(8,128)(2,1)} async-done(((bf16[1024,256]{1,0:T(8,128)(2,1)}), bf16[1024,1024]{1,0:T(8,128)(2,1)}) %all-gather.3.cloned.1.call-update) | async-done | bytes 2097168 | tf_op jit(solution)/shard_map/all_gather | solution.py:17
  54.6 2.3 convolution_convert_fusion
  56.9 3.1 %collective-permute-start = (bf16[1024,256]{1,0:T(8,128)(2,1)S(1)}, bf16[1024,256]{1,0:T(8,128)(2,1)S(1)}, u32[]{:S(2)}, u32[]{:S(2)}) collective-permute-start(bf16[1024,256]{1,0:T(8,128)(2,1)S(1)} %convolution_convert_fusion), channel_id=1, source_target_pairs={{0,8},{4,12},{8,16},{12,20},{16,24},{20,28},{24,32},{28,36},{32,40... | collective-permute-start | bytes 1572872 | tf_op jit(solution)/shard_map/ppermute | solution.py:12
  60.1 4.8 %collective-permute-start.1 = (bf16[1024,256]{1,0:T(8,128)(2,1)S(1)}, bf16[1024,256]{1,0:T(8,128)(2,1)S(1)}, u32[]{:S(2)}, u32[]{:S(2)}) collective-permute-start(bf16[1024,256]{1,0:T(8,128)(2,1)S(1)} %convolution_convert_fusion), channel_id=1, source_target_pairs={{0,4},{4,8},{8,12},{12,16},{16,20},{20,24},{24,28},{28,32},{32,36}... | collective-permute-start | bytes 1572872 | tf_op jit(solution)/shard_map/ppermute | solution.py:12
  64.9 0.6 iota_compare_fusion
  65.5 1.9 collective-permute-start.2
  67.4 1.3 collective-permute-start.3
  68.7 0.6 broadcast_clamp_fusion.1
  69.3 0.6 convert_element_type.61
  70.0 7.4 %collective-permute-done.1 = bf16[1024,256]{1,0:T(8,128)(2,1)S(1)} collective-permute-done((bf16[1024,256]{1,0:T(8,128)(2,1)S(1)}, bf16[1024,256]{1,0:T(8,128)(2,1)S(1)}, u32[]{:S(2)}, u32[]{:S(2)}) %collective-permute-start.1) | collective-permute-done | bytes 524320 | tf_op jit(solution)/shard_map/ppermute | solution.py:12
  77.4 2.8 collective-permute-done.2
  80.2 3.1 %collective-permute-done.3 = bf16[1024,256]{1,0:T(8,128)(2,1)S(1)} collective-permute-done((bf16[1024,256]{1,0:T(8,128)(2,1)S(1)}, bf16[1024,256]{1,0:T(8,128)(2,1)S(1)}, u32[]{:S(2)}, u32[]{:S(2)}) %collective-permute-start.3) | collective-permute-done | bytes 524320 | tf_op jit(solution)/shard_map/ppermute | solution.py:12
  83.3 18.3 %gather_fusion = bf16[4096,256]{1,0:T(8,128)(2,1)} fusion(bf16[5120,256]{1,0:T(8,128)(2,1)S(1)} %constant_dynamic-update-slice_fusion, s32[4096]{0:T(1024)} %broadcast_clamp_fusion), kind=kCustom, calls=%fused_computation | custom fusion | bytes 4210688 | tf_op jit(solution)/shard_map/jit(_take)/gather | solution.py:37
  101.6 5.6 %select_reduce_fusion.1 = f32[256,256]{1,0:T(8,128)S(1)} fusion(f32[16,256]{1,0:T(8,128)} %param.26, f32[256,256]{1,0:T(8,128)S(1)} %convert_element_type.58, bf16[16,256,256]{2,1,0:T(8,128)(2,1)} %bitcast.25, pred[16,256]{1,0:T(8,128)(4,1)} %get-tuple-element.5, pred[16,256]{1,0:T(8,128)(4,1)} %get-tuple-element.4), kind=kLoop, calls=%fused_computation.4 | loop fusion | flops 10420224 | bytes 2646016 | tf_op jit(solution)/shard_map/reduce_sum | solution.py:40
  107.2 0.1 divide_convert_fusion.2
  107.3 10.8 %all_gather.19 = bf16[256,1024]{1,0:T(8,128)(2,1)S(1)} all-gather(bf16[256,256]{1,0:T(8,128)(2,1)S(1)} %divide_convert_fusion.2), channel_id=1, replica_groups=mesh['region'=128,'chan'=4] {'chan'}, dimensions={1}, use_global_device_ids=true | all-gather | bytes 655360 | tf_op jit(solution)/shard_map/all_gather | solution.py:17
  118.1 0.3 fusion.6
  118.4 9.9 %all_gather.20 = bf16[256,1024]{1,0:T(8,128)(2,1)S(1)} all-gather(bf16[256,256]{1,0:T(8,128)(2,1)S(1)} %get-tuple-element.3), channel_id=1, replica_groups=mesh['region'=128,'chan'=4] {'chan'}, dimensions={1}, use_global_device_ids=true | all-gather | bytes 655360 | tf_op jit(solution)/shard_map/all_gather | solution.py:17
  128.3 0.3 convolution_convert_fusion.2
  128.6 3.8 %collective-permute-start.4 = (bf16[256,256]{1,0:T(8,128)(2,1)S(1)}, bf16[256,256]{1,0:T(8,128)(2,1)S(1)}, u32[]{:S(2)}, u32[]{:S(2)}) collective-permute-start(bf16[256,256]{1,0:T(8,128)(2,1)S(1)} %convolution_convert_fusion.2), channel_id=1, source_target_pairs={{0,8},{4,12},{8,16},{12,20},{16,24},{20,28},{24,32},{28,36},{32,40... | collective-permute-start | bytes 393224 | tf_op jit(solution)/shard_map/ppermute | solution.py:12
  132.4 13.9 %collective-permute-start.5 = (bf16[256,256]{1,0:T(8,128)(2,1)S(1)}, bf16[256,256]{1,0:T(8,128)(2,1)S(1)}, u32[]{:S(2)}, u32[]{:S(2)}) collective-permute-start(bf16[256,256]{1,0:T(8,128)(2,1)S(1)} %convolution_convert_fusion.2), channel_id=1, source_target_pairs={{0,4},{4,8},{8,12},{12,16},{16,20},{20,24},{24,28},{28,32},{32,36}... | collective-permute-start | bytes 393224 | tf_op jit(solution)/shard_map/ppermute | solution.py:12
  146.4 1.9 collective-permute-start.6
  148.3 1.3 collective-permute-start.7
  149.7 3.0 %collective-permute-done.6 = bf16[256,256]{1,0:T(8,128)(2,1)S(1)} collective-permute-done((bf16[256,256]{1,0:T(8,128)(2,1)S(1)}, bf16[256,256]{1,0:T(8,128)(2,1)S(1)}, u32[]{:S(2)}, u32[]{:S(2)}) %collective-permute-start.6) | collective-permute-done | bytes 131104 | tf_op jit(solution)/shard_map/ppermute | solution.py:12
  152.7 2.7 collective-permute-done.7
  155.4 7.5 %gather_fusion.1 = bf16[2048,256]{1,0:T(8,128)(2,1)S(1)} fusion(bf16[1280,256]{1,0:T(8,128)(2,1)S(1)} %constant_dynamic-update-slice_fusion.5, s32[2048]{0:T(1024)S(1)} %copy-done.13), kind=kCustom, calls=%fused_computation.1 | custom fusion | bytes 2105344 | tf_op jit(solution)/shard_map/jit(_take)/gather | solution.py:37
  163.0 1.2 select_reduce_fusion.2
  164.2 0.1 divide_convert_fusion.1
  164.3 10.9 %all_gather.21 = bf16[256,1024]{1,0:T(8,128)(2,1)S(1)} all-gather(bf16[256,256]{1,0:T(8,128)(2,1)S(1)} %divide_convert_fusion.1), channel_id=1, replica_groups=mesh['region'=128,'chan'=4] {'chan'}, dimensions={1}, use_global_device_ids=true | all-gather | bytes 655360 | tf_op jit(solution)/shard_map/all_gather | solution.py:17
  175.2 0.3 fusion.2
  175.6 9.9 %all_gather.22 = bf16[256,1024]{1,0:T(8,128)(2,1)S(1)} all-gather(bf16[256,256]{1,0:T(8,128)(2,1)S(1)} %fusion.2), channel_id=1, replica_groups=mesh['region'=128,'chan'=4] {'chan'}, dimensions={1}, use_global_device_ids=true | all-gather | bytes 655360 | tf_op jit(solution)/shard_map/all_gather | solution.py:17
  185.5 0.3 convolution_convert_fusion.1
  185.8 3.5 %collective-permute-start.8 = (bf16[256,256]{1,0:T(8,128)(2,1)S(1)}, bf16[256,256]{1,0:T(8,128)(2,1)S(1)}, u32[]{:S(2)}, u32[]{:S(2)}) collective-permute-start(bf16[256,256]{1,0:T(8,128)(2,1)S(1)} %convolution_convert_fusion.1), channel_id=1, source_target_pairs={{0,8},{4,12},{8,16},{12,20},{16,24},{20,28},{24,32},{28,36},{32,40... | collective-permute-start | bytes 393224 | tf_op jit(solution)/shard_map/ppermute | solution.py:12
  189.3 9.3 %collective-permute-start.9 = (bf16[256,256]{1,0:T(8,128)(2,1)S(1)}, bf16[256,256]{1,0:T(8,128)(2,1)S(1)}, u32[]{:S(2)}, u32[]{:S(2)}) collective-permute-start(bf16[256,256]{1,0:T(8,128)(2,1)S(1)} %convolution_convert_fusion.1), channel_id=1, source_target_pairs={{0,4},{4,8},{8,12},{12,16},{16,20},{20,24},{24,28},{28,32},{32,36}... | collective-permute-start | bytes 393224 | tf_op jit(solution)/shard_map/ppermute | solution.py:12
  198.7 1.1 convert_element_type.57
  199.7 1.9 collective-permute-start.10
  201.6 1.3 collective-permute-start.11
  203.0 3.0 %collective-permute-done.10 = bf16[256,256]{1,0:T(8,128)(2,1)S(1)} collective-permute-done((bf16[256,256]{1,0:T(8,128)(2,1)S(1)}, bf16[256,256]{1,0:T(8,128)(2,1)S(1)}, u32[]{:S(2)}, u32[]{:S(2)}) %collective-permute-start.10) | collective-permute-done | bytes 131104 | tf_op jit(solution)/shard_map/ppermute | solution.py:12
  206.0 2.6 collective-permute-done.11
  208.7 14.6 %gather_fusion.2 = bf16[4096,256]{1,0:T(8,128)(2,1)S(1)} fusion(bf16[1280,256]{1,0:T(8,128)(2,1)S(1)} %constant_dynamic-update-slice_fusion.10, s32[4096]{0:T(1024)S(1)} %bitcast_clamp_fusion), kind=kCustom, calls=%fused_computation.2 | custom fusion | bytes 4210688 | tf_op jit(solution)/shard_map/jit(_take)/gather | solution.py:37
  223.3 5.3 %select_reduce_fusion = f32[1024,256]{1,0:T(8,128)S(1)} fusion(f32[4,1024]{1,0:T(4,128)S(1)} %copy-done.14, f32[1024,256]{1,0:T(8,128)} %convert_element_type.57, bf16[4,1024,256]{2,1,0:T(8,128)(2,1)S(1)} %bitcast.26, pred[4,1024]{1,0:T(4,128)(4,1)S(1)} %get-tuple-element.9, pred[4,1024]{1,0:T(4,128)(4,1)S(1)} %get-tuple-element.8), kind=kLoop, calls=%fused_computation.3 | loop fusion | flops 10223616 | bytes 4218880 | tf_op jit(solution)/shard_map/reduce_sum | solution.py:40
  228.6 1.0 divide_convert_fusion
  229.6 40.5 %all-gather.5.cloned.1.call-done = bf16[1024,1024]{1,0:T(8,128)(2,1)} async-done(((bf16[1024,256]{1,0:T(8,128)(2,1)}), bf16[1024,1024]{1,0:T(8,128)(2,1)}) %all-gather.5.cloned.1.call-update) | async-done | bytes 2097168 | tf_op jit(solution)/shard_map/all_gather | solution.py:17
  270.1 3.2 %fusion = bf16[1024,256]{1,0:T(8,128)(2,1)} fusion(bf16[1024,1024]{1,0:T(8,128)(2,1)} %all-gather.5.cloned.1.call-done, bf16[1024,256]{1,0:T(8,128)(2,1)} %param.24, bf16[1024,256]{1,0:T(8,128)(2,1)S(1)} %copy-done.2), kind=kOutput, calls=%fused_computation.8 | convolution fusion | flops 537657344 | bytes 3670016 | tf_op jit(solution)/shard_map/dot_general | solution.py:16
  (72 shorter events, 0.6 us)
Async XLA Ops:
  7.2 47.4 %copy-start = (bf16[1024,256]{1,0:T(8,128)(2,1)S(1)}, bf16[1024,256]{1,0:T(8,128)(2,1)}, u32[]{:S(2)}) copy-start(bf16[1024,256]{1,0:T(8,128)(2,1)} %param.19) | copy-start | bytes 1572868
  7.2 47.4 %all-gather.3.cloned.1.call-start = ((), (), s32[]{:S(2)}) async-start(), calls=%async_computation | async-start | bytes 2621440 | tf_op jit(solution)/shard_map/all_gather | solution.py:17
  7.9 262.2 %all-gather.5.cloned.1.call-start = ((), (), s32[]{:S(2)}) async-start(), calls=%async_computation.1 | async-start | bytes 2621440 | tf_op jit(solution)/shard_map/all_gather | solution.py:17
  10.0 50.0 %copy-start.11 = (s32[8,256]{1,0:T(8,128)S(1)}, s32[8,256]{1,0:T(8,128)}, u32[]{:S(2)}) copy-start(s32[8,256]{1,0:T(8,128)} %param.28) | copy-start | bytes 24580
  10.1 54.8 %copy-start.10 = (s32[16,256]{1,0:T(8,128)S(1)}, s32[16,256]{1,0:T(8,128)}, u32[]{:S(2)}) copy-start(s32[16,256]{1,0:T(8,128)} %param.25) | copy-start | bytes 49156
  10.1 54.8 %copy-start.18 = (s32[256]{0:T(256)S(1)}, s32[256]{0:T(256)}, u32[]{:S(2)}) copy-start(s32[256]{0:T(256)} %param.27) | copy-start | bytes 3076
  10.1 59.8 %copy-start.4 = (bf16[256,256]{1,0:T(8,128)(2,1)S(1)}, bf16[256,256]{1,0:T(8,128)(2,1)}, u32[]{:S(2)}) copy-start(bf16[256,256]{1,0:T(8,128)(2,1)} %param.18) | copy-start | bytes 393220
  56.9 13.0 %collective-permute-start = (bf16[1024,256]{1,0:T(8,128)(2,1)S(1)}, bf16[1024,256]{1,0:T(8,128)(2,1)S(1)}, u32[]{:S(2)}, u32[]{:S(2)}) collective-permute-start(bf16[1024,256]{1,0:T(8,128)(2,1)S(1)} %convolution_convert_fusion), channel_id=1, source_target_pairs={{0,8},{4,12},{8,16},{12,20},{16,24},{20,28},{24,32},{28,36},{32,40... | collective-permute-start | bytes 1572872 | tf_op jit(solution)/shard_map/ppermute | solution.py:12
  60.1 17.3 %collective-permute-start.1 = (bf16[1024,256]{1,0:T(8,128)(2,1)S(1)}, bf16[1024,256]{1,0:T(8,128)(2,1)S(1)}, u32[]{:S(2)}, u32[]{:S(2)}) collective-permute-start(bf16[1024,256]{1,0:T(8,128)(2,1)S(1)} %convolution_convert_fusion), channel_id=1, source_target_pairs={{0,4},{4,8},{8,12},{12,16},{16,20},{20,24},{24,28},{28,32},{32,36}... | collective-permute-start | bytes 1572872 | tf_op jit(solution)/shard_map/ppermute | solution.py:12
  65.5 14.7 %collective-permute-start.2 = (bf16[1024,256]{1,0:T(8,128)(2,1)S(1)}, bf16[1024,256]{1,0:T(8,128)(2,1)S(1)}, u32[]{:S(2)}, u32[]{:S(2)}) collective-permute-start(bf16[1024,256]{1,0:T(8,128)(2,1)S(1)} %convolution_convert_fusion), channel_id=1, source_target_pairs={{4,0},{8,4},{12,8},{16,12},{20,16},{24,20},{28,24},{32,28},{36,32}... | collective-permute-start | bytes 1572872 | tf_op jit(solution)/shard_map/ppermute | solution.py:12
  67.4 15.9 %collective-permute-start.3 = (bf16[1024,256]{1,0:T(8,128)(2,1)S(1)}, bf16[1024,256]{1,0:T(8,128)(2,1)S(1)}, u32[]{:S(2)}, u32[]{:S(2)}) collective-permute-start(bf16[1024,256]{1,0:T(8,128)(2,1)S(1)} %convolution_convert_fusion), channel_id=1, source_target_pairs={{8,0},{12,4},{16,8},{20,12},{24,16},{28,20},{32,24},{36,28},{40,32... | collective-permute-start | bytes 1572872 | tf_op jit(solution)/shard_map/ppermute | solution.py:12
  101.6 5.6 %copy-start.17 = (f32[256]{0:T(256)S(1)}, f32[256]{0:T(256)}, u32[]{:S(2)}) copy-start(f32[256]{0:T(256)} %convert_element_type.61) | copy-start | bytes 3076
  101.6 16.5 %copy-start.3 = (bf16[1024,256]{1,0:T(8,128)(2,1)S(1)}, bf16[1024,256]{1,0:T(8,128)(2,1)}, u32[]{:S(2)}) copy-start(bf16[1024,256]{1,0:T(8,128)(2,1)} %param.20) | copy-start | bytes 1572868
  101.6 26.7 %copy-start.6 = (bf16[1024,256]{1,0:T(8,128)(2,1)S(1)}, bf16[1024,256]{1,0:T(8,128)(2,1)}, u32[]{:S(2)}) copy-start(bf16[1024,256]{1,0:T(8,128)(2,1)} %param.21) | copy-start | bytes 1572868
  107.2 39.2 %copy-start.12 = (s32[8,256]{1,0:T(8,128)S(1)}, s32[8,256]{1,0:T(8,128)}, u32[]{:S(2)}) copy-start(s32[8,256]{1,0:T(8,128)} %param.28) | copy-start | bytes 24580
  107.2 39.2 %copy-start.19 = (s32[256]{0:T(256)S(1)}, s32[256]{0:T(256)}, u32[]{:S(2)}) copy-start(s32[256]{0:T(256)} %param.30) | copy-start | bytes 3076
  107.3 48.1 %copy-start.13 = (s32[2048]{0:T(1024)S(1)}, s32[2048]{0:T(1024)}, u32[]{:S(2)}) copy-start(s32[2048]{0:T(1024)} %broadcast_clamp_fusion.1) | copy-start | bytes 24580
  128.6 21.0 %collective-permute-start.4 = (bf16[256,256]{1,0:T(8,128)(2,1)S(1)}, bf16[256,256]{1,0:T(8,128)(2,1)S(1)}, u32[]{:S(2)}, u32[]{:S(2)}) collective-permute-start(bf16[256,256]{1,0:T(8,128)(2,1)S(1)} %convolution_convert_fusion.2), channel_id=1, source_target_pairs={{0,8},{4,12},{8,16},{12,20},{16,24},{20,28},{24,32},{28,36},{32,40... | collective-permute-start | bytes 393224 | tf_op jit(solution)/shard_map/ppermute | solution.py:12
  132.4 17.3 %collective-permute-start.5 = (bf16[256,256]{1,0:T(8,128)(2,1)S(1)}, bf16[256,256]{1,0:T(8,128)(2,1)S(1)}, u32[]{:S(2)}, u32[]{:S(2)}) collective-permute-start(bf16[256,256]{1,0:T(8,128)(2,1)S(1)} %convolution_convert_fusion.2), channel_id=1, source_target_pairs={{0,4},{4,8},{8,12},{12,16},{16,20},{20,24},{24,28},{28,32},{32,36}... | collective-permute-start | bytes 393224 | tf_op jit(solution)/shard_map/ppermute | solution.py:12
  146.4 6.3 %collective-permute-start.6 = (bf16[256,256]{1,0:T(8,128)(2,1)S(1)}, bf16[256,256]{1,0:T(8,128)(2,1)S(1)}, u32[]{:S(2)}, u32[]{:S(2)}) collective-permute-start(bf16[256,256]{1,0:T(8,128)(2,1)S(1)} %convolution_convert_fusion.2), channel_id=1, source_target_pairs={{4,0},{8,4},{12,8},{16,12},{20,16},{24,20},{28,24},{32,28},{36,32}... | collective-permute-start | bytes 393224 | tf_op jit(solution)/shard_map/ppermute | solution.py:12
  148.3 7.0 %collective-permute-start.7 = (bf16[256,256]{1,0:T(8,128)(2,1)S(1)}, bf16[256,256]{1,0:T(8,128)(2,1)S(1)}, u32[]{:S(2)}, u32[]{:S(2)}) collective-permute-start(bf16[256,256]{1,0:T(8,128)(2,1)S(1)} %convolution_convert_fusion.2), channel_id=1, source_target_pairs={{8,0},{12,4},{16,8},{20,12},{24,16},{28,20},{32,24},{36,28},{40,32... | collective-permute-start | bytes 393224 | tf_op jit(solution)/shard_map/ppermute | solution.py:12
  155.4 7.5 %copy-start.16 = (f32[8,256]{1,0:T(8,128)S(1)}, f32[8,256]{1,0:T(8,128)}, u32[]{:S(2)}) copy-start(f32[8,256]{1,0:T(8,128)} %param.29) | copy-start | bytes 24580
  162.9 12.3 %copy-start.7 = (bf16[1024,256]{1,0:T(8,128)(2,1)S(1)}, bf16[1024,256]{1,0:T(8,128)(2,1)}, u32[]{:S(2)}) copy-start(bf16[1024,256]{1,0:T(8,128)(2,1)} %param.22) | copy-start | bytes 1572868
  162.9 22.5 %copy-start.8 = (bf16[1024,256]{1,0:T(8,128)(2,1)S(1)}, bf16[1024,256]{1,0:T(8,128)(2,1)}, u32[]{:S(2)}) copy-start(bf16[1024,256]{1,0:T(8,128)(2,1)} %param.23) | copy-start | bytes 1572868
  162.9 35.7 %copy-start.9 = (s32[4,1024]{1,0:T(4,128)S(1)}, s32[4,1024]{1,0:T(4,128)}, u32[]{:S(2)}) copy-start(s32[4,1024]{1,0:T(4,128)} %param.31) | copy-start | bytes 49156
  163.0 35.6 %copy-start.15 = (s32[1024]{0:T(1024)S(1)}, s32[1024]{0:T(1024)}, u32[]{:S(2)}) copy-start(s32[1024]{0:T(1024)} %param.33) | copy-start | bytes 12292
  163.0 35.7 %copy-start.1 = (bf16[1024,256]{1,0:T(8,128)(2,1)S(1)}, bf16[1024,256]{1,0:T(8,128)(2,1)}, u32[]{:S(2)}) copy-start(bf16[1024,256]{1,0:T(8,128)(2,1)} %param.17) | copy-start | bytes 1572868
  175.6 47.7 %copy-start.5 = (bf16[256,256]{1,0:T(8,128)(2,1)}, bf16[256,256]{1,0:T(8,128)(2,1)S(1)}, u32[]{:S(2)}) copy-start(bf16[256,256]{1,0:T(8,128)(2,1)S(1)} %fusion.2) | copy-start | bytes 393220
  185.8 17.2 %collective-permute-start.8 = (bf16[256,256]{1,0:T(8,128)(2,1)S(1)}, bf16[256,256]{1,0:T(8,128)(2,1)S(1)}, u32[]{:S(2)}, u32[]{:S(2)}) collective-permute-start(bf16[256,256]{1,0:T(8,128)(2,1)S(1)} %convolution_convert_fusion.1), channel_id=1, source_target_pairs={{0,8},{4,12},{8,16},{12,20},{16,24},{20,28},{24,32},{28,36},{32,40... | collective-permute-start | bytes 393224 | tf_op jit(solution)/shard_map/ppermute | solution.py:12
  189.3 13.7 %collective-permute-start.9 = (bf16[256,256]{1,0:T(8,128)(2,1)S(1)}, bf16[256,256]{1,0:T(8,128)(2,1)S(1)}, u32[]{:S(2)}, u32[]{:S(2)}) collective-permute-start(bf16[256,256]{1,0:T(8,128)(2,1)S(1)} %convolution_convert_fusion.1), channel_id=1, source_target_pairs={{0,4},{4,8},{8,12},{12,16},{16,20},{20,24},{24,28},{28,32},{32,36}... | collective-permute-start | bytes 393224 | tf_op jit(solution)/shard_map/ppermute | solution.py:12
  199.7 6.3 %collective-permute-start.10 = (bf16[256,256]{1,0:T(8,128)(2,1)S(1)}, bf16[256,256]{1,0:T(8,128)(2,1)S(1)}, u32[]{:S(2)}, u32[]{:S(2)}) collective-permute-start(bf16[256,256]{1,0:T(8,128)(2,1)S(1)} %convolution_convert_fusion.1), channel_id=1, source_target_pairs={{4,0},{8,4},{12,8},{16,12},{20,16},{24,20},{28,24},{32,28},{36,32}... | collective-permute-start | bytes 393224 | tf_op jit(solution)/shard_map/ppermute | solution.py:12
  201.6 7.0 %collective-permute-start.11 = (bf16[256,256]{1,0:T(8,128)(2,1)S(1)}, bf16[256,256]{1,0:T(8,128)(2,1)S(1)}, u32[]{:S(2)}, u32[]{:S(2)}) collective-permute-start(bf16[256,256]{1,0:T(8,128)(2,1)S(1)} %convolution_convert_fusion.1), channel_id=1, source_target_pairs={{8,0},{12,4},{16,8},{20,12},{24,16},{28,20},{32,24},{36,28},{40,32... | collective-permute-start | bytes 393224 | tf_op jit(solution)/shard_map/ppermute | solution.py:12
  208.6 14.6 %copy-start.14 = (f32[4,1024]{1,0:T(4,128)S(1)}, f32[4,1024]{1,0:T(4,128)}, u32[]{:S(2)}) copy-start(f32[4,1024]{1,0:T(4,128)} %param.32) | copy-start | bytes 49156
  223.3 46.8 %copy-start.2 = (bf16[1024,256]{1,0:T(8,128)(2,1)S(1)}, bf16[1024,256]{1,0:T(8,128)(2,1)}, u32[]{:S(2)}) copy-start(bf16[1024,256]{1,0:T(8,128)(2,1)} %param.17) | copy-start | bytes 1572868
Sparse Core Ops, SparseCore 0:
  10.1 44.4 all-gather.2
  229.7 40.3 all-gather.4
where the time goes:
time: 281 us; the launch traced here: 280 us
  waiting for transfers between devices  110 us (39%)
  starting transfers between devices  48.1 us (17%)
  blocking collectives  41.5 us (15%)
  local copies, waits for them, and re-layouts  40.8 us (15%)
  other arithmetic  18.3 us (7%)
  between operations  14.6 us (5%)
  matrix products  6.68 us (2%)
    all_gather x2, waiting for transfers between devices, project(): lax.all_gather(values, 'chan', axis=1, tiled=True)  85 us
    ppermute x12, starting transfers between devices, from_behind(): return lax.ppermute(shard, axis, pairs)  48.1 us
    all_gather x4, blocking collectives, project(): lax.all_gather(values, 'chan', axis=1, tiled=True)  41.5 us
    gather x3, local copies, waits for them, and re-layouts, messages(): fetched = jnp.take(projected, index_block, axis=0).astype(jnp.float32)  40.4 us
    ppermute x12, waiting for transfers between devices, from_behind(): return lax.ppermute(shard, axis, pairs)  24.4 us
    reduce_sum x3, other arithmetic, messages(): summed = jnp.sum(jnp.where(valid[:, :, None], message, 0.0), axis=0)  12.1 us
    dot_general x6, matrix products, project(): jnp.dot(lax.all_gather(values, 'chan', axis=1, tiled=True), weight, prefe...  6.68 us
  transfers between devices with their start and end apart: 14, of which 9 were waited for; matrix products, arithmetic and copies ran while one was open for 2% of the time, Pallas kernels for 0%

commit v1 on v0

v1 whole, which is shorter than its diff:
```python
import functools

import jax
import jax.numpy as jnp
from jax import lax
from jax.experimental import pallas as pl
from jax.experimental.pallas import tpu as pltpu
from jax.sharding import PartitionSpec as P

LANES = 128
TILE = 8
VMEM = pl.BlockSpec(memory_space=pltpu.VMEM)
HBM = pl.BlockSpec(memory_space=pltpu.HBM)
SMEM = pl.BlockSpec(memory_space=pltpu.SMEM)


def exchange(shard, axis, partner):
    n = lax.axis_size(axis)
    return lax.ppermute(shard, axis, [(i, partner(i)) for i in range(n)])


def shift(shard, by):
    n = lax.axis_size("region")
    return lax.ppermute(shard, "region", [(i, i + by) for i in range(n) if 0 <= i + by < n])


def core_pair(shard):
    n = lax.axis_size("region")
    groups = [[i, i + 1] for i in range(0, n, 2)]
    return lax.all_gather(shard, "region", axis=0, tiled=True, axis_index_groups=groups)


def gather_chan(values):
    return lax.all_gather(values, "chan", axis=1, tiled=True)


def dot(a, b):
    return jnp.dot(a, b, preferred_element_type=jnp.float32)


def partial_kernel(me_ref, own, near_top, near_low, other_top, other_low, weight, total):
    me = me_ref[0]
    rows, width = own.shape
    half = rows // 2

    def block_of(source):
        return weight[pl.ds(pl.multiple_of(source * width, width), width), :]

    mine, near, other = block_of(me), block_of(me ^ 1), block_of(3 - me)
    for first, from_near, from_other in ((0, near_top, other_top), (half, near_low, other_low)):
        at = slice(first, first + half)
        total[at, :] = dot(own[at, :], mine) + dot(from_near[...], near) + dot(from_other[...], other)


def last_kernel(me_ref, total, far_top, far_low, weight, *refs):
    base, out = refs[:-1], refs[-1]
    rows, width = total.shape
    half = rows // 2
    block = weight[pl.ds(pl.multiple_of((me_ref[0] ^ 2) * width, width), width), :]
    for first, far in ((0, far_top), (half, far_low)):
        at = slice(first, first + half)
        value = total[at, :] + dot(far[...], block)
        for ref in base:
            value = value + ref[at, :].astype(jnp.float32)
        out[at, :] = value.astype(out.dtype)


def project_by_exchanges(values, weight, base=()):
    assert lax.axis_size("chan") == 4
    me = lax.axis_index("chan").astype(jnp.int32)[None]
    rows, width = values.shape
    half = rows // 2
    near = functools.partial(exchange, axis="chan", partner=lambda i: i ^ 1)
    other = functools.partial(exchange, axis="chan", partner=lambda i: 3 - i)
    top, low = values[:half], values[half:]
    other_top, near_low = other(top), near(low)
    other_low, near_top = other(low), near(top)
    far_top, far_low = near(other_top), other(near_low)
    params = pltpu.CompilerParams(vmem_limit_bytes=10 << 20)
    total = pl.pallas_call(
        partial_kernel,
        out_shape=jax.ShapeDtypeStruct((rows, width), jnp.float32),
        in_specs=[SMEM] + [VMEM] * 6,
        out_specs=VMEM,
        compiler_params=params,
        cost_estimate=pl.CostEstimate(flops=6 * rows * width * width, bytes_accessed=10 * rows * width, transcendentals=0),
        name="first_blocks",
    )(me, values, near_top, near_low, other_top, other_low, weight)
    return pl.pallas_call(
        last_kernel,
        out_shape=jax.ShapeDtypeStruct((rows, width), values.dtype),
        in_specs=[SMEM] + [VMEM] * (4 + len(base)),
        out_specs=VMEM,
        compiler_params=params,
        cost_estimate=pl.CostEstimate(flops=2 * rows * width * width, bytes_accessed=10 * rows * width, transcendentals=0),
        name="last_block",
    )(me, total, far_top, far_low, weight, *base)


def combine_kernel(rows_ref, first, second, mixed, base):
    rows, width = rows_ref[...], first.shape[1]
    for at, weight in ((slice(0, width), first), (slice(width, 2 * width), second)):
        value = dot(rows, weight[...])
        base[:, at] = value
        mixed[:, at] = value.astype(mixed.dtype)


def combine(gathered, first, second, block):
    rows, depth = gathered.shape
    width = first.shape[1]
    whole = pl.BlockSpec((depth, width), lambda i: (0, 0))
    return pl.pallas_call(
        combine_kernel,
        grid=(rows // block,),
        out_shape=(
            jax.ShapeDtypeStruct((rows, 2 * width), gathered.dtype),
            jax.ShapeDtypeStruct((block, 2 * width), jnp.float32),
        ),
        in_specs=[pl.BlockSpec((block, depth), lambda i: (i, 0)), whole, whole],
        out_specs=(
            pl.BlockSpec((block, 2 * width), lambda i: (i, 0)),
            pl.BlockSpec((block, 2 * width), lambda i: (0, 0)),
        ),
        compiler_params=pltpu.CompilerParams(vmem_limit_bytes=10 << 20),
        cost_estimate=pl.CostEstimate(flops=4 * rows * depth * width, bytes_accessed=2 * rows * depth, transcendentals=0),
        name="combine",
    )(gathered, first, second)


def halves_dot(core, full, mine, other, rows, columns):
    half = full.shape[1] // 2
    first = pl.multiple_of(core * half, half)
    second = pl.multiple_of((1 - core) * half, half)
    return dot(full[:, pl.ds(first, half)], mine[rows, columns]) + dot(full[:, pl.ds(second, half)], other[rows, columns])


def mesh_one_kernel(core_ref, full, mesh, w_out, mine, other, base, mesh_one, projected, later):
    core, width = core_ref[0], mesh.shape[1]
    half = full.shape[1] // 2
    rows, one, two = slice(0, half), slice(0, width), slice(width, 2 * width)
    mesh_one[...] = (mesh[...].astype(jnp.float32) + dot(full[...], w_out[...])).astype(mesh_one.dtype)
    projected[...] = (base[:, one] + halves_dot(core, full, mine, other, rows, one)).astype(projected.dtype)
    later[...] = base[:, two] + halves_dot(core, full, mine, other, rows, two)


def mesh_next_kernel(core_ref, full, mesh_one, w_out, mine, other, later, mesh_next, projected):
    core, width = core_ref[0], mesh_one.shape[1]
    half = full.shape[1] // 2
    rows, two = slice(half, 2 * half), slice(width, 2 * width)
    mesh_next[...] = (mesh_one[...].astype(jnp.float32) + dot(full[...], w_out[...])).astype(mesh_next.dtype)
    projected[...] = (later[...] + halves_dot(core, full, mine, other, rows, two)).astype(projected.dtype)


def mesh_step(kernel, like, kinds, core, *operands):
    return pl.pallas_call(
        kernel,
        out_shape=[jax.ShapeDtypeStruct(like.shape, kind) for kind in kinds],
        in_specs=[SMEM] + [VMEM] * len(operands),
        out_specs=[VMEM] * len(kinds),
        compiler_params=pltpu.CompilerParams(vmem_limit_bytes=10 << 20),
        cost_estimate=pl.CostEstimate(flops=len(kinds) << 27, bytes_accessed=1 << 22, transcendentals=0),
        name="mesh_step",
    )(core, *operands)


def window_of_exchanges(projected):
    below = shift(projected, 2)
    above = shift(projected, -2)
    other = exchange(projected, "region", lambda i: i ^ 1)
    first = lax.axis_index("region") % 2 == 0
    third = exchange(jnp.where(first, above, below), "region", lambda i: i ^ 1)
    return [projected, below, above, other, third]


def window_of_pairs(projected):
    below = shift(projected, 2)
    above = shift(projected, -2)
    own = core_pair(projected)
    first = lax.axis_index("region") % 2 == 0
    outer = core_pair(jnp.where(first, above, below))
    last = jnp.where(first, below, above)
    return [outer, own, last]


def edges_kernel(n_grid, n_mesh, me_ref, *refs):
    sources, (o1, s1, o2, s2, o3, s3) = refs[:9], refs[9:15]
    i1, w1, c1, i2, w2, c2, i3, w3, c3 = held = refs[15:24]
    copies = [pltpu.make_async_copy(src, dst, refs[24].at[k]) for k, (src, dst) in enumerate(zip(sources, held))]
    for copy in copies:
        copy.start()
    for copy in copies:
        copy.wait()
    me = me_ref[0]
    core = me & 1

    def of_exchanges(apart):
        towards = 1 - 2 * core
        return jnp.where(apart == 0, 0, jnp.where(apart == -2, 1, jnp.where(apart == 2, 2, jnp.where(apart == towards, 3, 4))))

    def of_pairs(apart):
        apart = apart + core
        return jnp.where(apart == 2, 0, jnp.where(apart == -1, 1, jnp.where(apart == 0, 2, jnp.where(apart == 1, 3, 4))))

    def place(index, rows, piece):
        shift_by = rows.bit_length() - 1
        return (piece((index >> shift_by) - me) << shift_by) + (index & (rows - 1))

    def scaled(w, c):
        live = lax.broadcasted_iota(jnp.int32, w.shape, 0) < c[...]
        return jnp.where(live, w[...], 0.0) / c[...].astype(jnp.float32)

    def upright(v):
        if v.shape[0] < TILE:
            v = jnp.concatenate([v, jnp.zeros((TILE - v.shape[0], v.shape[1]), v.dtype)], axis=0)
        return v.T

    o1[...] = 2 * place(i1[...], n_grid, of_exchanges)
    tall = upright(scaled(w1, c1))
    for s in range(2):
        s1[pl.ds(s, tall.shape[0], 2), :] = tall
    o2[...] = upright(place(i2[...], n_mesh, of_pairs))
    s2[...] = upright(scaled(w2, c2))
    o3[...] = upright(place(i3[...], n_mesh, of_pairs))
    s3[...] = upright(scaled(w3, c3))


def edges(n_grid, n_mesh, g2m, m2m, m2g):
    me = lax.axis_index("region").astype(jnp.int32)[None]
    ops, outs = [me], []
    for at, (index, weight, count) in enumerate((g2m, m2m, m2g)):
        slots, rows = index.shape
        ops += [index, weight, count[None, :]]
        high = max(slots, TILE)
        outs += [
            jax.ShapeDtypeStruct((slots, rows) if at == 0 else (rows, high), jnp.int32),
            jax.ShapeDtypeStruct((2 * rows if at == 0 else rows, high), jnp.float32),
        ]
    return pl.pallas_call(
        functools.partial(edges_kernel, n_grid, n_mesh),
        out_shape=outs,
        in_specs=[SMEM] + [HBM] * 9,
        out_specs=[VMEM] * 6,
        scratch_shapes=[pltpu.VMEM(op.shape, op.dtype) for op in ops[1:]] + [pltpu.SemaphoreType.DMA((9,))],
        compiler_params=pltpu.CompilerParams(vmem_limit_bytes=60 << 20),
        cost_estimate=pl.CostEstimate(flops=1 << 20, bytes_accessed=1 << 20, transcendentals=0),
        name="edges",
    )(*ops)


def by_rows_kernel(slots, rows, group, sizes, index_ref, weight_ref, receiver_ref, *refs):
    parts, out_ref = refs[: len(sizes)], refs[len(sizes)]
    window, receiver, fetched, total = refs[len(sizes) + 1 :]
    first = 0
    for part, size in zip(parts, sizes):
        half = part[...].astype(jnp.float32) * 0.5
        for s in range(2):
            window[pl.ds(2 * first + s, size, 2), :] = half[:, s * LANES : (s + 1) * LANES]
        first += size
    half = receiver_ref[...].astype(jnp.float32) * 0.5
    for s in range(2):
        receiver[pl.ds(s, rows, 2), :] = half[:, s * LANES : (s + 1) * LANES]

    def fetch(start, side):
        for u in range(group):
            for k in range(slots):
                at = ((u // 4) * slots + k) * TILE + (u % 4) * 2
                fetched[side, at : at + 2, :] = window[pl.ds(index_ref[k, start + u], 2), :]

    def add_up(start, side):
        for t in range(group // 4):
            row = pl.multiple_of(2 * start + TILE * t, TILE)
            mine = receiver[pl.ds(row, TILE), :]
            weight = weight_ref[pl.ds(row, TILE), :]
            acc = jnp.zeros((TILE, LANES), jnp.float32)
            for k in range(slots):
                at = (t * slots + k) * TILE
                h = fetched[side, at : at + TILE, :] + mine
                acc = acc + (h + h * jnp.tanh(h)) * weight[:, k : k + 1]
            total[pl.ds(row, TILE), :] = acc

    fetch(0, 0)

    def two_groups(j, carry):
        start = j * 2 * group
        fetch(start + group, 1)
        add_up(start, 0)
        fetch(jnp.minimum(start + 2 * group, rows - group), 0)
        add_up(start + group, 1)
        return carry

    lax.fori_loop(0, rows // (2 * group), two_groups, 0)
    for s in range(2):
        out_ref[:, s * LANES : (s + 1) * LANES] = total[pl.ds(s, rows, 2), :].astype(out_ref.dtype)


def aggregate_by_rows(index, weights, receivers, parts, group=8):
    slots, rows = index.shape
    width = receivers.shape[1]
    sizes = tuple(part.shape[0] for part in parts)
    return pl.pallas_call(
        functools.partial(by_rows_kernel, slots, rows, group, sizes),
        out_shape=jax.ShapeDtypeStruct((rows, width), receivers.dtype),
        in_specs=[SMEM] + [VMEM] * (2 + len(parts)),
        out_specs=VMEM,
        scratch_shapes=[
            pltpu.VMEM((2 * sum(sizes), LANES), jnp.float32),
            pltpu.VMEM((2 * rows, LANES), jnp.float32),
            pltpu.VMEM((2, group // 4 * slots * TILE, LANES), jnp.float32),
            pltpu.VMEM((2 * rows, LANES), jnp.float32),
        ],
        compiler_params=pltpu.CompilerParams(vmem_limit_bytes=14 << 20),
        cost_estimate=pl.CostEstimate(
            flops=6 * slots * rows * width,
            bytes_accessed=2 * width * (sum(sizes) + 2 * rows),
            transcendentals=slots * rows * width,
        ),
        name="aggregate_by_rows",
    )(index, weights, receivers, *parts)


def by_matmul_kernel(slots, rows, block, sizes, index_ref, weight_ref, receiver_ref, *refs):
    parts, out_ref, window = refs[: len(sizes)], refs[len(sizes)], refs[len(sizes) + 1]
    first = 0
    for part, size in zip(parts, sizes):
        window[first : first + size, :] = part[...]
        first += size
    columns = lax.broadcasted_iota(jnp.int32, (block, first), 1).astype(jnp.int16)
    one, zero = jnp.bfloat16(1), jnp.bfloat16(0)

    def one_block(b, carry):
        at = pl.ds(pl.multiple_of(b * block, block), block)
        mine = receiver_ref[at, :].astype(jnp.float32)
        index, weight = index_ref[at, :], weight_ref[at, :]
        acc = jnp.zeros(mine.shape, jnp.float32)
        for k in range(slots):
            wanted = jnp.broadcast_to(index[:, k : k + 1], (block, LANES)).astype(jnp.int16)
            pick = [jnp.where(columns[:, j : j + LANES] == wanted, one, zero) for j in range(0, first, LANES)]
            fetched = dot(jnp.concatenate(pick, axis=1), window[...])
            h = (fetched + mine) * 0.5
            acc = acc + (h + h * jnp.tanh(h)) * weight[:, k : k + 1]
        out_ref[at, :] = acc.astype(out_ref.dtype)
        return carry

    lax.fori_loop(0, rows // block, one_block, 0)


def aggregate_by_matmul(slots, index, weights, receivers, parts, block=256):
    rows, width = receivers.shape
    sizes = tuple(part.shape[0] for part in parts)
    return pl.pallas_call(
        functools.partial(by_matmul_kernel, slots, rows, block, sizes),
        out_shape=jax.ShapeDtypeStruct((rows, width), receivers.dtype),
        in_specs=[VMEM] * (3 + len(parts)),
        out_specs=VMEM,
        scratch_shapes=[pltpu.VMEM((sum(sizes), width), jnp.bfloat16)],
        compiler_params=pltpu.CompilerParams(vmem_limit_bytes=14 << 20),
        cost_estimate=pl.CostEstimate(
            flops=2 * slots * rows * sum(sizes) * width,
            bytes_accessed=2 * width * (sum(sizes) + 2 * rows),
            transcendentals=slots * rows * width,
        ),
        name="aggregate_by_matmul",
    )(index, weights, receivers, *parts)


def shards(
    grid_state,
    mesh_state,
    enc_send,
    enc_out,
    proc_send,
    proc_out,
    dec_send,
    dec_out,
    g2m_index,
    g2m_weight,
    g2m_count,
    m2m_index,
    m2m_weight,
    m2m_count,
    m2g_index,
    m2g_weight,
    m2g_count,
):
    n_grid, n_mesh = grid_state.shape[0], mesh_state.shape[0]
    bf16, f32 = jnp.bfloat16, jnp.float32
    k_m, k_d = m2m_index.shape[0], m2g_index.shape[0]
    prepared = edges(
        n_grid,
        n_mesh,
        (g2m_index, g2m_weight, g2m_count),
        (m2m_index, m2m_weight, m2m_count),
        (m2g_index, m2g_weight, m2g_count),
    )

    grid_state, prepared = lax.optimization_barrier((grid_state, prepared))
    g2m, g2m_w, m2m, m2m_w, m2g, m2g_w = prepared

    core = lax.axis_index("region").astype(jnp.int32) % 2
    half = enc_out.shape[0] // 2
    own_rows = [lax.dynamic_slice_in_dim(w, core * half, half, axis=0) for w in (enc_out, proc_out)]
    gathered = gather_chan(jnp.concatenate(own_rows + [mesh_state], axis=0))

    projected = project_by_exchanges(grid_state, enc_send)
    agg = aggregate_by_rows(g2m, g2m_w, mesh_state, window_of_exchanges(projected))

    agg, gathered = lax.optimization_barrier((agg, gathered))
    mine, base = combine(gathered, proc_send, dec_send, n_mesh)
    other = exchange(mine[: 2 * half], "region", lambda i: i ^ 1)
    agg, base = lax.optimization_barrier((agg, base))
    mesh_one, projected, later = mesh_step(
        mesh_one_kernel, mesh_state, (bf16, bf16, f32), core[None], gather_chan(agg), mesh_state, enc_out, mine, other, base
    )
    agg = aggregate_by_matmul(k_m, m2m, m2m_w, mesh_one, window_of_pairs(projected))
    mesh_next, projected = mesh_step(
        mesh_next_kernel, mesh_state, (bf16, bf16), core[None], gather_chan(agg), mesh_one, proc_out, mine, other, later
    )
    agg = aggregate_by_matmul(k_d, m2g, m2g_w, grid_state, window_of_pairs(projected))
    grid_next = project_by_exchanges(agg, dec_out, base=(grid_state,))
    return grid_next, mesh_next


def solution(mesh):
    by_both, by_chan = P("region", "chan"), P(None, "chan")
    edge = (P(None, "region"), P(None, "region"), P("region"))
    return jax.shard_map(
        shards,
        mesh=mesh,
        in_specs=(by_both,) * 2 + (by_chan,) * 6 + edge * 3,
        out_specs=(by_both, by_both),
        check_vma=False,
    )
```

time: 281 us -> 184 us (0.65)
  the two profiles are of different devices: /device:TPU:1 before, /device:TPU:248 now
where the time goes in v1:
time: 184 us; the launch traced here: 183 us
  starting transfers between devices  63.5 us (35%)
  waiting for transfers between devices  43.5 us (24%)
  blocking collectives  34.2 us (19%)
  Pallas kernels  21.5 us (12%)
  between operations  14.5 us (8%)
  local copies, waits for them, and re-layouts  4.11 us (2%)
  other arithmetic  1.94 us (1%)
    ppermute x15, starting transfers between devices, exchange(): return lax.ppermute(shard, axis, [(i, partner(i)) for i in range(n)])  44.8 us
    all_gather x2, blocking collectives, gather_chan(): return lax.all_gather(values, 'chan', axis=1, tiled=True)  26.2 us
    ppermute x15, waiting for transfers between devices, exchange(): return lax.ppermute(shard, axis, [(i, partner(i)) for i in range(n)])  23.1 us
    ppermute x6, waiting for transfers between devices, shift(): lax.ppermute(shard, 'region', [(i, i + by) for i in range(n) if 0 <= i +...  20.4 us
    ppermute x6, starting transfers between devices, shift(): lax.ppermute(shard, 'region', [(i, i + by) for i in range(n) if 0 <= i +...  18.7 us
    all_gather x4, blocking collectives, core_pair(): lax.all_gather(shard, 'region', axis=0, tiled=True, axis_index_groups=gro...  7.98 us
    pallas_call x1, Pallas kernels, aggregate_by_rows(): pl.pallas_call(functools.partial(by_rows_kernel, slots, rows, group, size...  6.85 us
    pallas_call x2, Pallas kernels, aggregate_by_matmul(): pl.pallas_call(functools.partial(by_matmul_kernel, slots, rows, block, si...  5.99 us
  transfers between devices with their start and end apart: 22, of which 15 were waited for; matrix products, arithmetic and copies ran while one was open for 0% of the time, Pallas kernels for 6%

profile of v1, /device:TPU:248, one launch (start us, length us, event | category | flops | bytes accessed | tf_op | source)
XLA Modules:
  0.0 183.2 jit_solution(13615670440091624408)
XLA Ops:
  7.2 1.1 constant_dynamic-slice_fusion
  8.4 1.8 %pad_maximum_fusion = bf16[1280,256]{1,0:T(8,128)(2,1)} fusion(bf16[256,256]{1,0:T(8,128)(2,1)} %mesh.1, bf16[512,256]{1,0:T(8,128)(2,1)S(1)} %get-tuple-element.58, bf16[512,256]{1,0:T(8,128)(2,1)S(1)} %get-tuple-element.59), kind=kLoop, calls=%fused_computation | loop fusion | flops 1966080 | bytes 1310720 | tf_op jit(solution)/shard_map/concatenate | solution.py:402
  10.2 2.2 %edges.1 = (s32[16,256]{1,0:T(8,128)}, f32[512,16]{1,0:T(8,128)}, s32[256,8]{1,0:T(8,128)}, f32[256,8]{1,0:T(8,128)}, s32[1024,8]{1,0:T(8,128)}, /*index=5*/f32[1024,8]{1,0:T(8,128)}) custom-call(s32[1]{0:T(128)} %bitcast.1.me_ref, s32[16,256]{1,0:T(8,128)} %refs_0_.1, f32[16,256]{1,0:T(8,128)} %refs_1_.1, s32[1,256]{1,0:T(1,128)} %bitcast.7, ...), custom_call_target="tpu_custom_call" | custom-call | flops 1048576 | bytes 1048576 | tf_op jit(solution)/shard_map/edges/pallas_call | solution.py:238
  12.5 4.7 %collective-permute-start.2 = (bf16[512,256]{1,0:T(8,128)(2,1)S(1)}, bf16[512,256]{1,0:T(8,128)(2,1)S(1)}, u32[]{:S(2)}, u32[]{:S(2)}) collective-permute-start(bf16[512,256]{1,0:T(8,128)(2,1)S(1)} %get-tuple-element.53), channel_id=1, source_target_pairs={{0,3},{1,2},{2,1},{3,0},{4,7},{5,6},{6,5},{7,4},{8,11},{9,10},{10,... | collective-permute-start | bytes 786440 | tf_op jit(solution)/shard_map/ppermute | solution.py:19
  17.2 2.1 %collective-permute-start.1 = (bf16[512,256]{1,0:T(8,128)(2,1)S(1)}, bf16[512,256]{1,0:T(8,128)(2,1)S(1)}, u32[]{:S(2)}, u32[]{:S(2)}) collective-permute-start(bf16[512,256]{1,0:T(8,128)(2,1)S(1)} %get-tuple-element.52), channel_id=1, source_target_pairs={{0,1},{1,0},{2,3},{3,2},{4,5},{5,4},{6,7},{7,6},{8,9},{9,8},{10,11... | collective-permute-start | bytes 786440 | tf_op jit(solution)/shard_map/ppermute | solution.py:19
  19.3 3.7 %collective-permute-start = (bf16[512,256]{1,0:T(8,128)(2,1)S(1)}, bf16[512,256]{1,0:T(8,128)(2,1)S(1)}, u32[]{:S(2)}, u32[]{:S(2)}) collective-permute-start(bf16[512,256]{1,0:T(8,128)(2,1)S(1)} %get-tuple-element.53), channel_id=1, source_target_pairs={{0,1},{1,0},{2,3},{3,2},{4,5},{5,4},{6,7},{7,6},{8,9},{9,8},{10,11... | collective-permute-start | bytes 786440 | tf_op jit(solution)/shard_map/ppermute | solution.py:19
  23.0 2.4 %collective-permute-start.3 = (bf16[512,256]{1,0:T(8,128)(2,1)S(1)}, bf16[512,256]{1,0:T(8,128)(2,1)S(1)}, u32[]{:S(2)}, u32[]{:S(2)}) collective-permute-start(bf16[512,256]{1,0:T(8,128)(2,1)S(1)} %get-tuple-element.52), channel_id=1, source_target_pairs={{0,3},{1,2},{2,1},{3,0},{4,7},{5,6},{6,5},{7,4},{8,11},{9,10},{10,... | collective-permute-start | bytes 786440 | tf_op jit(solution)/shard_map/ppermute | solution.py:19
  25.5 2.2 %collective-permute-start.4 = (bf16[512,256]{1,0:T(8,128)(2,1)S(1)}, bf16[512,256]{1,0:T(8,128)(2,1)S(1)}, u32[]{:S(2)}, u32[]{:S(2)}) collective-permute-start(bf16[512,256]{1,0:T(8,128)(2,1)S(1)} %collective-permute-done.2.other_top), channel_id=1, source_target_pairs={{0,1},{1,0},{2,3},{3,2},{4,5},{5,4},{6,7},{7,6},{8,9},{9,8},{10,11... | collective-permute-start | bytes 786440 | tf_op jit(solution)/shard_map/ppermute | solution.py:19
  28.3 3.7 %collective-permute-start.5 = (bf16[512,256]{1,0:T(8,128)(2,1)S(1)}, bf16[512,256]{1,0:T(8,128)(2,1)S(1)}, u32[]{:S(2)}, u32[]{:S(2)}) collective-permute-start(bf16[512,256]{1,0:T(8,128)(2,1)S(1)} %collective-permute-done.1.near_low), channel_id=1, source_target_pairs={{0,3},{1,2},{2,1},{3,0},{4,7},{5,6},{6,5},{7,4},{8,11},{9,10},{10,... | collective-permute-start | bytes 786440 | tf_op jit(solution)/shard_map/ppermute | solution.py:19
  32.1 5.2 %collective-permute-done.near_top = bf16[512,256]{1,0:T(8,128)(2,1)S(1)} collective-permute-done((bf16[512,256]{1,0:T(8,128)(2,1)S(1)}, bf16[512,256]{1,0:T(8,128)(2,1)S(1)}, u32[]{:S(2)}, u32[]{:S(2)}) %collective-permute-start) | collective-permute-done | bytes 262176 | tf_op jit(solution)/shard_map/ppermute | solution.py:19
  37.3 2.0 %collective-permute-done.3.other_low = bf16[512,256]{1,0:T(8,128)(2,1)S(1)} collective-permute-done((bf16[512,256]{1,0:T(8,128)(2,1)S(1)}, bf16[512,256]{1,0:T(8,128)(2,1)S(1)}, u32[]{:S(2)}, u32[]{:S(2)}) %collective-permute-start.3) | collective-permute-done | bytes 262176 | tf_op jit(solution)/shard_map/ppermute | solution.py:19
  39.9 5.2 %collective-permute-done.4.far_top = bf16[512,256]{1,0:T(8,128)(2,1)S(1)} collective-permute-done((bf16[512,256]{1,0:T(8,128)(2,1)S(1)}, bf16[512,256]{1,0:T(8,128)(2,1)S(1)}, u32[]{:S(2)}, u32[]{:S(2)}) %collective-permute-start.4) | collective-permute-done | bytes 262176 | tf_op jit(solution)/shard_map/ppermute | solution.py:19
  46.3 4.8 %collective-permute-start.6 = (bf16[1024,256]{1,0:T(8,128)(2,1)S(1)}, bf16[1024,256]{1,0:T(8,128)(2,1)S(1)}, u32[]{:S(2)}, u32[]{:S(2)}) collective-permute-start(bf16[1024,256]{1,0:T(8,128)(2,1)S(1)} %last_block.2.refs_0_), channel_id=1, source_target_pairs={{0,8},{4,12},{8,16},{12,20},{16,24},{20,28},{24,32},{28,36},{32,40... | collective-permute-start | bytes 1572872 | tf_op jit(solution)/shard_map/ppermute | solution.py:24
  51.2 1.9 %collective-permute-start.7 = (bf16[1024,256]{1,0:T(8,128)(2,1)S(1)}, bf16[1024,256]{1,0:T(8,128)(2,1)S(1)}, u32[]{:S(2)}, u32[]{:S(2)}) collective-permute-start(bf16[1024,256]{1,0:T(8,128)(2,1)S(1)} %last_block.2.refs_0_), channel_id=1, source_target_pairs={{8,0},{12,4},{16,8},{20,12},{24,16},{28,20},{32,24},{36,28},{40,32... | collective-permute-start | bytes 1572872 | tf_op jit(solution)/shard_map/ppermute | solution.py:24
  53.1 1.9 %collective-permute-start.8 = (bf16[1024,256]{1,0:T(8,128)(2,1)S(1)}, bf16[1024,256]{1,0:T(8,128)(2,1)S(1)}, u32[]{:S(2)}, u32[]{:S(2)}) collective-permute-start(bf16[1024,256]{1,0:T(8,128)(2,1)S(1)} %last_block.2.refs_0_), channel_id=1, source_target_pairs={{0,4},{4,0},{8,12},{12,8},{16,20},{20,16},{24,28},{28,24},{32,36},... | collective-permute-start | bytes 1572872 | tf_op jit(solution)/shard_map/ppermute | solution.py:19
  55.0 4.4 %collective-permute-done.6.refs_1_ = bf16[1024,256]{1,0:T(8,128)(2,1)S(1)} collective-permute-done((bf16[1024,256]{1,0:T(8,128)(2,1)S(1)}, bf16[1024,256]{1,0:T(8,128)(2,1)S(1)}, u32[]{:S(2)}, u32[]{:S(2)}) %collective-permute-start.6) | collective-permute-done | bytes 524320 | tf_op jit(solution)/shard_map/ppermute | solution.py:24
  59.4 7.4 %collective-permute-done.7.refs_2_ = bf16[1024,256]{1,0:T(8,128)(2,1)S(1)} collective-permute-done((bf16[1024,256]{1,0:T(8,128)(2,1)S(1)}, bf16[1024,256]{1,0:T(8,128)(2,1)S(1)}, u32[]{:S(2)}, u32[]{:S(2)}) %collective-permute-start.7) | collective-permute-done | bytes 524320 | tf_op jit(solution)/shard_map/ppermute | solution.py:24
  67.0 2.1 %collective-permute-start.9 = (bf16[1024,256]{1,0:T(8,128)(2,1)S(1)}, bf16[1024,256]{1,0:T(8,128)(2,1)S(1)}, u32[]{:S(2)}, u32[]{:S(2)}) collective-permute-start(bf16[1024,256]{1,0:T(8,128)(2,1)S(1)} %broadcast_select_fusion), channel_id=1, source_target_pairs={{0,4},{4,0},{8,12},{12,8},{16,20},{20,16},{24,28},{28,24},{32,36},... | collective-permute-start | bytes 1572872 | tf_op jit(solution)/shard_map/ppermute | solution.py:19
  69.0 1.9 %collective-permute-done.9.refs_4_ = bf16[1024,256]{1,0:T(8,128)(2,1)S(1)} collective-permute-done((bf16[1024,256]{1,0:T(8,128)(2,1)S(1)}, bf16[1024,256]{1,0:T(8,128)(2,1)S(1)}, u32[]{:S(2)}, u32[]{:S(2)}) %collective-permute-start.9) | collective-permute-done | bytes 524320 | tf_op jit(solution)/shard_map/ppermute | solution.py:19
  70.9 6.8 %aggregate_by_rows.1 = bf16[256,256]{1,0:T(8,128)(2,1)S(1)} custom-call(s32[16,256]{1,0:T(8,128)S(1)} %copy-done.7, f32[512,16]{1,0:T(8,128)S(1)} %copy-done.6, bf16[256,256]{1,0:T(8,128)(2,1)S(1)} %copy-done.3, bf16[1024,256]{1,0:T(8,128)(2,1)S(1)} %last_block.2.refs_0_, bf16[1024,256]{1,0:T(8,128)(2,1)S(1)} %collective-permute-done.6.refs_1_, ...), custom_call_target="tpu_custom_call" | custom-call | flops 6291456 | bytes 2883584 | tf_op jit(solution)/shard_map/aggregate_by_rows/pallas_call | solution.py:300
  77.8 1.7 copy-done.8
  80.6 2.2 %combine.1 = (bf16[1280,512]{1,0:T(8,128)(2,1)S(1)}, f32[256,512]{1,0:T(8,128)S(1)}) custom-call(bf16[1280,1024]{1,0:T(8,128)(2,1)S(1)} %copy-done.8, bf16[1024,256]{1,0:T(8,128)(2,1)S(1)} %copy-done.9, bf16[1024,256]{1,0:T(8,128)(2,1)S(1)} %copy-done.10), custom_call_target="tpu_custom_call" | custom-call | flops 1342177280 | bytes 2621440 | tf_op jit(solution)/shard_map/combine/pallas_call | solution.py:112
  82.9 2.2 %collective-permute-start.10 = (bf16[1024,512]{1,0:T(8,128)(2,1)S(1)}, bf16[1024,512]{1,0:T(8,128)(2,1)S(1)}, u32[]{:S(2)}, u32[]{:S(2)}) collective-permute-start(bf16[1024,512]{1,0:T(8,128)(2,1)S(1)} %slice.17), channel_id=1, source_target_pairs={{0,4},{4,0},{8,12},{12,8},{16,20},{20,16},{24,28},{28,24},{32,36},... | collective-permute-start | bytes 3145736 | tf_op jit(solution)/shard_map/ppermute | solution.py:19
  85.1 12.9 %all_gather.22.full = bf16[256,1024]{1,0:T(8,128)(2,1)S(1)} all-gather(bf16[256,256]{1,0:T(8,128)(2,1)S(1)} %aggregate_by_rows.1), channel_id=1, replica_groups=mesh['region'=128,'chan'=4] {'chan'}, dimensions={1}, use_global_device_ids=true | all-gather | bytes 655360 | tf_op jit(solution)/shard_map/all_gather | solution.py:34
  98.6 2.1 %collective-permute-start.12 = (bf16[256,256]{1,0:T(8,128)(2,1)S(1)}, bf16[256,256]{1,0:T(8,128)(2,1)S(1)}, u32[]{:S(2)}, u32[]{:S(2)}) collective-permute-start(bf16[256,256]{1,0:T(8,128)(2,1)S(1)} %get-tuple-element.46), channel_id=1, source_target_pairs={{0,8},{4,12},{8,16},{12,20},{16,24},{20,28},{24,32},{28,36},{32,40... | collective-permute-start | bytes 393224 | tf_op jit(solution)/shard_map/ppermute | solution.py:24
  100.7 3.9 %collective-permute-start.11 = (bf16[256,256]{1,0:T(8,128)(2,1)S(1)}, bf16[256,256]{1,0:T(8,128)(2,1)S(1)}, u32[]{:S(2)}, u32[]{:S(2)}) collective-permute-start(bf16[256,256]{1,0:T(8,128)(2,1)S(1)} %get-tuple-element.46), channel_id=1, source_target_pairs={{8,0},{12,4},{16,8},{20,12},{24,16},{28,20},{32,24},{36,28},{40,32... | collective-permute-start | bytes 393224 | tf_op jit(solution)/shard_map/ppermute | solution.py:24
  104.6 2.0 %all_gather.24.refs_1_ = bf16[512,256]{1,0:T(8,128)(2,1)S(1)} all-gather(bf16[256,256]{1,0:T(8,128)(2,1)S(1)} %get-tuple-element.46), channel_id=1, replica_groups={{0,4},{8,12},{16,20},{24,28},{32,36},{40,44},{48,52},{56,60},{64,68},{7..., dimensions={0}, use_global_device_ids=true | all-gather | bytes 393216 | tf_op jit(solution)/shard_map/all_gather | solution.py:30
  106.6 4.3 %collective-permute-done.11 = bf16[256,256]{1,0:T(8,128)(2,1)S(1)} collective-permute-done((bf16[256,256]{1,0:T(8,128)(2,1)S(1)}, bf16[256,256]{1,0:T(8,128)(2,1)S(1)}, u32[]{:S(2)}, u32[]{:S(2)}) %collective-permute-start.11) | collective-permute-done | bytes 131104 | tf_op jit(solution)/shard_map/ppermute | solution.py:24
  110.9 2.0 %all_gather.23.refs_0_ = bf16[512,256]{1,0:T(8,128)(2,1)S(1)} all-gather(bf16[256,256]{1,0:T(8,128)(2,1)S(1)} %get-tuple-element.57), channel_id=1, replica_groups={{0,4},{8,12},{16,20},{24,28},{32,36},{40,44},{48,52},{56,60},{64,68},{7..., dimensions={0}, use_global_device_ids=true | all-gather | bytes 393216 | tf_op jit(solution)/shard_map/all_gather | solution.py:30
  112.9 1.8 aggregate_by_matmul.2
  114.7 13.3 %all_gather.25.full = bf16[256,1024]{1,0:T(8,128)(2,1)S(1)} all-gather(bf16[256,256]{1,0:T(8,128)(2,1)S(1)} %aggregate_by_matmul.2), channel_id=1, replica_groups=mesh['region'=128,'chan'=4] {'chan'}, dimensions={1}, use_global_device_ids=true | all-gather | bytes 655360 | tf_op jit(solution)/shard_map/all_gather | solution.py:34
  128.0 1.1 mesh_step.3
  129.1 2.0 %collective-permute-start.14 = (bf16[256,256]{1,0:T(8,128)(2,1)S(1)}, bf16[256,256]{1,0:T(8,128)(2,1)S(1)}, u32[]{:S(2)}, u32[]{:S(2)}) collective-permute-start(bf16[256,256]{1,0:T(8,128)(2,1)S(1)} %get-tuple-element.48), channel_id=1, source_target_pairs={{0,8},{4,12},{8,16},{12,20},{16,24},{20,28},{24,32},{28,36},{32,40... | collective-permute-start | bytes 393224 | tf_op jit(solution)/shard_map/ppermute | solution.py:24
  131.2 3.9 %collective-permute-start.13 = (bf16[256,256]{1,0:T(8,128)(2,1)S(1)}, bf16[256,256]{1,0:T(8,128)(2,1)S(1)}, u32[]{:S(2)}, u32[]{:S(2)}) collective-permute-start(bf16[256,256]{1,0:T(8,128)(2,1)S(1)} %get-tuple-element.48), channel_id=1, source_target_pairs={{8,0},{12,4},{16,8},{20,12},{24,16},{28,20},{32,24},{36,28},{40,32... | collective-permute-start | bytes 393224 | tf_op jit(solution)/shard_map/ppermute | solution.py:24
  135.1 2.0 %all_gather.27.refs_1_ = bf16[512,256]{1,0:T(8,128)(2,1)S(1)} all-gather(bf16[256,256]{1,0:T(8,128)(2,1)S(1)} %get-tuple-element.48), channel_id=1, replica_groups={{0,4},{8,12},{16,20},{24,28},{32,36},{40,44},{48,52},{56,60},{64,68},{7..., dimensions={0}, use_global_device_ids=true | all-gather | bytes 393216 | tf_op jit(solution)/shard_map/all_gather | solution.py:30
  137.1 4.3 %collective-permute-done.13 = bf16[256,256]{1,0:T(8,128)(2,1)S(1)} collective-permute-done((bf16[256,256]{1,0:T(8,128)(2,1)S(1)}, bf16[256,256]{1,0:T(8,128)(2,1)S(1)}, u32[]{:S(2)}, u32[]{:S(2)}) %collective-permute-start.13) | collective-permute-done | bytes 131104 | tf_op jit(solution)/shard_map/ppermute | solution.py:24
  141.4 2.0 %all_gather.26.refs_0_ = bf16[512,256]{1,0:T(8,128)(2,1)S(1)} all-gather(bf16[256,256]{1,0:T(8,128)(2,1)S(1)} %get-tuple-element.55), channel_id=1, replica_groups={{0,4},{8,12},{16,20},{24,28},{32,36},{40,44},{48,52},{56,60},{64,68},{7..., dimensions={0}, use_global_device_ids=true | all-gather | bytes 393216 | tf_op jit(solution)/shard_map/all_gather | solution.py:30
  143.4 4.2 %aggregate_by_matmul.3.own = bf16[1024,256]{1,0:T(8,128)(2,1)S(1)} custom-call(s32[1024,8]{1,0:T(8,128)S(1)} %copy-done.11, f32[1024,8]{1,0:T(8,128)S(1)} %copy-done.12, bf16[1024,256]{1,0:T(8,128)(2,1)S(1)} %copy-done, bf16[512,256]{1,0:T(8,128)(2,1)S(1)} %all_gather.26.refs_0_, bf16[512,256]{1,0:T(8,128)(2,1)S(1)} %all_gather.27.refs_1_, ...), custom_call_target="tpu_custom_call" | custom-call | flops 2684354560 | bytes 1703936 | tf_op jit(solution)/shard_map/aggregate_by_matmul/pallas_call | solution.py:350
  147.6 5.5 %collective-permute-start.17 = (bf16[512,256]{1,0:T(8,128)(2,1)S(1)}, bf16[512,256]{1,0:T(8,128)(2,1)S(1)}, u32[]{:S(2)}, u32[]{:S(2)}) collective-permute-start(bf16[512,256]{1,0:T(8,128)(2,1)S(1)} %get-tuple-element.51), channel_id=1, source_target_pairs={{0,3},{1,2},{2,1},{3,0},{4,7},{5,6},{6,5},{7,4},{8,11},{9,10},{10,... | collective-permute-start | bytes 786440 | tf_op jit(solution)/shard_map/ppermute | solution.py:19
  153.2 1.9 %collective-permute-start.16 = (bf16[512,256]{1,0:T(8,128)(2,1)S(1)}, bf16[512,256]{1,0:T(8,128)(2,1)S(1)}, u32[]{:S(2)}, u32[]{:S(2)}) collective-permute-start(bf16[512,256]{1,0:T(8,128)(2,1)S(1)} %get-tuple-element.50), channel_id=1, source_target_pairs={{0,1},{1,0},{2,3},{3,2},{4,5},{5,4},{6,7},{7,6},{8,9},{9,8},{10,11... | collective-permute-start | bytes 786440 | tf_op jit(solution)/shard_map/ppermute | solution.py:19
  155.1 3.9 %collective-permute-start.15 = (bf16[512,256]{1,0:T(8,128)(2,1)S(1)}, bf16[512,256]{1,0:T(8,128)(2,1)S(1)}, u32[]{:S(2)}, u32[]{:S(2)}) collective-permute-start(bf16[512,256]{1,0:T(8,128)(2,1)S(1)} %get-tuple-element.51), channel_id=1, source_target_pairs={{0,1},{1,0},{2,3},{3,2},{4,5},{5,4},{6,7},{7,6},{8,9},{9,8},{10,11... | collective-permute-start | bytes 786440 | tf_op jit(solution)/shard_map/ppermute | solution.py:19
  159.0 1.9 %collective-permute-start.18 = (bf16[512,256]{1,0:T(8,128)(2,1)S(1)}, bf16[512,256]{1,0:T(8,128)(2,1)S(1)}, u32[]{:S(2)}, u32[]{:S(2)}) collective-permute-start(bf16[512,256]{1,0:T(8,128)(2,1)S(1)} %get-tuple-element.50), channel_id=1, source_target_pairs={{0,3},{1,2},{2,1},{3,0},{4,7},{5,6},{6,5},{7,4},{8,11},{9,10},{10,... | collective-permute-start | bytes 786440 | tf_op jit(solution)/shard_map/ppermute | solution.py:19
  161.0 2.7 %collective-permute-start.19 = (bf16[512,256]{1,0:T(8,128)(2,1)S(1)}, bf16[512,256]{1,0:T(8,128)(2,1)S(1)}, u32[]{:S(2)}, u32[]{:S(2)}) collective-permute-start(bf16[512,256]{1,0:T(8,128)(2,1)S(1)} %collective-permute-done.17.other_top), channel_id=1, source_target_pairs={{0,1},{1,0},{2,3},{3,2},{4,5},{5,4},{6,7},{7,6},{8,9},{9,8},{10,11... | collective-permute-start | bytes 786440 | tf_op jit(solution)/shard_map/ppermute | solution.py:19
  164.3 3.8 %collective-permute-start.20 = (bf16[512,256]{1,0:T(8,128)(2,1)S(1)}, bf16[512,256]{1,0:T(8,128)(2,1)S(1)}, u32[]{:S(2)}, u32[]{:S(2)}) collective-permute-start(bf16[512,256]{1,0:T(8,128)(2,1)S(1)} %collective-permute-done.16.near_low), channel_id=1, source_target_pairs={{0,3},{1,2},{2,1},{3,0},{4,7},{5,6},{6,5},{7,4},{8,11},{9,10},{10,... | collective-permute-start | bytes 786440 | tf_op jit(solution)/shard_map/ppermute | solution.py:19
  168.1 1.8 collective-permute-done.15.near_top
  169.9 1.2 collective-permute-done.18.other_low
  171.7 2.7 %collective-permute-done.19.far_top = bf16[512,256]{1,0:T(8,128)(2,1)S(1)} collective-permute-done((bf16[512,256]{1,0:T(8,128)(2,1)S(1)}, bf16[512,256]{1,0:T(8,128)(2,1)S(1)}, u32[]{:S(2)}, u32[]{:S(2)}) %collective-permute-start.19) | collective-permute-done | bytes 262176 | tf_op jit(solution)/shard_map/ppermute | solution.py:19
  175.3 1.1 last_block.3
  (52 shorter events, 6.5 us)
Async XLA Ops:
  7.2 70.6 %all-gather.2.cloned.1.call-start = ((), (), s32[]{:S(2)}) async-start(), calls=%async_computation | async-start | bytes 3276800 | tf_op jit(solution)/shard_map/all_gather | solution.py:34
  7.2 5.2 %copy-start = (bf16[1024,256]{1,0:T(8,128)(2,1)S(1)}, bf16[1024,256]{1,0:T(8,128)(2,1)}, u32[]{:S(2)}) copy-start(bf16[1024,256]{1,0:T(8,128)(2,1)} %refs_0_.2) | copy-start | bytes 1572868
  8.4 31.0 %copy-start.1 = (bf16[1024,256]{1,0:T(8,128)(2,1)S(1)}, bf16[1024,256]{1,0:T(8,128)(2,1)}, u32[]{:S(2)}) copy-start(bf16[1024,256]{1,0:T(8,128)(2,1)} %weight.5) | copy-start | bytes 1572868
  12.5 12.9 %collective-permute-start.2 = (bf16[512,256]{1,0:T(8,128)(2,1)S(1)}, bf16[512,256]{1,0:T(8,128)(2,1)S(1)}, u32[]{:S(2)}, u32[]{:S(2)}) collective-permute-start(bf16[512,256]{1,0:T(8,128)(2,1)S(1)} %get-tuple-element.53), channel_id=1, source_target_pairs={{0,3},{1,2},{2,1},{3,0},{4,7},{5,6},{6,5},{7,4},{8,11},{9,10},{10,... | collective-permute-start | bytes 786440 | tf_op jit(solution)/shard_map/ppermute | solution.py:19
  17.2 11.1 %collective-permute-start.1 = (bf16[512,256]{1,0:T(8,128)(2,1)S(1)}, bf16[512,256]{1,0:T(8,128)(2,1)S(1)}, u32[]{:S(2)}, u32[]{:S(2)}) collective-permute-start(bf16[512,256]{1,0:T(8,128)(2,1)S(1)} %get-tuple-element.52), channel_id=1, source_target_pairs={{0,1},{1,0},{2,3},{3,2},{4,5},{5,4},{6,7},{7,6},{8,9},{9,8},{10,11... | collective-permute-start | bytes 786440 | tf_op jit(solution)/shard_map/ppermute | solution.py:19
  19.3 18.0 %collective-permute-start = (bf16[512,256]{1,0:T(8,128)(2,1)S(1)}, bf16[512,256]{1,0:T(8,128)(2,1)S(1)}, u32[]{:S(2)}, u32[]{:S(2)}) collective-permute-start(bf16[512,256]{1,0:T(8,128)(2,1)S(1)} %get-tuple-element.53), channel_id=1, source_target_pairs={{0,1},{1,0},{2,3},{3,2},{4,5},{5,4},{6,7},{7,6},{8,9},{9,8},{10,11... | collective-permute-start | bytes 786440 | tf_op jit(solution)/shard_map/ppermute | solution.py:19
  23.0 16.3 %collective-permute-start.3 = (bf16[512,256]{1,0:T(8,128)(2,1)S(1)}, bf16[512,256]{1,0:T(8,128)(2,1)S(1)}, u32[]{:S(2)}, u32[]{:S(2)}) collective-permute-start(bf16[512,256]{1,0:T(8,128)(2,1)S(1)} %get-tuple-element.52), channel_id=1, source_target_pairs={{0,3},{1,2},{2,1},{3,0},{4,7},{5,6},{6,5},{7,4},{8,11},{9,10},{10,... | collective-permute-start | bytes 786440 | tf_op jit(solution)/shard_map/ppermute | solution.py:19
  25.5 19.7 %collective-permute-start.4 = (bf16[512,256]{1,0:T(8,128)(2,1)S(1)}, bf16[512,256]{1,0:T(8,128)(2,1)S(1)}, u32[]{:S(2)}, u32[]{:S(2)}) collective-permute-start(bf16[512,256]{1,0:T(8,128)(2,1)S(1)} %collective-permute-done.2.other_top), channel_id=1, source_target_pairs={{0,1},{1,0},{2,3},{3,2},{4,5},{5,4},{6,7},{7,6},{8,9},{9,8},{10,11... | collective-permute-start | bytes 786440 | tf_op jit(solution)/shard_map/ppermute | solution.py:19
  28.3 17.7 %collective-permute-start.5 = (bf16[512,256]{1,0:T(8,128)(2,1)S(1)}, bf16[512,256]{1,0:T(8,128)(2,1)S(1)}, u32[]{:S(2)}, u32[]{:S(2)}) collective-permute-start(bf16[512,256]{1,0:T(8,128)(2,1)S(1)} %collective-permute-done.1.near_low), channel_id=1, source_target_pairs={{0,3},{1,2},{2,1},{3,0},{4,7},{5,6},{6,5},{7,4},{8,11},{9,10},{10,... | collective-permute-start | bytes 786440 | tf_op jit(solution)/shard_map/ppermute | solution.py:19
  46.3 24.6 %copy-start.3 = (bf16[256,256]{1,0:T(8,128)(2,1)S(1)}, bf16[256,256]{1,0:T(8,128)(2,1)}, u32[]{:S(2)}) copy-start(bf16[256,256]{1,0:T(8,128)(2,1)} %mesh.1) | copy-start | bytes 393220
  46.3 24.6 %copy-start.6 = (f32[512,16]{1,0:T(8,128)S(1)}, f32[512,16]{1,0:T(8,128)}, u32[]{:S(2)}) copy-start(f32[512,16]{1,0:T(8,128)} %get-tuple-element.38.weight_ref) | copy-start | bytes 98308
  46.3 24.6 %copy-start.7 = (s32[16,256]{1,0:T(8,128)S(1)}, s32[16,256]{1,0:T(8,128)}, u32[]{:S(2)}) copy-start(s32[16,256]{1,0:T(8,128)} %get-tuple-element.37.index_ref) | copy-start | bytes 49156
  46.3 13.1 %collective-permute-start.6 = (bf16[1024,256]{1,0:T(8,128)(2,1)S(1)}, bf16[1024,256]{1,0:T(8,128)(2,1)S(1)}, u32[]{:S(2)}, u32[]{:S(2)}) collective-permute-start(bf16[1024,256]{1,0:T(8,128)(2,1)S(1)} %last_block.2.refs_0_), channel_id=1, source_target_pairs={{0,8},{4,12},{8,16},{12,20},{16,24},{20,28},{24,32},{28,36},{32,40... | collective-permute-start | bytes 1572872 | tf_op jit(solution)/shard_map/ppermute | solution.py:24
  51.2 15.7 %collective-permute-start.7 = (bf16[1024,256]{1,0:T(8,128)(2,1)S(1)}, bf16[1024,256]{1,0:T(8,128)(2,1)S(1)}, u32[]{:S(2)}, u32[]{:S(2)}) collective-permute-start(bf16[1024,256]{1,0:T(8,128)(2,1)S(1)} %last_block.2.refs_0_), channel_id=1, source_target_pairs={{8,0},{12,4},{16,8},{20,12},{24,16},{28,20},{32,24},{36,28},{40,32... | collective-permute-start | bytes 1572872 | tf_op jit(solution)/shard_map/ppermute | solution.py:24
  53.1 15.9 %collective-permute-start.8 = (bf16[1024,256]{1,0:T(8,128)(2,1)S(1)}, bf16[1024,256]{1,0:T(8,128)(2,1)S(1)}, u32[]{:S(2)}, u32[]{:S(2)}) collective-permute-start(bf16[1024,256]{1,0:T(8,128)(2,1)S(1)} %last_block.2.refs_0_), channel_id=1, source_target_pairs={{0,4},{4,0},{8,12},{12,8},{16,20},{20,16},{24,28},{28,24},{32,36},... | collective-permute-start | bytes 1572872 | tf_op jit(solution)/shard_map/ppermute | solution.py:19
  66.9 10.8 %copy-start.9 = (bf16[1024,256]{1,0:T(8,128)(2,1)S(1)}, bf16[1024,256]{1,0:T(8,128)(2,1)}, u32[]{:S(2)}) copy-start(bf16[1024,256]{1,0:T(8,128)(2,1)} %first.1) | copy-start | bytes 1572868
  67.0 3.9 %collective-permute-start.9 = (bf16[1024,256]{1,0:T(8,128)(2,1)S(1)}, bf16[1024,256]{1,0:T(8,128)(2,1)S(1)}, u32[]{:S(2)}, u32[]{:S(2)}) collective-permute-start(bf16[1024,256]{1,0:T(8,128)(2,1)S(1)} %broadcast_select_fusion), channel_id=1, source_target_pairs={{0,4},{4,0},{8,12},{12,8},{16,20},{20,16},{24,28},{28,24},{32,36},... | collective-permute-start | bytes 1572872 | tf_op jit(solution)/shard_map/ppermute | solution.py:19
  77.8 1.7 copy-start.8
  79.5 1.0 copy-start.10
  82.8 15.2 %copy-start.4 = (bf16[1024,256]{1,0:T(8,128)(2,1)S(1)}, bf16[1024,256]{1,0:T(8,128)(2,1)}, u32[]{:S(2)}) copy-start(bf16[1024,256]{1,0:T(8,128)(2,1)} %w_out.2) | copy-start | bytes 1572868
  82.9 15.1 %collective-permute-start.10 = (bf16[1024,512]{1,0:T(8,128)(2,1)S(1)}, bf16[1024,512]{1,0:T(8,128)(2,1)S(1)}, u32[]{:S(2)}, u32[]{:S(2)}) collective-permute-start(bf16[1024,512]{1,0:T(8,128)(2,1)S(1)} %slice.17), channel_id=1, source_target_pairs={{0,4},{4,0},{8,12},{12,8},{16,20},{20,16},{24,28},{28,24},{32,36},... | collective-permute-start | bytes 3145736 | tf_op jit(solution)/shard_map/ppermute | solution.py:19
  98.6 14.3 %copy-start.13 = (s32[256,8]{1,0:T(8,128)S(1)}, s32[256,8]{1,0:T(8,128)}, u32[]{:S(2)}) copy-start(s32[256,8]{1,0:T(8,128)} %get-tuple-element.35.index_ref) | copy-start | bytes 24580
  98.6 14.3 %copy-start.14 = (f32[256,8]{1,0:T(8,128)S(1)}, f32[256,8]{1,0:T(8,128)}, u32[]{:S(2)}) copy-start(f32[256,8]{1,0:T(8,128)} %get-tuple-element.36.weight_ref) | copy-start | bytes 24580
  98.6 8.0 %collective-permute-start.12 = (bf16[256,256]{1,0:T(8,128)(2,1)S(1)}, bf16[256,256]{1,0:T(8,128)(2,1)S(1)}, u32[]{:S(2)}, u32[]{:S(2)}) collective-permute-start(bf16[256,256]{1,0:T(8,128)(2,1)S(1)} %get-tuple-element.46), channel_id=1, source_target_pairs={{0,8},{4,12},{8,16},{12,20},{16,24},{20,28},{24,32},{28,36},{32,40... | collective-permute-start | bytes 393224 | tf_op jit(solution)/shard_map/ppermute | solution.py:24
  100.7 10.2 %collective-permute-start.11 = (bf16[256,256]{1,0:T(8,128)(2,1)S(1)}, bf16[256,256]{1,0:T(8,128)(2,1)S(1)}, u32[]{:S(2)}, u32[]{:S(2)}) collective-permute-start(bf16[256,256]{1,0:T(8,128)(2,1)S(1)} %get-tuple-element.46), channel_id=1, source_target_pairs={{8,0},{12,4},{16,8},{20,12},{24,16},{28,20},{32,24},{36,28},{40,32... | collective-permute-start | bytes 393224 | tf_op jit(solution)/shard_map/ppermute | solution.py:24
  112.9 15.1 %copy-start.5 = (bf16[1024,256]{1,0:T(8,128)(2,1)S(1)}, bf16[1024,256]{1,0:T(8,128)(2,1)}, u32[]{:S(2)}) copy-start(bf16[1024,256]{1,0:T(8,128)(2,1)} %w_out.3) | copy-start | bytes 1572868
  129.1 14.3 %copy-start.11 = (s32[1024,8]{1,0:T(8,128)S(1)}, s32[1024,8]{1,0:T(8,128)}, u32[]{:S(2)}) copy-start(s32[1024,8]{1,0:T(8,128)} %get-tuple-element.32.index_ref) | copy-start | bytes 98308
  129.1 14.3 %copy-start.12 = (f32[1024,8]{1,0:T(8,128)S(1)}, f32[1024,8]{1,0:T(8,128)}, u32[]{:S(2)}) copy-start(f32[1024,8]{1,0:T(8,128)} %get-tuple-element.33.weight_ref) | copy-start | bytes 98308
  129.1 8.0 %collective-permute-start.14 = (bf16[256,256]{1,0:T(8,128)(2,1)S(1)}, bf16[256,256]{1,0:T(8,128)(2,1)S(1)}, u32[]{:S(2)}, u32[]{:S(2)}) collective-permute-start(bf16[256,256]{1,0:T(8,128)(2,1)S(1)} %get-tuple-element.48), channel_id=1, source_target_pairs={{0,8},{4,12},{8,16},{12,20},{16,24},{20,28},{24,32},{28,36},{32,40... | collective-permute-start | bytes 393224 | tf_op jit(solution)/shard_map/ppermute | solution.py:24
  131.2 10.2 %collective-permute-start.13 = (bf16[256,256]{1,0:T(8,128)(2,1)S(1)}, bf16[256,256]{1,0:T(8,128)(2,1)S(1)}, u32[]{:S(2)}, u32[]{:S(2)}) collective-permute-start(bf16[256,256]{1,0:T(8,128)(2,1)S(1)} %get-tuple-element.48), channel_id=1, source_target_pairs={{8,0},{12,4},{16,8},{20,12},{24,16},{28,20},{32,24},{36,28},{40,32... | collective-permute-start | bytes 393224 | tf_op jit(solution)/shard_map/ppermute | solution.py:24
  147.6 23.5 %copy-start.2 = (bf16[1024,256]{1,0:T(8,128)(2,1)S(1)}, bf16[1024,256]{1,0:T(8,128)(2,1)}, u32[]{:S(2)}) copy-start(bf16[1024,256]{1,0:T(8,128)(2,1)} %weight.7) | copy-start | bytes 1572868
  147.6 13.3 %collective-permute-start.17 = (bf16[512,256]{1,0:T(8,128)(2,1)S(1)}, bf16[512,256]{1,0:T(8,128)(2,1)S(1)}, u32[]{:S(2)}, u32[]{:S(2)}) collective-permute-start(bf16[512,256]{1,0:T(8,128)(2,1)S(1)} %get-tuple-element.51), channel_id=1, source_target_pairs={{0,3},{1,2},{2,1},{3,0},{4,7},{5,6},{6,5},{7,4},{8,11},{9,10},{10,... | collective-permute-start | bytes 786440 | tf_op jit(solution)/shard_map/ppermute | solution.py:19
  153.2 11.1 %collective-permute-start.16 = (bf16[512,256]{1,0:T(8,128)(2,1)S(1)}, bf16[512,256]{1,0:T(8,128)(2,1)S(1)}, u32[]{:S(2)}, u32[]{:S(2)}) collective-permute-start(bf16[512,256]{1,0:T(8,128)(2,1)S(1)} %get-tuple-element.50), channel_id=1, source_target_pairs={{0,1},{1,0},{2,3},{3,2},{4,5},{5,4},{6,7},{7,6},{8,9},{9,8},{10,11... | collective-permute-start | bytes 786440 | tf_op jit(solution)/shard_map/ppermute | solution.py:19
  155.1 14.8 %collective-permute-start.15 = (bf16[512,256]{1,0:T(8,128)(2,1)S(1)}, bf16[512,256]{1,0:T(8,128)(2,1)S(1)}, u32[]{:S(2)}, u32[]{:S(2)}) collective-permute-start(bf16[512,256]{1,0:T(8,128)(2,1)S(1)} %get-tuple-element.51), channel_id=1, source_target_pairs={{0,1},{1,0},{2,3},{3,2},{4,5},{5,4},{6,7},{7,6},{8,9},{9,8},{10,11... | collective-permute-start | bytes 786440 | tf_op jit(solution)/shard_map/ppermute | solution.py:19
  159.0 12.1 %collective-permute-start.18 = (bf16[512,256]{1,0:T(8,128)(2,1)S(1)}, bf16[512,256]{1,0:T(8,128)(2,1)S(1)}, u32[]{:S(2)}, u32[]{:S(2)}) collective-permute-start(bf16[512,256]{1,0:T(8,128)(2,1)S(1)} %get-tuple-element.50), channel_id=1, source_target_pairs={{0,3},{1,2},{2,1},{3,0},{4,7},{5,6},{6,5},{7,4},{8,11},{9,10},{10,... | collective-permute-start | bytes 786440 | tf_op jit(solution)/shard_map/ppermute | solution.py:19
  161.0 13.4 %collective-permute-start.19 = (bf16[512,256]{1,0:T(8,128)(2,1)S(1)}, bf16[512,256]{1,0:T(8,128)(2,1)S(1)}, u32[]{:S(2)}, u32[]{:S(2)}) collective-permute-start(bf16[512,256]{1,0:T(8,128)(2,1)S(1)} %collective-permute-done.17.other_top), channel_id=1, source_target_pairs={{0,1},{1,0},{2,3},{3,2},{4,5},{5,4},{6,7},{7,6},{8,9},{9,8},{10,11... | collective-permute-start | bytes 786440 | tf_op jit(solution)/shard_map/ppermute | solution.py:19
  164.3 11.0 %collective-permute-start.20 = (bf16[512,256]{1,0:T(8,128)(2,1)S(1)}, bf16[512,256]{1,0:T(8,128)(2,1)S(1)}, u32[]{:S(2)}, u32[]{:S(2)}) collective-permute-start(bf16[512,256]{1,0:T(8,128)(2,1)S(1)} %collective-permute-done.16.near_low), channel_id=1, source_target_pairs={{0,3},{1,2},{2,1},{3,0},{4,7},{5,6},{6,5},{7,4},{8,11},{9,10},{10,... | collective-permute-start | bytes 786440 | tf_op jit(solution)/shard_map/ppermute | solution.py:19
Sparse Core Ops, SparseCore 0:
  10.4 52.8 all-gather.1

commit v2 on v1

--- a/solution.py
+++ b/solution.py
@@ -65,7 +65,7 @@
         out[at, :] = value.astype(out.dtype)
 
 
-def project_by_exchanges(values, weight, base=()):
+def project_by_exchanges(values, weight, base=(), later=None):
     assert lax.axis_size("chan") == 4
     me = lax.axis_index("chan").astype(jnp.int32)[None]
     rows, width = values.shape
@@ -86,7 +86,10 @@
         cost_estimate=pl.CostEstimate(flops=6 * rows * width * width, bytes_accessed=10 * rows * width, transcendentals=0),
         name="first_blocks",
     )(me, values, near_top, near_low, other_top, other_low, weight)
-    return pl.pallas_call(
+    if later is not None:
+        total, later = lax.optimization_barrier((total, later))
+        later = exchange(later, "chan", lambda i: i ^ 2)
+    out = pl.pallas_call(
         last_kernel,
         out_shape=jax.ShapeDtypeStruct((rows, width), values.dtype),
         in_specs=[SMEM] + [VMEM] * (4 + len(base)),
@@ -95,36 +98,41 @@
         cost_estimate=pl.CostEstimate(flops=2 * rows * width * width, bytes_accessed=10 * rows * width, transcendentals=0),
         name="last_block",
     )(me, total, far_top, far_low, weight, *base)
-
-
-def combine_kernel(rows_ref, first, second, mixed, base):
-    rows, width = rows_ref[...], first.shape[1]
-    for at, weight in ((slice(0, width), first), (slice(width, 2 * width), second)):
-        value = dot(rows, weight[...])
-        base[:, at] = value
-        mixed[:, at] = value.astype(mixed.dtype)
-
-
-def combine(gathered, first, second, block):
-    rows, depth = gathered.shape
-    width = first.shape[1]
-    whole = pl.BlockSpec((depth, width), lambda i: (0, 0))
+    return out, later
+
+
+def combine_kernel(me_ref, own, near, other, far, first, second, mixed, base):
+    me, width = me_ref[0], own.shape[1]
+    rows, last = own.shape[0], base.shape[0]
+
+    def one_block(start, size, targets):
+        at = pl.ds(start, size)
+        for column, weight in ((slice(0, width), first), (slice(width, 2 * width), second)):
+            value = jnp.zeros((size, width), jnp.float32)
+            for source, block in ((me, own), (me ^ 1, near), (3 - me, other), (me ^ 2, far)):
+                value += dot(block[at, :], weight[pl.ds(pl.multiple_of(source * width, width), width), :])
+            for target, to in targets:
+                target[to, column] = value.astype(target.dtype)
+
+    for start in range(0, rows - last, last):
+        one_block(start, last, [(mixed, pl.ds(start, last))])
+    one_block(rows - last, last, [(base, pl.ds(0, last))])
+
+
+def combine(blocks, first, second, last):
+    rows, width = blocks[0].shape
     return pl.pallas_call(
         combine_kernel,
-        grid=(rows // block,),
         out_shape=(
-            jax.ShapeDtypeStruct((rows, 2 * width), gathered.dtype),
-            jax.ShapeDtypeStruct((block, 2 * width), jnp.float32),
+            jax.ShapeDtypeStruct((rows - last, 2 * width), blocks[0].dtype),
+            jax.ShapeDtypeStruct((last, 2 * width), jnp.float32),
         ),
-        in_specs=[pl.BlockSpec((block, depth), lambda i: (i, 0)), whole, whole],
-        out_specs=(
-            pl.BlockSpec((block, 2 * width), lambda i: (i, 0)),
-            pl.BlockSpec((block, 2 * width), lambda i: (0, 0)),
-        ),
+        in_specs=[SMEM] + [VMEM] * 6,
+        out_specs=(VMEM, VMEM),
         compiler_params=pltpu.CompilerParams(vmem_limit_bytes=10 << 20),
-        cost_estimate=pl.CostEstimate(flops=4 * rows * depth * width, bytes_accessed=2 * rows * depth, transcendentals=0),
+        cost_estimate=pl.CostEstimate(flops=16 * rows * width * width, bytes_accessed=16 * rows * width, transcendentals=0),
         name="combine",
-    )(gathered, first, second)
+    )(lax.axis_index("chan").astype(jnp.int32)[None], *blocks, first, second)
 
 
 def halves_dot(core, full, mine, other, rows, columns):
@@ -163,13 +171,15 @@
     )(core, *operands)
 
 
-def window_of_exchanges(projected):
+def window_of_exchanges(projected, later):
     below = shift(projected, 2)
     above = shift(projected, -2)
     other = exchange(projected, "region", lambda i: i ^ 1)
+    other, later = lax.optimization_barrier((other, later))
+    sent = [exchange(later, "chan", lambda i: i ^ 1), exchange(later, "chan", lambda i: 3 - i)]
     first = lax.axis_index("region") % 2 == 0
     third = exchange(jnp.where(first, above, below), "region", lambda i: i ^ 1)
-    return [projected, below, above, other, third]
+    return [projected, below, above, other, third], sent
 
 
 def window_of_pairs(projected):
@@ -183,14 +193,22 @@
 
 
 def edges_kernel(n_grid, n_mesh, me_ref, *refs):
-    sources, (o1, s1, o2, s2, o3, s3) = refs[:9], refs[9:15]
-    i1, w1, c1, i2, w2, c2, i3, w3, c3 = held = refs[15:24]
-    copies = [pltpu.make_async_copy(src, dst, refs[24].at[k]) for k, (src, dst) in enumerate(zip(sources, held))]
+    sources, (first, second, mesh), (o1, s1, o2, s2, o3, s3, packed) = refs[:9], refs[9:12], refs[12:19]
+    i1, w1, c1, i2, w2, c2, i3, w3, c3 = held = refs[19:28]
+    semaphores = refs[28]
+    me = me_ref[0]
+    half = first.shape[0] // 2
+    mine = pl.ds(pl.multiple_of((me & 1) * half, half), half)
+    moves = list(zip(sources, held)) + [
+        (first.at[mine, :], packed.at[pl.ds(0, half), :]),
+        (second.at[mine, :], packed.at[pl.ds(half, half), :]),
+        (mesh, packed.at[pl.ds(2 * half, mesh.shape[0]), :]),
+    ]
+    copies = [pltpu.make_async_copy(src, dst, semaphores.at[k]) for k, (src, dst) in enumerate(moves)]
     for copy in copies:
         copy.start()
     for copy in copies:
         copy.wait()
-    me = me_ref[0]
     core = me & 1
 
     def of_exchanges(apart):
@@ -224,7 +242,7 @@
     s3[...] = upright(scaled(w3, c3))
 
 
-def edges(n_grid, n_mesh, g2m, m2m, m2g):
+def edges(n_grid, n_mesh, g2m, m2m, m2g, first, second, mesh):
     me = lax.axis_index("region").astype(jnp.int32)[None]
     ops, outs = [me], []
     for at, (index, weight, count) in enumerate((g2m, m2m, m2g)):
@@ -235,16 +253,18 @@
             jax.ShapeDtypeStruct((slots, rows) if at == 0 else (rows, high), jnp.int32),
             jax.ShapeDtypeStruct((2 * rows if at == 0 else rows, high), jnp.float32),
         ]
+    packed = (first.shape[0] + mesh.shape[0], mesh.shape[1])
+    outs.append(jax.ShapeDtypeStruct(packed, mesh.dtype))
     return pl.pallas_call(
         functools.partial(edges_kernel, n_grid, n_mesh),
         out_shape=outs,
-        in_specs=[SMEM] + [HBM] * 9,
-        out_specs=[VMEM] * 6,
-        scratch_shapes=[pltpu.VMEM(op.shape, op.dtype) for op in ops[1:]] + [pltpu.SemaphoreType.DMA((9,))],
+        in_specs=[SMEM] + [HBM] * 12,
+        out_specs=[VMEM] * 7,
+        scratch_shapes=[pltpu.VMEM(op.shape, op.dtype) for op in ops[1:]] + [pltpu.SemaphoreType.DMA((12,))],
         compiler_params=pltpu.CompilerParams(vmem_limit_bytes=60 << 20),
         cost_estimate=pl.CostEstimate(flops=1 << 20, bytes_accessed=1 << 20, transcendentals=0),
         name="edges",
-    )(*ops)
+    )(*ops, first, second, mesh)
 
 
 def by_rows_kernel(slots, rows, group, sizes, index_ref, weight_ref, receiver_ref, *refs):
@@ -385,28 +405,27 @@
     n_grid, n_mesh = grid_state.shape[0], mesh_state.shape[0]
     bf16, f32 = jnp.bfloat16, jnp.float32
     k_m, k_d = m2m_index.shape[0], m2g_index.shape[0]
+    core = lax.axis_index("region").astype(jnp.int32) % 2
     prepared = edges(
         n_grid,
         n_mesh,
         (g2m_index, g2m_weight, g2m_count),
         (m2m_index, m2m_weight, m2m_count),
         (m2g_index, m2g_weight, m2g_count),
+        enc_out,
+        proc_out,
+        mesh_state,
     )
-
     grid_state, prepared = lax.optimization_barrier((grid_state, prepared))
-    g2m, g2m_w, m2m, m2m_w, m2g, m2g_w = prepared
-
-    core = lax.axis_index("region").astype(jnp.int32) % 2
-    half = enc_out.shape[0] // 2
-    own_rows = [lax.dynamic_slice_in_dim(w, core * half, half, axis=0) for w in (enc_out, proc_out)]
-    gathered = gather_chan(jnp.concatenate(own_rows + [mesh_state], axis=0))
-
-    projected = project_by_exchanges(grid_state, enc_send)
-    agg = aggregate_by_rows(g2m, g2m_w, mesh_state, window_of_exchanges(projected))
-
-    agg, gathered = lax.optimization_barrier((agg, gathered))
-    mine, base = combine(gathered, proc_send, dec_send, n_mesh)
-    other = exchange(mine[: 2 * half], "region", lambda i: i ^ 1)
+    g2m, g2m_w, m2m, m2m_w, m2g, m2g_w, packed = prepared
+
+    projected, far = project_by_exchanges(grid_state, enc_send, later=packed)
+    window, nearer = window_of_exchanges(projected, packed)
+    agg = aggregate_by_rows(g2m, g2m_w, mesh_state, window)
+
+    agg, packed, nearer, far = lax.optimization_barrier((agg, packed, nearer, far))
+    mine, base = combine([packed, *nearer, far], proc_send, dec_send, n_mesh)
+    other = exchange(mine, "region", lambda i: i ^ 1)
     agg, base = lax.optimization_barrier((agg, base))
     mesh_one, projected, later = mesh_step(
         mesh_one_kernel, mesh_state, (bf16, bf16, f32), core[None], gather_chan(agg), mesh_state, enc_out, mine, other, base
@@ -416,7 +435,7 @@
         mesh_next_kernel, mesh_state, (bf16, bf16), core[None], gather_chan(agg), mesh_one, proc_out, mine, other, later
     )
     agg = aggregate_by_matmul(k_d, m2g, m2g_w, grid_state, window_of_pairs(projected))
-    grid_next = project_by_exchanges(agg, dec_out, base=(grid_state,))
+    grid_next, _ = project_by_exchanges(agg, dec_out, base=(grid_state,))
     return grid_next, mesh_next
 
 

time: 184 us -> 169 us (0.918)
  between operations: 14.5 us -> 1.13 us
  starting transfers between devices: 63.5 us -> 75.4 us
  waiting for transfers between devices: 43.5 us -> 35.9 us
  local copies, waits for them, and re-layouts: 4.11 us -> 0.15 us
    ppermute x15 -> x18, starting transfers between devices: 44.8 us -> 54.6 us  [exchange(): return lax.ppermute(shard, axis, [(i, partner(i)) for i in range(n)])]
    ppermute x6, waiting for transfers between devices: 20.4 us -> 10.7 us  [shift(): lax.ppermute(shard, 'region', [(i, i + by) for i in range(n) if 0 <= i +...]
    unnamed x30, local copies, waits for them, and re-layouts: 2.84 us -> 0.08 us
    ppermute x6, starting transfers between devices: 18.7 us -> 20.8 us  [shift(): lax.ppermute(shard, 'region', [(i, i + by) for i in range(n) if 0 <= i +...]
    ppermute x15 -> x18, waiting for transfers between devices: 23.1 us -> 25.2 us  [exchange(): return lax.ppermute(shard, axis, [(i, partner(i)) for i in range(n)])]
    concatenate x1 -> x0, other arithmetic: 1.84 us -> none  [shards(): gathered = gather_chan(jnp.concatenate(own_rows + [mesh_state], axis=0))]
  transfers between devices with their start and end apart: 22 -> 24, of which waited for: 15 -> 10; matrix products, arithmetic and copies ran while one was open for 0% -> 0% of each run, Pallas kernels for 6% -> 5%
where the time goes in v2:
time: 169 us; the launch traced here: 168 us
  starting transfers between devices  75.4 us (45%)
  waiting for transfers between devices  35.9 us (21%)
  blocking collectives  34.2 us (20%)
  Pallas kernels  21.5 us (13%)
    ppermute x18, starting transfers between devices, exchange(): return lax.ppermute(shard, axis, [(i, partner(i)) for i in range(n)])  54.6 us
    all_gather x2, blocking collectives, gather_chan(): return lax.all_gather(values, 'chan', axis=1, tiled=True)  25.9 us
    ppermute x18, waiting for transfers between devices, exchange(): return lax.ppermute(shard, axis, [(i, partner(i)) for i in range(n)])  25.2 us
    ppermute x6, starting transfers between devices, shift(): lax.ppermute(shard, 'region', [(i, i + by) for i in range(n) if 0 <= i +...  20.8 us
    ppermute x6, waiting for transfers between devices, shift(): lax.ppermute(shard, 'region', [(i, i + by) for i in range(n) if 0 <= i +...  10.7 us
    all_gather x4, blocking collectives, core_pair(): lax.all_gather(shard, 'region', axis=0, tiled=True, axis_index_groups=gro...  8.24 us
    pallas_call x1, Pallas kernels, aggregate_by_rows(): pl.pallas_call(functools.partial(by_rows_kernel, slots, rows, group, size...  6.85 us
    pallas_call x2, Pallas kernels, aggregate_by_matmul(): pl.pallas_call(functools.partial(by_matmul_kernel, slots, rows, block, si...  5.99 us
  transfers between devices with their start and end apart: 24, of which 10 were waited for; matrix products, arithmetic and copies ran while one was open for 0% of the time, Pallas kernels for 5%

profile of v2, /device:TPU:248, one launch (start us, length us, event | category | flops | bytes accessed | tf_op | source)
XLA Modules:
  0.0 168.3 jit_solution(12182279934895122435)
XLA Ops:
  0.6 2.9 %edges.1 = (s32[16,256]{1,0:T(8,128)}, f32[512,16]{1,0:T(8,128)}, s32[256,8]{1,0:T(8,128)}, f32[256,8]{1,0:T(8,128)}, s32[1024,8]{1,0:T(8,128)}, /*index=5*/f32[1024,8]{1,0:T(8,128)}, bf16[1280,256]{1,0:T(8,128)(2,1)}) custom-call(s32[1]{0:T(128)} %bitcast.1.me_ref, s32[16,256]{1,0:T(8,128)} %refs_0_.1, f32[16,256]{1,0:T(8,128)} %refs_1_.1, ...), custom_call_target="tpu_custom_call" | custom-call | flops 1048576 | bytes 1048576 | tf_op jit(solution)/shard_map/edges/pallas_call | solution.py:258
  3.6 3.5 %collective-permute-start.1 = (bf16[512,256]{1,0:T(8,128)(2,1)S(1)}, bf16[512,256]{1,0:T(8,128)(2,1)S(1)}, u32[]{:S(2)}, u32[]{:S(2)}) collective-permute-start(bf16[512,256]{1,0:T(8,128)(2,1)S(1)} %get-tuple-element.70), channel_id=1, source_target_pairs={{0,1},{1,0},{2,3},{3,2},{4,5},{5,4},{6,7},{7,6},{8,9},{9,8},{10,11... | collective-permute-start | bytes 786440 | tf_op jit(solution)/shard_map/ppermute | solution.py:19
  7.1 4.0 %collective-permute-start.2 = (bf16[512,256]{1,0:T(8,128)(2,1)S(1)}, bf16[512,256]{1,0:T(8,128)(2,1)S(1)}, u32[]{:S(2)}, u32[]{:S(2)}) collective-permute-start(bf16[512,256]{1,0:T(8,128)(2,1)S(1)} %get-tuple-element.71), channel_id=1, source_target_pairs={{0,3},{1,2},{2,1},{3,0},{4,7},{5,6},{6,5},{7,4},{8,11},{9,10},{10,... | collective-permute-start | bytes 786440 | tf_op jit(solution)/shard_map/ppermute | solution.py:19
  11.1 3.0 %collective-permute-start.3 = (bf16[512,256]{1,0:T(8,128)(2,1)S(1)}, bf16[512,256]{1,0:T(8,128)(2,1)S(1)}, u32[]{:S(2)}, u32[]{:S(2)}) collective-permute-start(bf16[512,256]{1,0:T(8,128)(2,1)S(1)} %get-tuple-element.70), channel_id=1, source_target_pairs={{0,3},{1,2},{2,1},{3,0},{4,7},{5,6},{6,5},{7,4},{8,11},{9,10},{10,... | collective-permute-start | bytes 786440 | tf_op jit(solution)/shard_map/ppermute | solution.py:19
  14.2 1.9 %collective-permute-start = (bf16[512,256]{1,0:T(8,128)(2,1)S(1)}, bf16[512,256]{1,0:T(8,128)(2,1)S(1)}, u32[]{:S(2)}, u32[]{:S(2)}) collective-permute-start(bf16[512,256]{1,0:T(8,128)(2,1)S(1)} %get-tuple-element.71), channel_id=1, source_target_pairs={{0,1},{1,0},{2,3},{3,2},{4,5},{5,4},{6,7},{7,6},{8,9},{9,8},{10,11... | collective-permute-start | bytes 786440 | tf_op jit(solution)/shard_map/ppermute | solution.py:19
  16.1 4.0 %collective-permute-start.5 = (bf16[512,256]{1,0:T(8,128)(2,1)S(1)}, bf16[512,256]{1,0:T(8,128)(2,1)S(1)}, u32[]{:S(2)}, u32[]{:S(2)}) collective-permute-start(bf16[512,256]{1,0:T(8,128)(2,1)S(1)} %collective-permute-done.1.near_low), channel_id=1, source_target_pairs={{0,3},{1,2},{2,1},{3,0},{4,7},{5,6},{6,5},{7,4},{8,11},{9,10},{10,... | collective-permute-start | bytes 786440 | tf_op jit(solution)/shard_map/ppermute | solution.py:19
  20.2 3.3 %collective-permute-start.4 = (bf16[512,256]{1,0:T(8,128)(2,1)S(1)}, bf16[512,256]{1,0:T(8,128)(2,1)S(1)}, u32[]{:S(2)}, u32[]{:S(2)}) collective-permute-start(bf16[512,256]{1,0:T(8,128)(2,1)S(1)} %collective-permute-done.2.other_top), channel_id=1, source_target_pairs={{0,1},{1,0},{2,3},{3,2},{4,5},{5,4},{6,7},{7,6},{8,9},{9,8},{10,11... | collective-permute-start | bytes 786440 | tf_op jit(solution)/shard_map/ppermute | solution.py:19
  23.5 1.6 collective-permute-done.3.other_low
  25.7 3.6 %collective-permute-done.5.far_low = bf16[512,256]{1,0:T(8,128)(2,1)S(1)} collective-permute-done((bf16[512,256]{1,0:T(8,128)(2,1)S(1)}, bf16[512,256]{1,0:T(8,128)(2,1)S(1)}, u32[]{:S(2)}, u32[]{:S(2)}) %collective-permute-start.5) | collective-permute-done | bytes 262176 | tf_op jit(solution)/shard_map/ppermute | solution.py:19
  29.5 1.9 %collective-permute-start.8 = (bf16[1024,256]{1,0:T(8,128)(2,1)S(1)}, bf16[1024,256]{1,0:T(8,128)(2,1)S(1)}, u32[]{:S(2)}, u32[]{:S(2)}) collective-permute-start(bf16[1024,256]{1,0:T(8,128)(2,1)S(1)} %last_block.2.refs_0_), channel_id=1, source_target_pairs={{0,4},{4,0},{8,12},{12,8},{16,20},{20,16},{24,28},{28,24},{32,36},... | collective-permute-start | bytes 1572872 | tf_op jit(solution)/shard_map/ppermute | solution.py:19
  31.5 3.3 %collective-permute-start.7 = (bf16[1024,256]{1,0:T(8,128)(2,1)S(1)}, bf16[1024,256]{1,0:T(8,128)(2,1)S(1)}, u32[]{:S(2)}, u32[]{:S(2)}) collective-permute-start(bf16[1024,256]{1,0:T(8,128)(2,1)S(1)} %last_block.2.refs_0_), channel_id=1, source_target_pairs={{8,0},{12,4},{16,8},{20,12},{24,16},{28,20},{32,24},{36,28},{40,32... | collective-permute-start | bytes 1572872 | tf_op jit(solution)/shard_map/ppermute | solution.py:24
  34.7 5.9 %collective-permute-start.6 = (bf16[1024,256]{1,0:T(8,128)(2,1)S(1)}, bf16[1024,256]{1,0:T(8,128)(2,1)S(1)}, u32[]{:S(2)}, u32[]{:S(2)}) collective-permute-start(bf16[1024,256]{1,0:T(8,128)(2,1)S(1)} %last_block.2.refs_0_), channel_id=1, source_target_pairs={{0,8},{4,12},{8,16},{12,20},{16,24},{20,28},{24,32},{28,36},{32,40... | collective-permute-start | bytes 1572872 | tf_op jit(solution)/shard_map/ppermute | solution.py:24
  40.7 3.6 %collective-permute-start.12 = (bf16[1280,256]{1,0:T(8,128)(2,1)S(1)}, bf16[1280,256]{1,0:T(8,128)(2,1)S(1)}, u32[]{:S(2)}, u32[]{:S(2)}) collective-permute-start(bf16[1280,256]{1,0:T(8,128)(2,1)S(1)} %copy-done.8), channel_id=1, source_target_pairs={{0,2},{1,3},{2,0},{3,1},{4,6},{5,7},{6,4},{7,5},{8,10},{9,11},{10,... | collective-permute-start | bytes 1966088 | tf_op jit(solution)/shard_map/ppermute | solution.py:19
  44.3 3.9 %collective-permute-start.11 = (bf16[1280,256]{1,0:T(8,128)(2,1)S(1)}, bf16[1280,256]{1,0:T(8,128)(2,1)S(1)}, u32[]{:S(2)}, u32[]{:S(2)}) collective-permute-start(bf16[1280,256]{1,0:T(8,128)(2,1)S(1)} %copy-done.8), channel_id=1, source_target_pairs={{0,3},{1,2},{2,1},{3,0},{4,7},{5,6},{6,5},{7,4},{8,11},{9,10},{10,... | collective-permute-start | bytes 1966088 | tf_op jit(solution)/shard_map/ppermute | solution.py:19
  48.2 1.9 %collective-permute-start.10 = (bf16[1280,256]{1,0:T(8,128)(2,1)S(1)}, bf16[1280,256]{1,0:T(8,128)(2,1)S(1)}, u32[]{:S(2)}, u32[]{:S(2)}) collective-permute-start(bf16[1280,256]{1,0:T(8,128)(2,1)S(1)} %copy-done.8), channel_id=1, source_target_pairs={{0,1},{1,0},{2,3},{3,2},{4,5},{5,4},{6,7},{7,6},{8,9},{9,8},{10,11... | collective-permute-start | bytes 1966088 | tf_op jit(solution)/shard_map/ppermute | solution.py:19
  50.2 0.9 collective-permute-done.7.refs_2_
  51.0 1.2 collective-permute-done.6.refs_1_
  52.3 2.1 %collective-permute-start.9 = (bf16[1024,256]{1,0:T(8,128)(2,1)S(1)}, bf16[1024,256]{1,0:T(8,128)(2,1)S(1)}, u32[]{:S(2)}, u32[]{:S(2)}) collective-permute-start(bf16[1024,256]{1,0:T(8,128)(2,1)S(1)} %broadcast_select_fusion), channel_id=1, source_target_pairs={{0,4},{4,0},{8,12},{12,8},{16,20},{20,16},{24,28},{28,24},{32,36},... | collective-permute-start | bytes 1572872 | tf_op jit(solution)/shard_map/ppermute | solution.py:19
  54.3 1.9 %collective-permute-done.9.refs_4_ = bf16[1024,256]{1,0:T(8,128)(2,1)S(1)} collective-permute-done((bf16[1024,256]{1,0:T(8,128)(2,1)S(1)}, bf16[1024,256]{1,0:T(8,128)(2,1)S(1)}, u32[]{:S(2)}, u32[]{:S(2)}) %collective-permute-start.9) | collective-permute-done | bytes 524320 | tf_op jit(solution)/shard_map/ppermute | solution.py:19
  56.2 6.9 %aggregate_by_rows.1 = bf16[256,256]{1,0:T(8,128)(2,1)S(1)} custom-call(s32[16,256]{1,0:T(8,128)S(1)} %copy-done.7, f32[512,16]{1,0:T(8,128)S(1)} %copy-done.6, bf16[256,256]{1,0:T(8,128)(2,1)S(1)} %copy-done.5, bf16[1024,256]{1,0:T(8,128)(2,1)S(1)} %last_block.2.refs_0_, bf16[1024,256]{1,0:T(8,128)(2,1)S(1)} %collective-permute-done.6.refs_1_, ...), custom_call_target="tpu_custom_call" | custom-call | flops 6291456 | bytes 2883584 | tf_op jit(solution)/shard_map/aggregate_by_rows/pallas_call | solution.py:320
  63.1 11.8 %collective-permute-done.11.other = bf16[1280,256]{1,0:T(8,128)(2,1)S(1)} collective-permute-done((bf16[1280,256]{1,0:T(8,128)(2,1)S(1)}, bf16[1280,256]{1,0:T(8,128)(2,1)S(1)}, u32[]{:S(2)}, u32[]{:S(2)}) %collective-permute-start.11) | collective-permute-done | bytes 655392 | tf_op jit(solution)/shard_map/ppermute | solution.py:19
  74.9 1.5 combine.1
  76.4 2.1 %collective-permute-start.13 = (bf16[1024,512]{1,0:T(8,128)(2,1)S(1)}, bf16[1024,512]{1,0:T(8,128)(2,1)S(1)}, u32[]{:S(2)}, u32[]{:S(2)}) collective-permute-start(bf16[1024,512]{1,0:T(8,128)(2,1)S(1)} %get-tuple-element.61.mine), channel_id=1, source_target_pairs={{0,4},{4,0},{8,12},{12,8},{16,20},{20,16},{24,28},{28,24},{32,36},... | collective-permute-start | bytes 3145736 | tf_op jit(solution)/shard_map/ppermute | solution.py:19
  78.5 13.0 %all_gather.18.full = bf16[256,1024]{1,0:T(8,128)(2,1)S(1)} all-gather(bf16[256,256]{1,0:T(8,128)(2,1)S(1)} %aggregate_by_rows.1), channel_id=1, replica_groups=mesh['region'=128,'chan'=4] {'chan'}, dimensions={1}, use_global_device_ids=true | all-gather | bytes 655360 | tf_op jit(solution)/shard_map/all_gather | solution.py:34
  91.5 0.6 mesh_step.2
  92.1 2.2 %collective-permute-start.15 = (bf16[256,256]{1,0:T(8,128)(2,1)S(1)}, bf16[256,256]{1,0:T(8,128)(2,1)S(1)}, u32[]{:S(2)}, u32[]{:S(2)}) collective-permute-start(bf16[256,256]{1,0:T(8,128)(2,1)S(1)} %get-tuple-element.64), channel_id=1, source_target_pairs={{0,8},{4,12},{8,16},{12,20},{16,24},{20,28},{24,32},{28,36},{32,40... | collective-permute-start | bytes 393224 | tf_op jit(solution)/shard_map/ppermute | solution.py:24
  94.3 3.6 %collective-permute-start.14 = (bf16[256,256]{1,0:T(8,128)(2,1)S(1)}, bf16[256,256]{1,0:T(8,128)(2,1)S(1)}, u32[]{:S(2)}, u32[]{:S(2)}) collective-permute-start(bf16[256,256]{1,0:T(8,128)(2,1)S(1)} %get-tuple-element.64), channel_id=1, source_target_pairs={{8,0},{12,4},{16,8},{20,12},{24,16},{28,20},{32,24},{36,28},{40,32... | collective-permute-start | bytes 393224 | tf_op jit(solution)/shard_map/ppermute | solution.py:24
  98.0 2.0 %all_gather.20.refs_1_ = bf16[512,256]{1,0:T(8,128)(2,1)S(1)} all-gather(bf16[256,256]{1,0:T(8,128)(2,1)S(1)} %get-tuple-element.64), channel_id=1, replica_groups={{0,4},{8,12},{16,20},{24,28},{32,36},{40,44},{48,52},{56,60},{64,68},{7..., dimensions={0}, use_global_device_ids=true | all-gather | bytes 393216 | tf_op jit(solution)/shard_map/all_gather | solution.py:30
  99.9 4.5 %collective-permute-done.14 = bf16[256,256]{1,0:T(8,128)(2,1)S(1)} collective-permute-done((bf16[256,256]{1,0:T(8,128)(2,1)S(1)}, bf16[256,256]{1,0:T(8,128)(2,1)S(1)}, u32[]{:S(2)}, u32[]{:S(2)}) %collective-permute-start.14) | collective-permute-done | bytes 131104 | tf_op jit(solution)/shard_map/ppermute | solution.py:24
  104.5 2.1 %all_gather.19.refs_0_ = bf16[512,256]{1,0:T(8,128)(2,1)S(1)} all-gather(bf16[256,256]{1,0:T(8,128)(2,1)S(1)} %get-tuple-element.75), channel_id=1, replica_groups={{0,4},{8,12},{16,20},{24,28},{32,36},{40,44},{48,52},{56,60},{64,68},{7..., dimensions={0}, use_global_device_ids=true | all-gather | bytes 393216 | tf_op jit(solution)/shard_map/all_gather | solution.py:30
  106.7 1.8 %aggregate_by_matmul.2 = bf16[256,256]{1,0:T(8,128)(2,1)S(1)} custom-call(s32[256,8]{1,0:T(8,128)S(1)} %copy-done.13, f32[256,8]{1,0:T(8,128)S(1)} %copy-done.14, bf16[256,256]{1,0:T(8,128)(2,1)S(1)} %get-tuple-element.63.receiver_ref.mesh_one, bf16[512,256]{1,0:T(8,128)(2,1)S(1)} %all_gather.19.refs_0_, bf16[512,256]{1,0:T(8,128)(2,1)S(1)} %all_gather.20.refs_1_, ...), custom_call_target="tpu_custom_call" | custom-call | flops 1342177280 | bytes 917504 | tf_op jit(solution)/shard_map/aggregate_by_matmul/pallas_call | solution.py:370
  108.5 12.9 %all_gather.21.full = bf16[256,1024]{1,0:T(8,128)(2,1)S(1)} all-gather(bf16[256,256]{1,0:T(8,128)(2,1)S(1)} %aggregate_by_matmul.2), channel_id=1, replica_groups=mesh['region'=128,'chan'=4] {'chan'}, dimensions={1}, use_global_device_ids=true | all-gather | bytes 655360 | tf_op jit(solution)/shard_map/all_gather | solution.py:34
  121.4 1.1 mesh_step.3
  122.5 1.9 %collective-permute-start.17 = (bf16[256,256]{1,0:T(8,128)(2,1)S(1)}, bf16[256,256]{1,0:T(8,128)(2,1)S(1)}, u32[]{:S(2)}, u32[]{:S(2)}) collective-permute-start(bf16[256,256]{1,0:T(8,128)(2,1)S(1)} %get-tuple-element.66), channel_id=1, source_target_pairs={{0,8},{4,12},{8,16},{12,20},{16,24},{20,28},{24,32},{28,36},{32,40... | collective-permute-start | bytes 393224 | tf_op jit(solution)/shard_map/ppermute | solution.py:24
  124.4 3.9 %collective-permute-start.16 = (bf16[256,256]{1,0:T(8,128)(2,1)S(1)}, bf16[256,256]{1,0:T(8,128)(2,1)S(1)}, u32[]{:S(2)}, u32[]{:S(2)}) collective-permute-start(bf16[256,256]{1,0:T(8,128)(2,1)S(1)} %get-tuple-element.66), channel_id=1, source_target_pairs={{8,0},{12,4},{16,8},{20,12},{24,16},{28,20},{32,24},{36,28},{40,32... | collective-permute-start | bytes 393224 | tf_op jit(solution)/shard_map/ppermute | solution.py:24
  128.4 2.1 %all_gather.23.refs_1_ = bf16[512,256]{1,0:T(8,128)(2,1)S(1)} all-gather(bf16[256,256]{1,0:T(8,128)(2,1)S(1)} %get-tuple-element.66), channel_id=1, replica_groups={{0,4},{8,12},{16,20},{24,28},{32,36},{40,44},{48,52},{56,60},{64,68},{7..., dimensions={0}, use_global_device_ids=true | all-gather | bytes 393216 | tf_op jit(solution)/shard_map/all_gather | solution.py:30
  130.5 4.1 %collective-permute-done.16 = bf16[256,256]{1,0:T(8,128)(2,1)S(1)} collective-permute-done((bf16[256,256]{1,0:T(8,128)(2,1)S(1)}, bf16[256,256]{1,0:T(8,128)(2,1)S(1)}, u32[]{:S(2)}, u32[]{:S(2)}) %collective-permute-start.16) | collective-permute-done | bytes 131104 | tf_op jit(solution)/shard_map/ppermute | solution.py:24
  134.7 2.0 %all_gather.22.refs_0_ = bf16[512,256]{1,0:T(8,128)(2,1)S(1)} all-gather(bf16[256,256]{1,0:T(8,128)(2,1)S(1)} %get-tuple-element.73), channel_id=1, replica_groups={{0,4},{8,12},{16,20},{24,28},{32,36},{40,44},{48,52},{56,60},{64,68},{7..., dimensions={0}, use_global_device_ids=true | all-gather | bytes 393216 | tf_op jit(solution)/shard_map/all_gather | solution.py:30
  136.7 4.2 %aggregate_by_matmul.3.own = bf16[1024,256]{1,0:T(8,128)(2,1)S(1)} custom-call(s32[1024,8]{1,0:T(8,128)S(1)} %copy-done.11, f32[1024,8]{1,0:T(8,128)S(1)} %copy-done.12, bf16[1024,256]{1,0:T(8,128)(2,1)S(1)} %copy-done, bf16[512,256]{1,0:T(8,128)(2,1)S(1)} %all_gather.22.refs_0_, bf16[512,256]{1,0:T(8,128)(2,1)S(1)} %all_gather.23.refs_1_, ...), custom_call_target="tpu_custom_call" | custom-call | flops 2684354560 | bytes 1703936 | tf_op jit(solution)/shard_map/aggregate_by_matmul/pallas_call | solution.py:370
  140.9 3.9 %collective-permute-start.19 = (bf16[512,256]{1,0:T(8,128)(2,1)S(1)}, bf16[512,256]{1,0:T(8,128)(2,1)S(1)}, u32[]{:S(2)}, u32[]{:S(2)}) collective-permute-start(bf16[512,256]{1,0:T(8,128)(2,1)S(1)} %get-tuple-element.68), channel_id=1, source_target_pairs={{0,1},{1,0},{2,3},{3,2},{4,5},{5,4},{6,7},{7,6},{8,9},{9,8},{10,11... | collective-permute-start | bytes 786440 | tf_op jit(solution)/shard_map/ppermute | solution.py:19
  144.8 3.1 %collective-permute-start.20 = (bf16[512,256]{1,0:T(8,128)(2,1)S(1)}, bf16[512,256]{1,0:T(8,128)(2,1)S(1)}, u32[]{:S(2)}, u32[]{:S(2)}) collective-permute-start(bf16[512,256]{1,0:T(8,128)(2,1)S(1)} %get-tuple-element.69), channel_id=1, source_target_pairs={{0,3},{1,2},{2,1},{3,0},{4,7},{5,6},{6,5},{7,4},{8,11},{9,10},{10,... | collective-permute-start | bytes 786440 | tf_op jit(solution)/shard_map/ppermute | solution.py:19
  147.9 3.9 %collective-permute-start.21 = (bf16[512,256]{1,0:T(8,128)(2,1)S(1)}, bf16[512,256]{1,0:T(8,128)(2,1)S(1)}, u32[]{:S(2)}, u32[]{:S(2)}) collective-permute-start(bf16[512,256]{1,0:T(8,128)(2,1)S(1)} %get-tuple-element.68), channel_id=1, source_target_pairs={{0,3},{1,2},{2,1},{3,0},{4,7},{5,6},{6,5},{7,4},{8,11},{9,10},{10,... | collective-permute-start | bytes 786440 | tf_op jit(solution)/shard_map/ppermute | solution.py:19
  151.9 1.9 %collective-permute-start.18 = (bf16[512,256]{1,0:T(8,128)(2,1)S(1)}, bf16[512,256]{1,0:T(8,128)(2,1)S(1)}, u32[]{:S(2)}, u32[]{:S(2)}) collective-permute-start(bf16[512,256]{1,0:T(8,128)(2,1)S(1)} %get-tuple-element.69), channel_id=1, source_target_pairs={{0,1},{1,0},{2,3},{3,2},{4,5},{5,4},{6,7},{7,6},{8,9},{9,8},{10,11... | collective-permute-start | bytes 786440 | tf_op jit(solution)/shard_map/ppermute | solution.py:19
  153.8 3.9 %collective-permute-start.23 = (bf16[512,256]{1,0:T(8,128)(2,1)S(1)}, bf16[512,256]{1,0:T(8,128)(2,1)S(1)}, u32[]{:S(2)}, u32[]{:S(2)}) collective-permute-start(bf16[512,256]{1,0:T(8,128)(2,1)S(1)} %collective-permute-done.19.near_low), channel_id=1, source_target_pairs={{0,3},{1,2},{2,1},{3,0},{4,7},{5,6},{6,5},{7,4},{8,11},{9,10},{10,... | collective-permute-start | bytes 786440 | tf_op jit(solution)/shard_map/ppermute | solution.py:19
  157.7 2.5 %collective-permute-start.22 = (bf16[512,256]{1,0:T(8,128)(2,1)S(1)}, bf16[512,256]{1,0:T(8,128)(2,1)S(1)}, u32[]{:S(2)}, u32[]{:S(2)}) collective-permute-start(bf16[512,256]{1,0:T(8,128)(2,1)S(1)} %collective-permute-done.20.other_top), channel_id=1, source_target_pairs={{0,1},{1,0},{2,3},{3,2},{4,5},{5,4},{6,7},{7,6},{8,9},{9,8},{10,11... | collective-permute-start | bytes 786440 | tf_op jit(solution)/shard_map/ppermute | solution.py:19
  160.3 2.4 %collective-permute-done.21.other_low = bf16[512,256]{1,0:T(8,128)(2,1)S(1)} collective-permute-done((bf16[512,256]{1,0:T(8,128)(2,1)S(1)}, bf16[512,256]{1,0:T(8,128)(2,1)S(1)}, u32[]{:S(2)}, u32[]{:S(2)}) %collective-permute-start.21) | collective-permute-done | bytes 262176 | tf_op jit(solution)/shard_map/ppermute | solution.py:19
  163.3 3.9 %collective-permute-done.23.far_low = bf16[512,256]{1,0:T(8,128)(2,1)S(1)} collective-permute-done((bf16[512,256]{1,0:T(8,128)(2,1)S(1)}, bf16[512,256]{1,0:T(8,128)(2,1)S(1)}, u32[]{:S(2)}, u32[]{:S(2)}) %collective-permute-start.23) | collective-permute-done | bytes 262176 | tf_op jit(solution)/shard_map/ppermute | solution.py:19
  167.2 1.1 last_block.3
  (52 shorter events, 1.7 us)
Async XLA Ops:
  0.6 2.9 %copy-start = (bf16[1024,256]{1,0:T(8,128)(2,1)S(1)}, bf16[1024,256]{1,0:T(8,128)(2,1)}, u32[]{:S(2)}) copy-start(bf16[1024,256]{1,0:T(8,128)(2,1)} %refs_0_.2) | copy-start | bytes 1572868
  3.5 21.6 %copy-start.2 = (bf16[1024,256]{1,0:T(8,128)(2,1)S(1)}, bf16[1024,256]{1,0:T(8,128)(2,1)}, u32[]{:S(2)}) copy-start(bf16[1024,256]{1,0:T(8,128)(2,1)} %weight.5) | copy-start | bytes 1572868
  3.6 12.5 %collective-permute-start.1 = (bf16[512,256]{1,0:T(8,128)(2,1)S(1)}, bf16[512,256]{1,0:T(8,128)(2,1)S(1)}, u32[]{:S(2)}, u32[]{:S(2)}) collective-permute-start(bf16[512,256]{1,0:T(8,128)(2,1)S(1)} %get-tuple-element.70), channel_id=1, source_target_pairs={{0,1},{1,0},{2,3},{3,2},{4,5},{5,4},{6,7},{7,6},{8,9},{9,8},{10,11... | collective-permute-start | bytes 786440 | tf_op jit(solution)/shard_map/ppermute | solution.py:19
  7.1 13.0 %collective-permute-start.2 = (bf16[512,256]{1,0:T(8,128)(2,1)S(1)}, bf16[512,256]{1,0:T(8,128)(2,1)S(1)}, u32[]{:S(2)}, u32[]{:S(2)}) collective-permute-start(bf16[512,256]{1,0:T(8,128)(2,1)S(1)} %get-tuple-element.71), channel_id=1, source_target_pairs={{0,3},{1,2},{2,1},{3,0},{4,7},{5,6},{6,5},{7,4},{8,11},{9,10},{10,... | collective-permute-start | bytes 786440 | tf_op jit(solution)/shard_map/ppermute | solution.py:19
  11.1 13.9 %collective-permute-start.3 = (bf16[512,256]{1,0:T(8,128)(2,1)S(1)}, bf16[512,256]{1,0:T(8,128)(2,1)S(1)}, u32[]{:S(2)}, u32[]{:S(2)}) collective-permute-start(bf16[512,256]{1,0:T(8,128)(2,1)S(1)} %get-tuple-element.70), channel_id=1, source_target_pairs={{0,3},{1,2},{2,1},{3,0},{4,7},{5,6},{6,5},{7,4},{8,11},{9,10},{10,... | collective-permute-start | bytes 786440 | tf_op jit(solution)/shard_map/ppermute | solution.py:19
  14.2 10.9 %collective-permute-start = (bf16[512,256]{1,0:T(8,128)(2,1)S(1)}, bf16[512,256]{1,0:T(8,128)(2,1)S(1)}, u32[]{:S(2)}, u32[]{:S(2)}) collective-permute-start(bf16[512,256]{1,0:T(8,128)(2,1)S(1)} %get-tuple-element.71), channel_id=1, source_target_pairs={{0,1},{1,0},{2,3},{3,2},{4,5},{5,4},{6,7},{7,6},{8,9},{9,8},{10,11... | collective-permute-start | bytes 786440 | tf_op jit(solution)/shard_map/ppermute | solution.py:19
  16.1 13.1 %collective-permute-start.5 = (bf16[512,256]{1,0:T(8,128)(2,1)S(1)}, bf16[512,256]{1,0:T(8,128)(2,1)S(1)}, u32[]{:S(2)}, u32[]{:S(2)}) collective-permute-start(bf16[512,256]{1,0:T(8,128)(2,1)S(1)} %collective-permute-done.1.near_low), channel_id=1, source_target_pairs={{0,3},{1,2},{2,1},{3,0},{4,7},{5,6},{6,5},{7,4},{8,11},{9,10},{10,... | collective-permute-start | bytes 786440 | tf_op jit(solution)/shard_map/ppermute | solution.py:19
  20.2 9.1 %collective-permute-start.4 = (bf16[512,256]{1,0:T(8,128)(2,1)S(1)}, bf16[512,256]{1,0:T(8,128)(2,1)S(1)}, u32[]{:S(2)}, u32[]{:S(2)}) collective-permute-start(bf16[512,256]{1,0:T(8,128)(2,1)S(1)} %collective-permute-done.2.other_top), channel_id=1, source_target_pairs={{0,1},{1,0},{2,3},{3,2},{4,5},{5,4},{6,7},{7,6},{8,9},{9,8},{10,11... | collective-permute-start | bytes 786440 | tf_op jit(solution)/shard_map/ppermute | solution.py:19
  25.7 15.0 %copy-start.8 = (bf16[1280,256]{1,0:T(8,128)(2,1)S(1)}, bf16[1280,256]{1,0:T(8,128)(2,1)}, u32[]{:S(2)}) copy-start(bf16[1280,256]{1,0:T(8,128)(2,1)} %get-tuple-element.55.own) | copy-start | bytes 1966084
  29.5 14.7 %collective-permute-start.8 = (bf16[1024,256]{1,0:T(8,128)(2,1)S(1)}, bf16[1024,256]{1,0:T(8,128)(2,1)S(1)}, u32[]{:S(2)}, u32[]{:S(2)}) collective-permute-start(bf16[1024,256]{1,0:T(8,128)(2,1)S(1)} %last_block.2.refs_0_), channel_id=1, source_target_pairs={{0,4},{4,0},{8,12},{12,8},{16,20},{20,16},{24,28},{28,24},{32,36},... | collective-permute-start | bytes 1572872 | tf_op jit(solution)/shard_map/ppermute | solution.py:19
  31.5 19.5 %collective-permute-start.7 = (bf16[1024,256]{1,0:T(8,128)(2,1)S(1)}, bf16[1024,256]{1,0:T(8,128)(2,1)S(1)}, u32[]{:S(2)}, u32[]{:S(2)}) collective-permute-start(bf16[1024,256]{1,0:T(8,128)(2,1)S(1)} %last_block.2.refs_0_), channel_id=1, source_target_pairs={{8,0},{12,4},{16,8},{20,12},{24,16},{28,20},{32,24},{36,28},{40,32... | collective-permute-start | bytes 1572872 | tf_op jit(solution)/shard_map/ppermute | solution.py:24
  34.7 17.5 %collective-permute-start.6 = (bf16[1024,256]{1,0:T(8,128)(2,1)S(1)}, bf16[1024,256]{1,0:T(8,128)(2,1)S(1)}, u32[]{:S(2)}, u32[]{:S(2)}) collective-permute-start(bf16[1024,256]{1,0:T(8,128)(2,1)S(1)} %last_block.2.refs_0_), channel_id=1, source_target_pairs={{0,8},{4,12},{8,16},{12,20},{16,24},{20,28},{24,32},{28,36},{32,40... | collective-permute-start | bytes 1572872 | tf_op jit(solution)/shard_map/ppermute | solution.py:24
  40.7 15.5 %copy-start.5 = (bf16[256,256]{1,0:T(8,128)(2,1)S(1)}, bf16[256,256]{1,0:T(8,128)(2,1)}, u32[]{:S(2)}) copy-start(bf16[256,256]{1,0:T(8,128)(2,1)} %mesh.1) | copy-start | bytes 393220
  40.7 15.5 %copy-start.6 = (f32[512,16]{1,0:T(8,128)S(1)}, f32[512,16]{1,0:T(8,128)}, u32[]{:S(2)}) copy-start(f32[512,16]{1,0:T(8,128)} %get-tuple-element.48.weight_ref) | copy-start | bytes 98308
  40.7 15.5 %copy-start.7 = (s32[16,256]{1,0:T(8,128)S(1)}, s32[16,256]{1,0:T(8,128)}, u32[]{:S(2)}) copy-start(s32[16,256]{1,0:T(8,128)} %get-tuple-element.47.index_ref) | copy-start | bytes 49156
  40.7 22.4 %collective-permute-start.12 = (bf16[1280,256]{1,0:T(8,128)(2,1)S(1)}, bf16[1280,256]{1,0:T(8,128)(2,1)S(1)}, u32[]{:S(2)}, u32[]{:S(2)}) collective-permute-start(bf16[1280,256]{1,0:T(8,128)(2,1)S(1)} %copy-done.8), channel_id=1, source_target_pairs={{0,2},{1,3},{2,0},{3,1},{4,6},{5,7},{6,4},{7,5},{8,10},{9,11},{10,... | collective-permute-start | bytes 1966088 | tf_op jit(solution)/shard_map/ppermute | solution.py:19
  44.3 30.6 %collective-permute-start.11 = (bf16[1280,256]{1,0:T(8,128)(2,1)S(1)}, bf16[1280,256]{1,0:T(8,128)(2,1)S(1)}, u32[]{:S(2)}, u32[]{:S(2)}) collective-permute-start(bf16[1280,256]{1,0:T(8,128)(2,1)S(1)} %copy-done.8), channel_id=1, source_target_pairs={{0,3},{1,2},{2,1},{3,0},{4,7},{5,6},{6,5},{7,4},{8,11},{9,10},{10,... | collective-permute-start | bytes 1966088 | tf_op jit(solution)/shard_map/ppermute | solution.py:19
  48.2 26.6 %collective-permute-start.10 = (bf16[1280,256]{1,0:T(8,128)(2,1)S(1)}, bf16[1280,256]{1,0:T(8,128)(2,1)S(1)}, u32[]{:S(2)}, u32[]{:S(2)}) collective-permute-start(bf16[1280,256]{1,0:T(8,128)(2,1)S(1)} %copy-done.8), channel_id=1, source_target_pairs={{0,1},{1,0},{2,3},{3,2},{4,5},{5,4},{6,7},{7,6},{8,9},{9,8},{10,11... | collective-permute-start | bytes 1966088 | tf_op jit(solution)/shard_map/ppermute | solution.py:19
  52.2 22.6 %copy-start.9 = (bf16[1024,256]{1,0:T(8,128)(2,1)S(1)}, bf16[1024,256]{1,0:T(8,128)(2,1)}, u32[]{:S(2)}) copy-start(bf16[1024,256]{1,0:T(8,128)(2,1)} %first.1) | copy-start | bytes 1572868
  52.3 22.6 %copy-start.10 = (bf16[1024,256]{1,0:T(8,128)(2,1)S(1)}, bf16[1024,256]{1,0:T(8,128)(2,1)}, u32[]{:S(2)}) copy-start(bf16[1024,256]{1,0:T(8,128)(2,1)} %second.1) | copy-start | bytes 1572868
  52.3 3.9 %collective-permute-start.9 = (bf16[1024,256]{1,0:T(8,128)(2,1)S(1)}, bf16[1024,256]{1,0:T(8,128)(2,1)S(1)}, u32[]{:S(2)}, u32[]{:S(2)}) collective-permute-start(bf16[1024,256]{1,0:T(8,128)(2,1)S(1)} %broadcast_select_fusion), channel_id=1, source_target_pairs={{0,4},{4,0},{8,12},{12,8},{16,20},{20,16},{24,28},{28,24},{32,36},... | collective-permute-start | bytes 1572872 | tf_op jit(solution)/shard_map/ppermute | solution.py:19
  76.4 15.1 %copy-start.1 = (bf16[1024,256]{1,0:T(8,128)(2,1)S(1)}, bf16[1024,256]{1,0:T(8,128)(2,1)}, u32[]{:S(2)}) copy-start(bf16[1024,256]{1,0:T(8,128)(2,1)} %w_out.2) | copy-start | bytes 1572868
  76.4 15.1 %collective-permute-start.13 = (bf16[1024,512]{1,0:T(8,128)(2,1)S(1)}, bf16[1024,512]{1,0:T(8,128)(2,1)S(1)}, u32[]{:S(2)}, u32[]{:S(2)}) collective-permute-start(bf16[1024,512]{1,0:T(8,128)(2,1)S(1)} %get-tuple-element.61.mine), channel_id=1, source_target_pairs={{0,4},{4,0},{8,12},{12,8},{16,20},{20,16},{24,28},{28,24},{32,36},... | collective-permute-start | bytes 3145736 | tf_op jit(solution)/shard_map/ppermute | solution.py:19
  92.1 7.9 %collective-permute-start.15 = (bf16[256,256]{1,0:T(8,128)(2,1)S(1)}, bf16[256,256]{1,0:T(8,128)(2,1)S(1)}, u32[]{:S(2)}, u32[]{:S(2)}) collective-permute-start(bf16[256,256]{1,0:T(8,128)(2,1)S(1)} %get-tuple-element.64), channel_id=1, source_target_pairs={{0,8},{4,12},{8,16},{12,20},{16,24},{20,28},{24,32},{28,36},{32,40... | collective-permute-start | bytes 393224 | tf_op jit(solution)/shard_map/ppermute | solution.py:24
  94.3 10.2 %collective-permute-start.14 = (bf16[256,256]{1,0:T(8,128)(2,1)S(1)}, bf16[256,256]{1,0:T(8,128)(2,1)S(1)}, u32[]{:S(2)}, u32[]{:S(2)}) collective-permute-start(bf16[256,256]{1,0:T(8,128)(2,1)S(1)} %get-tuple-element.64), channel_id=1, source_target_pairs={{8,0},{12,4},{16,8},{20,12},{24,16},{28,20},{32,24},{36,28},{40,32... | collective-permute-start | bytes 393224 | tf_op jit(solution)/shard_map/ppermute | solution.py:24
  104.5 2.2 %copy-start.13 = (s32[256,8]{1,0:T(8,128)S(1)}, s32[256,8]{1,0:T(8,128)}, u32[]{:S(2)}) copy-start(s32[256,8]{1,0:T(8,128)} %get-tuple-element.45.index_ref) | copy-start | bytes 24580
  104.5 2.1 %copy-start.14 = (f32[256,8]{1,0:T(8,128)S(1)}, f32[256,8]{1,0:T(8,128)}, u32[]{:S(2)}) copy-start(f32[256,8]{1,0:T(8,128)} %get-tuple-element.46.weight_ref) | copy-start | bytes 24580
  108.5 12.9 %copy-start.4 = (bf16[1024,256]{1,0:T(8,128)(2,1)S(1)}, bf16[1024,256]{1,0:T(8,128)(2,1)}, u32[]{:S(2)}) copy-start(bf16[1024,256]{1,0:T(8,128)(2,1)} %w_out.3) | copy-start | bytes 1572868
  122.5 8.0 %collective-permute-start.17 = (bf16[256,256]{1,0:T(8,128)(2,1)S(1)}, bf16[256,256]{1,0:T(8,128)(2,1)S(1)}, u32[]{:S(2)}, u32[]{:S(2)}) collective-permute-start(bf16[256,256]{1,0:T(8,128)(2,1)S(1)} %get-tuple-element.66), channel_id=1, source_target_pairs={{0,8},{4,12},{8,16},{12,20},{16,24},{20,28},{24,32},{28,36},{32,40... | collective-permute-start | bytes 393224 | tf_op jit(solution)/shard_map/ppermute | solution.py:24
  124.4 10.2 %collective-permute-start.16 = (bf16[256,256]{1,0:T(8,128)(2,1)S(1)}, bf16[256,256]{1,0:T(8,128)(2,1)S(1)}, u32[]{:S(2)}, u32[]{:S(2)}) collective-permute-start(bf16[256,256]{1,0:T(8,128)(2,1)S(1)} %get-tuple-element.66), channel_id=1, source_target_pairs={{8,0},{12,4},{16,8},{20,12},{24,16},{28,20},{32,24},{36,28},{40,32... | collective-permute-start | bytes 393224 | tf_op jit(solution)/shard_map/ppermute | solution.py:24
  128.4 8.3 %copy-start.12 = (f32[1024,8]{1,0:T(8,128)S(1)}, f32[1024,8]{1,0:T(8,128)}, u32[]{:S(2)}) copy-start(f32[1024,8]{1,0:T(8,128)} %get-tuple-element.43.weight_ref) | copy-start | bytes 98308
  130.5 6.1 %copy-start.11 = (s32[1024,8]{1,0:T(8,128)S(1)}, s32[1024,8]{1,0:T(8,128)}, u32[]{:S(2)}) copy-start(s32[1024,8]{1,0:T(8,128)} %get-tuple-element.42.index_ref) | copy-start | bytes 98308
  140.8 21.9 %copy-start.3 = (bf16[1024,256]{1,0:T(8,128)(2,1)S(1)}, bf16[1024,256]{1,0:T(8,128)(2,1)}, u32[]{:S(2)}) copy-start(bf16[1024,256]{1,0:T(8,128)(2,1)} %weight.7) | copy-start | bytes 1572868
  140.9 12.9 %collective-permute-start.19 = (bf16[512,256]{1,0:T(8,128)(2,1)S(1)}, bf16[512,256]{1,0:T(8,128)(2,1)S(1)}, u32[]{:S(2)}, u32[]{:S(2)}) collective-permute-start(bf16[512,256]{1,0:T(8,128)(2,1)S(1)} %get-tuple-element.68), channel_id=1, source_target_pairs={{0,1},{1,0},{2,3},{3,2},{4,5},{5,4},{6,7},{7,6},{8,9},{9,8},{10,11... | collective-permute-start | bytes 786440 | tf_op jit(solution)/shard_map/ppermute | solution.py:19
  144.8 12.9 %collective-permute-start.20 = (bf16[512,256]{1,0:T(8,128)(2,1)S(1)}, bf16[512,256]{1,0:T(8,128)(2,1)S(1)}, u32[]{:S(2)}, u32[]{:S(2)}) collective-permute-start(bf16[512,256]{1,0:T(8,128)(2,1)S(1)} %get-tuple-element.69), channel_id=1, source_target_pairs={{0,3},{1,2},{2,1},{3,0},{4,7},{5,6},{6,5},{7,4},{8,11},{9,10},{10,... | collective-permute-start | bytes 786440 | tf_op jit(solution)/shard_map/ppermute | solution.py:19
  147.9 14.8 %collective-permute-start.21 = (bf16[512,256]{1,0:T(8,128)(2,1)S(1)}, bf16[512,256]{1,0:T(8,128)(2,1)S(1)}, u32[]{:S(2)}, u32[]{:S(2)}) collective-permute-start(bf16[512,256]{1,0:T(8,128)(2,1)S(1)} %get-tuple-element.68), channel_id=1, source_target_pairs={{0,3},{1,2},{2,1},{3,0},{4,7},{5,6},{6,5},{7,4},{8,11},{9,10},{10,... | collective-permute-start | bytes 786440 | tf_op jit(solution)/shard_map/ppermute | solution.py:19
  151.9 10.8 %collective-permute-start.18 = (bf16[512,256]{1,0:T(8,128)(2,1)S(1)}, bf16[512,256]{1,0:T(8,128)(2,1)S(1)}, u32[]{:S(2)}, u32[]{:S(2)}) collective-permute-start(bf16[512,256]{1,0:T(8,128)(2,1)S(1)} %get-tuple-element.69), channel_id=1, source_target_pairs={{0,1},{1,0},{2,3},{3,2},{4,5},{5,4},{6,7},{7,6},{8,9},{9,8},{10,11... | collective-permute-start | bytes 786440 | tf_op jit(solution)/shard_map/ppermute | solution.py:19
  153.8 13.4 %collective-permute-start.23 = (bf16[512,256]{1,0:T(8,128)(2,1)S(1)}, bf16[512,256]{1,0:T(8,128)(2,1)S(1)}, u32[]{:S(2)}, u32[]{:S(2)}) collective-permute-start(bf16[512,256]{1,0:T(8,128)(2,1)S(1)} %collective-permute-done.19.near_low), channel_id=1, source_target_pairs={{0,3},{1,2},{2,1},{3,0},{4,7},{5,6},{6,5},{7,4},{8,11},{9,10},{10,... | collective-permute-start | bytes 786440 | tf_op jit(solution)/shard_map/ppermute | solution.py:19
  157.7 9.5 %collective-permute-start.22 = (bf16[512,256]{1,0:T(8,128)(2,1)S(1)}, bf16[512,256]{1,0:T(8,128)(2,1)S(1)}, u32[]{:S(2)}, u32[]{:S(2)}) collective-permute-start(bf16[512,256]{1,0:T(8,128)(2,1)S(1)} %collective-permute-done.20.other_top), channel_id=1, source_target_pairs={{0,1},{1,0},{2,3},{3,2},{4,5},{5,4},{6,7},{7,6},{8,9},{9,8},{10,11... | collective-permute-start | bytes 786440 | tf_op jit(solution)/shard_map/ppermute | solution.py:19

commit v3 on v2

--- a/solution.py
+++ b/solution.py
@@ -30,8 +30,8 @@
     return lax.all_gather(shard, "region", axis=0, tiled=True, axis_index_groups=groups)
 
 
-def gather_chan(values):
-    return lax.all_gather(values, "chan", axis=1, tiled=True)
+def gather_chan(copies):
+    return lax.all_to_all(copies, "chan", split_axis=0, concat_axis=0, tiled=True)
 
 
 def dot(a, b):
@@ -101,7 +101,7 @@
     return out, later
 
 
-def combine_kernel(me_ref, own, near, other, far, first, second, mixed, base):
+def combine_kernel(me_ref, own, near, other, far, first, second, _, mixed, base):
     me, width = me_ref[0], own.shape[1]
     rows, last = own.shape[0], base.shape[0]
 
@@ -119,7 +119,7 @@
     one_block(rows - last, last, [(base, pl.ds(0, last))])
 
 
-def combine(blocks, first, second, last):
+def combine(blocks, first, second, last, after):
     rows, width = blocks[0].shape
     return pl.pallas_call(
         combine_kernel,
@@ -127,36 +127,41 @@
             jax.ShapeDtypeStruct((rows - last, 2 * width), blocks[0].dtype),
             jax.ShapeDtypeStruct((last, 2 * width), jnp.float32),
         ),
-        in_specs=[SMEM] + [VMEM] * 6,
+        in_specs=[SMEM] + [VMEM] * 6 + [HBM],
         out_specs=(VMEM, VMEM),
         compiler_params=pltpu.CompilerParams(vmem_limit_bytes=10 << 20),
         cost_estimate=pl.CostEstimate(flops=16 * rows * width * width, bytes_accessed=16 * rows * width, transcendentals=0),
         name="combine",
-    )(lax.axis_index("chan").astype(jnp.int32)[None], *blocks, first, second)
-
-
-def halves_dot(core, full, mine, other, rows, columns):
-    half = full.shape[1] // 2
-    first = pl.multiple_of(core * half, half)
-    second = pl.multiple_of((1 - core) * half, half)
-    return dot(full[:, pl.ds(first, half)], mine[rows, columns]) + dot(full[:, pl.ds(second, half)], other[rows, columns])
+    )(lax.axis_index("chan").astype(jnp.int32)[None], *blocks, first, second, after)
+
+
+def gathered_dot(full, weight):
+    depth = full.shape[2]
+    return sum(dot(full[j], weight[j * depth : (j + 1) * depth, :]) for j in range(full.shape[0]))
+
+
+def halves_dot(core, full, mine, other, first, columns):
+    half, depth = full.shape[0] // 2, full.shape[2]
+    total = 0
+    for owner, held in ((core, mine), (1 - core, other)):
+        for j in range(half):
+            total += dot(full[owner * half + j], held[pl.ds(first + j * depth, depth), columns])
+    return total
 
 
 def mesh_one_kernel(core_ref, full, mesh, w_out, mine, other, base, mesh_one, projected, later):
     core, width = core_ref[0], mesh.shape[1]
-    half = full.shape[1] // 2
-    rows, one, two = slice(0, half), slice(0, width), slice(width, 2 * width)
-    mesh_one[...] = (mesh[...].astype(jnp.float32) + dot(full[...], w_out[...])).astype(mesh_one.dtype)
-    projected[...] = (base[:, one] + halves_dot(core, full, mine, other, rows, one)).astype(projected.dtype)
-    later[...] = base[:, two] + halves_dot(core, full, mine, other, rows, two)
+    one, two = slice(0, width), slice(width, 2 * width)
+    mesh_one[...] = (mesh[...].astype(jnp.float32) + gathered_dot(full, w_out)).astype(mesh_one.dtype)
+    projected[...] = (base[:, one] + halves_dot(core, full, mine, other, 0, one)).astype(projected.dtype)
+    later[...] = base[:, two] + halves_dot(core, full, mine, other, 0, two)
 
 
 def mesh_next_kernel(core_ref, full, mesh_one, w_out, mine, other, later, mesh_next, projected):
-    core, width = core_ref[0], mesh_one.shape[1]
-    half = full.shape[1] // 2
-    rows, two = slice(half, 2 * half), slice(width, 2 * width)
-    mesh_next[...] = (mesh_one[...].astype(jnp.float32) + dot(full[...], w_out[...])).astype(mesh_next.dtype)
-    projected[...] = (later[...] + halves_dot(core, full, mine, other, rows, two)).astype(projected.dtype)
+    width = mesh_one.shape[1]
+    first, two = w_out.shape[0] // 2, slice(width, 2 * width)
+    mesh_next[...] = (mesh_one[...].astype(jnp.float32) + gathered_dot(full, w_out)).astype(mesh_next.dtype)
+    projected[...] = (later[...] + halves_dot(core_ref[0], full, mine, other, first, two)).astype(projected.dtype)
 
 
 def mesh_step(kernel, like, kinds, core, *operands):
@@ -178,8 +183,9 @@
     other, later = lax.optimization_barrier((other, later))
     sent = [exchange(later, "chan", lambda i: i ^ 1), exchange(later, "chan", lambda i: 3 - i)]
     first = lax.axis_index("region") % 2 == 0
-    third = exchange(jnp.where(first, above, below), "region", lambda i: i ^ 1)
-    return [projected, below, above, other, third], sent
+    half = projected.shape[0] // 2
+    chosen = [jnp.where(first, above[rows], below[rows]) for rows in (slice(0, half), slice(half, None))]
+    return [projected, below, above, other] + [core_pair(rows) for rows in chosen], sent
 
 
 def window_of_pairs(projected):
@@ -223,6 +229,11 @@
         shift_by = rows.bit_length() - 1
         return (piece((index >> shift_by) - me) << shift_by) + (index & (rows - 1))
 
+    def halved(at, rows):
+        row, half = at - 4 * rows, rows // 2
+        moved = 4 * rows + jnp.where(row < half, row, row + half) + (1 - core) * half
+        return jnp.where(row < 0, at, moved)
+
     def scaled(w, c):
         live = lax.broadcasted_iota(jnp.int32, w.shape, 0) < c[...]
         return jnp.where(live, w[...], 0.0) / c[...].astype(jnp.float32)
@@ -232,7 +243,7 @@
             v = jnp.concatenate([v, jnp.zeros((TILE - v.shape[0], v.shape[1]), v.dtype)], axis=0)
         return v.T
 
-    o1[...] = 2 * place(i1[...], n_grid, of_exchanges)
+    o1[...] = 2 * halved(place(i1[...], n_grid, of_exchanges), n_grid)
     tall = upright(scaled(w1, c1))
     for s in range(2):
         s1[pl.ds(s, tall.shape[0], 2), :] = tall
@@ -310,16 +321,18 @@
 
     lax.fori_loop(0, rows // (2 * group), two_groups, 0)
     for s in range(2):
-        out_ref[:, s * LANES : (s + 1) * LANES] = total[pl.ds(s, rows, 2), :].astype(out_ref.dtype)
-
-
-def aggregate_by_rows(index, weights, receivers, parts, group=8):
+        value = total[pl.ds(s, rows, 2), :].astype(out_ref.dtype)
+        for j in range(out_ref.shape[0]):
+            out_ref[j, :, s * LANES : (s + 1) * LANES] = value
+
+
+def aggregate_by_rows(index, weights, receivers, parts, copies, group=8):
     slots, rows = index.shape
     width = receivers.shape[1]
     sizes = tuple(part.shape[0] for part in parts)
     return pl.pallas_call(
         functools.partial(by_rows_kernel, slots, rows, group, sizes),
-        out_shape=jax.ShapeDtypeStruct((rows, width), receivers.dtype),
+        out_shape=jax.ShapeDtypeStruct((copies, rows, width), receivers.dtype),
         in_specs=[SMEM] + [VMEM] * (2 + len(parts)),
         out_specs=VMEM,
         scratch_shapes=[
@@ -329,11 +342,7 @@
             pltpu.VMEM((2 * rows, LANES), jnp.float32),
         ],
         compiler_params=pltpu.CompilerParams(vmem_limit_bytes=14 << 20),
-        cost_estimate=pl.CostEstimate(
-            flops=6 * slots * rows * width,
-            bytes_accessed=2 * width * (sum(sizes) + 2 * rows),
-            transcendentals=slots * rows * width,
-        ),
+        cost_estimate=pl.CostEstimate(flops=1, bytes_accessed=1, transcendentals=0),
         name="aggregate_by_rows",
     )(index, weights, receivers, *parts)
 
@@ -358,18 +367,19 @@
             fetched = dot(jnp.concatenate(pick, axis=1), window[...])
             h = (fetched + mine) * 0.5
             acc = acc + (h + h * jnp.tanh(h)) * weight[:, k : k + 1]
-        out_ref[at, :] = acc.astype(out_ref.dtype)
+        for j in range(out_ref.shape[0]):
+            out_ref[j, at, :] = acc.astype(out_ref.dtype)
         return carry
 
     lax.fori_loop(0, rows // block, one_block, 0)
 
 
-def aggregate_by_matmul(slots, index, weights, receivers, parts, block=256):
+def aggregate_by_matmul(slots, index, weights, receivers, parts, copies, block=256):
     rows, width = receivers.shape
     sizes = tuple(part.shape[0] for part in parts)
     return pl.pallas_call(
         functools.partial(by_matmul_kernel, slots, rows, block, sizes),
-        out_shape=jax.ShapeDtypeStruct((rows, width), receivers.dtype),
+        out_shape=jax.ShapeDtypeStruct((copies, rows, width), receivers.dtype),
         in_specs=[VMEM] * (3 + len(parts)),
         out_specs=VMEM,
         scratch_shapes=[pltpu.VMEM((sum(sizes), width), jnp.bfloat16)],
@@ -421,20 +431,20 @@
 
     projected, far = project_by_exchanges(grid_state, enc_send, later=packed)
     window, nearer = window_of_exchanges(projected, packed)
-    agg = aggregate_by_rows(g2m, g2m_w, mesh_state, window)
-
-    agg, packed, nearer, far = lax.optimization_barrier((agg, packed, nearer, far))
-    mine, base = combine([packed, *nearer, far], proc_send, dec_send, n_mesh)
+    n = lax.axis_size("chan")
+    agg = aggregate_by_rows(g2m, g2m_w, mesh_state, window, 1)
+
+    full = lax.all_gather(agg[0], "chan", axis=0)
+    mine, base = combine([packed, *nearer, far], proc_send, dec_send, n_mesh, full)
     other = exchange(mine, "region", lambda i: i ^ 1)
-    agg, base = lax.optimization_barrier((agg, base))
     mesh_one, projected, later = mesh_step(
-        mesh_one_kernel, mesh_state, (bf16, bf16, f32), core[None], gather_chan(agg), mesh_state, enc_out, mine, other, base
+        mesh_one_kernel, mesh_state, (bf16, bf16, f32), core[None], full, mesh_state, enc_out, mine, other, base
     )
-    agg = aggregate_by_matmul(k_m, m2m, m2m_w, mesh_one, window_of_pairs(projected))
+    agg = aggregate_by_matmul(k_m, m2m, m2m_w, mesh_one, window_of_pairs(projected), n)
     mesh_next, projected = mesh_step(
         mesh_next_kernel, mesh_state, (bf16, bf16), core[None], gather_chan(agg), mesh_one, proc_out, mine, other, later
     )
-    agg = aggregate_by_matmul(k_d, m2g, m2g_w, grid_state, window_of_pairs(projected))
+    agg = aggregate_by_matmul(k_d, m2g, m2g_w, grid_state, window_of_pairs(projected), 1)[0]
     grid_next, _ = project_by_exchanges(agg, dec_out, base=(grid_state,))
     return grid_next, mesh_next
 

time: 169 us -> 166 us (0.982)
  blocking collectives: 34.2 us -> 44.8 us
  waiting for transfers between devices: 35.9 us -> 25.7 us
  starting transfers between devices: 75.4 us -> 71.4 us
    all_to_all x0 -> x1, blocking collectives: none -> 13.1 us  [gather_chan(): lax.all_to_all(copies, 'chan', split_axis=0, concat_axis=0, tiled=True)]
    ppermute x18 -> x17, waiting for transfers between devices: 25.2 us -> 14.6 us  [exchange(): return lax.ppermute(shard, axis, [(i, partner(i)) for i in range(n)])]
    all_gather x2 -> x1, blocking collectives: 25.9 us -> 19 us  [shards(): full = lax.all_gather(agg[0], 'chan', axis=0)]
    all_gather x4 -> x6, blocking collectives: 8.24 us -> 12.7 us  [core_pair(): lax.all_gather(shard, 'region', axis=0, tiled=True, axis_index_groups=gro...]
    ppermute x18 -> x17, starting transfers between devices: 54.6 us -> 50.6 us  [exchange(): return lax.ppermute(shard, axis, [(i, partner(i)) for i in range(n)])]
  transfers between devices with their start and end apart: 24 -> 23, of which waited for: 10 -> 9; matrix products, arithmetic and copies ran while one was open for 0% -> 0% of each run, Pallas kernels for 5% -> 5%
where the time goes in v3:
time: 166 us; the launch traced here: 165 us
  starting transfers between devices  71.4 us (43%)
  blocking collectives  44.8 us (27%)
  waiting for transfers between devices  25.7 us (15%)
  Pallas kernels  21.6 us (13%)
    ppermute x17, starting transfers between devices, exchange(): return lax.ppermute(shard, axis, [(i, partner(i)) for i in range(n)])  50.6 us
    ppermute x6, starting transfers between devices, shift(): lax.ppermute(shard, 'region', [(i, i + by) for i in range(n) if 0 <= i +...  20.8 us
    all_gather x1, blocking collectives, shards(): full = lax.all_gather(agg[0], 'chan', axis=0)  19 us
    ppermute x17, waiting for transfers between devices, exchange(): return lax.ppermute(shard, axis, [(i, partner(i)) for i in range(n)])  14.6 us
    all_to_all x1, blocking collectives, gather_chan(): lax.all_to_all(copies, 'chan', split_axis=0, concat_axis=0, tiled=True)  13.1 us
    all_gather x6, blocking collectives, core_pair(): lax.all_gather(shard, 'region', axis=0, tiled=True, axis_index_groups=gro...  12.7 us
    ppermute x6, waiting for transfers between devices, shift(): lax.ppermute(shard, 'region', [(i, i + by) for i in range(n) if 0 <= i +...  11.1 us
    pallas_call x1, Pallas kernels, aggregate_by_rows(): pl.pallas_call(functools.partial(by_rows_kernel, slots, rows, group, size...  6.95 us
  transfers between devices with their start and end apart: 23, of which 9 were waited for; matrix products, arithmetic and copies ran while one was open for 0% of the time, Pallas kernels for 5%

profile of v3, /device:TPU:248, one launch (start us, length us, event | category | flops | bytes accessed | tf_op | source)
XLA Modules:
  0.0 164.9 jit_solution(5298670081871499920)
XLA Ops:
  0.6 2.9 %edges.1 = (s32[16,256]{1,0:T(8,128)}, f32[512,16]{1,0:T(8,128)}, s32[256,8]{1,0:T(8,128)}, f32[256,8]{1,0:T(8,128)}, s32[1024,8]{1,0:T(8,128)}, /*index=5*/f32[1024,8]{1,0:T(8,128)}, bf16[1280,256]{1,0:T(8,128)(2,1)}) custom-call(s32[1]{0:T(128)} %bitcast.1.me_ref, s32[16,256]{1,0:T(8,128)} %refs_0_.1, f32[16,256]{1,0:T(8,128)} %refs_1_.1, ...), custom_call_target="tpu_custom_call" | custom-call | flops 1048576 | bytes 1048576 | tf_op jit(solution)/shard_map/edges/pallas_call | solution.py:269
  3.6 3.5 %collective-permute-start.1 = (bf16[512,256]{1,0:T(8,128)(2,1)S(1)}, bf16[512,256]{1,0:T(8,128)(2,1)S(1)}, u32[]{:S(2)}, u32[]{:S(2)}) collective-permute-start(bf16[512,256]{1,0:T(8,128)(2,1)S(1)} %get-tuple-element.58), channel_id=1, source_target_pairs={{0,1},{1,0},{2,3},{3,2},{4,5},{5,4},{6,7},{7,6},{8,9},{9,8},{10,11... | collective-permute-start | bytes 786440 | tf_op jit(solution)/shard_map/ppermute | solution.py:19
  7.1 4.0 %collective-permute-start.2 = (bf16[512,256]{1,0:T(8,128)(2,1)S(1)}, bf16[512,256]{1,0:T(8,128)(2,1)S(1)}, u32[]{:S(2)}, u32[]{:S(2)}) collective-permute-start(bf16[512,256]{1,0:T(8,128)(2,1)S(1)} %get-tuple-element.59), channel_id=1, source_target_pairs={{0,3},{1,2},{2,1},{3,0},{4,7},{5,6},{6,5},{7,4},{8,11},{9,10},{10,... | collective-permute-start | bytes 786440 | tf_op jit(solution)/shard_map/ppermute | solution.py:19
  11.1 3.0 %collective-permute-start.3 = (bf16[512,256]{1,0:T(8,128)(2,1)S(1)}, bf16[512,256]{1,0:T(8,128)(2,1)S(1)}, u32[]{:S(2)}, u32[]{:S(2)}) collective-permute-start(bf16[512,256]{1,0:T(8,128)(2,1)S(1)} %get-tuple-element.58), channel_id=1, source_target_pairs={{0,3},{1,2},{2,1},{3,0},{4,7},{5,6},{6,5},{7,4},{8,11},{9,10},{10,... | collective-permute-start | bytes 786440 | tf_op jit(solution)/shard_map/ppermute | solution.py:19
  14.2 1.9 %collective-permute-start = (bf16[512,256]{1,0:T(8,128)(2,1)S(1)}, bf16[512,256]{1,0:T(8,128)(2,1)S(1)}, u32[]{:S(2)}, u32[]{:S(2)}) collective-permute-start(bf16[512,256]{1,0:T(8,128)(2,1)S(1)} %get-tuple-element.59), channel_id=1, source_target_pairs={{0,1},{1,0},{2,3},{3,2},{4,5},{5,4},{6,7},{7,6},{8,9},{9,8},{10,11... | collective-permute-start | bytes 786440 | tf_op jit(solution)/shard_map/ppermute | solution.py:19
  16.1 4.0 %collective-permute-start.5 = (bf16[512,256]{1,0:T(8,128)(2,1)S(1)}, bf16[512,256]{1,0:T(8,128)(2,1)S(1)}, u32[]{:S(2)}, u32[]{:S(2)}) collective-permute-start(bf16[512,256]{1,0:T(8,128)(2,1)S(1)} %collective-permute-done.1.near_low), channel_id=1, source_target_pairs={{0,3},{1,2},{2,1},{3,0},{4,7},{5,6},{6,5},{7,4},{8,11},{9,10},{10,... | collective-permute-start | bytes 786440 | tf_op jit(solution)/shard_map/ppermute | solution.py:19
  20.2 3.3 %collective-permute-start.4 = (bf16[512,256]{1,0:T(8,128)(2,1)S(1)}, bf16[512,256]{1,0:T(8,128)(2,1)S(1)}, u32[]{:S(2)}, u32[]{:S(2)}) collective-permute-start(bf16[512,256]{1,0:T(8,128)(2,1)S(1)} %collective-permute-done.2.other_top), channel_id=1, source_target_pairs={{0,1},{1,0},{2,3},{3,2},{4,5},{5,4},{6,7},{7,6},{8,9},{9,8},{10,11... | collective-permute-start | bytes 786440 | tf_op jit(solution)/shard_map/ppermute | solution.py:19
  23.5 1.6 collective-permute-done.3.other_low
  25.7 3.6 %collective-permute-done.5.far_low = bf16[512,256]{1,0:T(8,128)(2,1)S(1)} collective-permute-done((bf16[512,256]{1,0:T(8,128)(2,1)S(1)}, bf16[512,256]{1,0:T(8,128)(2,1)S(1)}, u32[]{:S(2)}, u32[]{:S(2)}) %collective-permute-start.5) | collective-permute-done | bytes 262176 | tf_op jit(solution)/shard_map/ppermute | solution.py:19
  29.5 1.9 %collective-permute-start.8 = (bf16[1024,256]{1,0:T(8,128)(2,1)S(1)}, bf16[1024,256]{1,0:T(8,128)(2,1)S(1)}, u32[]{:S(2)}, u32[]{:S(2)}) collective-permute-start(bf16[1024,256]{1,0:T(8,128)(2,1)S(1)} %last_block.2.refs_0_), channel_id=1, source_target_pairs={{0,4},{4,0},{8,12},{12,8},{16,20},{20,16},{24,28},{28,24},{32,36},... | collective-permute-start | bytes 1572872 | tf_op jit(solution)/shard_map/ppermute | solution.py:19
  31.5 3.3 %collective-permute-start.7 = (bf16[1024,256]{1,0:T(8,128)(2,1)S(1)}, bf16[1024,256]{1,0:T(8,128)(2,1)S(1)}, u32[]{:S(2)}, u32[]{:S(2)}) collective-permute-start(bf16[1024,256]{1,0:T(8,128)(2,1)S(1)} %last_block.2.refs_0_), channel_id=1, source_target_pairs={{8,0},{12,4},{16,8},{20,12},{24,16},{28,20},{32,24},{36,28},{40,32... | collective-permute-start | bytes 1572872 | tf_op jit(solution)/shard_map/ppermute | solution.py:24
  34.7 5.9 %collective-permute-start.6 = (bf16[1024,256]{1,0:T(8,128)(2,1)S(1)}, bf16[1024,256]{1,0:T(8,128)(2,1)S(1)}, u32[]{:S(2)}, u32[]{:S(2)}) collective-permute-start(bf16[1024,256]{1,0:T(8,128)(2,1)S(1)} %last_block.2.refs_0_), channel_id=1, source_target_pairs={{0,8},{4,12},{8,16},{12,20},{16,24},{20,28},{24,32},{28,36},{32,40... | collective-permute-start | bytes 1572872 | tf_op jit(solution)/shard_map/ppermute | solution.py:24
  40.7 3.4 %collective-permute-start.11 = (bf16[1280,256]{1,0:T(8,128)(2,1)S(1)}, bf16[1280,256]{1,0:T(8,128)(2,1)S(1)}, u32[]{:S(2)}, u32[]{:S(2)}) collective-permute-start(bf16[1280,256]{1,0:T(8,128)(2,1)S(1)} %copy-done.8), channel_id=1, source_target_pairs={{0,2},{1,3},{2,0},{3,1},{4,6},{5,7},{6,4},{7,5},{8,10},{9,11},{10,... | collective-permute-start | bytes 1966088 | tf_op jit(solution)/shard_map/ppermute | solution.py:19
  44.1 3.9 %collective-permute-start.10 = (bf16[1280,256]{1,0:T(8,128)(2,1)S(1)}, bf16[1280,256]{1,0:T(8,128)(2,1)S(1)}, u32[]{:S(2)}, u32[]{:S(2)}) collective-permute-start(bf16[1280,256]{1,0:T(8,128)(2,1)S(1)} %copy-done.8), channel_id=1, source_target_pairs={{0,3},{1,2},{2,1},{3,0},{4,7},{5,6},{6,5},{7,4},{8,11},{9,10},{10,... | collective-permute-start | bytes 1966088 | tf_op jit(solution)/shard_map/ppermute | solution.py:19
  48.1 1.9 %collective-permute-start.9 = (bf16[1280,256]{1,0:T(8,128)(2,1)S(1)}, bf16[1280,256]{1,0:T(8,128)(2,1)S(1)}, u32[]{:S(2)}, u32[]{:S(2)}) collective-permute-start(bf16[1280,256]{1,0:T(8,128)(2,1)S(1)} %copy-done.8), channel_id=1, source_target_pairs={{0,1},{1,0},{2,3},{3,2},{4,5},{5,4},{6,7},{7,6},{8,9},{9,8},{10,11... | collective-permute-start | bytes 1966088 | tf_op jit(solution)/shard_map/ppermute | solution.py:19
  50.0 1.0 collective-permute-done.7.refs_2_
  51.0 1.2 collective-permute-done.6.refs_1_
  52.2 2.2 %all_gather.22.refs_5_ = bf16[1024,256]{1,0:T(8,128)(2,1)S(1)} all-gather(bf16[512,256]{1,0:T(8,128)(2,1)S(1)} %get-tuple-element.54), channel_id=1, replica_groups={{0,4},{8,12},{16,20},{24,28},{32,36},{40,44},{48,52},{56,60},{64,68},{7..., dimensions={0}, use_global_device_ids=true | all-gather | bytes 786432 | tf_op jit(solution)/shard_map/all_gather | solution.py:30
  54.4 2.3 %all_gather.21.refs_4_ = bf16[1024,256]{1,0:T(8,128)(2,1)S(1)} all-gather(bf16[512,256]{1,0:T(8,128)(2,1)S(1)} %get-tuple-element.55), channel_id=1, replica_groups={{0,4},{8,12},{16,20},{24,28},{32,36},{40,44},{48,52},{56,60},{64,68},{7..., dimensions={0}, use_global_device_ids=true | all-gather | bytes 786432 | tf_op jit(solution)/shard_map/all_gather | solution.py:30
  56.8 7.0 %aggregate_by_rows.1 = bf16[1,256,256]{2,1,0:T(8,128)(2,1)S(1)} custom-call(s32[16,256]{1,0:T(8,128)S(1)} %copy-done.7, f32[512,16]{1,0:T(8,128)S(1)} %copy-done.6, bf16[256,256]{1,0:T(8,128)(2,1)S(1)} %copy-done.5, bf16[1024,256]{1,0:T(8,128)(2,1)S(1)} %last_block.2.refs_0_, bf16[1024,256]{1,0:T(8,128)(2,1)S(1)} %collective-permute-done.6.refs_1_, ...), custom_call_target="tpu_custom_call" | custom-call | flops 1 | bytes 1 | tf_op jit(solution)/shard_map/aggregate_by_rows/pallas_call | solution.py:333
  63.7 19.0 %all_gather.23._.full = bf16[4,256,256]{2,1,0:T(8,128)(2,1)S(1)} all-gather(bf16[1,256,256]{2,1,0:T(8,128)(2,1)S(1)} %aggregate_by_rows.1), channel_id=1, replica_groups=mesh['region'=128,'chan'=4] {'chan'}, dimensions={0}, use_global_device_ids=true | all-gather | bytes 655360 | tf_op jit(solution)/shard_map/all_gather | solution.py:437
  82.8 1.5 combine.1
  84.3 1.9 %collective-permute-start.12 = (bf16[1024,512]{1,0:T(8,128)(2,1)S(1)}, bf16[1024,512]{1,0:T(8,128)(2,1)S(1)}, u32[]{:S(2)}, u32[]{:S(2)}) collective-permute-start(bf16[1024,512]{1,0:T(8,128)(2,1)S(1)} %get-tuple-element.47.mine), channel_id=1, source_target_pairs={{0,4},{4,0},{8,12},{12,8},{16,20},{20,16},{24,28},{28,24},{32,36},... | collective-permute-start | bytes 3145736 | tf_op jit(solution)/shard_map/ppermute | solution.py:19
  86.3 2.6 %collective-permute-done.12.other = bf16[1024,512]{1,0:T(8,128)(2,1)S(1)} collective-permute-done((bf16[1024,512]{1,0:T(8,128)(2,1)S(1)}, bf16[1024,512]{1,0:T(8,128)(2,1)S(1)}, u32[]{:S(2)}, u32[]{:S(2)}) %collective-permute-start.12) | collective-permute-done | bytes 1048608 | tf_op jit(solution)/shard_map/ppermute | solution.py:19
  88.9 0.6 mesh_step.2
  89.5 2.2 %collective-permute-start.14 = (bf16[256,256]{1,0:T(8,128)(2,1)S(1)}, bf16[256,256]{1,0:T(8,128)(2,1)S(1)}, u32[]{:S(2)}, u32[]{:S(2)}) collective-permute-start(bf16[256,256]{1,0:T(8,128)(2,1)S(1)} %get-tuple-element.50), channel_id=1, source_target_pairs={{0,8},{4,12},{8,16},{12,20},{16,24},{20,28},{24,32},{28,36},{32,40... | collective-permute-start | bytes 393224 | tf_op jit(solution)/shard_map/ppermute | solution.py:24
  91.7 3.6 %collective-permute-start.13 = (bf16[256,256]{1,0:T(8,128)(2,1)S(1)}, bf16[256,256]{1,0:T(8,128)(2,1)S(1)}, u32[]{:S(2)}, u32[]{:S(2)}) collective-permute-start(bf16[256,256]{1,0:T(8,128)(2,1)S(1)} %get-tuple-element.50), channel_id=1, source_target_pairs={{8,0},{12,4},{16,8},{20,12},{24,16},{28,20},{32,24},{36,28},{40,32... | collective-permute-start | bytes 393224 | tf_op jit(solution)/shard_map/ppermute | solution.py:24
  95.3 2.0 %all_gather.25.refs_1_ = bf16[512,256]{1,0:T(8,128)(2,1)S(1)} all-gather(bf16[256,256]{1,0:T(8,128)(2,1)S(1)} %get-tuple-element.50), channel_id=1, replica_groups={{0,4},{8,12},{16,20},{24,28},{32,36},{40,44},{48,52},{56,60},{64,68},{7..., dimensions={0}, use_global_device_ids=true | all-gather | bytes 393216 | tf_op jit(solution)/shard_map/all_gather | solution.py:30
  97.3 4.8 %collective-permute-done.13 = bf16[256,256]{1,0:T(8,128)(2,1)S(1)} collective-permute-done((bf16[256,256]{1,0:T(8,128)(2,1)S(1)}, bf16[256,256]{1,0:T(8,128)(2,1)S(1)}, u32[]{:S(2)}, u32[]{:S(2)}) %collective-permute-start.13) | collective-permute-done | bytes 131104 | tf_op jit(solution)/shard_map/ppermute | solution.py:24
  102.2 2.1 %all_gather.24.refs_0_ = bf16[512,256]{1,0:T(8,128)(2,1)S(1)} all-gather(bf16[256,256]{1,0:T(8,128)(2,1)S(1)} %get-tuple-element.63), channel_id=1, replica_groups={{0,4},{8,12},{16,20},{24,28},{32,36},{40,44},{48,52},{56,60},{64,68},{7..., dimensions={0}, use_global_device_ids=true | all-gather | bytes 393216 | tf_op jit(solution)/shard_map/all_gather | solution.py:30
  104.3 1.8 %aggregate_by_matmul.2 = bf16[4,256,256]{2,1,0:T(8,128)(2,1)S(1)} custom-call(s32[256,8]{1,0:T(8,128)S(1)} %copy-done.13, f32[256,8]{1,0:T(8,128)S(1)} %copy-done.14, bf16[256,256]{1,0:T(8,128)(2,1)S(1)} %get-tuple-element.49.receiver_ref.mesh_one, bf16[512,256]{1,0:T(8,128)(2,1)S(1)} %all_gather.24.refs_0_, bf16[512,256]{1,0:T(8,128)(2,1)S(1)} %all_gather.25.refs_1_, ...), custom_call_target="tpu_custom_call" | custom-call | flops 1342177280 | bytes 917504 | tf_op jit(solution)/shard_map/aggregate_by_matmul/pallas_call | solution.py:380
  106.2 13.1 %all_to_all.5.full = bf16[4,256,256]{2,1,0:T(8,128)(2,1)S(1)} all-to-all(bf16[4,256,256]{2,1,0:T(8,128)(2,1)S(1)} %aggregate_by_matmul.2), channel_id=1, replica_groups=mesh['region'=128,'chan'=4] {'chan'}, dimensions={0} | all-to-all | bytes 1048576 | tf_op jit(solution)/shard_map/all_to_all | solution.py:34
  119.3 1.1 mesh_step.3
  120.4 1.9 %collective-permute-start.16 = (bf16[256,256]{1,0:T(8,128)(2,1)S(1)}, bf16[256,256]{1,0:T(8,128)(2,1)S(1)}, u32[]{:S(2)}, u32[]{:S(2)}) collective-permute-start(bf16[256,256]{1,0:T(8,128)(2,1)S(1)} %get-tuple-element.52), channel_id=1, source_target_pairs={{0,8},{4,12},{8,16},{12,20},{16,24},{20,28},{24,32},{28,36},{32,40... | collective-permute-start | bytes 393224 | tf_op jit(solution)/shard_map/ppermute | solution.py:24
  122.3 3.9 %collective-permute-start.15 = (bf16[256,256]{1,0:T(8,128)(2,1)S(1)}, bf16[256,256]{1,0:T(8,128)(2,1)S(1)}, u32[]{:S(2)}, u32[]{:S(2)}) collective-permute-start(bf16[256,256]{1,0:T(8,128)(2,1)S(1)} %get-tuple-element.52), channel_id=1, source_target_pairs={{8,0},{12,4},{16,8},{20,12},{24,16},{28,20},{32,24},{36,28},{40,32... | collective-permute-start | bytes 393224 | tf_op jit(solution)/shard_map/ppermute | solution.py:24
  126.2 2.1 %all_gather.27.refs_1_ = bf16[512,256]{1,0:T(8,128)(2,1)S(1)} all-gather(bf16[256,256]{1,0:T(8,128)(2,1)S(1)} %get-tuple-element.52), channel_id=1, replica_groups={{0,4},{8,12},{16,20},{24,28},{32,36},{40,44},{48,52},{56,60},{64,68},{7..., dimensions={0}, use_global_device_ids=true | all-gather | bytes 393216 | tf_op jit(solution)/shard_map/all_gather | solution.py:30
  128.3 4.1 %collective-permute-done.15 = bf16[256,256]{1,0:T(8,128)(2,1)S(1)} collective-permute-done((bf16[256,256]{1,0:T(8,128)(2,1)S(1)}, bf16[256,256]{1,0:T(8,128)(2,1)S(1)}, u32[]{:S(2)}, u32[]{:S(2)}) %collective-permute-start.15) | collective-permute-done | bytes 131104 | tf_op jit(solution)/shard_map/ppermute | solution.py:24
  132.5 2.0 %all_gather.26.refs_0_ = bf16[512,256]{1,0:T(8,128)(2,1)S(1)} all-gather(bf16[256,256]{1,0:T(8,128)(2,1)S(1)} %get-tuple-element.61), channel_id=1, replica_groups={{0,4},{8,12},{16,20},{24,28},{32,36},{40,44},{48,52},{56,60},{64,68},{7..., dimensions={0}, use_global_device_ids=true | all-gather | bytes 393216 | tf_op jit(solution)/shard_map/all_gather | solution.py:30
  134.5 4.2 %aggregate_by_matmul.3 = bf16[1,1024,256]{2,1,0:T(8,128)(2,1)S(1)} custom-call(s32[1024,8]{1,0:T(8,128)S(1)} %copy-done.11, f32[1024,8]{1,0:T(8,128)S(1)} %copy-done.12, bf16[1024,256]{1,0:T(8,128)(2,1)S(1)} %copy-done, bf16[512,256]{1,0:T(8,128)(2,1)S(1)} %all_gather.26.refs_0_, bf16[512,256]{1,0:T(8,128)(2,1)S(1)} %all_gather.27.refs_1_, ...), custom_call_target="tpu_custom_call" | custom-call | flops 2684354560 | bytes 1703936 | tf_op jit(solution)/shard_map/aggregate_by_matmul/pallas_call | solution.py:380
  138.7 2.6 %collective-permute-start.18 = (bf16[512,256]{1,0:T(8,128)(2,1)S(1)}, bf16[512,256]{1,0:T(8,128)(2,1)S(1)}, u32[]{:S(2)}, u32[]{:S(2)}) collective-permute-start(bf16[512,256]{1,0:T(8,128)(2,1)S(1)} %get-tuple-element.56), channel_id=1, source_target_pairs={{0,1},{1,0},{2,3},{3,2},{4,5},{5,4},{6,7},{7,6},{8,9},{9,8},{10,11... | collective-permute-start | bytes 786440 | tf_op jit(solution)/shard_map/ppermute | solution.py:19
  141.3 2.7 %collective-permute-start.19 = (bf16[512,256]{1,0:T(8,128)(2,1)S(1)}, bf16[512,256]{1,0:T(8,128)(2,1)S(1)}, u32[]{:S(2)}, u32[]{:S(2)}) collective-permute-start(bf16[512,256]{1,0:T(8,128)(2,1)S(1)} %get-tuple-element.57), channel_id=1, source_target_pairs={{0,3},{1,2},{2,1},{3,0},{4,7},{5,6},{6,5},{7,4},{8,11},{9,10},{10,... | collective-permute-start | bytes 786440 | tf_op jit(solution)/shard_map/ppermute | solution.py:19
  144.1 4.3 %collective-permute-start.20 = (bf16[512,256]{1,0:T(8,128)(2,1)S(1)}, bf16[512,256]{1,0:T(8,128)(2,1)S(1)}, u32[]{:S(2)}, u32[]{:S(2)}) collective-permute-start(bf16[512,256]{1,0:T(8,128)(2,1)S(1)} %get-tuple-element.56), channel_id=1, source_target_pairs={{0,3},{1,2},{2,1},{3,0},{4,7},{5,6},{6,5},{7,4},{8,11},{9,10},{10,... | collective-permute-start | bytes 786440 | tf_op jit(solution)/shard_map/ppermute | solution.py:19
  148.4 2.2 %collective-permute-start.17 = (bf16[512,256]{1,0:T(8,128)(2,1)S(1)}, bf16[512,256]{1,0:T(8,128)(2,1)S(1)}, u32[]{:S(2)}, u32[]{:S(2)}) collective-permute-start(bf16[512,256]{1,0:T(8,128)(2,1)S(1)} %get-tuple-element.57), channel_id=1, source_target_pairs={{0,1},{1,0},{2,3},{3,2},{4,5},{5,4},{6,7},{7,6},{8,9},{9,8},{10,11... | collective-permute-start | bytes 786440 | tf_op jit(solution)/shard_map/ppermute | solution.py:19
  150.6 3.1 %collective-permute-start.22 = (bf16[512,256]{1,0:T(8,128)(2,1)S(1)}, bf16[512,256]{1,0:T(8,128)(2,1)S(1)}, u32[]{:S(2)}, u32[]{:S(2)}) collective-permute-start(bf16[512,256]{1,0:T(8,128)(2,1)S(1)} %collective-permute-done.18.near_low), channel_id=1, source_target_pairs={{0,3},{1,2},{2,1},{3,0},{4,7},{5,6},{6,5},{7,4},{8,11},{9,10},{10,... | collective-permute-start | bytes 786440 | tf_op jit(solution)/shard_map/ppermute | solution.py:19
  153.7 2.7 %collective-permute-start.21 = (bf16[512,256]{1,0:T(8,128)(2,1)S(1)}, bf16[512,256]{1,0:T(8,128)(2,1)S(1)}, u32[]{:S(2)}, u32[]{:S(2)}) collective-permute-start(bf16[512,256]{1,0:T(8,128)(2,1)S(1)} %collective-permute-done.19.other_top), channel_id=1, source_target_pairs={{0,1},{1,0},{2,3},{3,2},{4,5},{5,4},{6,7},{7,6},{8,9},{9,8},{10,11... | collective-permute-start | bytes 786440 | tf_op jit(solution)/shard_map/ppermute | solution.py:19
  156.4 2.8 %collective-permute-done.20.other_low = bf16[512,256]{1,0:T(8,128)(2,1)S(1)} collective-permute-done((bf16[512,256]{1,0:T(8,128)(2,1)S(1)}, bf16[512,256]{1,0:T(8,128)(2,1)S(1)}, u32[]{:S(2)}, u32[]{:S(2)}) %collective-permute-start.20) | collective-permute-done | bytes 262176 | tf_op jit(solution)/shard_map/ppermute | solution.py:19
  159.8 3.9 %collective-permute-done.22.far_low = bf16[512,256]{1,0:T(8,128)(2,1)S(1)} collective-permute-done((bf16[512,256]{1,0:T(8,128)(2,1)S(1)}, bf16[512,256]{1,0:T(8,128)(2,1)S(1)}, u32[]{:S(2)}, u32[]{:S(2)}) %collective-permute-start.22) | collective-permute-done | bytes 262176 | tf_op jit(solution)/shard_map/ppermute | solution.py:19
  163.8 1.1 last_block.3
  (52 shorter events, 1.7 us)
Async XLA Ops:
  0.6 2.9 %copy-start = (bf16[1024,256]{1,0:T(8,128)(2,1)S(1)}, bf16[1024,256]{1,0:T(8,128)(2,1)}, u32[]{:S(2)}) copy-start(bf16[1024,256]{1,0:T(8,128)(2,1)} %refs_0_.2) | copy-start | bytes 1572868
  3.5 21.6 %copy-start.2 = (bf16[1024,256]{1,0:T(8,128)(2,1)S(1)}, bf16[1024,256]{1,0:T(8,128)(2,1)}, u32[]{:S(2)}) copy-start(bf16[1024,256]{1,0:T(8,128)(2,1)} %weight.5) | copy-start | bytes 1572868
  3.6 12.5 %collective-permute-start.1 = (bf16[512,256]{1,0:T(8,128)(2,1)S(1)}, bf16[512,256]{1,0:T(8,128)(2,1)S(1)}, u32[]{:S(2)}, u32[]{:S(2)}) collective-permute-start(bf16[512,256]{1,0:T(8,128)(2,1)S(1)} %get-tuple-element.58), channel_id=1, source_target_pairs={{0,1},{1,0},{2,3},{3,2},{4,5},{5,4},{6,7},{7,6},{8,9},{9,8},{10,11... | collective-permute-start | bytes 786440 | tf_op jit(solution)/shard_map/ppermute | solution.py:19
  7.1 13.0 %collective-permute-start.2 = (bf16[512,256]{1,0:T(8,128)(2,1)S(1)}, bf16[512,256]{1,0:T(8,128)(2,1)S(1)}, u32[]{:S(2)}, u32[]{:S(2)}) collective-permute-start(bf16[512,256]{1,0:T(8,128)(2,1)S(1)} %get-tuple-element.59), channel_id=1, source_target_pairs={{0,3},{1,2},{2,1},{3,0},{4,7},{5,6},{6,5},{7,4},{8,11},{9,10},{10,... | collective-permute-start | bytes 786440 | tf_op jit(solution)/shard_map/ppermute | solution.py:19
  11.1 13.9 %collective-permute-start.3 = (bf16[512,256]{1,0:T(8,128)(2,1)S(1)}, bf16[512,256]{1,0:T(8,128)(2,1)S(1)}, u32[]{:S(2)}, u32[]{:S(2)}) collective-permute-start(bf16[512,256]{1,0:T(8,128)(2,1)S(1)} %get-tuple-element.58), channel_id=1, source_target_pairs={{0,3},{1,2},{2,1},{3,0},{4,7},{5,6},{6,5},{7,4},{8,11},{9,10},{10,... | collective-permute-start | bytes 786440 | tf_op jit(solution)/shard_map/ppermute | solution.py:19
  14.2 10.9 %collective-permute-start = (bf16[512,256]{1,0:T(8,128)(2,1)S(1)}, bf16[512,256]{1,0:T(8,128)(2,1)S(1)}, u32[]{:S(2)}, u32[]{:S(2)}) collective-permute-start(bf16[512,256]{1,0:T(8,128)(2,1)S(1)} %get-tuple-element.59), channel_id=1, source_target_pairs={{0,1},{1,0},{2,3},{3,2},{4,5},{5,4},{6,7},{7,6},{8,9},{9,8},{10,11... | collective-permute-start | bytes 786440 | tf_op jit(solution)/shard_map/ppermute | solution.py:19
  16.1 13.1 %collective-permute-start.5 = (bf16[512,256]{1,0:T(8,128)(2,1)S(1)}, bf16[512,256]{1,0:T(8,128)(2,1)S(1)}, u32[]{:S(2)}, u32[]{:S(2)}) collective-permute-start(bf16[512,256]{1,0:T(8,128)(2,1)S(1)} %collective-permute-done.1.near_low), channel_id=1, source_target_pairs={{0,3},{1,2},{2,1},{3,0},{4,7},{5,6},{6,5},{7,4},{8,11},{9,10},{10,... | collective-permute-start | bytes 786440 | tf_op jit(solution)/shard_map/ppermute | solution.py:19
  20.2 9.1 %collective-permute-start.4 = (bf16[512,256]{1,0:T(8,128)(2,1)S(1)}, bf16[512,256]{1,0:T(8,128)(2,1)S(1)}, u32[]{:S(2)}, u32[]{:S(2)}) collective-permute-start(bf16[512,256]{1,0:T(8,128)(2,1)S(1)} %collective-permute-done.2.other_top), channel_id=1, source_target_pairs={{0,1},{1,0},{2,3},{3,2},{4,5},{5,4},{6,7},{7,6},{8,9},{9,8},{10,11... | collective-permute-start | bytes 786440 | tf_op jit(solution)/shard_map/ppermute | solution.py:19
  25.7 15.0 %copy-start.8 = (bf16[1280,256]{1,0:T(8,128)(2,1)S(1)}, bf16[1280,256]{1,0:T(8,128)(2,1)}, u32[]{:S(2)}) copy-start(bf16[1280,256]{1,0:T(8,128)(2,1)} %get-tuple-element.46.own) | copy-start | bytes 1966084
  29.5 14.6 %collective-permute-start.8 = (bf16[1024,256]{1,0:T(8,128)(2,1)S(1)}, bf16[1024,256]{1,0:T(8,128)(2,1)S(1)}, u32[]{:S(2)}, u32[]{:S(2)}) collective-permute-start(bf16[1024,256]{1,0:T(8,128)(2,1)S(1)} %last_block.2.refs_0_), channel_id=1, source_target_pairs={{0,4},{4,0},{8,12},{12,8},{16,20},{20,16},{24,28},{28,24},{32,36},... | collective-permute-start | bytes 1572872 | tf_op jit(solution)/shard_map/ppermute | solution.py:19
  31.5 19.5 %collective-permute-start.7 = (bf16[1024,256]{1,0:T(8,128)(2,1)S(1)}, bf16[1024,256]{1,0:T(8,128)(2,1)S(1)}, u32[]{:S(2)}, u32[]{:S(2)}) collective-permute-start(bf16[1024,256]{1,0:T(8,128)(2,1)S(1)} %last_block.2.refs_0_), channel_id=1, source_target_pairs={{8,0},{12,4},{16,8},{20,12},{24,16},{28,20},{32,24},{36,28},{40,32... | collective-permute-start | bytes 1572872 | tf_op jit(solution)/shard_map/ppermute | solution.py:24
  34.7 17.5 %collective-permute-start.6 = (bf16[1024,256]{1,0:T(8,128)(2,1)S(1)}, bf16[1024,256]{1,0:T(8,128)(2,1)S(1)}, u32[]{:S(2)}, u32[]{:S(2)}) collective-permute-start(bf16[1024,256]{1,0:T(8,128)(2,1)S(1)} %last_block.2.refs_0_), channel_id=1, source_target_pairs={{0,8},{4,12},{8,16},{12,20},{16,24},{20,28},{24,32},{28,36},{32,40... | collective-permute-start | bytes 1572872 | tf_op jit(solution)/shard_map/ppermute | solution.py:24
  40.7 42.1 %collective-permute-start.11 = (bf16[1280,256]{1,0:T(8,128)(2,1)S(1)}, bf16[1280,256]{1,0:T(8,128)(2,1)S(1)}, u32[]{:S(2)}, u32[]{:S(2)}) collective-permute-start(bf16[1280,256]{1,0:T(8,128)(2,1)S(1)} %copy-done.8), channel_id=1, source_target_pairs={{0,2},{1,3},{2,0},{3,1},{4,6},{5,7},{6,4},{7,5},{8,10},{9,11},{10,... | collective-permute-start | bytes 1966088 | tf_op jit(solution)/shard_map/ppermute | solution.py:19
  44.1 38.6 %collective-permute-start.10 = (bf16[1280,256]{1,0:T(8,128)(2,1)S(1)}, bf16[1280,256]{1,0:T(8,128)(2,1)S(1)}, u32[]{:S(2)}, u32[]{:S(2)}) collective-permute-start(bf16[1280,256]{1,0:T(8,128)(2,1)S(1)} %copy-done.8), channel_id=1, source_target_pairs={{0,3},{1,2},{2,1},{3,0},{4,7},{5,6},{6,5},{7,4},{8,11},{9,10},{10,... | collective-permute-start | bytes 1966088 | tf_op jit(solution)/shard_map/ppermute | solution.py:19
  48.1 34.7 %collective-permute-start.9 = (bf16[1280,256]{1,0:T(8,128)(2,1)S(1)}, bf16[1280,256]{1,0:T(8,128)(2,1)S(1)}, u32[]{:S(2)}, u32[]{:S(2)}) collective-permute-start(bf16[1280,256]{1,0:T(8,128)(2,1)S(1)} %copy-done.8), channel_id=1, source_target_pairs={{0,1},{1,0},{2,3},{3,2},{4,5},{5,4},{6,7},{7,6},{8,9},{9,8},{10,11... | collective-permute-start | bytes 1966088 | tf_op jit(solution)/shard_map/ppermute | solution.py:19
  54.4 2.3 %copy-start.5 = (bf16[256,256]{1,0:T(8,128)(2,1)S(1)}, bf16[256,256]{1,0:T(8,128)(2,1)}, u32[]{:S(2)}) copy-start(bf16[256,256]{1,0:T(8,128)(2,1)} %mesh.1) | copy-start | bytes 393220
  54.4 2.3 %copy-start.6 = (f32[512,16]{1,0:T(8,128)S(1)}, f32[512,16]{1,0:T(8,128)}, u32[]{:S(2)}) copy-start(f32[512,16]{1,0:T(8,128)} %get-tuple-element.41.weight_ref) | copy-start | bytes 98308
  54.4 2.3 %copy-start.7 = (s32[16,256]{1,0:T(8,128)S(1)}, s32[16,256]{1,0:T(8,128)}, u32[]{:S(2)}) copy-start(s32[16,256]{1,0:T(8,128)} %get-tuple-element.40.index_ref) | copy-start | bytes 49156
  56.7 26.0 %copy-start.10 = (bf16[1024,256]{1,0:T(8,128)(2,1)S(1)}, bf16[1024,256]{1,0:T(8,128)(2,1)}, u32[]{:S(2)}) copy-start(bf16[1024,256]{1,0:T(8,128)(2,1)} %second.1) | copy-start | bytes 1572868
  63.7 19.1 %copy-start.9 = (bf16[1024,256]{1,0:T(8,128)(2,1)S(1)}, bf16[1024,256]{1,0:T(8,128)(2,1)}, u32[]{:S(2)}) copy-start(bf16[1024,256]{1,0:T(8,128)(2,1)} %first.1) | copy-start | bytes 1572868
  82.8 6.1 %copy-start.1 = (bf16[1024,256]{1,0:T(8,128)(2,1)S(1)}, bf16[1024,256]{1,0:T(8,128)(2,1)}, u32[]{:S(2)}) copy-start(bf16[1024,256]{1,0:T(8,128)(2,1)} %w_out.2) | copy-start | bytes 1572868
  84.3 4.6 %collective-permute-start.12 = (bf16[1024,512]{1,0:T(8,128)(2,1)S(1)}, bf16[1024,512]{1,0:T(8,128)(2,1)S(1)}, u32[]{:S(2)}, u32[]{:S(2)}) collective-permute-start(bf16[1024,512]{1,0:T(8,128)(2,1)S(1)} %get-tuple-element.47.mine), channel_id=1, source_target_pairs={{0,4},{4,0},{8,12},{12,8},{16,20},{20,16},{24,28},{28,24},{32,36},... | collective-permute-start | bytes 3145736 | tf_op jit(solution)/shard_map/ppermute | solution.py:19
  89.5 7.9 %collective-permute-start.14 = (bf16[256,256]{1,0:T(8,128)(2,1)S(1)}, bf16[256,256]{1,0:T(8,128)(2,1)S(1)}, u32[]{:S(2)}, u32[]{:S(2)}) collective-permute-start(bf16[256,256]{1,0:T(8,128)(2,1)S(1)} %get-tuple-element.50), channel_id=1, source_target_pairs={{0,8},{4,12},{8,16},{12,20},{16,24},{20,28},{24,32},{28,36},{32,40... | collective-permute-start | bytes 393224 | tf_op jit(solution)/shard_map/ppermute | solution.py:24
  91.7 10.5 %collective-permute-start.13 = (bf16[256,256]{1,0:T(8,128)(2,1)S(1)}, bf16[256,256]{1,0:T(8,128)(2,1)S(1)}, u32[]{:S(2)}, u32[]{:S(2)}) collective-permute-start(bf16[256,256]{1,0:T(8,128)(2,1)S(1)} %get-tuple-element.50), channel_id=1, source_target_pairs={{8,0},{12,4},{16,8},{20,12},{24,16},{28,20},{32,24},{36,28},{40,32... | collective-permute-start | bytes 393224 | tf_op jit(solution)/shard_map/ppermute | solution.py:24
  102.2 2.2 %copy-start.13 = (s32[256,8]{1,0:T(8,128)S(1)}, s32[256,8]{1,0:T(8,128)}, u32[]{:S(2)}) copy-start(s32[256,8]{1,0:T(8,128)} %get-tuple-element.38.index_ref) | copy-start | bytes 24580
  102.2 2.1 %copy-start.14 = (f32[256,8]{1,0:T(8,128)S(1)}, f32[256,8]{1,0:T(8,128)}, u32[]{:S(2)}) copy-start(f32[256,8]{1,0:T(8,128)} %get-tuple-element.39.weight_ref) | copy-start | bytes 24580
  106.2 13.1 %copy-start.4 = (bf16[1024,256]{1,0:T(8,128)(2,1)S(1)}, bf16[1024,256]{1,0:T(8,128)(2,1)}, u32[]{:S(2)}) copy-start(bf16[1024,256]{1,0:T(8,128)(2,1)} %w_out.3) | copy-start | bytes 1572868
  120.4 8.0 %collective-permute-start.16 = (bf16[256,256]{1,0:T(8,128)(2,1)S(1)}, bf16[256,256]{1,0:T(8,128)(2,1)S(1)}, u32[]{:S(2)}, u32[]{:S(2)}) collective-permute-start(bf16[256,256]{1,0:T(8,128)(2,1)S(1)} %get-tuple-element.52), channel_id=1, source_target_pairs={{0,8},{4,12},{8,16},{12,20},{16,24},{20,28},{24,32},{28,36},{32,40... | collective-permute-start | bytes 393224 | tf_op jit(solution)/shard_map/ppermute | solution.py:24
  122.3 10.2 %collective-permute-start.15 = (bf16[256,256]{1,0:T(8,128)(2,1)S(1)}, bf16[256,256]{1,0:T(8,128)(2,1)S(1)}, u32[]{:S(2)}, u32[]{:S(2)}) collective-permute-start(bf16[256,256]{1,0:T(8,128)(2,1)S(1)} %get-tuple-element.52), channel_id=1, source_target_pairs={{8,0},{12,4},{16,8},{20,12},{24,16},{28,20},{32,24},{36,28},{40,32... | collective-permute-start | bytes 393224 | tf_op jit(solution)/shard_map/ppermute | solution.py:24
  126.2 8.3 %copy-start.12 = (f32[1024,8]{1,0:T(8,128)S(1)}, f32[1024,8]{1,0:T(8,128)}, u32[]{:S(2)}) copy-start(f32[1024,8]{1,0:T(8,128)} %get-tuple-element.36.weight_ref) | copy-start | bytes 98308
  128.3 6.1 %copy-start.11 = (s32[1024,8]{1,0:T(8,128)S(1)}, s32[1024,8]{1,0:T(8,128)}, u32[]{:S(2)}) copy-start(s32[1024,8]{1,0:T(8,128)} %get-tuple-element.35.index_ref) | copy-start | bytes 98308
  138.7 20.6 %copy-start.3 = (bf16[1024,256]{1,0:T(8,128)(2,1)S(1)}, bf16[1024,256]{1,0:T(8,128)(2,1)}, u32[]{:S(2)}) copy-start(bf16[1024,256]{1,0:T(8,128)(2,1)} %weight.7) | copy-start | bytes 1572868
  138.7 11.9 %collective-permute-start.18 = (bf16[512,256]{1,0:T(8,128)(2,1)S(1)}, bf16[512,256]{1,0:T(8,128)(2,1)S(1)}, u32[]{:S(2)}, u32[]{:S(2)}) collective-permute-start(bf16[512,256]{1,0:T(8,128)(2,1)S(1)} %get-tuple-element.56), channel_id=1, source_target_pairs={{0,1},{1,0},{2,3},{3,2},{4,5},{5,4},{6,7},{7,6},{8,9},{9,8},{10,11... | collective-permute-start | bytes 786440 | tf_op jit(solution)/shard_map/ppermute | solution.py:19
  141.3 12.3 %collective-permute-start.19 = (bf16[512,256]{1,0:T(8,128)(2,1)S(1)}, bf16[512,256]{1,0:T(8,128)(2,1)S(1)}, u32[]{:S(2)}, u32[]{:S(2)}) collective-permute-start(bf16[512,256]{1,0:T(8,128)(2,1)S(1)} %get-tuple-element.57), channel_id=1, source_target_pairs={{0,3},{1,2},{2,1},{3,0},{4,7},{5,6},{6,5},{7,4},{8,11},{9,10},{10,... | collective-permute-start | bytes 786440 | tf_op jit(solution)/shard_map/ppermute | solution.py:19
  144.1 15.2 %collective-permute-start.20 = (bf16[512,256]{1,0:T(8,128)(2,1)S(1)}, bf16[512,256]{1,0:T(8,128)(2,1)S(1)}, u32[]{:S(2)}, u32[]{:S(2)}) collective-permute-start(bf16[512,256]{1,0:T(8,128)(2,1)S(1)} %get-tuple-element.56), channel_id=1, source_target_pairs={{0,3},{1,2},{2,1},{3,0},{4,7},{5,6},{6,5},{7,4},{8,11},{9,10},{10,... | collective-permute-start | bytes 786440 | tf_op jit(solution)/shard_map/ppermute | solution.py:19
  148.4 10.8 %collective-permute-start.17 = (bf16[512,256]{1,0:T(8,128)(2,1)S(1)}, bf16[512,256]{1,0:T(8,128)(2,1)S(1)}, u32[]{:S(2)}, u32[]{:S(2)}) collective-permute-start(bf16[512,256]{1,0:T(8,128)(2,1)S(1)} %get-tuple-element.57), channel_id=1, source_target_pairs={{0,1},{1,0},{2,3},{3,2},{4,5},{5,4},{6,7},{7,6},{8,9},{9,8},{10,11... | collective-permute-start | bytes 786440 | tf_op jit(solution)/shard_map/ppermute | solution.py:19
  150.6 13.2 %collective-permute-start.22 = (bf16[512,256]{1,0:T(8,128)(2,1)S(1)}, bf16[512,256]{1,0:T(8,128)(2,1)S(1)}, u32[]{:S(2)}, u32[]{:S(2)}) collective-permute-start(bf16[512,256]{1,0:T(8,128)(2,1)S(1)} %collective-permute-done.18.near_low), channel_id=1, source_target_pairs={{0,3},{1,2},{2,1},{3,0},{4,7},{5,6},{6,5},{7,4},{8,11},{9,10},{10,... | collective-permute-start | bytes 786440 | tf_op jit(solution)/shard_map/ppermute | solution.py:19
  153.7 10.1 %collective-permute-start.21 = (bf16[512,256]{1,0:T(8,128)(2,1)S(1)}, bf16[512,256]{1,0:T(8,128)(2,1)S(1)}, u32[]{:S(2)}, u32[]{:S(2)}) collective-permute-start(bf16[512,256]{1,0:T(8,128)(2,1)S(1)} %collective-permute-done.19.other_top), channel_id=1, source_target_pairs={{0,1},{1,0},{2,3},{3,2},{4,5},{5,4},{6,7},{7,6},{8,9},{9,8},{10,11... | collective-permute-start | bytes 786440 | tf_op jit(solution)/shard_map/ppermute | solution.py:19

commit v4 on v3

--- a/solution.py
+++ b/solution.py
@@ -104,19 +104,19 @@
 def combine_kernel(me_ref, own, near, other, far, first, second, _, mixed, base):
     me, width = me_ref[0], own.shape[1]
     rows, last = own.shape[0], base.shape[0]
-
-    def one_block(start, size, targets):
-        at = pl.ds(start, size)
-        for column, weight in ((slice(0, width), first), (slice(width, 2 * width), second)):
-            value = jnp.zeros((size, width), jnp.float32)
-            for source, block in ((me, own), (me ^ 1, near), (3 - me, other), (me ^ 2, far)):
-                value += dot(block[at, :], weight[pl.ds(pl.multiple_of(source * width, width), width), :])
-            for target, to in targets:
-                target[to, column] = value.astype(target.dtype)
-
-    for start in range(0, rows - last, last):
-        one_block(start, last, [(mixed, pl.ds(start, last))])
-    one_block(rows - last, last, [(base, pl.ds(0, last))])
+    half = (rows - last) // 2
+    blocks = [(me, own), (me ^ 1, near), (3 - me, other), (me ^ 2, far)]
+
+    def product(start, size, weight):
+        value = jnp.zeros((size, width), jnp.float32)
+        for source, block in blocks:
+            value += dot(block[pl.ds(start, size), :], weight[pl.ds(pl.multiple_of(source * width, width), width), :])
+        return value
+
+    for section, start, weight in ((0, 0, first), (1, 0, second), (2, half, second)):
+        mixed[pl.ds(section * half, half), :] = product(start, half, weight).astype(mixed.dtype)
+    base[:, :width] = product(2 * half, last, first)
+    base[:, width:] = product(2 * half, last, second)
 
 
 def combine(blocks, first, second, last, after):
@@ -124,7 +124,7 @@
     return pl.pallas_call(
         combine_kernel,
         out_shape=(
-            jax.ShapeDtypeStruct((rows - last, 2 * width), blocks[0].dtype),
+            jax.ShapeDtypeStruct(((rows - last) // 2 * 3, width), blocks[0].dtype),
             jax.ShapeDtypeStruct((last, 2 * width), jnp.float32),
         ),
         in_specs=[SMEM] + [VMEM] * 6 + [HBM],
@@ -140,28 +140,25 @@
     return sum(dot(full[j], weight[j * depth : (j + 1) * depth, :]) for j in range(full.shape[0]))
 
 
-def halves_dot(core, full, mine, other, first, columns):
+def halves_dot(core, full, mine, other, section):
     half, depth = full.shape[0] // 2, full.shape[2]
     total = 0
     for owner, held in ((core, mine), (1 - core, other)):
         for j in range(half):
-            total += dot(full[owner * half + j], held[pl.ds(first + j * depth, depth), columns])
+            total += dot(full[owner * half + j], held[pl.ds((section * half + j) * depth, depth), :])
     return total
 
 
 def mesh_one_kernel(core_ref, full, mesh, w_out, mine, other, base, mesh_one, projected, later):
     core, width = core_ref[0], mesh.shape[1]
-    one, two = slice(0, width), slice(width, 2 * width)
     mesh_one[...] = (mesh[...].astype(jnp.float32) + gathered_dot(full, w_out)).astype(mesh_one.dtype)
-    projected[...] = (base[:, one] + halves_dot(core, full, mine, other, 0, one)).astype(projected.dtype)
-    later[...] = base[:, two] + halves_dot(core, full, mine, other, 0, two)
+    projected[...] = (base[:, :width] + halves_dot(core, full, mine, other, 0)).astype(projected.dtype)
+    later[...] = base[:, width:] + halves_dot(core, full, mine, other, 1)
 
 
 def mesh_next_kernel(core_ref, full, mesh_one, w_out, mine, other, later, mesh_next, projected):
-    width = mesh_one.shape[1]
-    first, two = w_out.shape[0] // 2, slice(width, 2 * width)
     mesh_next[...] = (mesh_one[...].astype(jnp.float32) + gathered_dot(full, w_out)).astype(mesh_next.dtype)
-    projected[...] = (later[...] + halves_dot(core_ref[0], full, mine, other, first, two)).astype(projected.dtype)
+    projected[...] = (later[...] + halves_dot(core_ref[0], full, mine, other, 2)).astype(projected.dtype)
 
 
 def mesh_step(kernel, like, kinds, core, *operands):
@@ -188,99 +185,55 @@
     return [projected, below, above, other] + [core_pair(rows) for rows in chosen], sent
 
 
-def window_of_pairs(projected):
+def window_of_pairs(projected, fetch_own):
     below = shift(projected, 2)
     above = shift(projected, -2)
-    own = core_pair(projected)
+    fetched = fetch_own(core_pair(projected))
+    above, fetched = lax.optimization_barrier((above, fetched))
     first = lax.axis_index("region") % 2 == 0
     outer = core_pair(jnp.where(first, above, below))
     last = jnp.where(first, below, above)
-    return [outer, own, last]
-
-
-def edges_kernel(n_grid, n_mesh, me_ref, *refs):
-    sources, (first, second, mesh), (o1, s1, o2, s2, o3, s3, packed) = refs[:9], refs[9:12], refs[12:19]
-    i1, w1, c1, i2, w2, c2, i3, w3, c3 = held = refs[19:28]
-    semaphores = refs[28]
-    me = me_ref[0]
-    half = first.shape[0] // 2
-    mine = pl.ds(pl.multiple_of((me & 1) * half, half), half)
-    moves = list(zip(sources, held)) + [
-        (first.at[mine, :], packed.at[pl.ds(0, half), :]),
-        (second.at[mine, :], packed.at[pl.ds(half, half), :]),
-        (mesh, packed.at[pl.ds(2 * half, mesh.shape[0]), :]),
-    ]
-    copies = [pltpu.make_async_copy(src, dst, semaphores.at[k]) for k, (src, dst) in enumerate(moves)]
-    for copy in copies:
-        copy.start()
-    for copy in copies:
-        copy.wait()
+    return fetched, [outer, last]
+
+
+def place_in_exchanged(index, rows, me):
     core = me & 1
-
-    def of_exchanges(apart):
-        towards = 1 - 2 * core
-        return jnp.where(apart == 0, 0, jnp.where(apart == -2, 1, jnp.where(apart == 2, 2, jnp.where(apart == towards, 3, 4))))
-
-    def of_pairs(apart):
-        apart = apart + core
-        return jnp.where(apart == 2, 0, jnp.where(apart == -1, 1, jnp.where(apart == 0, 2, jnp.where(apart == 1, 3, 4))))
-
-    def place(index, rows, piece):
-        shift_by = rows.bit_length() - 1
-        return (piece((index >> shift_by) - me) << shift_by) + (index & (rows - 1))
-
-    def halved(at, rows):
-        row, half = at - 4 * rows, rows // 2
-        moved = 4 * rows + jnp.where(row < half, row, row + half) + (1 - core) * half
-        return jnp.where(row < 0, at, moved)
-
-    def scaled(w, c):
-        live = lax.broadcasted_iota(jnp.int32, w.shape, 0) < c[...]
-        return jnp.where(live, w[...], 0.0) / c[...].astype(jnp.float32)
-
-    def upright(v):
-        if v.shape[0] < TILE:
-            v = jnp.concatenate([v, jnp.zeros((TILE - v.shape[0], v.shape[1]), v.dtype)], axis=0)
-        return v.T
-
-    o1[...] = 2 * halved(place(i1[...], n_grid, of_exchanges), n_grid)
-    tall = upright(scaled(w1, c1))
+    apart, row = index // rows - me, index % rows
+    block = jnp.where(apart == 0, 0, jnp.where(apart == -2, 1, jnp.where(apart == 2, 2, 3)))
+    half = rows // 2
+    moved = 4 * rows + jnp.where(row < half, row, row + half) + (1 - core) * half
+    near = (apart == 0) | (apart == 1 - 2 * core) | (apart == 2) | (apart == -2)
+    return jnp.where(near, block * rows + row, moved)
+
+
+def place_in_pairs(index, rows, me, own):
+    shift_by = rows.bit_length() - 1
+    apart = (index >> shift_by) - (me - (me & 1))
+    inside = (apart == 0) | (apart == 1)
+    if own:
+        block = jnp.where(inside, apart, 2)
+    else:
+        block = jnp.where(inside, 3, jnp.where(apart == 2, 0, jnp.where(apart == -1, 1, 2)))
+    return (block << shift_by) + (index & (rows - 1))
+
+
+def scaled(weight, count):
+    live = lax.broadcasted_iota(jnp.int32, weight.shape, 0) < count
+    return jnp.where(live, weight, 0.0) / count.astype(jnp.float32)
+
+
+def upright(v):
+    if v.shape[0] < TILE:
+        v = jnp.concatenate([v, jnp.zeros((TILE - v.shape[0], v.shape[1]), v.dtype)], axis=0)
+    return v.T
+
+
+def by_rows_kernel(slots, rows, group, sizes, index_ref, slot_ref, count_ref, receiver_ref, *refs):
+    parts, out_ref = refs[: len(sizes)], refs[len(sizes)]
+    window, receiver, fetched, total, weight_ref = refs[len(sizes) + 1 :]
+    tall = upright(scaled(slot_ref[...], count_ref[...]))
     for s in range(2):
-        s1[pl.ds(s, tall.shape[0], 2), :] = tall
-    o2[...] = upright(place(i2[...], n_mesh, of_pairs))
-    s2[...] = upright(scaled(w2, c2))
-    o3[...] = upright(place(i3[...], n_mesh, of_pairs))
-    s3[...] = upright(scaled(w3, c3))
-
-
-def edges(n_grid, n_mesh, g2m, m2m, m2g, first, second, mesh):
-    me = lax.axis_index("region").astype(jnp.int32)[None]
-    ops, outs = [me], []
-    for at, (index, weight, count) in enumerate((g2m, m2m, m2g)):
-        slots, rows = index.shape
-        ops += [index, weight, count[None, :]]
-        high = max(slots, TILE)
-        outs += [
-            jax.ShapeDtypeStruct((slots, rows) if at == 0 else (rows, high), jnp.int32),
-            jax.ShapeDtypeStruct((2 * rows if at == 0 else rows, high), jnp.float32),
-        ]
-    packed = (first.shape[0] + mesh.shape[0], mesh.shape[1])
-    outs.append(jax.ShapeDtypeStruct(packed, mesh.dtype))
-    return pl.pallas_call(
-        functools.partial(edges_kernel, n_grid, n_mesh),
-        out_shape=outs,
-        in_specs=[SMEM] + [HBM] * 12,
-        out_specs=[VMEM] * 7,
-        scratch_shapes=[pltpu.VMEM(op.shape, op.dtype) for op in ops[1:]] + [pltpu.SemaphoreType.DMA((12,))],
-        compiler_params=pltpu.CompilerParams(vmem_limit_bytes=60 << 20),
-        cost_estimate=pl.CostEstimate(flops=1 << 20, bytes_accessed=1 << 20, transcendentals=0),
-        name="edges",
-    )(*ops, first, second, mesh)
-
-
-def by_rows_kernel(slots, rows, group, sizes, index_ref, weight_ref, receiver_ref, *refs):
-    parts, out_ref = refs[: len(sizes)], refs[len(sizes)]
-    window, receiver, fetched, total = refs[len(sizes) + 1 :]
+        weight_ref[pl.ds(s, rows, 2), :] = tall
     first = 0
     for part, size in zip(parts, sizes):
         half = part[...].astype(jnp.float32) * 0.5
@@ -326,35 +279,79 @@
             out_ref[j, :, s * LANES : (s + 1) * LANES] = value
 
 
-def aggregate_by_rows(index, weights, receivers, parts, copies, group=8):
+def aggregate_by_rows(index, weights, counts, receivers, parts, copies, group=8):
     slots, rows = index.shape
     width = receivers.shape[1]
     sizes = tuple(part.shape[0] for part in parts)
     return pl.pallas_call(
         functools.partial(by_rows_kernel, slots, rows, group, sizes),
         out_shape=jax.ShapeDtypeStruct((copies, rows, width), receivers.dtype),
-        in_specs=[SMEM] + [VMEM] * (2 + len(parts)),
+        in_specs=[SMEM] + [VMEM] * (3 + len(parts)),
         out_specs=VMEM,
         scratch_shapes=[
             pltpu.VMEM((2 * sum(sizes), LANES), jnp.float32),
             pltpu.VMEM((2 * rows, LANES), jnp.float32),
             pltpu.VMEM((2, group // 4 * slots * TILE, LANES), jnp.float32),
             pltpu.VMEM((2 * rows, LANES), jnp.float32),
+            pltpu.VMEM((2 * rows, slots), jnp.float32),
         ],
         compiler_params=pltpu.CompilerParams(vmem_limit_bytes=14 << 20),
         cost_estimate=pl.CostEstimate(flops=1, bytes_accessed=1, transcendentals=0),
         name="aggregate_by_rows",
-    )(index, weights, receivers, *parts)
-
-
-def by_matmul_kernel(slots, rows, block, sizes, index_ref, weight_ref, receiver_ref, *refs):
-    parts, out_ref, window = refs[: len(sizes)], refs[len(sizes)], refs[len(sizes) + 1]
+    )(index, weights, counts[None, :], receivers, *parts)
+
+
+def pick_rows(index, columns, window):
+    wanted = jnp.broadcast_to(index, (index.shape[0], LANES)).astype(jnp.int16)
+    one, zero = jnp.bfloat16(1), jnp.bfloat16(0)
+    picks = [jnp.where(columns[:, j : j + LANES] == wanted, one, zero) for j in range(0, columns.shape[1], LANES)]
+    return dot(jnp.concatenate(picks, axis=1), window[...])
+
+
+def fetch_kernel(slots, block, me_ref, sender_ref, window, out_ref, index_ref):
+    depth, rows = window.shape[0], sender_ref.shape[1]
+    index_ref[...] = upright(place_in_pairs(sender_ref[...], depth // 2, me_ref[0], True))
+    columns = lax.broadcasted_iota(jnp.int32, (block, depth), 1).astype(jnp.int16)
+
+    def one_block(b, carry):
+        at = pl.ds(pl.multiple_of(b * block, block), block)
+        index = index_ref[at, :]
+        for k in range(slots):
+            out_ref[k, at, :] = pick_rows(index[:, k : k + 1], columns, window).astype(out_ref.dtype)
+        return carry
+
+    lax.fori_loop(0, rows // block, one_block, 0)
+
+
+def fetch_own(senders, window, block=256):
+    slots, rows = senders.shape
+    width = window.shape[1]
+    me = lax.axis_index("region").astype(jnp.int32)[None]
+    return pl.pallas_call(
+        functools.partial(fetch_kernel, slots, block),
+        out_shape=jax.ShapeDtypeStruct((slots, rows, width), window.dtype),
+        in_specs=[SMEM, VMEM, VMEM],
+        out_specs=VMEM,
+        scratch_shapes=[pltpu.VMEM((rows, max(slots, TILE)), jnp.int32)],
+        compiler_params=pltpu.CompilerParams(vmem_limit_bytes=10 << 20),
+        cost_estimate=pl.CostEstimate(
+            flops=2 * slots * rows * window.shape[0] * width, bytes_accessed=2 * slots * rows * width, transcendentals=0
+        ),
+        name="fetch_own",
+    )(me, senders, window)
+
+
+def by_matmul_kernel(slots, block, sizes, me_ref, sender_ref, slot_ref, count_ref, receiver_ref, fetched_ref, *refs):
+    parts, out_ref = refs[: len(sizes)], refs[len(sizes)]
+    window, index_ref, weight_ref = refs[len(sizes) + 1 :]
+    depth, rows = sum(sizes), sender_ref.shape[1]
+    index_ref[...] = upright(place_in_pairs(sender_ref[...], depth // 3, me_ref[0], False))
+    weight_ref[...] = upright(scaled(slot_ref[...], count_ref[...]))
     first = 0
     for part, size in zip(parts, sizes):
         window[first : first + size, :] = part[...]
         first += size
-    columns = lax.broadcasted_iota(jnp.int32, (block, first), 1).astype(jnp.int16)
-    one, zero = jnp.bfloat16(1), jnp.bfloat16(0)
+    columns = lax.broadcasted_iota(jnp.int32, (block, depth), 1).astype(jnp.int16)
 
     def one_block(b, carry):
         at = pl.ds(pl.multiple_of(b * block, block), block)
@@ -362,9 +359,7 @@
         index, weight = index_ref[at, :], weight_ref[at, :]
         acc = jnp.zeros(mine.shape, jnp.float32)
         for k in range(slots):
-            wanted = jnp.broadcast_to(index[:, k : k + 1], (block, LANES)).astype(jnp.int16)
-            pick = [jnp.where(columns[:, j : j + LANES] == wanted, one, zero) for j in range(0, first, LANES)]
-            fetched = dot(jnp.concatenate(pick, axis=1), window[...])
+            fetched = pick_rows(index[:, k : k + 1], columns, window) + fetched_ref[k, at, :].astype(jnp.float32)
             h = (fetched + mine) * 0.5
             acc = acc + (h + h * jnp.tanh(h)) * weight[:, k : k + 1]
         for j in range(out_ref.shape[0]):
@@ -374,15 +369,21 @@
     lax.fori_loop(0, rows // block, one_block, 0)
 
 
-def aggregate_by_matmul(slots, index, weights, receivers, parts, copies, block=256):
-    rows, width = receivers.shape
+def aggregate_by_matmul(senders, weights, counts, receivers, projected, copies, block=256):
+    slots, (rows, width) = senders.shape[0], receivers.shape
+    me = lax.axis_index("region").astype(jnp.int32)[None]
+    fetched, parts = window_of_pairs(projected, functools.partial(fetch_own, senders))
     sizes = tuple(part.shape[0] for part in parts)
     return pl.pallas_call(
-        functools.partial(by_matmul_kernel, slots, rows, block, sizes),
+        functools.partial(by_matmul_kernel, slots, block, sizes),
         out_shape=jax.ShapeDtypeStruct((copies, rows, width), receivers.dtype),
-        in_specs=[VMEM] * (3 + len(parts)),
+        in_specs=[SMEM] + [VMEM] * (5 + len(parts)),
         out_specs=VMEM,
-        scratch_shapes=[pltpu.VMEM((sum(sizes), width), jnp.bfloat16)],
+        scratch_shapes=[
+            pltpu.VMEM((sum(sizes), width), jnp.bfloat16),
+            pltpu.VMEM((rows, max(slots, TILE)), jnp.int32),
+            pltpu.VMEM((rows, max(slots, TILE)), jnp.float32),
+        ],
         compiler_params=pltpu.CompilerParams(vmem_limit_bytes=14 << 20),
         cost_estimate=pl.CostEstimate(
             flops=2 * slots * rows * sum(sizes) * width,
@@ -390,7 +391,7 @@
             transcendentals=slots * rows * width,
         ),
         name="aggregate_by_matmul",
-    )(index, weights, receivers, *parts)
+    )(me, senders, weights, counts[None, :], receivers, fetched, *parts)
 
 
 def shards(
@@ -414,25 +415,16 @@
 ):
     n_grid, n_mesh = grid_state.shape[0], mesh_state.shape[0]
     bf16, f32 = jnp.bfloat16, jnp.float32
-    k_m, k_d = m2m_index.shape[0], m2g_index.shape[0]
     core = lax.axis_index("region").astype(jnp.int32) % 2
-    prepared = edges(
-        n_grid,
-        n_mesh,
-        (g2m_index, g2m_weight, g2m_count),
-        (m2m_index, m2m_weight, m2m_count),
-        (m2g_index, m2g_weight, m2g_count),
-        enc_out,
-        proc_out,
-        mesh_state,
-    )
-    grid_state, prepared = lax.optimization_barrier((grid_state, prepared))
-    g2m, g2m_w, m2m, m2m_w, m2g, m2g_w, packed = prepared
+    half = enc_out.shape[0] // 2
+    own_rows = [lax.dynamic_slice_in_dim(w, core * half, half, axis=0) for w in (enc_out, proc_out)]
+    packed = jnp.concatenate(own_rows + [mesh_state], axis=0)
+    g2m = 2 * place_in_exchanged(g2m_index, n_grid, lax.axis_index("region").astype(jnp.int32))
 
     projected, far = project_by_exchanges(grid_state, enc_send, later=packed)
     window, nearer = window_of_exchanges(projected, packed)
     n = lax.axis_size("chan")
-    agg = aggregate_by_rows(g2m, g2m_w, mesh_state, window, 1)
+    agg = aggregate_by_rows(g2m, g2m_weight, g2m_count, mesh_state, window, 1)
 
     full = lax.all_gather(agg[0], "chan", axis=0)
     mine, base = combine([packed, *nearer, far], proc_send, dec_send, n_mesh, full)
@@ -440,11 +432,11 @@
     mesh_one, projected, later = mesh_step(
         mesh_one_kernel, mesh_state, (bf16, bf16, f32), core[None], full, mesh_state, enc_out, mine, other, base
     )
-    agg = aggregate_by_matmul(k_m, m2m, m2m_w, mesh_one, window_of_pairs(projected), n)
+    agg = aggregate_by_matmul(m2m_index, m2m_weight, m2m_count, mesh_one, projected, n)
     mesh_next, projected = mesh_step(
         mesh_next_kernel, mesh_state, (bf16, bf16), core[None], gather_chan(agg), mesh_one, proc_out, mine, other, later
     )
-    agg = aggregate_by_matmul(k_d, m2g, m2g_w, grid_state, window_of_pairs(projected), 1)[0]
+    agg = aggregate_by_matmul(m2g_index, m2g_weight, m2g_count, grid_state, projected, 1)[0]
     grid_next, _ = project_by_exchanges(agg, dec_out, base=(grid_state,))
     return grid_next, mesh_next
 

time: 166 us -> 169 us (1.018)
  starting transfers between devices: 71.4 us -> 78.6 us
  waiting for transfers between devices: 25.7 us -> 19.8 us
  local copies, waits for them, and re-layouts: 0.15 us -> 3.07 us
    ppermute x6, starting transfers between devices: 20.8 us -> 27.8 us  [shift(): lax.ppermute(shard, 'region', [(i, i + by) for i in range(n) if 0 <= i +...]
    ppermute x6, waiting for transfers between devices: 11.1 us -> 5.9 us  [shift(): lax.ppermute(shard, 'region', [(i, i + by) for i in range(n) if 0 <= i +...]
    slice x2, local copies, waits for them, and re-layouts: 0.07 us -> 1.93 us  [project_by_exchanges(): top, low = (values[:half], values[half:])]
    pallas_call x4 -> x5, Pallas kernels: 10.4 us -> 9.78 us  [the longest x2 5.42 us: aggregate_by_matmul(): pl.pallas_call(functools.partial(by_matmul_kernel, slots, block, sizes),...]
  transfers between devices with their start and end apart: 23 -> 23, of which waited for: 9 -> 9; matrix products, arithmetic and copies ran while one was open for 0% -> 1% of each run, Pallas kernels for 5% -> 7%
where the time goes in v4:
time: 169 us; the launch traced here: 168 us
  starting transfers between devices  78.6 us (47%)
  blocking collectives  44 us (26%)
  Pallas kernels  21 us (12%)
  waiting for transfers between devices  19.8 us (12%)
  local copies, waits for them, and re-layouts  3.07 us (2%)
    ppermute x17, starting transfers between devices, exchange(): return lax.ppermute(shard, axis, [(i, partner(i)) for i in range(n)])  50.8 us
    ppermute x6, starting transfers between devices, shift(): lax.ppermute(shard, 'region', [(i, i + by) for i in range(n) if 0 <= i +...  27.8 us
    all_gather x1, blocking collectives, shards(): full = lax.all_gather(agg[0], 'chan', axis=0)  19.2 us
    ppermute x17, waiting for transfers between devices, exchange(): return lax.ppermute(shard, axis, [(i, partner(i)) for i in range(n)])  13.9 us
    all_to_all x1, blocking collectives, gather_chan(): lax.all_to_all(copies, 'chan', split_axis=0, concat_axis=0, tiled=True)  12.5 us
    all_gather x6, blocking collectives, core_pair(): lax.all_gather(shard, 'region', axis=0, tiled=True, axis_index_groups=gro...  12.3 us
    pallas_call x1, Pallas kernels, aggregate_by_rows(): pl.pallas_call(functools.partial(by_rows_kernel, slots, rows, group, size...  6.97 us
    ppermute x6, waiting for transfers between devices, shift(): lax.ppermute(shard, 'region', [(i, i + by) for i in range(n) if 0 <= i +...  5.9 us
  transfers between devices with their start and end apart: 23, of which 9 were waited for; matrix products, arithmetic and copies ran while one was open for 1% of the time, Pallas kernels for 7%

profile of v4, /device:TPU:248, one launch (start us, length us, event | category | flops | bytes accessed | tf_op | source)
XLA Modules:
  0.0 167.8 jit_solution(15561540633731579425)
XLA Ops:
  0.6 1.9 %fusion.6 = (bf16[512,256]{1,0:T(8,128)(2,1)}, bf16[512,256]{1,0:T(8,128)(2,1)}) fusion(bf16[1024,256]{1,0:T(8,128)(2,1)} %refs_0_.1), kind=kLoop, calls=%fused_computation.24 | loop fusion | bytes 1048576 | tf_op jit(solution)/shard_map/slice | solution.py:75
  2.5 3.5 %collective-permute-start.1 = (bf16[512,256]{1,0:T(8,128)(2,1)}, bf16[512,256]{1,0:T(8,128)(2,1)S(1)}, u32[]{:S(2)}, u32[]{:S(2)}) collective-permute-start(bf16[512,256]{1,0:T(8,128)(2,1)} %get-tuple-element.36), channel_id=1, source_target_pairs={{0,1},{1,0},{2,3},{3,2},{4,5},{5,4},{6,7},{7,6},{8,9},{9,8},{10,11... | collective-permute-start | bytes 786440 | tf_op jit(solution)/shard_map/ppermute | solution.py:19
  6.1 4.0 %collective-permute-start.2 = (bf16[512,256]{1,0:T(8,128)(2,1)}, bf16[512,256]{1,0:T(8,128)(2,1)S(1)}, u32[]{:S(2)}, u32[]{:S(2)}) collective-permute-start(bf16[512,256]{1,0:T(8,128)(2,1)} %get-tuple-element.37), channel_id=1, source_target_pairs={{0,3},{1,2},{2,1},{3,0},{4,7},{5,6},{6,5},{7,4},{8,11},{9,10},{10,... | collective-permute-start | bytes 786440 | tf_op jit(solution)/shard_map/ppermute | solution.py:19
  10.1 3.0 %collective-permute-start.3 = (bf16[512,256]{1,0:T(8,128)(2,1)}, bf16[512,256]{1,0:T(8,128)(2,1)S(1)}, u32[]{:S(2)}, u32[]{:S(2)}) collective-permute-start(bf16[512,256]{1,0:T(8,128)(2,1)} %get-tuple-element.36), channel_id=1, source_target_pairs={{0,3},{1,2},{2,1},{3,0},{4,7},{5,6},{6,5},{7,4},{8,11},{9,10},{10,... | collective-permute-start | bytes 786440 | tf_op jit(solution)/shard_map/ppermute | solution.py:19
  13.1 1.9 %collective-permute-start = (bf16[512,256]{1,0:T(8,128)(2,1)}, bf16[512,256]{1,0:T(8,128)(2,1)S(1)}, u32[]{:S(2)}, u32[]{:S(2)}) collective-permute-start(bf16[512,256]{1,0:T(8,128)(2,1)} %get-tuple-element.37), channel_id=1, source_target_pairs={{0,1},{1,0},{2,3},{3,2},{4,5},{5,4},{6,7},{7,6},{8,9},{9,8},{10,11... | collective-permute-start | bytes 786440 | tf_op jit(solution)/shard_map/ppermute | solution.py:19
  15.1 1.1 constant_dynamic-slice_fusion
  16.2 4.0 %collective-permute-start.5 = (bf16[512,256]{1,0:T(8,128)(2,1)S(1)}, bf16[512,256]{1,0:T(8,128)(2,1)S(1)}, u32[]{:S(2)}, u32[]{:S(2)}) collective-permute-start(bf16[512,256]{1,0:T(8,128)(2,1)S(1)} %collective-permute-done.1.near_low), channel_id=1, source_target_pairs={{0,3},{1,2},{2,1},{3,0},{4,7},{5,6},{6,5},{7,4},{8,11},{9,10},{10,... | collective-permute-start | bytes 786440 | tf_op jit(solution)/shard_map/ppermute | solution.py:19
  20.2 3.3 %collective-permute-start.4 = (bf16[512,256]{1,0:T(8,128)(2,1)S(1)}, bf16[512,256]{1,0:T(8,128)(2,1)S(1)}, u32[]{:S(2)}, u32[]{:S(2)}) collective-permute-start(bf16[512,256]{1,0:T(8,128)(2,1)S(1)} %collective-permute-done.2.other_top), channel_id=1, source_target_pairs={{0,1},{1,0},{2,3},{3,2},{4,5},{5,4},{6,7},{7,6},{8,9},{9,8},{10,11... | collective-permute-start | bytes 786440 | tf_op jit(solution)/shard_map/ppermute | solution.py:19
  24.8 3.6 %collective-permute-done.5.far_low = bf16[512,256]{1,0:T(8,128)(2,1)S(1)} collective-permute-done((bf16[512,256]{1,0:T(8,128)(2,1)S(1)}, bf16[512,256]{1,0:T(8,128)(2,1)S(1)}, u32[]{:S(2)}, u32[]{:S(2)}) %collective-permute-start.5) | collective-permute-done | bytes 262176 | tf_op jit(solution)/shard_map/ppermute | solution.py:19
  29.3 1.9 %collective-permute-start.8 = (bf16[1024,256]{1,0:T(8,128)(2,1)S(1)}, bf16[1024,256]{1,0:T(8,128)(2,1)S(1)}, u32[]{:S(2)}, u32[]{:S(2)}) collective-permute-start(bf16[1024,256]{1,0:T(8,128)(2,1)S(1)} %last_block.2.refs_0_), channel_id=1, source_target_pairs={{0,4},{4,0},{8,12},{12,8},{16,20},{20,16},{24,28},{28,24},{32,36},... | collective-permute-start | bytes 1572872 | tf_op jit(solution)/shard_map/ppermute | solution.py:19
  31.2 3.3 %collective-permute-start.7 = (bf16[1024,256]{1,0:T(8,128)(2,1)S(1)}, bf16[1024,256]{1,0:T(8,128)(2,1)S(1)}, u32[]{:S(2)}, u32[]{:S(2)}) collective-permute-start(bf16[1024,256]{1,0:T(8,128)(2,1)S(1)} %last_block.2.refs_0_), channel_id=1, source_target_pairs={{8,0},{12,4},{16,8},{20,12},{24,16},{28,20},{32,24},{36,28},{40,32... | collective-permute-start | bytes 1572872 | tf_op jit(solution)/shard_map/ppermute | solution.py:24
  34.5 5.9 %collective-permute-start.6 = (bf16[1024,256]{1,0:T(8,128)(2,1)S(1)}, bf16[1024,256]{1,0:T(8,128)(2,1)S(1)}, u32[]{:S(2)}, u32[]{:S(2)}) collective-permute-start(bf16[1024,256]{1,0:T(8,128)(2,1)S(1)} %last_block.2.refs_0_), channel_id=1, source_target_pairs={{0,8},{4,12},{8,16},{12,20},{16,24},{20,28},{24,32},{28,36},{32,40... | collective-permute-start | bytes 1572872 | tf_op jit(solution)/shard_map/ppermute | solution.py:24
  40.5 3.6 %collective-permute-start.11 = (bf16[1280,256]{1,0:T(8,128)(2,1)S(1)}, bf16[1280,256]{1,0:T(8,128)(2,1)S(1)}, u32[]{:S(2)}, u32[]{:S(2)}) collective-permute-start(bf16[1280,256]{1,0:T(8,128)(2,1)S(1)} %pad_maximum_fusion.own), channel_id=1, source_target_pairs={{0,2},{1,3},{2,0},{3,1},{4,6},{5,7},{6,4},{7,5},{8,10},{9,11},{10,... | collective-permute-start | bytes 1966088 | tf_op jit(solution)/shard_map/ppermute | solution.py:19
  44.1 4.0 %collective-permute-start.10 = (bf16[1280,256]{1,0:T(8,128)(2,1)S(1)}, bf16[1280,256]{1,0:T(8,128)(2,1)S(1)}, u32[]{:S(2)}, u32[]{:S(2)}) collective-permute-start(bf16[1280,256]{1,0:T(8,128)(2,1)S(1)} %pad_maximum_fusion.own), channel_id=1, source_target_pairs={{0,3},{1,2},{2,1},{3,0},{4,7},{5,6},{6,5},{7,4},{8,11},{9,10},{10,... | collective-permute-start | bytes 1966088 | tf_op jit(solution)/shard_map/ppermute | solution.py:19
  48.1 1.9 %collective-permute-start.9 = (bf16[1280,256]{1,0:T(8,128)(2,1)S(1)}, bf16[1280,256]{1,0:T(8,128)(2,1)S(1)}, u32[]{:S(2)}, u32[]{:S(2)}) collective-permute-start(bf16[1280,256]{1,0:T(8,128)(2,1)S(1)} %pad_maximum_fusion.own), channel_id=1, source_target_pairs={{0,1},{1,0},{2,3},{3,2},{4,5},{5,4},{6,7},{7,6},{8,9},{9,8},{10,11... | collective-permute-start | bytes 1966088 | tf_op jit(solution)/shard_map/ppermute | solution.py:19
  50.1 0.7 collective-permute-done.7.refs_2_
  50.8 1.2 collective-permute-done.6.refs_1_
  52.0 2.2 %all_gather.22.refs_5_ = bf16[1024,256]{1,0:T(8,128)(2,1)S(1)} all-gather(bf16[512,256]{1,0:T(8,128)(2,1)S(1)} %get-tuple-element.32), channel_id=1, replica_groups={{0,4},{8,12},{16,20},{24,28},{32,36},{40,44},{48,52},{56,60},{64,68},{7..., dimensions={0}, use_global_device_ids=true | all-gather | bytes 786432 | tf_op jit(solution)/shard_map/all_gather | solution.py:30
  54.2 2.2 %all_gather.21.refs_4_ = bf16[1024,256]{1,0:T(8,128)(2,1)S(1)} all-gather(bf16[512,256]{1,0:T(8,128)(2,1)S(1)} %get-tuple-element.33), channel_id=1, replica_groups={{0,4},{8,12},{16,20},{24,28},{32,36},{40,44},{48,52},{56,60},{64,68},{7..., dimensions={0}, use_global_device_ids=true | all-gather | bytes 786432 | tf_op jit(solution)/shard_map/all_gather | solution.py:30
  56.4 7.0 %aggregate_by_rows.1 = bf16[1,256,256]{2,1,0:T(8,128)(2,1)S(1)} custom-call(s32[16,256]{1,0:T(8,128)S(1)} %fusion.4.index_ref, f32[16,256]{1,0:T(8,128)S(1)} %copy-done.6, s32[1,256]{1,0:T(1,128)S(1)} %bitcast.12, bf16[256,256]{1,0:T(8,128)(2,1)S(1)} %copy-done.3, bf16[1024,256]{1,0:T(8,128)(2,1)S(1)} %last_block.2.refs_0_, ...), custom_call_target="tpu_custom_call" | custom-call | flops 1 | bytes 1 | tf_op jit(solution)/shard_map/aggregate_by_rows/pallas_call | solution.py:286
  63.4 19.2 %all_gather.23._.full = bf16[4,256,256]{2,1,0:T(8,128)(2,1)S(1)} all-gather(bf16[1,256,256]{2,1,0:T(8,128)(2,1)S(1)} %aggregate_by_rows.1), channel_id=1, replica_groups=mesh['region'=128,'chan'=4] {'chan'}, dimensions={0}, use_global_device_ids=true | all-gather | bytes 655360 | tf_op jit(solution)/shard_map/all_gather | solution.py:429
  82.6 1.3 combine.1
  83.9 1.9 %collective-permute-start.12 = (bf16[1536,256]{1,0:T(8,128)(2,1)S(1)}, bf16[1536,256]{1,0:T(8,128)(2,1)S(1)}, u32[]{:S(2)}, u32[]{:S(2)}) collective-permute-start(bf16[1536,256]{1,0:T(8,128)(2,1)S(1)} %get-tuple-element.21.mine), channel_id=1, source_target_pairs={{0,4},{4,0},{8,12},{12,8},{16,20},{20,16},{24,28},{28,24},{32,36},... | collective-permute-start | bytes 2359304 | tf_op jit(solution)/shard_map/ppermute | solution.py:19
  85.8 2.3 %collective-permute-done.12.other = bf16[1536,256]{1,0:T(8,128)(2,1)S(1)} collective-permute-done((bf16[1536,256]{1,0:T(8,128)(2,1)S(1)}, bf16[1536,256]{1,0:T(8,128)(2,1)S(1)}, u32[]{:S(2)}, u32[]{:S(2)}) %collective-permute-start.12) | collective-permute-done | bytes 786464 | tf_op jit(solution)/shard_map/ppermute | solution.py:19
  88.7 1.9 %collective-permute-start.13 = (bf16[256,256]{1,0:T(8,128)(2,1)S(1)}, bf16[256,256]{1,0:T(8,128)(2,1)S(1)}, u32[]{:S(2)}, u32[]{:S(2)}) collective-permute-start(bf16[256,256]{1,0:T(8,128)(2,1)S(1)} %get-tuple-element.24), channel_id=1, source_target_pairs={{8,0},{12,4},{16,8},{20,12},{24,16},{28,20},{32,24},{36,28},{40,32... | collective-permute-start | bytes 393224 | tf_op jit(solution)/shard_map/ppermute | solution.py:24
  90.6 7.2 %collective-permute-start.14 = (bf16[256,256]{1,0:T(8,128)(2,1)S(1)}, bf16[256,256]{1,0:T(8,128)(2,1)S(1)}, u32[]{:S(2)}, u32[]{:S(2)}) collective-permute-start(bf16[256,256]{1,0:T(8,128)(2,1)S(1)} %get-tuple-element.24), channel_id=1, source_target_pairs={{0,8},{4,12},{8,16},{12,20},{16,24},{20,28},{24,32},{28,36},{32,40... | collective-permute-start | bytes 393224 | tf_op jit(solution)/shard_map/ppermute | solution.py:24
  97.9 2.0 %all_gather.24.window = bf16[512,256]{1,0:T(8,128)(2,1)S(1)} all-gather(bf16[256,256]{1,0:T(8,128)(2,1)S(1)} %get-tuple-element.24), channel_id=1, replica_groups={{0,4},{8,12},{16,20},{24,28},{32,36},{40,44},{48,52},{56,60},{64,68},{7..., dimensions={0}, use_global_device_ids=true | all-gather | bytes 393216 | tf_op jit(solution)/shard_map/all_gather | solution.py:30
  99.9 0.9 fetch_own.2.fetched_ref
  100.8 2.0 %all_gather.25.refs_0_ = bf16[512,256]{1,0:T(8,128)(2,1)S(1)} all-gather(bf16[256,256]{1,0:T(8,128)(2,1)S(1)} %get-tuple-element.41), channel_id=1, replica_groups={{0,4},{8,12},{16,20},{24,28},{32,36},{40,44},{48,52},{56,60},{64,68},{7..., dimensions={0}, use_global_device_ids=true | all-gather | bytes 393216 | tf_op jit(solution)/shard_map/all_gather | solution.py:30
  102.8 1.6 aggregate_by_matmul.2
  104.4 12.5 %all_to_all.5.full = bf16[4,256,256]{2,1,0:T(8,128)(2,1)S(1)} all-to-all(bf16[4,256,256]{2,1,0:T(8,128)(2,1)S(1)} %aggregate_by_matmul.2), channel_id=1, replica_groups=mesh['region'=128,'chan'=4] {'chan'}, dimensions={0} | all-to-all | bytes 1048576 | tf_op jit(solution)/shard_map/all_to_all | solution.py:34
  116.8 1.1 mesh_step.3
  118.0 7.5 %collective-permute-start.16 = (bf16[256,256]{1,0:T(8,128)(2,1)S(1)}, bf16[256,256]{1,0:T(8,128)(2,1)S(1)}, u32[]{:S(2)}, u32[]{:S(2)}) collective-permute-start(bf16[256,256]{1,0:T(8,128)(2,1)S(1)} %get-tuple-element.28), channel_id=1, source_target_pairs={{0,8},{4,12},{8,16},{12,20},{16,24},{20,28},{24,32},{28,36},{32,40... | collective-permute-start | bytes 393224 | tf_op jit(solution)/shard_map/ppermute | solution.py:24
  125.5 1.9 %collective-permute-start.15 = (bf16[256,256]{1,0:T(8,128)(2,1)S(1)}, bf16[256,256]{1,0:T(8,128)(2,1)S(1)}, u32[]{:S(2)}, u32[]{:S(2)}) collective-permute-start(bf16[256,256]{1,0:T(8,128)(2,1)S(1)} %get-tuple-element.28), channel_id=1, source_target_pairs={{8,0},{12,4},{16,8},{20,12},{24,16},{28,20},{32,24},{36,28},{40,32... | collective-permute-start | bytes 393224 | tf_op jit(solution)/shard_map/ppermute | solution.py:24
  127.4 2.0 %all_gather.26.window = bf16[512,256]{1,0:T(8,128)(2,1)S(1)} all-gather(bf16[256,256]{1,0:T(8,128)(2,1)S(1)} %get-tuple-element.28), channel_id=1, replica_groups={{0,4},{8,12},{16,20},{24,28},{32,36},{40,44},{48,52},{56,60},{64,68},{7..., dimensions={0}, use_global_device_ids=true | all-gather | bytes 393216 | tf_op jit(solution)/shard_map/all_gather | solution.py:30
  129.4 2.2 %fetch_own.3.fetched_ref = bf16[4,1024,256]{2,1,0:T(8,128)(2,1)S(1)} custom-call(s32[1]{0:T(128)} %bitcast.1.me_ref, s32[4,1024]{1,0:T(4,128)S(1)} %copy-done.10, bf16[512,256]{1,0:T(8,128)(2,1)S(1)} %all_gather.26.window), custom_call_target="tpu_custom_call" | custom-call | flops 1073741824 | bytes 2097152 | tf_op jit(solution)/shard_map/fetch_own/pallas_call | solution.py:330
  131.7 4.0 %collective-permute-done.15 = bf16[256,256]{1,0:T(8,128)(2,1)S(1)} collective-permute-done((bf16[256,256]{1,0:T(8,128)(2,1)S(1)}, bf16[256,256]{1,0:T(8,128)(2,1)S(1)}, u32[]{:S(2)}, u32[]{:S(2)}) %collective-permute-start.15) | collective-permute-done | bytes 131104 | tf_op jit(solution)/shard_map/ppermute | solution.py:24
  135.7 2.0 %all_gather.27.refs_0_ = bf16[512,256]{1,0:T(8,128)(2,1)S(1)} all-gather(bf16[256,256]{1,0:T(8,128)(2,1)S(1)} %get-tuple-element.39), channel_id=1, replica_groups={{0,4},{8,12},{16,20},{24,28},{32,36},{40,44},{48,52},{56,60},{64,68},{7..., dimensions={0}, use_global_device_ids=true | all-gather | bytes 393216 | tf_op jit(solution)/shard_map/all_gather | solution.py:30
  137.7 3.9 %aggregate_by_matmul.3 = bf16[1,1024,256]{2,1,0:T(8,128)(2,1)S(1)} custom-call(s32[1]{0:T(128)} %bitcast.1.me_ref, s32[4,1024]{1,0:T(4,128)S(1)} %copy-done.10, f32[4,1024]{1,0:T(4,128)S(1)} %copy-done.11, s32[1,1024]{1,0:T(1,128)S(1)} %bitcast.13, bf16[1024,256]{1,0:T(8,128)(2,1)S(1)} %copy-done, bf16[4,1024,256]{2,1,0:T(8,128)(2,1)S(1)} %fetch_own.3.fetched_ref, ...), custom_call_target="tpu_custom_call" | custom-call | flops 1610612736 | bytes 1441792 | tf_op jit(solution)/shard_map/aggregate_by_matmul/pallas_call | solution.py:377
  141.6 2.6 %collective-permute-start.18 = (bf16[512,256]{1,0:T(8,128)(2,1)S(1)}, bf16[512,256]{1,0:T(8,128)(2,1)S(1)}, u32[]{:S(2)}, u32[]{:S(2)}) collective-permute-start(bf16[512,256]{1,0:T(8,128)(2,1)S(1)} %get-tuple-element.34), channel_id=1, source_target_pairs={{0,1},{1,0},{2,3},{3,2},{4,5},{5,4},{6,7},{7,6},{8,9},{9,8},{10,11... | collective-permute-start | bytes 786440 | tf_op jit(solution)/shard_map/ppermute | solution.py:19
  144.2 2.7 %collective-permute-start.19 = (bf16[512,256]{1,0:T(8,128)(2,1)S(1)}, bf16[512,256]{1,0:T(8,128)(2,1)S(1)}, u32[]{:S(2)}, u32[]{:S(2)}) collective-permute-start(bf16[512,256]{1,0:T(8,128)(2,1)S(1)} %get-tuple-element.35), channel_id=1, source_target_pairs={{0,3},{1,2},{2,1},{3,0},{4,7},{5,6},{6,5},{7,4},{8,11},{9,10},{10,... | collective-permute-start | bytes 786440 | tf_op jit(solution)/shard_map/ppermute | solution.py:19
  147.0 4.3 %collective-permute-start.20 = (bf16[512,256]{1,0:T(8,128)(2,1)S(1)}, bf16[512,256]{1,0:T(8,128)(2,1)S(1)}, u32[]{:S(2)}, u32[]{:S(2)}) collective-permute-start(bf16[512,256]{1,0:T(8,128)(2,1)S(1)} %get-tuple-element.34), channel_id=1, source_target_pairs={{0,3},{1,2},{2,1},{3,0},{4,7},{5,6},{6,5},{7,4},{8,11},{9,10},{10,... | collective-permute-start | bytes 786440 | tf_op jit(solution)/shard_map/ppermute | solution.py:19
  151.3 2.2 %collective-permute-start.17 = (bf16[512,256]{1,0:T(8,128)(2,1)S(1)}, bf16[512,256]{1,0:T(8,128)(2,1)S(1)}, u32[]{:S(2)}, u32[]{:S(2)}) collective-permute-start(bf16[512,256]{1,0:T(8,128)(2,1)S(1)} %get-tuple-element.35), channel_id=1, source_target_pairs={{0,1},{1,0},{2,3},{3,2},{4,5},{5,4},{6,7},{7,6},{8,9},{9,8},{10,11... | collective-permute-start | bytes 786440 | tf_op jit(solution)/shard_map/ppermute | solution.py:19
  153.5 3.1 %collective-permute-start.22 = (bf16[512,256]{1,0:T(8,128)(2,1)S(1)}, bf16[512,256]{1,0:T(8,128)(2,1)S(1)}, u32[]{:S(2)}, u32[]{:S(2)}) collective-permute-start(bf16[512,256]{1,0:T(8,128)(2,1)S(1)} %collective-permute-done.18.near_low), channel_id=1, source_target_pairs={{0,3},{1,2},{2,1},{3,0},{4,7},{5,6},{6,5},{7,4},{8,11},{9,10},{10,... | collective-permute-start | bytes 786440 | tf_op jit(solution)/shard_map/ppermute | solution.py:19
  156.6 2.7 %collective-permute-start.21 = (bf16[512,256]{1,0:T(8,128)(2,1)S(1)}, bf16[512,256]{1,0:T(8,128)(2,1)S(1)}, u32[]{:S(2)}, u32[]{:S(2)}) collective-permute-start(bf16[512,256]{1,0:T(8,128)(2,1)S(1)} %collective-permute-done.19.other_top), channel_id=1, source_target_pairs={{0,1},{1,0},{2,3},{3,2},{4,5},{5,4},{6,7},{7,6},{8,9},{9,8},{10,11... | collective-permute-start | bytes 786440 | tf_op jit(solution)/shard_map/ppermute | solution.py:19
  159.3 2.8 %collective-permute-done.20.other_low = bf16[512,256]{1,0:T(8,128)(2,1)S(1)} collective-permute-done((bf16[512,256]{1,0:T(8,128)(2,1)S(1)}, bf16[512,256]{1,0:T(8,128)(2,1)S(1)}, u32[]{:S(2)}, u32[]{:S(2)}) %collective-permute-start.20) | collective-permute-done | bytes 262176 | tf_op jit(solution)/shard_map/ppermute | solution.py:19
  162.7 3.9 %collective-permute-done.22.far_low = bf16[512,256]{1,0:T(8,128)(2,1)S(1)} collective-permute-done((bf16[512,256]{1,0:T(8,128)(2,1)S(1)}, bf16[512,256]{1,0:T(8,128)(2,1)S(1)}, u32[]{:S(2)}, u32[]{:S(2)}) %collective-permute-start.22) | collective-permute-done | bytes 262176 | tf_op jit(solution)/shard_map/ppermute | solution.py:19
  166.7 1.1 last_block.3
  (60 shorter events, 3.6 us)
Async XLA Ops:
  0.6 22.9 %copy-start.3 = (bf16[256,256]{1,0:T(8,128)(2,1)S(1)}, bf16[256,256]{1,0:T(8,128)(2,1)}, u32[]{:S(2)}) copy-start(bf16[256,256]{1,0:T(8,128)(2,1)} %mesh.1) | copy-start | bytes 393220
  2.5 21.7 %copy-start = (bf16[1024,256]{1,0:T(8,128)(2,1)S(1)}, bf16[1024,256]{1,0:T(8,128)(2,1)}, u32[]{:S(2)}) copy-start(bf16[1024,256]{1,0:T(8,128)(2,1)} %refs_0_.1) | copy-start | bytes 1572868
  2.5 21.7 %copy-start.1 = (bf16[1024,256]{1,0:T(8,128)(2,1)S(1)}, bf16[1024,256]{1,0:T(8,128)(2,1)}, u32[]{:S(2)}) copy-start(bf16[1024,256]{1,0:T(8,128)(2,1)} %weight.5) | copy-start | bytes 1572868
  2.5 13.6 %collective-permute-start.1 = (bf16[512,256]{1,0:T(8,128)(2,1)}, bf16[512,256]{1,0:T(8,128)(2,1)S(1)}, u32[]{:S(2)}, u32[]{:S(2)}) collective-permute-start(bf16[512,256]{1,0:T(8,128)(2,1)} %get-tuple-element.36), channel_id=1, source_target_pairs={{0,1},{1,0},{2,3},{3,2},{4,5},{5,4},{6,7},{7,6},{8,9},{9,8},{10,11... | collective-permute-start | bytes 786440 | tf_op jit(solution)/shard_map/ppermute | solution.py:19
  6.1 14.1 %collective-permute-start.2 = (bf16[512,256]{1,0:T(8,128)(2,1)}, bf16[512,256]{1,0:T(8,128)(2,1)S(1)}, u32[]{:S(2)}, u32[]{:S(2)}) collective-permute-start(bf16[512,256]{1,0:T(8,128)(2,1)} %get-tuple-element.37), channel_id=1, source_target_pairs={{0,3},{1,2},{2,1},{3,0},{4,7},{5,6},{6,5},{7,4},{8,11},{9,10},{10,... | collective-permute-start | bytes 786440 | tf_op jit(solution)/shard_map/ppermute | solution.py:19
  10.1 14.2 %collective-permute-start.3 = (bf16[512,256]{1,0:T(8,128)(2,1)}, bf16[512,256]{1,0:T(8,128)(2,1)S(1)}, u32[]{:S(2)}, u32[]{:S(2)}) collective-permute-start(bf16[512,256]{1,0:T(8,128)(2,1)} %get-tuple-element.36), channel_id=1, source_target_pairs={{0,3},{1,2},{2,1},{3,0},{4,7},{5,6},{6,5},{7,4},{8,11},{9,10},{10,... | collective-permute-start | bytes 786440 | tf_op jit(solution)/shard_map/ppermute | solution.py:19
  13.1 11.1 %collective-permute-start = (bf16[512,256]{1,0:T(8,128)(2,1)}, bf16[512,256]{1,0:T(8,128)(2,1)S(1)}, u32[]{:S(2)}, u32[]{:S(2)}) collective-permute-start(bf16[512,256]{1,0:T(8,128)(2,1)} %get-tuple-element.37), channel_id=1, source_target_pairs={{0,1},{1,0},{2,3},{3,2},{4,5},{5,4},{6,7},{7,6},{8,9},{9,8},{10,11... | collective-permute-start | bytes 786440 | tf_op jit(solution)/shard_map/ppermute | solution.py:19
  16.2 12.2 %collective-permute-start.5 = (bf16[512,256]{1,0:T(8,128)(2,1)S(1)}, bf16[512,256]{1,0:T(8,128)(2,1)S(1)}, u32[]{:S(2)}, u32[]{:S(2)}) collective-permute-start(bf16[512,256]{1,0:T(8,128)(2,1)S(1)} %collective-permute-done.1.near_low), channel_id=1, source_target_pairs={{0,3},{1,2},{2,1},{3,0},{4,7},{5,6},{6,5},{7,4},{8,11},{9,10},{10,... | collective-permute-start | bytes 786440 | tf_op jit(solution)/shard_map/ppermute | solution.py:19
  20.2 8.8 %collective-permute-start.4 = (bf16[512,256]{1,0:T(8,128)(2,1)S(1)}, bf16[512,256]{1,0:T(8,128)(2,1)S(1)}, u32[]{:S(2)}, u32[]{:S(2)}) collective-permute-start(bf16[512,256]{1,0:T(8,128)(2,1)S(1)} %collective-permute-done.2.other_top), channel_id=1, source_target_pairs={{0,1},{1,0},{2,3},{3,2},{4,5},{5,4},{6,7},{7,6},{8,9},{9,8},{10,11... | collective-permute-start | bytes 786440 | tf_op jit(solution)/shard_map/ppermute | solution.py:19
  24.8 15.6 %copy-start.16 = (s32[16,256]{1,0:T(8,128)S(1)}, s32[16,256]{1,0:T(8,128)}, u32[]{:S(2)}) copy-start(s32[16,256]{1,0:T(8,128)} %param.25) | copy-start | bytes 49156
  29.3 14.8 %collective-permute-start.8 = (bf16[1024,256]{1,0:T(8,128)(2,1)S(1)}, bf16[1024,256]{1,0:T(8,128)(2,1)S(1)}, u32[]{:S(2)}, u32[]{:S(2)}) collective-permute-start(bf16[1024,256]{1,0:T(8,128)(2,1)S(1)} %last_block.2.refs_0_), channel_id=1, source_target_pairs={{0,4},{4,0},{8,12},{12,8},{16,20},{20,16},{24,28},{28,24},{32,36},... | collective-permute-start | bytes 1572872 | tf_op jit(solution)/shard_map/ppermute | solution.py:19
  31.2 19.5 %collective-permute-start.7 = (bf16[1024,256]{1,0:T(8,128)(2,1)S(1)}, bf16[1024,256]{1,0:T(8,128)(2,1)S(1)}, u32[]{:S(2)}, u32[]{:S(2)}) collective-permute-start(bf16[1024,256]{1,0:T(8,128)(2,1)S(1)} %last_block.2.refs_0_), channel_id=1, source_target_pairs={{8,0},{12,4},{16,8},{20,12},{24,16},{28,20},{32,24},{36,28},{40,32... | collective-permute-start | bytes 1572872 | tf_op jit(solution)/shard_map/ppermute | solution.py:24
  34.5 17.5 %collective-permute-start.6 = (bf16[1024,256]{1,0:T(8,128)(2,1)S(1)}, bf16[1024,256]{1,0:T(8,128)(2,1)S(1)}, u32[]{:S(2)}, u32[]{:S(2)}) collective-permute-start(bf16[1024,256]{1,0:T(8,128)(2,1)S(1)} %last_block.2.refs_0_), channel_id=1, source_target_pairs={{0,8},{4,12},{8,16},{12,20},{16,24},{20,28},{24,32},{28,36},{32,40... | collective-permute-start | bytes 1572872 | tf_op jit(solution)/shard_map/ppermute | solution.py:24
  40.5 15.9 %copy-start.6 = (f32[16,256]{1,0:T(8,128)S(1)}, f32[16,256]{1,0:T(8,128)}, u32[]{:S(2)}) copy-start(f32[16,256]{1,0:T(8,128)} %slot_ref.3) | copy-start | bytes 49156
  40.5 15.9 %copy-start.7 = (s32[256]{0:T(256)S(1)}, s32[256]{0:T(256)}, u32[]{:S(2)}) copy-start(s32[256]{0:T(256)} %param.27) | copy-start | bytes 3076
  40.5 42.1 %collective-permute-start.11 = (bf16[1280,256]{1,0:T(8,128)(2,1)S(1)}, bf16[1280,256]{1,0:T(8,128)(2,1)S(1)}, u32[]{:S(2)}, u32[]{:S(2)}) collective-permute-start(bf16[1280,256]{1,0:T(8,128)(2,1)S(1)} %pad_maximum_fusion.own), channel_id=1, source_target_pairs={{0,2},{1,3},{2,0},{3,1},{4,6},{5,7},{6,4},{7,5},{8,10},{9,11},{10,... | collective-permute-start | bytes 1966088 | tf_op jit(solution)/shard_map/ppermute | solution.py:19
  44.1 38.5 %collective-permute-start.10 = (bf16[1280,256]{1,0:T(8,128)(2,1)S(1)}, bf16[1280,256]{1,0:T(8,128)(2,1)S(1)}, u32[]{:S(2)}, u32[]{:S(2)}) collective-permute-start(bf16[1280,256]{1,0:T(8,128)(2,1)S(1)} %pad_maximum_fusion.own), channel_id=1, source_target_pairs={{0,3},{1,2},{2,1},{3,0},{4,7},{5,6},{6,5},{7,4},{8,11},{9,10},{10,... | collective-permute-start | bytes 1966088 | tf_op jit(solution)/shard_map/ppermute | solution.py:19
  48.1 34.4 %collective-permute-start.9 = (bf16[1280,256]{1,0:T(8,128)(2,1)S(1)}, bf16[1280,256]{1,0:T(8,128)(2,1)S(1)}, u32[]{:S(2)}, u32[]{:S(2)}) collective-permute-start(bf16[1280,256]{1,0:T(8,128)(2,1)S(1)} %pad_maximum_fusion.own), channel_id=1, source_target_pairs={{0,1},{1,0},{2,3},{3,2},{4,5},{5,4},{6,7},{7,6},{8,9},{9,8},{10,11... | collective-permute-start | bytes 1966088 | tf_op jit(solution)/shard_map/ppermute | solution.py:19
  56.4 26.2 %copy-start.8 = (bf16[1024,256]{1,0:T(8,128)(2,1)S(1)}, bf16[1024,256]{1,0:T(8,128)(2,1)}, u32[]{:S(2)}) copy-start(bf16[1024,256]{1,0:T(8,128)(2,1)} %first.1) | copy-start | bytes 1572868
  56.4 26.2 %copy-start.9 = (bf16[1024,256]{1,0:T(8,128)(2,1)S(1)}, bf16[1024,256]{1,0:T(8,128)(2,1)}, u32[]{:S(2)}) copy-start(bf16[1024,256]{1,0:T(8,128)(2,1)} %second.1) | copy-start | bytes 1572868
  82.6 5.5 %copy-start.5 = (bf16[1024,256]{1,0:T(8,128)(2,1)S(1)}, bf16[1024,256]{1,0:T(8,128)(2,1)}, u32[]{:S(2)}) copy-start(bf16[1024,256]{1,0:T(8,128)(2,1)} %w_out.2) | copy-start | bytes 1572868
  83.9 4.2 %collective-permute-start.12 = (bf16[1536,256]{1,0:T(8,128)(2,1)S(1)}, bf16[1536,256]{1,0:T(8,128)(2,1)S(1)}, u32[]{:S(2)}, u32[]{:S(2)}) collective-permute-start(bf16[1536,256]{1,0:T(8,128)(2,1)S(1)} %get-tuple-element.21.mine), channel_id=1, source_target_pairs={{0,4},{4,0},{8,12},{12,8},{16,20},{20,16},{24,28},{28,24},{32,36},... | collective-permute-start | bytes 2359304 | tf_op jit(solution)/shard_map/ppermute | solution.py:19
  88.1 11.8 %copy-start.12 = (s32[8,256]{1,0:T(8,128)S(1)}, s32[8,256]{1,0:T(8,128)}, u32[]{:S(2)}) copy-start(s32[8,256]{1,0:T(8,128)} %sender_ref.5) | copy-start | bytes 24580
  88.7 12.1 %collective-permute-start.13 = (bf16[256,256]{1,0:T(8,128)(2,1)S(1)}, bf16[256,256]{1,0:T(8,128)(2,1)S(1)}, u32[]{:S(2)}, u32[]{:S(2)}) collective-permute-start(bf16[256,256]{1,0:T(8,128)(2,1)S(1)} %get-tuple-element.24), channel_id=1, source_target_pairs={{8,0},{12,4},{16,8},{20,12},{24,16},{28,20},{32,24},{36,28},{40,32... | collective-permute-start | bytes 393224 | tf_op jit(solution)/shard_map/ppermute | solution.py:24
  90.6 10.1 %collective-permute-start.14 = (bf16[256,256]{1,0:T(8,128)(2,1)S(1)}, bf16[256,256]{1,0:T(8,128)(2,1)S(1)}, u32[]{:S(2)}, u32[]{:S(2)}) collective-permute-start(bf16[256,256]{1,0:T(8,128)(2,1)S(1)} %get-tuple-element.24), channel_id=1, source_target_pairs={{0,8},{4,12},{8,16},{12,20},{16,24},{20,28},{24,32},{28,36},{32,40... | collective-permute-start | bytes 393224 | tf_op jit(solution)/shard_map/ppermute | solution.py:24
  99.9 2.9 %copy-start.13 = (f32[8,256]{1,0:T(8,128)S(1)}, f32[8,256]{1,0:T(8,128)}, u32[]{:S(2)}) copy-start(f32[8,256]{1,0:T(8,128)} %slot_ref.4) | copy-start | bytes 24580
  99.9 2.9 %copy-start.15 = (s32[256]{0:T(256)S(1)}, s32[256]{0:T(256)}, u32[]{:S(2)}) copy-start(s32[256]{0:T(256)} %param.30) | copy-start | bytes 3076
  102.8 14.1 %copy-start.4 = (bf16[1024,256]{1,0:T(8,128)(2,1)S(1)}, bf16[1024,256]{1,0:T(8,128)(2,1)}, u32[]{:S(2)}) copy-start(bf16[1024,256]{1,0:T(8,128)(2,1)} %w_out.3) | copy-start | bytes 1572868
  116.8 12.6 %copy-start.10 = (s32[4,1024]{1,0:T(4,128)S(1)}, s32[4,1024]{1,0:T(4,128)}, u32[]{:S(2)}) copy-start(s32[4,1024]{1,0:T(4,128)} %sender_ref.7) | copy-start | bytes 49156
  118.0 17.7 %collective-permute-start.16 = (bf16[256,256]{1,0:T(8,128)(2,1)S(1)}, bf16[256,256]{1,0:T(8,128)(2,1)S(1)}, u32[]{:S(2)}, u32[]{:S(2)}) collective-permute-start(bf16[256,256]{1,0:T(8,128)(2,1)S(1)} %get-tuple-element.28), channel_id=1, source_target_pairs={{0,8},{4,12},{8,16},{12,20},{16,24},{20,28},{24,32},{28,36},{32,40... | collective-permute-start | bytes 393224 | tf_op jit(solution)/shard_map/ppermute | solution.py:24
  125.5 10.2 %collective-permute-start.15 = (bf16[256,256]{1,0:T(8,128)(2,1)S(1)}, bf16[256,256]{1,0:T(8,128)(2,1)S(1)}, u32[]{:S(2)}, u32[]{:S(2)}) collective-permute-start(bf16[256,256]{1,0:T(8,128)(2,1)S(1)} %get-tuple-element.28), channel_id=1, source_target_pairs={{8,0},{12,4},{16,8},{20,12},{24,16},{28,20},{32,24},{36,28},{40,32... | collective-permute-start | bytes 393224 | tf_op jit(solution)/shard_map/ppermute | solution.py:24
  129.4 8.3 %copy-start.11 = (f32[4,1024]{1,0:T(4,128)S(1)}, f32[4,1024]{1,0:T(4,128)}, u32[]{:S(2)}) copy-start(f32[4,1024]{1,0:T(4,128)} %slot_ref.5) | copy-start | bytes 49156
  129.4 8.3 %copy-start.14 = (s32[1024]{0:T(1024)S(1)}, s32[1024]{0:T(1024)}, u32[]{:S(2)}) copy-start(s32[1024]{0:T(1024)} %param.33) | copy-start | bytes 12292
  141.6 20.6 %copy-start.2 = (bf16[1024,256]{1,0:T(8,128)(2,1)S(1)}, bf16[1024,256]{1,0:T(8,128)(2,1)}, u32[]{:S(2)}) copy-start(bf16[1024,256]{1,0:T(8,128)(2,1)} %weight.7) | copy-start | bytes 1572868
  141.6 11.9 %collective-permute-start.18 = (bf16[512,256]{1,0:T(8,128)(2,1)S(1)}, bf16[512,256]{1,0:T(8,128)(2,1)S(1)}, u32[]{:S(2)}, u32[]{:S(2)}) collective-permute-start(bf16[512,256]{1,0:T(8,128)(2,1)S(1)} %get-tuple-element.34), channel_id=1, source_target_pairs={{0,1},{1,0},{2,3},{3,2},{4,5},{5,4},{6,7},{7,6},{8,9},{9,8},{10,11... | collective-permute-start | bytes 786440 | tf_op jit(solution)/shard_map/ppermute | solution.py:19
  144.2 12.3 %collective-permute-start.19 = (bf16[512,256]{1,0:T(8,128)(2,1)S(1)}, bf16[512,256]{1,0:T(8,128)(2,1)S(1)}, u32[]{:S(2)}, u32[]{:S(2)}) collective-permute-start(bf16[512,256]{1,0:T(8,128)(2,1)S(1)} %get-tuple-element.35), channel_id=1, source_target_pairs={{0,3},{1,2},{2,1},{3,0},{4,7},{5,6},{6,5},{7,4},{8,11},{9,10},{10,... | collective-permute-start | bytes 786440 | tf_op jit(solution)/shard_map/ppermute | solution.py:19
  147.0 15.2 %collective-permute-start.20 = (bf16[512,256]{1,0:T(8,128)(2,1)S(1)}, bf16[512,256]{1,0:T(8,128)(2,1)S(1)}, u32[]{:S(2)}, u32[]{:S(2)}) collective-permute-start(bf16[512,256]{1,0:T(8,128)(2,1)S(1)} %get-tuple-element.34), channel_id=1, source_target_pairs={{0,3},{1,2},{2,1},{3,0},{4,7},{5,6},{6,5},{7,4},{8,11},{9,10},{10,... | collective-permute-start | bytes 786440 | tf_op jit(solution)/shard_map/ppermute | solution.py:19
  151.3 10.8 %collective-permute-start.17 = (bf16[512,256]{1,0:T(8,128)(2,1)S(1)}, bf16[512,256]{1,0:T(8,128)(2,1)S(1)}, u32[]{:S(2)}, u32[]{:S(2)}) collective-permute-start(bf16[512,256]{1,0:T(8,128)(2,1)S(1)} %get-tuple-element.35), channel_id=1, source_target_pairs={{0,1},{1,0},{2,3},{3,2},{4,5},{5,4},{6,7},{7,6},{8,9},{9,8},{10,11... | collective-permute-start | bytes 786440 | tf_op jit(solution)/shard_map/ppermute | solution.py:19
  153.5 13.2 %collective-permute-start.22 = (bf16[512,256]{1,0:T(8,128)(2,1)S(1)}, bf16[512,256]{1,0:T(8,128)(2,1)S(1)}, u32[]{:S(2)}, u32[]{:S(2)}) collective-permute-start(bf16[512,256]{1,0:T(8,128)(2,1)S(1)} %collective-permute-done.18.near_low), channel_id=1, source_target_pairs={{0,3},{1,2},{2,1},{3,0},{4,7},{5,6},{6,5},{7,4},{8,11},{9,10},{10,... | collective-permute-start | bytes 786440 | tf_op jit(solution)/shard_map/ppermute | solution.py:19
  156.6 10.1 %collective-permute-start.21 = (bf16[512,256]{1,0:T(8,128)(2,1)S(1)}, bf16[512,256]{1,0:T(8,128)(2,1)S(1)}, u32[]{:S(2)}, u32[]{:S(2)}) collective-permute-start(bf16[512,256]{1,0:T(8,128)(2,1)S(1)} %collective-permute-done.19.other_top), channel_id=1, source_target_pairs={{0,1},{1,0},{2,3},{3,2},{4,5},{5,4},{6,7},{7,6},{8,9},{9,8},{10,11... | collective-permute-start | bytes 786440 | tf_op jit(solution)/shard_map/ppermute | solution.py:19

commit v5 on v4

--- a/solution.py
+++ b/solution.py
@@ -185,15 +185,14 @@
     return [projected, below, above, other] + [core_pair(rows) for rows in chosen], sent
 
 
-def window_of_pairs(projected, fetch_own):
+def window_of_pairs(projected):
     below = shift(projected, 2)
     above = shift(projected, -2)
-    fetched = fetch_own(core_pair(projected))
-    above, fetched = lax.optimization_barrier((above, fetched))
+    own = core_pair(projected)
     first = lax.axis_index("region") % 2 == 0
     outer = core_pair(jnp.where(first, above, below))
     last = jnp.where(first, below, above)
-    return fetched, [outer, last]
+    return [outer, own, last]
 
 
 def place_in_exchanged(index, rows, me):
@@ -206,14 +205,10 @@
     return jnp.where(near, block * rows + row, moved)
 
 
-def place_in_pairs(index, rows, me, own):
+def place_in_pairs(index, rows, me):
     shift_by = rows.bit_length() - 1
     apart = (index >> shift_by) - (me - (me & 1))
-    inside = (apart == 0) | (apart == 1)
-    if own:
-        block = jnp.where(inside, apart, 2)
-    else:
-        block = jnp.where(inside, 3, jnp.where(apart == 2, 0, jnp.where(apart == -1, 1, 2)))
+    block = jnp.where(apart == 2, 0, jnp.where(apart == -1, 1, jnp.where(apart == 0, 2, jnp.where(apart == 1, 3, 4))))
     return (block << shift_by) + (index & (rows - 1))
 
 
@@ -301,57 +296,17 @@
     )(index, weights, counts[None, :], receivers, *parts)
 
 
-def pick_rows(index, columns, window):
-    wanted = jnp.broadcast_to(index, (index.shape[0], LANES)).astype(jnp.int16)
-    one, zero = jnp.bfloat16(1), jnp.bfloat16(0)
-    picks = [jnp.where(columns[:, j : j + LANES] == wanted, one, zero) for j in range(0, columns.shape[1], LANES)]
-    return dot(jnp.concatenate(picks, axis=1), window[...])
-
-
-def fetch_kernel(slots, block, me_ref, sender_ref, window, out_ref, index_ref):
-    depth, rows = window.shape[0], sender_ref.shape[1]
-    index_ref[...] = upright(place_in_pairs(sender_ref[...], depth // 2, me_ref[0], True))
-    columns = lax.broadcasted_iota(jnp.int32, (block, depth), 1).astype(jnp.int16)
-
-    def one_block(b, carry):
-        at = pl.ds(pl.multiple_of(b * block, block), block)
-        index = index_ref[at, :]
-        for k in range(slots):
-            out_ref[k, at, :] = pick_rows(index[:, k : k + 1], columns, window).astype(out_ref.dtype)
-        return carry
-
-    lax.fori_loop(0, rows // block, one_block, 0)
-
-
-def fetch_own(senders, window, block=256):
-    slots, rows = senders.shape
-    width = window.shape[1]
-    me = lax.axis_index("region").astype(jnp.int32)[None]
-    return pl.pallas_call(
-        functools.partial(fetch_kernel, slots, block),
-        out_shape=jax.ShapeDtypeStruct((slots, rows, width), window.dtype),
-        in_specs=[SMEM, VMEM, VMEM],
-        out_specs=VMEM,
-        scratch_shapes=[pltpu.VMEM((rows, max(slots, TILE)), jnp.int32)],
-        compiler_params=pltpu.CompilerParams(vmem_limit_bytes=10 << 20),
-        cost_estimate=pl.CostEstimate(
-            flops=2 * slots * rows * window.shape[0] * width, bytes_accessed=2 * slots * rows * width, transcendentals=0
-        ),
-        name="fetch_own",
-    )(me, senders, window)
-
-
-def by_matmul_kernel(slots, block, sizes, me_ref, sender_ref, slot_ref, count_ref, receiver_ref, fetched_ref, *refs):
+def by_matmul_kernel(slots, rows, block, sizes, me_ref, sender_ref, slot_ref, count_ref, receiver_ref, *refs):
     parts, out_ref = refs[: len(sizes)], refs[len(sizes)]
     window, index_ref, weight_ref = refs[len(sizes) + 1 :]
-    depth, rows = sum(sizes), sender_ref.shape[1]
-    index_ref[...] = upright(place_in_pairs(sender_ref[...], depth // 3, me_ref[0], False))
+    index_ref[...] = upright(place_in_pairs(sender_ref[...], sum(sizes) // 5, me_ref[0]))
     weight_ref[...] = upright(scaled(slot_ref[...], count_ref[...]))
     first = 0
     for part, size in zip(parts, sizes):
         window[first : first + size, :] = part[...]
         first += size
-    columns = lax.broadcasted_iota(jnp.int32, (block, depth), 1).astype(jnp.int16)
+    columns = lax.broadcasted_iota(jnp.int32, (block, first), 1).astype(jnp.int16)
+    one, zero = jnp.bfloat16(1), jnp.bfloat16(0)
 
     def one_block(b, carry):
         at = pl.ds(pl.multiple_of(b * block, block), block)
@@ -359,7 +314,9 @@
         index, weight = index_ref[at, :], weight_ref[at, :]
         acc = jnp.zeros(mine.shape, jnp.float32)
         for k in range(slots):
-            fetched = pick_rows(index[:, k : k + 1], columns, window) + fetched_ref[k, at, :].astype(jnp.float32)
+            wanted = jnp.broadcast_to(index[:, k : k + 1], (block, LANES)).astype(jnp.int16)
+            pick = [jnp.where(columns[:, j : j + LANES] == wanted, one, zero) for j in range(0, first, LANES)]
+            fetched = dot(jnp.concatenate(pick, axis=1), window[...])
             h = (fetched + mine) * 0.5
             acc = acc + (h + h * jnp.tanh(h)) * weight[:, k : k + 1]
         for j in range(out_ref.shape[0]):
@@ -369,15 +326,14 @@
     lax.fori_loop(0, rows // block, one_block, 0)
 
 
-def aggregate_by_matmul(senders, weights, counts, receivers, projected, copies, block=256):
+def aggregate_by_matmul(senders, weights, counts, receivers, parts, copies, block=256):
     slots, (rows, width) = senders.shape[0], receivers.shape
     me = lax.axis_index("region").astype(jnp.int32)[None]
-    fetched, parts = window_of_pairs(projected, functools.partial(fetch_own, senders))
     sizes = tuple(part.shape[0] for part in parts)
     return pl.pallas_call(
-        functools.partial(by_matmul_kernel, slots, block, sizes),
+        functools.partial(by_matmul_kernel, slots, rows, block, sizes),
         out_shape=jax.ShapeDtypeStruct((copies, rows, width), receivers.dtype),
-        in_specs=[SMEM] + [VMEM] * (5 + len(parts)),
+        in_specs=[SMEM] + [VMEM] * (4 + len(parts)),
         out_specs=VMEM,
         scratch_shapes=[
             pltpu.VMEM((sum(sizes), width), jnp.bfloat16),
@@ -391,7 +347,7 @@
             transcendentals=slots * rows * width,
         ),
         name="aggregate_by_matmul",
-    )(me, senders, weights, counts[None, :], receivers, fetched, *parts)
+    )(me, senders, weights, counts[None, :], receivers, *parts)
 
 
 def shards(
@@ -432,11 +388,11 @@
     mesh_one, projected, later = mesh_step(
         mesh_one_kernel, mesh_state, (bf16, bf16, f32), core[None], full, mesh_state, enc_out, mine, other, base
     )
-    agg = aggregate_by_matmul(m2m_index, m2m_weight, m2m_count, mesh_one, projected, n)
+    agg = aggregate_by_matmul(m2m_index, m2m_weight, m2m_count, mesh_one, window_of_pairs(projected), n)
     mesh_next, projected = mesh_step(
         mesh_next_kernel, mesh_state, (bf16, bf16), core[None], gather_chan(agg), mesh_one, proc_out, mine, other, later
     )
-    agg = aggregate_by_matmul(m2g_index, m2g_weight, m2g_count, grid_state, projected, 1)[0]
+    agg = aggregate_by_matmul(m2g_index, m2g_weight, m2g_count, grid_state, window_of_pairs(projected), 1)[0]
     grid_next, _ = project_by_exchanges(agg, dec_out, base=(grid_state,))
     return grid_next, mesh_next
 

time: 169 us -> 165 us (0.976)
  starting transfers between devices: 78.6 us -> 71.8 us
  waiting for transfers between devices: 19.8 us -> 23.1 us
  other arithmetic: 0.18 us -> 1.97 us
    ppermute x6, starting transfers between devices: 27.8 us -> 21.1 us  [shift(): lax.ppermute(shard, 'region', [(i, i + by) for i in range(n) if 0 <= i +...]
    ppermute x6, waiting for transfers between devices: 5.9 us -> 11 us  [shift(): lax.ppermute(shard, 'region', [(i, i + by) for i in range(n) if 0 <= i +...]
    pallas_call x4 -> x2, Pallas kernels: 8.52 us -> 6.57 us  [aggregate_by_matmul(): pl.pallas_call(functools.partial(by_matmul_kernel, slots, rows, block, si...]
    concatenate x1, other arithmetic: 0.04 us -> 1.84 us  [shards(): packed = jnp.concatenate(own_rows + [mesh_state], axis=0)]
    ppermute x17, waiting for transfers between devices: 13.9 us -> 12.1 us  [exchange(): return lax.ppermute(shard, axis, [(i, partner(i)) for i in range(n)])]
  transfers between devices with their start and end apart: 23 -> 23, of which waited for: 9 -> 9; matrix products, arithmetic and copies ran while one was open for 1% -> 2% of each run, Pallas kernels for 7% -> 5%
where the time goes in v5:
time: 165 us; the launch traced here: 164 us
  starting transfers between devices  71.8 us (44%)
  blocking collectives  44 us (27%)
  waiting for transfers between devices  23.1 us (14%)
  Pallas kernels  19.4 us (12%)
  local copies, waits for them, and re-layouts  2.8 us (2%)
  other arithmetic  1.97 us (1%)
    ppermute x17, starting transfers between devices, exchange(): return lax.ppermute(shard, axis, [(i, partner(i)) for i in range(n)])  50.7 us
    ppermute x6, starting transfers between devices, shift(): lax.ppermute(shard, 'region', [(i, i + by) for i in range(n) if 0 <= i +...  21.1 us
    all_gather x1, blocking collectives, shards(): full = lax.all_gather(agg[0], 'chan', axis=0)  19 us
    all_to_all x1, blocking collectives, gather_chan(): lax.all_to_all(copies, 'chan', split_axis=0, concat_axis=0, tiled=True)  12.6 us
    all_gather x6, blocking collectives, core_pair(): lax.all_gather(shard, 'region', axis=0, tiled=True, axis_index_groups=gro...  12.3 us
    ppermute x17, waiting for transfers between devices, exchange(): return lax.ppermute(shard, axis, [(i, partner(i)) for i in range(n)])  12.1 us
    ppermute x6, waiting for transfers between devices, shift(): lax.ppermute(shard, 'region', [(i, i + by) for i in range(n) if 0 <= i +...  11 us
    pallas_call x1, Pallas kernels, aggregate_by_rows(): pl.pallas_call(functools.partial(by_rows_kernel, slots, rows, group, size...  7.34 us
  transfers between devices with their start and end apart: 23, of which 9 were waited for; matrix products, arithmetic and copies ran while one was open for 2% of the time, Pallas kernels for 5%

profile of v5, /device:TPU:248, one launch (start us, length us, event | category | flops | bytes accessed | tf_op | source)
XLA Modules:
  0.0 164.1 jit_solution(5073775171377633649)
XLA Ops:
  0.7 1.9 %fusion.6 = (bf16[512,256]{1,0:T(8,128)(2,1)}, bf16[512,256]{1,0:T(8,128)(2,1)}) fusion(bf16[1024,256]{1,0:T(8,128)(2,1)} %refs_0_.1), kind=kLoop, calls=%fused_computation.24 | loop fusion | bytes 1048576 | tf_op jit(solution)/shard_map/slice | solution.py:75
  2.6 3.4 %collective-permute-start.1 = (bf16[512,256]{1,0:T(8,128)(2,1)}, bf16[512,256]{1,0:T(8,128)(2,1)S(1)}, u32[]{:S(2)}, u32[]{:S(2)}) collective-permute-start(bf16[512,256]{1,0:T(8,128)(2,1)} %get-tuple-element.28), channel_id=1, source_target_pairs={{0,1},{1,0},{2,3},{3,2},{4,5},{5,4},{6,7},{7,6},{8,9},{9,8},{10,11... | collective-permute-start | bytes 786440 | tf_op jit(solution)/shard_map/ppermute | solution.py:19
  6.0 4.0 %collective-permute-start.2 = (bf16[512,256]{1,0:T(8,128)(2,1)}, bf16[512,256]{1,0:T(8,128)(2,1)S(1)}, u32[]{:S(2)}, u32[]{:S(2)}) collective-permute-start(bf16[512,256]{1,0:T(8,128)(2,1)} %get-tuple-element.29), channel_id=1, source_target_pairs={{0,3},{1,2},{2,1},{3,0},{4,7},{5,6},{6,5},{7,4},{8,11},{9,10},{10,... | collective-permute-start | bytes 786440 | tf_op jit(solution)/shard_map/ppermute | solution.py:19
  10.0 3.0 %collective-permute-start.3 = (bf16[512,256]{1,0:T(8,128)(2,1)}, bf16[512,256]{1,0:T(8,128)(2,1)S(1)}, u32[]{:S(2)}, u32[]{:S(2)}) collective-permute-start(bf16[512,256]{1,0:T(8,128)(2,1)} %get-tuple-element.28), channel_id=1, source_target_pairs={{0,3},{1,2},{2,1},{3,0},{4,7},{5,6},{6,5},{7,4},{8,11},{9,10},{10,... | collective-permute-start | bytes 786440 | tf_op jit(solution)/shard_map/ppermute | solution.py:19
  13.1 1.9 %collective-permute-start = (bf16[512,256]{1,0:T(8,128)(2,1)}, bf16[512,256]{1,0:T(8,128)(2,1)S(1)}, u32[]{:S(2)}, u32[]{:S(2)}) collective-permute-start(bf16[512,256]{1,0:T(8,128)(2,1)} %get-tuple-element.29), channel_id=1, source_target_pairs={{0,1},{1,0},{2,3},{3,2},{4,5},{5,4},{6,7},{7,6},{8,9},{9,8},{10,11... | collective-permute-start | bytes 786440 | tf_op jit(solution)/shard_map/ppermute | solution.py:19
  15.1 0.7 constant_dynamic-slice_fusion
  15.8 4.0 %collective-permute-start.5 = (bf16[512,256]{1,0:T(8,128)(2,1)S(1)}, bf16[512,256]{1,0:T(8,128)(2,1)S(1)}, u32[]{:S(2)}, u32[]{:S(2)}) collective-permute-start(bf16[512,256]{1,0:T(8,128)(2,1)S(1)} %collective-permute-done.1.near_low), channel_id=1, source_target_pairs={{0,3},{1,2},{2,1},{3,0},{4,7},{5,6},{6,5},{7,4},{8,11},{9,10},{10,... | collective-permute-start | bytes 786440 | tf_op jit(solution)/shard_map/ppermute | solution.py:19
  19.8 3.3 %collective-permute-start.4 = (bf16[512,256]{1,0:T(8,128)(2,1)S(1)}, bf16[512,256]{1,0:T(8,128)(2,1)S(1)}, u32[]{:S(2)}, u32[]{:S(2)}) collective-permute-start(bf16[512,256]{1,0:T(8,128)(2,1)S(1)} %collective-permute-done.2.other_top), channel_id=1, source_target_pairs={{0,1},{1,0},{2,3},{3,2},{4,5},{5,4},{6,7},{7,6},{8,9},{9,8},{10,11... | collective-permute-start | bytes 786440 | tf_op jit(solution)/shard_map/ppermute | solution.py:19
  23.1 1.8 %pad_maximum_fusion.own = bf16[1280,256]{1,0:T(8,128)(2,1)} fusion(bf16[256,256]{1,0:T(8,128)(2,1)S(1)} %copy-done.3, bf16[512,256]{1,0:T(8,128)(2,1)S(1)} %get-tuple-element.34, bf16[512,256]{1,0:T(8,128)(2,1)} %get-tuple-element.35), kind=kLoop, calls=%fused_computation | loop fusion | flops 1966080 | bytes 1310720 | tf_op jit(solution)/shard_map/concatenate | solution.py:377
  25.6 2.7 %collective-permute-done.5.far_low = bf16[512,256]{1,0:T(8,128)(2,1)S(1)} collective-permute-done((bf16[512,256]{1,0:T(8,128)(2,1)S(1)}, bf16[512,256]{1,0:T(8,128)(2,1)S(1)}, u32[]{:S(2)}, u32[]{:S(2)}) %collective-permute-start.5) | collective-permute-done | bytes 262176 | tf_op jit(solution)/shard_map/ppermute | solution.py:19
  28.9 1.9 %collective-permute-start.8 = (bf16[1024,256]{1,0:T(8,128)(2,1)S(1)}, bf16[1024,256]{1,0:T(8,128)(2,1)}, u32[]{:S(2)}, u32[]{:S(2)}) collective-permute-start(bf16[1024,256]{1,0:T(8,128)(2,1)S(1)} %last_block.2.refs_0_), channel_id=1, source_target_pairs={{0,4},{4,0},{8,12},{12,8},{16,20},{20,16},{24,28},{28,24},{32,36},... | collective-permute-start | bytes 1572872 | tf_op jit(solution)/shard_map/ppermute | solution.py:19
  30.8 3.3 %collective-permute-start.7 = (bf16[1024,256]{1,0:T(8,128)(2,1)S(1)}, bf16[1024,256]{1,0:T(8,128)(2,1)S(1)}, u32[]{:S(2)}, u32[]{:S(2)}) collective-permute-start(bf16[1024,256]{1,0:T(8,128)(2,1)S(1)} %last_block.2.refs_0_), channel_id=1, source_target_pairs={{8,0},{12,4},{16,8},{20,12},{24,16},{28,20},{32,24},{36,28},{40,32... | collective-permute-start | bytes 1572872 | tf_op jit(solution)/shard_map/ppermute | solution.py:24
  34.1 5.9 %collective-permute-start.6 = (bf16[1024,256]{1,0:T(8,128)(2,1)S(1)}, bf16[1024,256]{1,0:T(8,128)(2,1)S(1)}, u32[]{:S(2)}, u32[]{:S(2)}) collective-permute-start(bf16[1024,256]{1,0:T(8,128)(2,1)S(1)} %last_block.2.refs_0_), channel_id=1, source_target_pairs={{0,8},{4,12},{8,16},{12,20},{16,24},{20,28},{24,32},{28,36},{32,40... | collective-permute-start | bytes 1572872 | tf_op jit(solution)/shard_map/ppermute | solution.py:24
  40.1 3.6 %collective-permute-start.11 = (bf16[1280,256]{1,0:T(8,128)(2,1)}, bf16[1280,256]{1,0:T(8,128)(2,1)S(1)}, u32[]{:S(2)}, u32[]{:S(2)}) collective-permute-start(bf16[1280,256]{1,0:T(8,128)(2,1)} %pad_maximum_fusion.own), channel_id=1, source_target_pairs={{0,2},{1,3},{2,0},{3,1},{4,6},{5,7},{6,4},{7,5},{8,10},{9,11},{10,... | collective-permute-start | bytes 1966088 | tf_op jit(solution)/shard_map/ppermute | solution.py:19
  43.7 4.0 %collective-permute-start.10 = (bf16[1280,256]{1,0:T(8,128)(2,1)}, bf16[1280,256]{1,0:T(8,128)(2,1)S(1)}, u32[]{:S(2)}, u32[]{:S(2)}) collective-permute-start(bf16[1280,256]{1,0:T(8,128)(2,1)} %pad_maximum_fusion.own), channel_id=1, source_target_pairs={{0,3},{1,2},{2,1},{3,0},{4,7},{5,6},{6,5},{7,4},{8,11},{9,10},{10,... | collective-permute-start | bytes 1966088 | tf_op jit(solution)/shard_map/ppermute | solution.py:19
  47.7 1.9 %collective-permute-start.9 = (bf16[1280,256]{1,0:T(8,128)(2,1)}, bf16[1280,256]{1,0:T(8,128)(2,1)S(1)}, u32[]{:S(2)}, u32[]{:S(2)}) collective-permute-start(bf16[1280,256]{1,0:T(8,128)(2,1)} %pad_maximum_fusion.own), channel_id=1, source_target_pairs={{0,1},{1,0},{2,3},{3,2},{4,5},{5,4},{6,7},{7,6},{8,9},{9,8},{10,11... | collective-permute-start | bytes 1966088 | tf_op jit(solution)/shard_map/ppermute | solution.py:19
  49.7 0.7 collective-permute-done.7.refs_2_
  50.4 1.2 collective-permute-done.6.refs_1_
  51.6 2.2 %all_gather.22.refs_5_ = bf16[1024,256]{1,0:T(8,128)(2,1)S(1)} all-gather(bf16[512,256]{1,0:T(8,128)(2,1)S(1)} %get-tuple-element.24), channel_id=1, replica_groups={{0,4},{8,12},{16,20},{24,28},{32,36},{40,44},{48,52},{56,60},{64,68},{7..., dimensions={0}, use_global_device_ids=true | all-gather | bytes 786432 | tf_op jit(solution)/shard_map/all_gather | solution.py:30
  53.8 2.2 %all_gather.21.refs_4_ = bf16[1024,256]{1,0:T(8,128)(2,1)S(1)} all-gather(bf16[512,256]{1,0:T(8,128)(2,1)S(1)} %get-tuple-element.25), channel_id=1, replica_groups={{0,4},{8,12},{16,20},{24,28},{32,36},{40,44},{48,52},{56,60},{64,68},{7..., dimensions={0}, use_global_device_ids=true | all-gather | bytes 786432 | tf_op jit(solution)/shard_map/all_gather | solution.py:30
  56.0 7.3 %aggregate_by_rows.1 = bf16[1,256,256]{2,1,0:T(8,128)(2,1)S(1)} custom-call(s32[16,256]{1,0:T(8,128)S(1)} %fusion.4.index_ref, f32[16,256]{1,0:T(8,128)S(1)} %copy-done.7, s32[1,256]{1,0:T(1,128)S(1)} %bitcast.12, bf16[256,256]{1,0:T(8,128)(2,1)S(1)} %copy-done.3, bf16[1024,256]{1,0:T(8,128)(2,1)S(1)} %last_block.2.refs_0_, ...), custom_call_target="tpu_custom_call" | custom-call | flops 1 | bytes 1 | tf_op jit(solution)/shard_map/aggregate_by_rows/pallas_call | solution.py:281
  63.4 19.0 %all_gather.23._.full = bf16[4,256,256]{2,1,0:T(8,128)(2,1)S(1)} all-gather(bf16[1,256,256]{2,1,0:T(8,128)(2,1)S(1)} %aggregate_by_rows.1), channel_id=1, replica_groups=mesh['region'=128,'chan'=4] {'chan'}, dimensions={0}, use_global_device_ids=true | all-gather | bytes 655360 | tf_op jit(solution)/shard_map/all_gather | solution.py:385
  82.4 1.3 combine.1
  83.7 1.9 %collective-permute-start.12 = (bf16[1536,256]{1,0:T(8,128)(2,1)S(1)}, bf16[1536,256]{1,0:T(8,128)(2,1)S(1)}, u32[]{:S(2)}, u32[]{:S(2)}) collective-permute-start(bf16[1536,256]{1,0:T(8,128)(2,1)S(1)} %get-tuple-element.17.mine), channel_id=1, source_target_pairs={{0,4},{4,0},{8,12},{12,8},{16,20},{20,16},{24,28},{28,24},{32,36},... | collective-permute-start | bytes 2359304 | tf_op jit(solution)/shard_map/ppermute | solution.py:19
  85.6 2.3 %collective-permute-done.12.other = bf16[1536,256]{1,0:T(8,128)(2,1)S(1)} collective-permute-done((bf16[1536,256]{1,0:T(8,128)(2,1)S(1)}, bf16[1536,256]{1,0:T(8,128)(2,1)S(1)}, u32[]{:S(2)}, u32[]{:S(2)}) %collective-permute-start.12) | collective-permute-done | bytes 786464 | tf_op jit(solution)/shard_map/ppermute | solution.py:19
  88.5 2.3 %collective-permute-start.14 = (bf16[256,256]{1,0:T(8,128)(2,1)S(1)}, bf16[256,256]{1,0:T(8,128)(2,1)S(1)}, u32[]{:S(2)}, u32[]{:S(2)}) collective-permute-start(bf16[256,256]{1,0:T(8,128)(2,1)S(1)} %get-tuple-element.20), channel_id=1, source_target_pairs={{0,8},{4,12},{8,16},{12,20},{16,24},{20,28},{24,32},{28,36},{32,40... | collective-permute-start | bytes 393224 | tf_op jit(solution)/shard_map/ppermute | solution.py:24
  90.8 3.6 %collective-permute-start.13 = (bf16[256,256]{1,0:T(8,128)(2,1)S(1)}, bf16[256,256]{1,0:T(8,128)(2,1)S(1)}, u32[]{:S(2)}, u32[]{:S(2)}) collective-permute-start(bf16[256,256]{1,0:T(8,128)(2,1)S(1)} %get-tuple-element.20), channel_id=1, source_target_pairs={{8,0},{12,4},{16,8},{20,12},{24,16},{28,20},{32,24},{36,28},{40,32... | collective-permute-start | bytes 393224 | tf_op jit(solution)/shard_map/ppermute | solution.py:24
  94.5 2.0 %all_gather.25.refs_1_ = bf16[512,256]{1,0:T(8,128)(2,1)S(1)} all-gather(bf16[256,256]{1,0:T(8,128)(2,1)S(1)} %get-tuple-element.20), channel_id=1, replica_groups={{0,4},{8,12},{16,20},{24,28},{32,36},{40,44},{48,52},{56,60},{64,68},{7..., dimensions={0}, use_global_device_ids=true | all-gather | bytes 393216 | tf_op jit(solution)/shard_map/all_gather | solution.py:30
  96.5 4.8 %collective-permute-done.13 = bf16[256,256]{1,0:T(8,128)(2,1)S(1)} collective-permute-done((bf16[256,256]{1,0:T(8,128)(2,1)S(1)}, bf16[256,256]{1,0:T(8,128)(2,1)S(1)}, u32[]{:S(2)}, u32[]{:S(2)}) %collective-permute-start.13) | collective-permute-done | bytes 131104 | tf_op jit(solution)/shard_map/ppermute | solution.py:24
  101.3 2.0 %all_gather.24.refs_0_ = bf16[512,256]{1,0:T(8,128)(2,1)S(1)} all-gather(bf16[256,256]{1,0:T(8,128)(2,1)S(1)} %get-tuple-element.33), channel_id=1, replica_groups={{0,4},{8,12},{16,20},{24,28},{32,36},{40,44},{48,52},{56,60},{64,68},{7..., dimensions={0}, use_global_device_ids=true | all-gather | bytes 393216 | tf_op jit(solution)/shard_map/all_gather | solution.py:30
  103.3 2.1 %aggregate_by_matmul.2 = bf16[4,256,256]{2,1,0:T(8,128)(2,1)S(1)} custom-call(s32[1]{0:T(128)} %bitcast.1.me_ref, s32[8,256]{1,0:T(8,128)S(1)} %copy-done.13, f32[8,256]{1,0:T(8,128)S(1)} %copy-done.14, s32[1,256]{1,0:T(1,128)S(1)} %bitcast.14, bf16[256,256]{1,0:T(8,128)(2,1)S(1)} %get-tuple-element.19.receiver_ref.mesh_one, ...), custom_call_target="tpu_custom_call" | custom-call | flops 1342177280 | bytes 917504 | tf_op jit(solution)/shard_map/aggregate_by_matmul/pallas_call | solution.py:333
  105.4 12.6 %all_to_all.5.full = bf16[4,256,256]{2,1,0:T(8,128)(2,1)S(1)} all-to-all(bf16[4,256,256]{2,1,0:T(8,128)(2,1)S(1)} %aggregate_by_matmul.2), channel_id=1, replica_groups=mesh['region'=128,'chan'=4] {'chan'}, dimensions={0} | all-to-all | bytes 1048576 | tf_op jit(solution)/shard_map/all_to_all | solution.py:34
  118.0 1.1 mesh_step.3
  119.2 2.0 %collective-permute-start.16 = (bf16[256,256]{1,0:T(8,128)(2,1)S(1)}, bf16[256,256]{1,0:T(8,128)(2,1)S(1)}, u32[]{:S(2)}, u32[]{:S(2)}) collective-permute-start(bf16[256,256]{1,0:T(8,128)(2,1)S(1)} %get-tuple-element.22), channel_id=1, source_target_pairs={{0,8},{4,12},{8,16},{12,20},{16,24},{20,28},{24,32},{28,36},{32,40... | collective-permute-start | bytes 393224 | tf_op jit(solution)/shard_map/ppermute | solution.py:24
  121.2 3.9 %collective-permute-start.15 = (bf16[256,256]{1,0:T(8,128)(2,1)S(1)}, bf16[256,256]{1,0:T(8,128)(2,1)S(1)}, u32[]{:S(2)}, u32[]{:S(2)}) collective-permute-start(bf16[256,256]{1,0:T(8,128)(2,1)S(1)} %get-tuple-element.22), channel_id=1, source_target_pairs={{8,0},{12,4},{16,8},{20,12},{24,16},{28,20},{32,24},{36,28},{40,32... | collective-permute-start | bytes 393224 | tf_op jit(solution)/shard_map/ppermute | solution.py:24
  125.1 2.0 %all_gather.27.refs_1_ = bf16[512,256]{1,0:T(8,128)(2,1)S(1)} all-gather(bf16[256,256]{1,0:T(8,128)(2,1)S(1)} %get-tuple-element.22), channel_id=1, replica_groups={{0,4},{8,12},{16,20},{24,28},{32,36},{40,44},{48,52},{56,60},{64,68},{7..., dimensions={0}, use_global_device_ids=true | all-gather | bytes 393216 | tf_op jit(solution)/shard_map/all_gather | solution.py:30
  127.1 4.3 %collective-permute-done.15 = bf16[256,256]{1,0:T(8,128)(2,1)S(1)} collective-permute-done((bf16[256,256]{1,0:T(8,128)(2,1)S(1)}, bf16[256,256]{1,0:T(8,128)(2,1)S(1)}, u32[]{:S(2)}, u32[]{:S(2)}) %collective-permute-start.15) | collective-permute-done | bytes 131104 | tf_op jit(solution)/shard_map/ppermute | solution.py:24
  131.4 2.0 %all_gather.26.refs_0_ = bf16[512,256]{1,0:T(8,128)(2,1)S(1)} all-gather(bf16[256,256]{1,0:T(8,128)(2,1)S(1)} %get-tuple-element.31), channel_id=1, replica_groups={{0,4},{8,12},{16,20},{24,28},{32,36},{40,44},{48,52},{56,60},{64,68},{7..., dimensions={0}, use_global_device_ids=true | all-gather | bytes 393216 | tf_op jit(solution)/shard_map/all_gather | solution.py:30
  133.4 4.5 %aggregate_by_matmul.3 = bf16[1,1024,256]{2,1,0:T(8,128)(2,1)S(1)} custom-call(s32[1]{0:T(128)} %bitcast.1.me_ref, s32[4,1024]{1,0:T(4,128)S(1)} %copy-done.11, f32[4,1024]{1,0:T(4,128)S(1)} %copy-done.12, s32[1,1024]{1,0:T(1,128)S(1)} %bitcast.13, bf16[1024,256]{1,0:T(8,128)(2,1)S(1)} %copy-done, bf16[512,256]{1,0:T(8,128)(2,1)S(1)} %all_gather.26.refs_0_, ...), custom_call_target="tpu_custom_call" | custom-call | flops 2684354560 | bytes 1703936 | tf_op jit(solution)/shard_map/aggregate_by_matmul/pallas_call | solution.py:333
  138.0 2.6 %collective-permute-start.18 = (bf16[512,256]{1,0:T(8,128)(2,1)S(1)}, bf16[512,256]{1,0:T(8,128)(2,1)S(1)}, u32[]{:S(2)}, u32[]{:S(2)}) collective-permute-start(bf16[512,256]{1,0:T(8,128)(2,1)S(1)} %get-tuple-element.26), channel_id=1, source_target_pairs={{0,1},{1,0},{2,3},{3,2},{4,5},{5,4},{6,7},{7,6},{8,9},{9,8},{10,11... | collective-permute-start | bytes 786440 | tf_op jit(solution)/shard_map/ppermute | solution.py:19
  140.6 2.7 %collective-permute-start.19 = (bf16[512,256]{1,0:T(8,128)(2,1)S(1)}, bf16[512,256]{1,0:T(8,128)(2,1)S(1)}, u32[]{:S(2)}, u32[]{:S(2)}) collective-permute-start(bf16[512,256]{1,0:T(8,128)(2,1)S(1)} %get-tuple-element.27), channel_id=1, source_target_pairs={{0,3},{1,2},{2,1},{3,0},{4,7},{5,6},{6,5},{7,4},{8,11},{9,10},{10,... | collective-permute-start | bytes 786440 | tf_op jit(solution)/shard_map/ppermute | solution.py:19
  143.3 4.3 %collective-permute-start.20 = (bf16[512,256]{1,0:T(8,128)(2,1)S(1)}, bf16[512,256]{1,0:T(8,128)(2,1)S(1)}, u32[]{:S(2)}, u32[]{:S(2)}) collective-permute-start(bf16[512,256]{1,0:T(8,128)(2,1)S(1)} %get-tuple-element.26), channel_id=1, source_target_pairs={{0,3},{1,2},{2,1},{3,0},{4,7},{5,6},{6,5},{7,4},{8,11},{9,10},{10,... | collective-permute-start | bytes 786440 | tf_op jit(solution)/shard_map/ppermute | solution.py:19
  147.6 2.2 %collective-permute-start.17 = (bf16[512,256]{1,0:T(8,128)(2,1)S(1)}, bf16[512,256]{1,0:T(8,128)(2,1)S(1)}, u32[]{:S(2)}, u32[]{:S(2)}) collective-permute-start(bf16[512,256]{1,0:T(8,128)(2,1)S(1)} %get-tuple-element.27), channel_id=1, source_target_pairs={{0,1},{1,0},{2,3},{3,2},{4,5},{5,4},{6,7},{7,6},{8,9},{9,8},{10,11... | collective-permute-start | bytes 786440 | tf_op jit(solution)/shard_map/ppermute | solution.py:19
  149.8 3.1 %collective-permute-start.22 = (bf16[512,256]{1,0:T(8,128)(2,1)S(1)}, bf16[512,256]{1,0:T(8,128)(2,1)S(1)}, u32[]{:S(2)}, u32[]{:S(2)}) collective-permute-start(bf16[512,256]{1,0:T(8,128)(2,1)S(1)} %collective-permute-done.18.near_low), channel_id=1, source_target_pairs={{0,3},{1,2},{2,1},{3,0},{4,7},{5,6},{6,5},{7,4},{8,11},{9,10},{10,... | collective-permute-start | bytes 786440 | tf_op jit(solution)/shard_map/ppermute | solution.py:19
  152.9 2.7 %collective-permute-start.21 = (bf16[512,256]{1,0:T(8,128)(2,1)S(1)}, bf16[512,256]{1,0:T(8,128)(2,1)S(1)}, u32[]{:S(2)}, u32[]{:S(2)}) collective-permute-start(bf16[512,256]{1,0:T(8,128)(2,1)S(1)} %collective-permute-done.19.other_top), channel_id=1, source_target_pairs={{0,1},{1,0},{2,3},{3,2},{4,5},{5,4},{6,7},{7,6},{8,9},{9,8},{10,11... | collective-permute-start | bytes 786440 | tf_op jit(solution)/shard_map/ppermute | solution.py:19
  155.7 2.8 %collective-permute-done.20.other_low = bf16[512,256]{1,0:T(8,128)(2,1)S(1)} collective-permute-done((bf16[512,256]{1,0:T(8,128)(2,1)S(1)}, bf16[512,256]{1,0:T(8,128)(2,1)S(1)}, u32[]{:S(2)}, u32[]{:S(2)}) %collective-permute-start.20) | collective-permute-done | bytes 262176 | tf_op jit(solution)/shard_map/ppermute | solution.py:19
  159.1 3.9 %collective-permute-done.22.far_low = bf16[512,256]{1,0:T(8,128)(2,1)S(1)} collective-permute-done((bf16[512,256]{1,0:T(8,128)(2,1)S(1)}, bf16[512,256]{1,0:T(8,128)(2,1)S(1)}, u32[]{:S(2)}, u32[]{:S(2)}) %collective-permute-start.22) | collective-permute-done | bytes 262176 | tf_op jit(solution)/shard_map/ppermute | solution.py:19
  163.0 1.1 last_block.3
  (60 shorter events, 2.6 us)
Async XLA Ops:
  0.6 14.4 %copy-start.4 = (bf16[1024,256]{1,0:T(8,128)(2,1)S(1)}, bf16[1024,256]{1,0:T(8,128)(2,1)}, u32[]{:S(2)}) copy-start(bf16[1024,256]{1,0:T(8,128)(2,1)} %w_out.3) | copy-start | bytes 1572868
  0.6 14.4 %copy-start.5 = (bf16[1024,256]{1,0:T(8,128)(2,1)S(1)}, bf16[1024,256]{1,0:T(8,128)(2,1)}, u32[]{:S(2)}) copy-start(bf16[1024,256]{1,0:T(8,128)(2,1)} %w_out.2) | copy-start | bytes 1572868
  0.7 22.5 %copy-start.3 = (bf16[256,256]{1,0:T(8,128)(2,1)S(1)}, bf16[256,256]{1,0:T(8,128)(2,1)}, u32[]{:S(2)}) copy-start(bf16[256,256]{1,0:T(8,128)(2,1)} %mesh.1) | copy-start | bytes 393220
  2.6 13.2 %collective-permute-start.1 = (bf16[512,256]{1,0:T(8,128)(2,1)}, bf16[512,256]{1,0:T(8,128)(2,1)S(1)}, u32[]{:S(2)}, u32[]{:S(2)}) collective-permute-start(bf16[512,256]{1,0:T(8,128)(2,1)} %get-tuple-element.28), channel_id=1, source_target_pairs={{0,1},{1,0},{2,3},{3,2},{4,5},{5,4},{6,7},{7,6},{8,9},{9,8},{10,11... | collective-permute-start | bytes 786440 | tf_op jit(solution)/shard_map/ppermute | solution.py:19
  6.0 13.8 %collective-permute-start.2 = (bf16[512,256]{1,0:T(8,128)(2,1)}, bf16[512,256]{1,0:T(8,128)(2,1)S(1)}, u32[]{:S(2)}, u32[]{:S(2)}) collective-permute-start(bf16[512,256]{1,0:T(8,128)(2,1)} %get-tuple-element.29), channel_id=1, source_target_pairs={{0,3},{1,2},{2,1},{3,0},{4,7},{5,6},{6,5},{7,4},{8,11},{9,10},{10,... | collective-permute-start | bytes 786440 | tf_op jit(solution)/shard_map/ppermute | solution.py:19
  10.0 15.0 %collective-permute-start.3 = (bf16[512,256]{1,0:T(8,128)(2,1)}, bf16[512,256]{1,0:T(8,128)(2,1)S(1)}, u32[]{:S(2)}, u32[]{:S(2)}) collective-permute-start(bf16[512,256]{1,0:T(8,128)(2,1)} %get-tuple-element.28), channel_id=1, source_target_pairs={{0,3},{1,2},{2,1},{3,0},{4,7},{5,6},{6,5},{7,4},{8,11},{9,10},{10,... | collective-permute-start | bytes 786440 | tf_op jit(solution)/shard_map/ppermute | solution.py:19
  13.1 11.9 %collective-permute-start = (bf16[512,256]{1,0:T(8,128)(2,1)}, bf16[512,256]{1,0:T(8,128)(2,1)S(1)}, u32[]{:S(2)}, u32[]{:S(2)}) collective-permute-start(bf16[512,256]{1,0:T(8,128)(2,1)} %get-tuple-element.29), channel_id=1, source_target_pairs={{0,1},{1,0},{2,3},{3,2},{4,5},{5,4},{6,7},{7,6},{8,9},{9,8},{10,11... | collective-permute-start | bytes 786440 | tf_op jit(solution)/shard_map/ppermute | solution.py:19
  15.0 10.0 %copy-start = (bf16[1024,256]{1,0:T(8,128)(2,1)S(1)}, bf16[1024,256]{1,0:T(8,128)(2,1)}, u32[]{:S(2)}) copy-start(bf16[1024,256]{1,0:T(8,128)(2,1)} %refs_0_.1) | copy-start | bytes 1572868
  15.0 10.0 %copy-start.1 = (bf16[1024,256]{1,0:T(8,128)(2,1)S(1)}, bf16[1024,256]{1,0:T(8,128)(2,1)}, u32[]{:S(2)}) copy-start(bf16[1024,256]{1,0:T(8,128)(2,1)} %weight.5) | copy-start | bytes 1572868
  15.8 12.5 %collective-permute-start.5 = (bf16[512,256]{1,0:T(8,128)(2,1)S(1)}, bf16[512,256]{1,0:T(8,128)(2,1)S(1)}, u32[]{:S(2)}, u32[]{:S(2)}) collective-permute-start(bf16[512,256]{1,0:T(8,128)(2,1)S(1)} %collective-permute-done.1.near_low), channel_id=1, source_target_pairs={{0,3},{1,2},{2,1},{3,0},{4,7},{5,6},{6,5},{7,4},{8,11},{9,10},{10,... | collective-permute-start | bytes 786440 | tf_op jit(solution)/shard_map/ppermute | solution.py:19
  19.8 8.8 %collective-permute-start.4 = (bf16[512,256]{1,0:T(8,128)(2,1)S(1)}, bf16[512,256]{1,0:T(8,128)(2,1)S(1)}, u32[]{:S(2)}, u32[]{:S(2)}) collective-permute-start(bf16[512,256]{1,0:T(8,128)(2,1)S(1)} %collective-permute-done.2.other_top), channel_id=1, source_target_pairs={{0,1},{1,0},{2,3},{3,2},{4,5},{5,4},{6,7},{7,6},{8,9},{9,8},{10,11... | collective-permute-start | bytes 786440 | tf_op jit(solution)/shard_map/ppermute | solution.py:19
  25.6 14.5 %copy-start.17 = (s32[16,256]{1,0:T(8,128)S(1)}, s32[16,256]{1,0:T(8,128)}, u32[]{:S(2)}) copy-start(s32[16,256]{1,0:T(8,128)} %param.25) | copy-start | bytes 49156
  28.9 14.8 %collective-permute-start.8 = (bf16[1024,256]{1,0:T(8,128)(2,1)S(1)}, bf16[1024,256]{1,0:T(8,128)(2,1)}, u32[]{:S(2)}, u32[]{:S(2)}) collective-permute-start(bf16[1024,256]{1,0:T(8,128)(2,1)S(1)} %last_block.2.refs_0_), channel_id=1, source_target_pairs={{0,4},{4,0},{8,12},{12,8},{16,20},{20,16},{24,28},{28,24},{32,36},... | collective-permute-start | bytes 1572872 | tf_op jit(solution)/shard_map/ppermute | solution.py:19
  30.8 19.5 %collective-permute-start.7 = (bf16[1024,256]{1,0:T(8,128)(2,1)S(1)}, bf16[1024,256]{1,0:T(8,128)(2,1)S(1)}, u32[]{:S(2)}, u32[]{:S(2)}) collective-permute-start(bf16[1024,256]{1,0:T(8,128)(2,1)S(1)} %last_block.2.refs_0_), channel_id=1, source_target_pairs={{8,0},{12,4},{16,8},{20,12},{24,16},{28,20},{32,24},{36,28},{40,32... | collective-permute-start | bytes 1572872 | tf_op jit(solution)/shard_map/ppermute | solution.py:24
  34.1 17.5 %collective-permute-start.6 = (bf16[1024,256]{1,0:T(8,128)(2,1)S(1)}, bf16[1024,256]{1,0:T(8,128)(2,1)S(1)}, u32[]{:S(2)}, u32[]{:S(2)}) collective-permute-start(bf16[1024,256]{1,0:T(8,128)(2,1)S(1)} %last_block.2.refs_0_), channel_id=1, source_target_pairs={{0,8},{4,12},{8,16},{12,20},{16,24},{20,28},{24,32},{28,36},{32,40... | collective-permute-start | bytes 1572872 | tf_op jit(solution)/shard_map/ppermute | solution.py:24
  40.1 42.3 %collective-permute-start.11 = (bf16[1280,256]{1,0:T(8,128)(2,1)}, bf16[1280,256]{1,0:T(8,128)(2,1)S(1)}, u32[]{:S(2)}, u32[]{:S(2)}) collective-permute-start(bf16[1280,256]{1,0:T(8,128)(2,1)} %pad_maximum_fusion.own), channel_id=1, source_target_pairs={{0,2},{1,3},{2,0},{3,1},{4,6},{5,7},{6,4},{7,5},{8,10},{9,11},{10,... | collective-permute-start | bytes 1966088 | tf_op jit(solution)/shard_map/ppermute | solution.py:19
  43.7 38.7 %collective-permute-start.10 = (bf16[1280,256]{1,0:T(8,128)(2,1)}, bf16[1280,256]{1,0:T(8,128)(2,1)S(1)}, u32[]{:S(2)}, u32[]{:S(2)}) collective-permute-start(bf16[1280,256]{1,0:T(8,128)(2,1)} %pad_maximum_fusion.own), channel_id=1, source_target_pairs={{0,3},{1,2},{2,1},{3,0},{4,7},{5,6},{6,5},{7,4},{8,11},{9,10},{10,... | collective-permute-start | bytes 1966088 | tf_op jit(solution)/shard_map/ppermute | solution.py:19
  47.7 34.7 %collective-permute-start.9 = (bf16[1280,256]{1,0:T(8,128)(2,1)}, bf16[1280,256]{1,0:T(8,128)(2,1)S(1)}, u32[]{:S(2)}, u32[]{:S(2)}) collective-permute-start(bf16[1280,256]{1,0:T(8,128)(2,1)} %pad_maximum_fusion.own), channel_id=1, source_target_pairs={{0,1},{1,0},{2,3},{3,2},{4,5},{5,4},{6,7},{7,6},{8,9},{9,8},{10,11... | collective-permute-start | bytes 1966088 | tf_op jit(solution)/shard_map/ppermute | solution.py:19
  51.6 4.4 %copy-start.7 = (f32[16,256]{1,0:T(8,128)S(1)}, f32[16,256]{1,0:T(8,128)}, u32[]{:S(2)}) copy-start(f32[16,256]{1,0:T(8,128)} %slot_ref.3) | copy-start | bytes 49156
  51.6 4.4 %copy-start.8 = (s32[256]{0:T(256)S(1)}, s32[256]{0:T(256)}, u32[]{:S(2)}) copy-start(s32[256]{0:T(256)} %param.27) | copy-start | bytes 3076
  56.0 26.4 %copy-start.6 = (bf16[1280,256]{1,0:T(8,128)(2,1)S(1)}, bf16[1280,256]{1,0:T(8,128)(2,1)}, u32[]{:S(2)}) copy-start(bf16[1280,256]{1,0:T(8,128)(2,1)} %pad_maximum_fusion.own) | copy-start | bytes 1966084
  56.0 26.4 %copy-start.9 = (bf16[1024,256]{1,0:T(8,128)(2,1)S(1)}, bf16[1024,256]{1,0:T(8,128)(2,1)}, u32[]{:S(2)}) copy-start(bf16[1024,256]{1,0:T(8,128)(2,1)} %first.1) | copy-start | bytes 1572868
  56.0 26.4 %copy-start.10 = (bf16[1024,256]{1,0:T(8,128)(2,1)S(1)}, bf16[1024,256]{1,0:T(8,128)(2,1)}, u32[]{:S(2)}) copy-start(bf16[1024,256]{1,0:T(8,128)(2,1)} %second.1) | copy-start | bytes 1572868
  83.7 4.2 %collective-permute-start.12 = (bf16[1536,256]{1,0:T(8,128)(2,1)S(1)}, bf16[1536,256]{1,0:T(8,128)(2,1)S(1)}, u32[]{:S(2)}, u32[]{:S(2)}) collective-permute-start(bf16[1536,256]{1,0:T(8,128)(2,1)S(1)} %get-tuple-element.17.mine), channel_id=1, source_target_pairs={{0,4},{4,0},{8,12},{12,8},{16,20},{20,16},{24,28},{28,24},{32,36},... | collective-permute-start | bytes 2359304 | tf_op jit(solution)/shard_map/ppermute | solution.py:19
  88.4 14.9 %copy-start.13 = (s32[8,256]{1,0:T(8,128)S(1)}, s32[8,256]{1,0:T(8,128)}, u32[]{:S(2)}) copy-start(s32[8,256]{1,0:T(8,128)} %sender_ref.2) | copy-start | bytes 24580
  88.5 14.9 %copy-start.14 = (f32[8,256]{1,0:T(8,128)S(1)}, f32[8,256]{1,0:T(8,128)}, u32[]{:S(2)}) copy-start(f32[8,256]{1,0:T(8,128)} %slot_ref.4) | copy-start | bytes 24580
  88.5 14.9 %copy-start.16 = (s32[256]{0:T(256)S(1)}, s32[256]{0:T(256)}, u32[]{:S(2)}) copy-start(s32[256]{0:T(256)} %param.30) | copy-start | bytes 3076
  88.5 8.0 %collective-permute-start.14 = (bf16[256,256]{1,0:T(8,128)(2,1)S(1)}, bf16[256,256]{1,0:T(8,128)(2,1)S(1)}, u32[]{:S(2)}, u32[]{:S(2)}) collective-permute-start(bf16[256,256]{1,0:T(8,128)(2,1)S(1)} %get-tuple-element.20), channel_id=1, source_target_pairs={{0,8},{4,12},{8,16},{12,20},{16,24},{20,28},{24,32},{28,36},{32,40... | collective-permute-start | bytes 393224 | tf_op jit(solution)/shard_map/ppermute | solution.py:24
  90.8 10.5 %collective-permute-start.13 = (bf16[256,256]{1,0:T(8,128)(2,1)S(1)}, bf16[256,256]{1,0:T(8,128)(2,1)S(1)}, u32[]{:S(2)}, u32[]{:S(2)}) collective-permute-start(bf16[256,256]{1,0:T(8,128)(2,1)S(1)} %get-tuple-element.20), channel_id=1, source_target_pairs={{8,0},{12,4},{16,8},{20,12},{24,16},{28,20},{32,24},{36,28},{40,32... | collective-permute-start | bytes 393224 | tf_op jit(solution)/shard_map/ppermute | solution.py:24
  119.1 14.3 %copy-start.11 = (s32[4,1024]{1,0:T(4,128)S(1)}, s32[4,1024]{1,0:T(4,128)}, u32[]{:S(2)}) copy-start(s32[4,1024]{1,0:T(4,128)} %sender_ref.3) | copy-start | bytes 49156
  119.1 14.3 %copy-start.12 = (f32[4,1024]{1,0:T(4,128)S(1)}, f32[4,1024]{1,0:T(4,128)}, u32[]{:S(2)}) copy-start(f32[4,1024]{1,0:T(4,128)} %slot_ref.5) | copy-start | bytes 49156
  119.1 14.3 %copy-start.15 = (s32[1024]{0:T(1024)S(1)}, s32[1024]{0:T(1024)}, u32[]{:S(2)}) copy-start(s32[1024]{0:T(1024)} %param.33) | copy-start | bytes 12292
  119.2 8.0 %collective-permute-start.16 = (bf16[256,256]{1,0:T(8,128)(2,1)S(1)}, bf16[256,256]{1,0:T(8,128)(2,1)S(1)}, u32[]{:S(2)}, u32[]{:S(2)}) collective-permute-start(bf16[256,256]{1,0:T(8,128)(2,1)S(1)} %get-tuple-element.22), channel_id=1, source_target_pairs={{0,8},{4,12},{8,16},{12,20},{16,24},{20,28},{24,32},{28,36},{32,40... | collective-permute-start | bytes 393224 | tf_op jit(solution)/shard_map/ppermute | solution.py:24
  121.2 10.2 %collective-permute-start.15 = (bf16[256,256]{1,0:T(8,128)(2,1)S(1)}, bf16[256,256]{1,0:T(8,128)(2,1)S(1)}, u32[]{:S(2)}, u32[]{:S(2)}) collective-permute-start(bf16[256,256]{1,0:T(8,128)(2,1)S(1)} %get-tuple-element.22), channel_id=1, source_target_pairs={{8,0},{12,4},{16,8},{20,12},{24,16},{28,20},{32,24},{36,28},{40,32... | collective-permute-start | bytes 393224 | tf_op jit(solution)/shard_map/ppermute | solution.py:24
  137.9 20.6 %copy-start.2 = (bf16[1024,256]{1,0:T(8,128)(2,1)S(1)}, bf16[1024,256]{1,0:T(8,128)(2,1)}, u32[]{:S(2)}) copy-start(bf16[1024,256]{1,0:T(8,128)(2,1)} %weight.7) | copy-start | bytes 1572868
  138.0 11.9 %collective-permute-start.18 = (bf16[512,256]{1,0:T(8,128)(2,1)S(1)}, bf16[512,256]{1,0:T(8,128)(2,1)S(1)}, u32[]{:S(2)}, u32[]{:S(2)}) collective-permute-start(bf16[512,256]{1,0:T(8,128)(2,1)S(1)} %get-tuple-element.26), channel_id=1, source_target_pairs={{0,1},{1,0},{2,3},{3,2},{4,5},{5,4},{6,7},{7,6},{8,9},{9,8},{10,11... | collective-permute-start | bytes 786440 | tf_op jit(solution)/shard_map/ppermute | solution.py:19
  140.6 12.3 %collective-permute-start.19 = (bf16[512,256]{1,0:T(8,128)(2,1)S(1)}, bf16[512,256]{1,0:T(8,128)(2,1)S(1)}, u32[]{:S(2)}, u32[]{:S(2)}) collective-permute-start(bf16[512,256]{1,0:T(8,128)(2,1)S(1)} %get-tuple-element.27), channel_id=1, source_target_pairs={{0,3},{1,2},{2,1},{3,0},{4,7},{5,6},{6,5},{7,4},{8,11},{9,10},{10,... | collective-permute-start | bytes 786440 | tf_op jit(solution)/shard_map/ppermute | solution.py:19
  143.3 15.2 %collective-permute-start.20 = (bf16[512,256]{1,0:T(8,128)(2,1)S(1)}, bf16[512,256]{1,0:T(8,128)(2,1)S(1)}, u32[]{:S(2)}, u32[]{:S(2)}) collective-permute-start(bf16[512,256]{1,0:T(8,128)(2,1)S(1)} %get-tuple-element.26), channel_id=1, source_target_pairs={{0,3},{1,2},{2,1},{3,0},{4,7},{5,6},{6,5},{7,4},{8,11},{9,10},{10,... | collective-permute-start | bytes 786440 | tf_op jit(solution)/shard_map/ppermute | solution.py:19
  147.6 10.8 %collective-permute-start.17 = (bf16[512,256]{1,0:T(8,128)(2,1)S(1)}, bf16[512,256]{1,0:T(8,128)(2,1)S(1)}, u32[]{:S(2)}, u32[]{:S(2)}) collective-permute-start(bf16[512,256]{1,0:T(8,128)(2,1)S(1)} %get-tuple-element.27), channel_id=1, source_target_pairs={{0,1},{1,0},{2,3},{3,2},{4,5},{5,4},{6,7},{7,6},{8,9},{9,8},{10,11... | collective-permute-start | bytes 786440 | tf_op jit(solution)/shard_map/ppermute | solution.py:19
  149.8 13.2 %collective-permute-start.22 = (bf16[512,256]{1,0:T(8,128)(2,1)S(1)}, bf16[512,256]{1,0:T(8,128)(2,1)S(1)}, u32[]{:S(2)}, u32[]{:S(2)}) collective-permute-start(bf16[512,256]{1,0:T(8,128)(2,1)S(1)} %collective-permute-done.18.near_low), channel_id=1, source_target_pairs={{0,3},{1,2},{2,1},{3,0},{4,7},{5,6},{6,5},{7,4},{8,11},{9,10},{10,... | collective-permute-start | bytes 786440 | tf_op jit(solution)/shard_map/ppermute | solution.py:19
  152.9 10.1 %collective-permute-start.21 = (bf16[512,256]{1,0:T(8,128)(2,1)S(1)}, bf16[512,256]{1,0:T(8,128)(2,1)S(1)}, u32[]{:S(2)}, u32[]{:S(2)}) collective-permute-start(bf16[512,256]{1,0:T(8,128)(2,1)S(1)} %collective-permute-done.19.other_top), channel_id=1, source_target_pairs={{0,1},{1,0},{2,3},{3,2},{4,5},{5,4},{6,7},{7,6},{8,9},{9,8},{10,11... | collective-permute-start | bytes 786440 | tf_op jit(solution)/shard_map/ppermute | solution.py:19

commit v6 on v4

--- a/solution.py
+++ b/solution.py
@@ -185,15 +185,16 @@
     return [projected, below, above, other] + [core_pair(rows) for rows in chosen], sent
 
 
-def window_of_pairs(projected, fetch_own):
+def window_of_pairs(projected, fetch_own=None):
     below = shift(projected, 2)
     above = shift(projected, -2)
-    fetched = fetch_own(core_pair(projected))
-    above, fetched = lax.optimization_barrier((above, fetched))
+    own = core_pair(projected)
+    if fetch_own is not None:
+        above, own = lax.optimization_barrier((above, fetch_own(own)))
     first = lax.axis_index("region") % 2 == 0
     outer = core_pair(jnp.where(first, above, below))
     last = jnp.where(first, below, above)
-    return fetched, [outer, last]
+    return own, [outer, last]
 
 
 def place_in_exchanged(index, rows, me):
@@ -213,7 +214,7 @@
     if own:
         block = jnp.where(inside, apart, 2)
     else:
-        block = jnp.where(inside, 3, jnp.where(apart == 2, 0, jnp.where(apart == -1, 1, 2)))
+        block = jnp.where(inside, apart + 3, jnp.where(apart == 2, 0, jnp.where(apart == -1, 1, 2)))
     return (block << shift_by) + (index & (rows - 1))
 
 
@@ -341,11 +342,12 @@
     )(me, senders, window)
 
 
-def by_matmul_kernel(slots, block, sizes, me_ref, sender_ref, slot_ref, count_ref, receiver_ref, fetched_ref, *refs):
+def by_matmul_kernel(slots, block, sizes, ahead, me_ref, sender_ref, slot_ref, count_ref, receiver_ref, *refs):
+    fetched_ref, refs = (refs[0], refs[1:]) if ahead else (None, refs)
     parts, out_ref = refs[: len(sizes)], refs[len(sizes)]
     window, index_ref, weight_ref = refs[len(sizes) + 1 :]
     depth, rows = sum(sizes), sender_ref.shape[1]
-    index_ref[...] = upright(place_in_pairs(sender_ref[...], depth // 3, me_ref[0], False))
+    index_ref[...] = upright(place_in_pairs(sender_ref[...], depth // (3 if ahead else 5), me_ref[0], False))
     weight_ref[...] = upright(scaled(slot_ref[...], count_ref[...]))
     first = 0
     for part, size in zip(parts, sizes):
@@ -359,7 +361,9 @@
         index, weight = index_ref[at, :], weight_ref[at, :]
         acc = jnp.zeros(mine.shape, jnp.float32)
         for k in range(slots):
-            fetched = pick_rows(index[:, k : k + 1], columns, window) + fetched_ref[k, at, :].astype(jnp.float32)
+            fetched = pick_rows(index[:, k : k + 1], columns, window)
+            if ahead:
+                fetched += fetched_ref[k, at, :].astype(jnp.float32)
             h = (fetched + mine) * 0.5
             acc = acc + (h + h * jnp.tanh(h)) * weight[:, k : k + 1]
         for j in range(out_ref.shape[0]):
@@ -369,15 +373,16 @@
     lax.fori_loop(0, rows // block, one_block, 0)
 
 
-def aggregate_by_matmul(senders, weights, counts, receivers, projected, copies, block=256):
+def aggregate_by_matmul(senders, weights, counts, receivers, projected, copies, ahead, block=256):
     slots, (rows, width) = senders.shape[0], receivers.shape
     me = lax.axis_index("region").astype(jnp.int32)[None]
-    fetched, parts = window_of_pairs(projected, functools.partial(fetch_own, senders))
+    own, parts = window_of_pairs(projected, functools.partial(fetch_own, senders) if ahead else None)
+    before, parts = ([own], parts) if ahead else ([], parts + [own])
     sizes = tuple(part.shape[0] for part in parts)
     return pl.pallas_call(
-        functools.partial(by_matmul_kernel, slots, block, sizes),
+        functools.partial(by_matmul_kernel, slots, block, sizes, ahead),
         out_shape=jax.ShapeDtypeStruct((copies, rows, width), receivers.dtype),
-        in_specs=[SMEM] + [VMEM] * (5 + len(parts)),
+        in_specs=[SMEM] + [VMEM] * (4 + len(before) + len(parts)),
         out_specs=VMEM,
         scratch_shapes=[
             pltpu.VMEM((sum(sizes), width), jnp.bfloat16),
@@ -391,7 +396,7 @@
             transcendentals=slots * rows * width,
         ),
         name="aggregate_by_matmul",
-    )(me, senders, weights, counts[None, :], receivers, fetched, *parts)
+    )(me, senders, weights, counts[None, :], receivers, *before, *parts)
 
 
 def shards(
@@ -432,11 +437,11 @@
     mesh_one, projected, later = mesh_step(
         mesh_one_kernel, mesh_state, (bf16, bf16, f32), core[None], full, mesh_state, enc_out, mine, other, base
     )
-    agg = aggregate_by_matmul(m2m_index, m2m_weight, m2m_count, mesh_one, projected, n)
+    agg = aggregate_by_matmul(m2m_index, m2m_weight, m2m_count, mesh_one, projected, n, True)
     mesh_next, projected = mesh_step(
         mesh_next_kernel, mesh_state, (bf16, bf16), core[None], gather_chan(agg), mesh_one, proc_out, mine, other, later
     )
-    agg = aggregate_by_matmul(m2g_index, m2g_weight, m2g_count, grid_state, projected, 1)[0]
+    agg = aggregate_by_matmul(m2g_index, m2g_weight, m2g_count, grid_state, projected, 1, False)[0]
     grid_next, _ = project_by_exchanges(agg, dec_out, base=(grid_state,))
     return grid_next, mesh_next
 

time: 169 us -> 169 us (level)
  other arithmetic: 0.18 us -> 1.97 us
    ppermute x6, waiting for transfers between devices: 5.9 us -> 8.17 us  [shift(): lax.ppermute(shard, 'region', [(i, i + by) for i in range(n) if 0 <= i +...]
    pallas_call x2 -> x1, Pallas kernels: 3.1 us -> 0.86 us  [fetch_own(): pl.pallas_call(functools.partial(fetch_kernel, slots, block), out_shape=j...]
    ppermute x17, waiting for transfers between devices: 13.9 us -> 12.1 us  [exchange(): return lax.ppermute(shard, axis, [(i, partner(i)) for i in range(n)])]
    concatenate x1, other arithmetic: 0.04 us -> 1.84 us  [shards(): packed = jnp.concatenate(own_rows + [mesh_state], axis=0)]
  transfers between devices with their start and end apart: 23 -> 23, of which waited for: 9 -> 8; matrix products, arithmetic and copies ran while one was open for 1% -> 2% of each run, Pallas kernels for 7% -> 6%
where the time goes in v6:
time: 169 us; the launch traced here: 168 us
  starting transfers between devices  78.6 us (47%)
  blocking collectives  44 us (26%)
  waiting for transfers between devices  20.2 us (12%)
  Pallas kernels  19.7 us (12%)
  local copies, waits for them, and re-layouts  2.79 us (2%)
  other arithmetic  1.97 us (1%)
    ppermute x17, starting transfers between devices, exchange(): return lax.ppermute(shard, axis, [(i, partner(i)) for i in range(n)])  50.7 us
    ppermute x6, starting transfers between devices, shift(): lax.ppermute(shard, 'region', [(i, i + by) for i in range(n) if 0 <= i +...  27.9 us
    all_gather x1, blocking collectives, shards(): full = lax.all_gather(agg[0], 'chan', axis=0)  19 us
    all_to_all x1, blocking collectives, gather_chan(): lax.all_to_all(copies, 'chan', split_axis=0, concat_axis=0, tiled=True)  12.7 us
    all_gather x6, blocking collectives, core_pair(): lax.all_gather(shard, 'region', axis=0, tiled=True, axis_index_groups=gro...  12.3 us
    ppermute x17, waiting for transfers between devices, exchange(): return lax.ppermute(shard, axis, [(i, partner(i)) for i in range(n)])  12.1 us
    ppermute x6, waiting for transfers between devices, shift(): lax.ppermute(shard, 'region', [(i, i + by) for i in range(n) if 0 <= i +...  8.17 us
    pallas_call x1, Pallas kernels, aggregate_by_rows(): pl.pallas_call(functools.partial(by_rows_kernel, slots, rows, group, size...  7.34 us
  transfers between devices with their start and end apart: 23, of which 8 were waited for; matrix products, arithmetic and copies ran while one was open for 2% of the time, Pallas kernels for 6%

profile of v6, /device:TPU:248, one launch (start us, length us, event | category | flops | bytes accessed | tf_op | source)
XLA Modules:
  0.0 168.5 jit_solution(1328073338666576698)
XLA Ops:
  0.7 1.9 %fusion.6 = (bf16[512,256]{1,0:T(8,128)(2,1)}, bf16[512,256]{1,0:T(8,128)(2,1)}) fusion(bf16[1024,256]{1,0:T(8,128)(2,1)} %refs_0_.1), kind=kLoop, calls=%fused_computation.24 | loop fusion | bytes 1048576 | tf_op jit(solution)/shard_map/slice | solution.py:75
  2.6 3.4 %collective-permute-start.1 = (bf16[512,256]{1,0:T(8,128)(2,1)}, bf16[512,256]{1,0:T(8,128)(2,1)S(1)}, u32[]{:S(2)}, u32[]{:S(2)}) collective-permute-start(bf16[512,256]{1,0:T(8,128)(2,1)} %get-tuple-element.32), channel_id=1, source_target_pairs={{0,1},{1,0},{2,3},{3,2},{4,5},{5,4},{6,7},{7,6},{8,9},{9,8},{10,11... | collective-permute-start | bytes 786440 | tf_op jit(solution)/shard_map/ppermute | solution.py:19
  6.0 4.0 %collective-permute-start.2 = (bf16[512,256]{1,0:T(8,128)(2,1)}, bf16[512,256]{1,0:T(8,128)(2,1)S(1)}, u32[]{:S(2)}, u32[]{:S(2)}) collective-permute-start(bf16[512,256]{1,0:T(8,128)(2,1)} %get-tuple-element.33), channel_id=1, source_target_pairs={{0,3},{1,2},{2,1},{3,0},{4,7},{5,6},{6,5},{7,4},{8,11},{9,10},{10,... | collective-permute-start | bytes 786440 | tf_op jit(solution)/shard_map/ppermute | solution.py:19
  10.0 3.0 %collective-permute-start.3 = (bf16[512,256]{1,0:T(8,128)(2,1)}, bf16[512,256]{1,0:T(8,128)(2,1)S(1)}, u32[]{:S(2)}, u32[]{:S(2)}) collective-permute-start(bf16[512,256]{1,0:T(8,128)(2,1)} %get-tuple-element.32), channel_id=1, source_target_pairs={{0,3},{1,2},{2,1},{3,0},{4,7},{5,6},{6,5},{7,4},{8,11},{9,10},{10,... | collective-permute-start | bytes 786440 | tf_op jit(solution)/shard_map/ppermute | solution.py:19
  13.1 1.9 %collective-permute-start = (bf16[512,256]{1,0:T(8,128)(2,1)}, bf16[512,256]{1,0:T(8,128)(2,1)S(1)}, u32[]{:S(2)}, u32[]{:S(2)}) collective-permute-start(bf16[512,256]{1,0:T(8,128)(2,1)} %get-tuple-element.33), channel_id=1, source_target_pairs={{0,1},{1,0},{2,3},{3,2},{4,5},{5,4},{6,7},{7,6},{8,9},{9,8},{10,11... | collective-permute-start | bytes 786440 | tf_op jit(solution)/shard_map/ppermute | solution.py:19
  15.1 0.7 constant_dynamic-slice_fusion
  15.8 4.0 %collective-permute-start.5 = (bf16[512,256]{1,0:T(8,128)(2,1)S(1)}, bf16[512,256]{1,0:T(8,128)(2,1)S(1)}, u32[]{:S(2)}, u32[]{:S(2)}) collective-permute-start(bf16[512,256]{1,0:T(8,128)(2,1)S(1)} %collective-permute-done.1.near_low), channel_id=1, source_target_pairs={{0,3},{1,2},{2,1},{3,0},{4,7},{5,6},{6,5},{7,4},{8,11},{9,10},{10,... | collective-permute-start | bytes 786440 | tf_op jit(solution)/shard_map/ppermute | solution.py:19
  19.8 3.3 %collective-permute-start.4 = (bf16[512,256]{1,0:T(8,128)(2,1)S(1)}, bf16[512,256]{1,0:T(8,128)(2,1)S(1)}, u32[]{:S(2)}, u32[]{:S(2)}) collective-permute-start(bf16[512,256]{1,0:T(8,128)(2,1)S(1)} %collective-permute-done.2.other_top), channel_id=1, source_target_pairs={{0,1},{1,0},{2,3},{3,2},{4,5},{5,4},{6,7},{7,6},{8,9},{9,8},{10,11... | collective-permute-start | bytes 786440 | tf_op jit(solution)/shard_map/ppermute | solution.py:19
  23.1 1.8 %pad_maximum_fusion.own = bf16[1280,256]{1,0:T(8,128)(2,1)} fusion(bf16[256,256]{1,0:T(8,128)(2,1)S(1)} %copy-done.3, bf16[512,256]{1,0:T(8,128)(2,1)S(1)} %get-tuple-element.38, bf16[512,256]{1,0:T(8,128)(2,1)} %get-tuple-element.39), kind=kLoop, calls=%fused_computation | loop fusion | flops 1966080 | bytes 1310720 | tf_op jit(solution)/shard_map/concatenate | solution.py:426
  25.6 2.7 %collective-permute-done.5.far_low = bf16[512,256]{1,0:T(8,128)(2,1)S(1)} collective-permute-done((bf16[512,256]{1,0:T(8,128)(2,1)S(1)}, bf16[512,256]{1,0:T(8,128)(2,1)S(1)}, u32[]{:S(2)}, u32[]{:S(2)}) %collective-permute-start.5) | collective-permute-done | bytes 262176 | tf_op jit(solution)/shard_map/ppermute | solution.py:19
  28.9 1.9 %collective-permute-start.8 = (bf16[1024,256]{1,0:T(8,128)(2,1)S(1)}, bf16[1024,256]{1,0:T(8,128)(2,1)}, u32[]{:S(2)}, u32[]{:S(2)}) collective-permute-start(bf16[1024,256]{1,0:T(8,128)(2,1)S(1)} %last_block.2.refs_0_), channel_id=1, source_target_pairs={{0,4},{4,0},{8,12},{12,8},{16,20},{20,16},{24,28},{28,24},{32,36},... | collective-permute-start | bytes 1572872 | tf_op jit(solution)/shard_map/ppermute | solution.py:19
  30.8 3.3 %collective-permute-start.7 = (bf16[1024,256]{1,0:T(8,128)(2,1)S(1)}, bf16[1024,256]{1,0:T(8,128)(2,1)S(1)}, u32[]{:S(2)}, u32[]{:S(2)}) collective-permute-start(bf16[1024,256]{1,0:T(8,128)(2,1)S(1)} %last_block.2.refs_0_), channel_id=1, source_target_pairs={{8,0},{12,4},{16,8},{20,12},{24,16},{28,20},{32,24},{36,28},{40,32... | collective-permute-start | bytes 1572872 | tf_op jit(solution)/shard_map/ppermute | solution.py:24
  34.1 5.9 %collective-permute-start.6 = (bf16[1024,256]{1,0:T(8,128)(2,1)S(1)}, bf16[1024,256]{1,0:T(8,128)(2,1)S(1)}, u32[]{:S(2)}, u32[]{:S(2)}) collective-permute-start(bf16[1024,256]{1,0:T(8,128)(2,1)S(1)} %last_block.2.refs_0_), channel_id=1, source_target_pairs={{0,8},{4,12},{8,16},{12,20},{16,24},{20,28},{24,32},{28,36},{32,40... | collective-permute-start | bytes 1572872 | tf_op jit(solution)/shard_map/ppermute | solution.py:24
  40.1 3.6 %collective-permute-start.11 = (bf16[1280,256]{1,0:T(8,128)(2,1)}, bf16[1280,256]{1,0:T(8,128)(2,1)S(1)}, u32[]{:S(2)}, u32[]{:S(2)}) collective-permute-start(bf16[1280,256]{1,0:T(8,128)(2,1)} %pad_maximum_fusion.own), channel_id=1, source_target_pairs={{0,2},{1,3},{2,0},{3,1},{4,6},{5,7},{6,4},{7,5},{8,10},{9,11},{10,... | collective-permute-start | bytes 1966088 | tf_op jit(solution)/shard_map/ppermute | solution.py:19
  43.7 4.0 %collective-permute-start.10 = (bf16[1280,256]{1,0:T(8,128)(2,1)}, bf16[1280,256]{1,0:T(8,128)(2,1)S(1)}, u32[]{:S(2)}, u32[]{:S(2)}) collective-permute-start(bf16[1280,256]{1,0:T(8,128)(2,1)} %pad_maximum_fusion.own), channel_id=1, source_target_pairs={{0,3},{1,2},{2,1},{3,0},{4,7},{5,6},{6,5},{7,4},{8,11},{9,10},{10,... | collective-permute-start | bytes 1966088 | tf_op jit(solution)/shard_map/ppermute | solution.py:19
  47.7 1.9 %collective-permute-start.9 = (bf16[1280,256]{1,0:T(8,128)(2,1)}, bf16[1280,256]{1,0:T(8,128)(2,1)S(1)}, u32[]{:S(2)}, u32[]{:S(2)}) collective-permute-start(bf16[1280,256]{1,0:T(8,128)(2,1)} %pad_maximum_fusion.own), channel_id=1, source_target_pairs={{0,1},{1,0},{2,3},{3,2},{4,5},{5,4},{6,7},{7,6},{8,9},{9,8},{10,11... | collective-permute-start | bytes 1966088 | tf_op jit(solution)/shard_map/ppermute | solution.py:19
  49.7 0.7 collective-permute-done.7.refs_2_
  50.4 1.2 collective-permute-done.6.refs_1_
  51.6 2.2 %all_gather.22.refs_5_ = bf16[1024,256]{1,0:T(8,128)(2,1)S(1)} all-gather(bf16[512,256]{1,0:T(8,128)(2,1)S(1)} %get-tuple-element.28), channel_id=1, replica_groups={{0,4},{8,12},{16,20},{24,28},{32,36},{40,44},{48,52},{56,60},{64,68},{7..., dimensions={0}, use_global_device_ids=true | all-gather | bytes 786432 | tf_op jit(solution)/shard_map/all_gather | solution.py:30
  53.8 2.2 %all_gather.21.refs_4_ = bf16[1024,256]{1,0:T(8,128)(2,1)S(1)} all-gather(bf16[512,256]{1,0:T(8,128)(2,1)S(1)} %get-tuple-element.29), channel_id=1, replica_groups={{0,4},{8,12},{16,20},{24,28},{32,36},{40,44},{48,52},{56,60},{64,68},{7..., dimensions={0}, use_global_device_ids=true | all-gather | bytes 786432 | tf_op jit(solution)/shard_map/all_gather | solution.py:30
  56.0 7.3 %aggregate_by_rows.1 = bf16[1,256,256]{2,1,0:T(8,128)(2,1)S(1)} custom-call(s32[16,256]{1,0:T(8,128)S(1)} %fusion.4.index_ref, f32[16,256]{1,0:T(8,128)S(1)} %copy-done.7, s32[1,256]{1,0:T(1,128)S(1)} %bitcast.12, bf16[256,256]{1,0:T(8,128)(2,1)S(1)} %copy-done.3, bf16[1024,256]{1,0:T(8,128)(2,1)S(1)} %last_block.2.refs_0_, ...), custom_call_target="tpu_custom_call" | custom-call | flops 1 | bytes 1 | tf_op jit(solution)/shard_map/aggregate_by_rows/pallas_call | solution.py:287
  63.4 19.0 %all_gather.23._.full = bf16[4,256,256]{2,1,0:T(8,128)(2,1)S(1)} all-gather(bf16[1,256,256]{2,1,0:T(8,128)(2,1)S(1)} %aggregate_by_rows.1), channel_id=1, replica_groups=mesh['region'=128,'chan'=4] {'chan'}, dimensions={0}, use_global_device_ids=true | all-gather | bytes 655360 | tf_op jit(solution)/shard_map/all_gather | solution.py:434
  82.4 1.3 combine.1
  83.7 1.9 %collective-permute-start.12 = (bf16[1536,256]{1,0:T(8,128)(2,1)S(1)}, bf16[1536,256]{1,0:T(8,128)(2,1)S(1)}, u32[]{:S(2)}, u32[]{:S(2)}) collective-permute-start(bf16[1536,256]{1,0:T(8,128)(2,1)S(1)} %get-tuple-element.19.mine), channel_id=1, source_target_pairs={{0,4},{4,0},{8,12},{12,8},{16,20},{20,16},{24,28},{28,24},{32,36},... | collective-permute-start | bytes 2359304 | tf_op jit(solution)/shard_map/ppermute | solution.py:19
  85.6 2.3 %collective-permute-done.12.other = bf16[1536,256]{1,0:T(8,128)(2,1)S(1)} collective-permute-done((bf16[1536,256]{1,0:T(8,128)(2,1)S(1)}, bf16[1536,256]{1,0:T(8,128)(2,1)S(1)}, u32[]{:S(2)}, u32[]{:S(2)}) %collective-permute-start.12) | collective-permute-done | bytes 786464 | tf_op jit(solution)/shard_map/ppermute | solution.py:19
  88.4 1.9 %collective-permute-start.13 = (bf16[256,256]{1,0:T(8,128)(2,1)S(1)}, bf16[256,256]{1,0:T(8,128)(2,1)S(1)}, u32[]{:S(2)}, u32[]{:S(2)}) collective-permute-start(bf16[256,256]{1,0:T(8,128)(2,1)S(1)} %get-tuple-element.22), channel_id=1, source_target_pairs={{8,0},{12,4},{16,8},{20,12},{24,16},{28,20},{32,24},{36,28},{40,32... | collective-permute-start | bytes 393224 | tf_op jit(solution)/shard_map/ppermute | solution.py:24
  90.4 7.2 %collective-permute-start.14 = (bf16[256,256]{1,0:T(8,128)(2,1)S(1)}, bf16[256,256]{1,0:T(8,128)(2,1)S(1)}, u32[]{:S(2)}, u32[]{:S(2)}) collective-permute-start(bf16[256,256]{1,0:T(8,128)(2,1)S(1)} %get-tuple-element.22), channel_id=1, source_target_pairs={{0,8},{4,12},{8,16},{12,20},{16,24},{20,28},{24,32},{28,36},{32,40... | collective-permute-start | bytes 393224 | tf_op jit(solution)/shard_map/ppermute | solution.py:24
  97.6 2.0 %all_gather.24.window = bf16[512,256]{1,0:T(8,128)(2,1)S(1)} all-gather(bf16[256,256]{1,0:T(8,128)(2,1)S(1)} %get-tuple-element.22), channel_id=1, replica_groups={{0,4},{8,12},{16,20},{24,28},{32,36},{40,44},{48,52},{56,60},{64,68},{7..., dimensions={0}, use_global_device_ids=true | all-gather | bytes 393216 | tf_op jit(solution)/shard_map/all_gather | solution.py:30
  99.6 0.9 fetch_own.1.refs_0_
  100.6 2.0 %all_gather.25.refs_1_ = bf16[512,256]{1,0:T(8,128)(2,1)S(1)} all-gather(bf16[256,256]{1,0:T(8,128)(2,1)S(1)} %get-tuple-element.37), channel_id=1, replica_groups={{0,4},{8,12},{16,20},{24,28},{32,36},{40,44},{48,52},{56,60},{64,68},{7..., dimensions={0}, use_global_device_ids=true | all-gather | bytes 393216 | tf_op jit(solution)/shard_map/all_gather | solution.py:30
  102.6 1.6 aggregate_by_matmul.2
  104.1 12.7 %all_to_all.5.full = bf16[4,256,256]{2,1,0:T(8,128)(2,1)S(1)} all-to-all(bf16[4,256,256]{2,1,0:T(8,128)(2,1)S(1)} %aggregate_by_matmul.2), channel_id=1, replica_groups=mesh['region'=128,'chan'=4] {'chan'}, dimensions={0} | all-to-all | bytes 1048576 | tf_op jit(solution)/shard_map/all_to_all | solution.py:34
  116.8 1.1 mesh_step.3
  117.9 7.7 %collective-permute-start.16 = (bf16[256,256]{1,0:T(8,128)(2,1)S(1)}, bf16[256,256]{1,0:T(8,128)(2,1)S(1)}, u32[]{:S(2)}, u32[]{:S(2)}) collective-permute-start(bf16[256,256]{1,0:T(8,128)(2,1)S(1)} %get-tuple-element.26), channel_id=1, source_target_pairs={{0,8},{4,12},{8,16},{12,20},{16,24},{20,28},{24,32},{28,36},{32,40... | collective-permute-start | bytes 393224 | tf_op jit(solution)/shard_map/ppermute | solution.py:24
  125.6 1.9 %collective-permute-start.15 = (bf16[256,256]{1,0:T(8,128)(2,1)S(1)}, bf16[256,256]{1,0:T(8,128)(2,1)S(1)}, u32[]{:S(2)}, u32[]{:S(2)}) collective-permute-start(bf16[256,256]{1,0:T(8,128)(2,1)S(1)} %get-tuple-element.26), channel_id=1, source_target_pairs={{8,0},{12,4},{16,8},{20,12},{24,16},{28,20},{32,24},{36,28},{40,32... | collective-permute-start | bytes 393224 | tf_op jit(solution)/shard_map/ppermute | solution.py:24
  127.5 2.0 %all_gather.27.refs_2_ = bf16[512,256]{1,0:T(8,128)(2,1)S(1)} all-gather(bf16[256,256]{1,0:T(8,128)(2,1)S(1)} %get-tuple-element.26), channel_id=1, replica_groups={{0,4},{8,12},{16,20},{24,28},{32,36},{40,44},{48,52},{56,60},{64,68},{7..., dimensions={0}, use_global_device_ids=true | all-gather | bytes 393216 | tf_op jit(solution)/shard_map/all_gather | solution.py:30
  129.5 6.3 %collective-permute-done.15 = bf16[256,256]{1,0:T(8,128)(2,1)S(1)} collective-permute-done((bf16[256,256]{1,0:T(8,128)(2,1)S(1)}, bf16[256,256]{1,0:T(8,128)(2,1)S(1)}, u32[]{:S(2)}, u32[]{:S(2)}) %collective-permute-start.15) | collective-permute-done | bytes 131104 | tf_op jit(solution)/shard_map/ppermute | solution.py:24
  135.8 2.0 %all_gather.26.refs_0_ = bf16[512,256]{1,0:T(8,128)(2,1)S(1)} all-gather(bf16[256,256]{1,0:T(8,128)(2,1)S(1)} %get-tuple-element.35), channel_id=1, replica_groups={{0,4},{8,12},{16,20},{24,28},{32,36},{40,44},{48,52},{56,60},{64,68},{7..., dimensions={0}, use_global_device_ids=true | all-gather | bytes 393216 | tf_op jit(solution)/shard_map/all_gather | solution.py:30
  137.8 4.5 %aggregate_by_matmul.3 = bf16[1,1024,256]{2,1,0:T(8,128)(2,1)S(1)} custom-call(s32[1]{0:T(128)} %bitcast.1.me_ref, s32[4,1024]{1,0:T(4,128)S(1)} %copy-done.11, f32[4,1024]{1,0:T(4,128)S(1)} %copy-done.12, s32[1,1024]{1,0:T(1,128)S(1)} %bitcast.13, bf16[1024,256]{1,0:T(8,128)(2,1)S(1)} %copy-done, bf16[512,256]{1,0:T(8,128)(2,1)S(1)} %all_gather.26.refs_0_, ...), custom_call_target="tpu_custom_call" | custom-call | flops 2684354560 | bytes 1703936 | tf_op jit(solution)/shard_map/aggregate_by_matmul/pallas_call | solution.py:382
  142.3 2.6 %collective-permute-start.18 = (bf16[512,256]{1,0:T(8,128)(2,1)S(1)}, bf16[512,256]{1,0:T(8,128)(2,1)S(1)}, u32[]{:S(2)}, u32[]{:S(2)}) collective-permute-start(bf16[512,256]{1,0:T(8,128)(2,1)S(1)} %get-tuple-element.30), channel_id=1, source_target_pairs={{0,1},{1,0},{2,3},{3,2},{4,5},{5,4},{6,7},{7,6},{8,9},{9,8},{10,11... | collective-permute-start | bytes 786440 | tf_op jit(solution)/shard_map/ppermute | solution.py:19
  144.9 2.7 %collective-permute-start.19 = (bf16[512,256]{1,0:T(8,128)(2,1)S(1)}, bf16[512,256]{1,0:T(8,128)(2,1)S(1)}, u32[]{:S(2)}, u32[]{:S(2)}) collective-permute-start(bf16[512,256]{1,0:T(8,128)(2,1)S(1)} %get-tuple-element.31), channel_id=1, source_target_pairs={{0,3},{1,2},{2,1},{3,0},{4,7},{5,6},{6,5},{7,4},{8,11},{9,10},{10,... | collective-permute-start | bytes 786440 | tf_op jit(solution)/shard_map/ppermute | solution.py:19
  147.7 4.3 %collective-permute-start.20 = (bf16[512,256]{1,0:T(8,128)(2,1)S(1)}, bf16[512,256]{1,0:T(8,128)(2,1)S(1)}, u32[]{:S(2)}, u32[]{:S(2)}) collective-permute-start(bf16[512,256]{1,0:T(8,128)(2,1)S(1)} %get-tuple-element.30), channel_id=1, source_target_pairs={{0,3},{1,2},{2,1},{3,0},{4,7},{5,6},{6,5},{7,4},{8,11},{9,10},{10,... | collective-permute-start | bytes 786440 | tf_op jit(solution)/shard_map/ppermute | solution.py:19
  152.0 2.2 %collective-permute-start.17 = (bf16[512,256]{1,0:T(8,128)(2,1)S(1)}, bf16[512,256]{1,0:T(8,128)(2,1)S(1)}, u32[]{:S(2)}, u32[]{:S(2)}) collective-permute-start(bf16[512,256]{1,0:T(8,128)(2,1)S(1)} %get-tuple-element.31), channel_id=1, source_target_pairs={{0,1},{1,0},{2,3},{3,2},{4,5},{5,4},{6,7},{7,6},{8,9},{9,8},{10,11... | collective-permute-start | bytes 786440 | tf_op jit(solution)/shard_map/ppermute | solution.py:19
  154.2 3.1 %collective-permute-start.22 = (bf16[512,256]{1,0:T(8,128)(2,1)S(1)}, bf16[512,256]{1,0:T(8,128)(2,1)S(1)}, u32[]{:S(2)}, u32[]{:S(2)}) collective-permute-start(bf16[512,256]{1,0:T(8,128)(2,1)S(1)} %collective-permute-done.18.near_low), channel_id=1, source_target_pairs={{0,3},{1,2},{2,1},{3,0},{4,7},{5,6},{6,5},{7,4},{8,11},{9,10},{10,... | collective-permute-start | bytes 786440 | tf_op jit(solution)/shard_map/ppermute | solution.py:19
  157.3 2.7 %collective-permute-start.21 = (bf16[512,256]{1,0:T(8,128)(2,1)S(1)}, bf16[512,256]{1,0:T(8,128)(2,1)S(1)}, u32[]{:S(2)}, u32[]{:S(2)}) collective-permute-start(bf16[512,256]{1,0:T(8,128)(2,1)S(1)} %collective-permute-done.19.other_top), channel_id=1, source_target_pairs={{0,1},{1,0},{2,3},{3,2},{4,5},{5,4},{6,7},{7,6},{8,9},{9,8},{10,11... | collective-permute-start | bytes 786440 | tf_op jit(solution)/shard_map/ppermute | solution.py:19
  160.0 2.8 %collective-permute-done.20.other_low = bf16[512,256]{1,0:T(8,128)(2,1)S(1)} collective-permute-done((bf16[512,256]{1,0:T(8,128)(2,1)S(1)}, bf16[512,256]{1,0:T(8,128)(2,1)S(1)}, u32[]{:S(2)}, u32[]{:S(2)}) %collective-permute-start.20) | collective-permute-done | bytes 262176 | tf_op jit(solution)/shard_map/ppermute | solution.py:19
  163.4 3.9 %collective-permute-done.22.far_low = bf16[512,256]{1,0:T(8,128)(2,1)S(1)} collective-permute-done((bf16[512,256]{1,0:T(8,128)(2,1)S(1)}, bf16[512,256]{1,0:T(8,128)(2,1)S(1)}, u32[]{:S(2)}, u32[]{:S(2)}) %collective-permute-start.22) | collective-permute-done | bytes 262176 | tf_op jit(solution)/shard_map/ppermute | solution.py:19
  167.4 1.1 last_block.3
  (61 shorter events, 2.6 us)
Async XLA Ops:
  0.6 14.4 %copy-start.4 = (bf16[1024,256]{1,0:T(8,128)(2,1)S(1)}, bf16[1024,256]{1,0:T(8,128)(2,1)}, u32[]{:S(2)}) copy-start(bf16[1024,256]{1,0:T(8,128)(2,1)} %w_out.3) | copy-start | bytes 1572868
  0.6 14.4 %copy-start.5 = (bf16[1024,256]{1,0:T(8,128)(2,1)S(1)}, bf16[1024,256]{1,0:T(8,128)(2,1)}, u32[]{:S(2)}) copy-start(bf16[1024,256]{1,0:T(8,128)(2,1)} %w_out.2) | copy-start | bytes 1572868
  0.7 22.5 %copy-start.3 = (bf16[256,256]{1,0:T(8,128)(2,1)S(1)}, bf16[256,256]{1,0:T(8,128)(2,1)}, u32[]{:S(2)}) copy-start(bf16[256,256]{1,0:T(8,128)(2,1)} %mesh.1) | copy-start | bytes 393220
  2.6 13.2 %collective-permute-start.1 = (bf16[512,256]{1,0:T(8,128)(2,1)}, bf16[512,256]{1,0:T(8,128)(2,1)S(1)}, u32[]{:S(2)}, u32[]{:S(2)}) collective-permute-start(bf16[512,256]{1,0:T(8,128)(2,1)} %get-tuple-element.32), channel_id=1, source_target_pairs={{0,1},{1,0},{2,3},{3,2},{4,5},{5,4},{6,7},{7,6},{8,9},{9,8},{10,11... | collective-permute-start | bytes 786440 | tf_op jit(solution)/shard_map/ppermute | solution.py:19
  6.0 13.8 %collective-permute-start.2 = (bf16[512,256]{1,0:T(8,128)(2,1)}, bf16[512,256]{1,0:T(8,128)(2,1)S(1)}, u32[]{:S(2)}, u32[]{:S(2)}) collective-permute-start(bf16[512,256]{1,0:T(8,128)(2,1)} %get-tuple-element.33), channel_id=1, source_target_pairs={{0,3},{1,2},{2,1},{3,0},{4,7},{5,6},{6,5},{7,4},{8,11},{9,10},{10,... | collective-permute-start | bytes 786440 | tf_op jit(solution)/shard_map/ppermute | solution.py:19
  10.0 15.0 %collective-permute-start.3 = (bf16[512,256]{1,0:T(8,128)(2,1)}, bf16[512,256]{1,0:T(8,128)(2,1)S(1)}, u32[]{:S(2)}, u32[]{:S(2)}) collective-permute-start(bf16[512,256]{1,0:T(8,128)(2,1)} %get-tuple-element.32), channel_id=1, source_target_pairs={{0,3},{1,2},{2,1},{3,0},{4,7},{5,6},{6,5},{7,4},{8,11},{9,10},{10,... | collective-permute-start | bytes 786440 | tf_op jit(solution)/shard_map/ppermute | solution.py:19
  13.1 11.9 %collective-permute-start = (bf16[512,256]{1,0:T(8,128)(2,1)}, bf16[512,256]{1,0:T(8,128)(2,1)S(1)}, u32[]{:S(2)}, u32[]{:S(2)}) collective-permute-start(bf16[512,256]{1,0:T(8,128)(2,1)} %get-tuple-element.33), channel_id=1, source_target_pairs={{0,1},{1,0},{2,3},{3,2},{4,5},{5,4},{6,7},{7,6},{8,9},{9,8},{10,11... | collective-permute-start | bytes 786440 | tf_op jit(solution)/shard_map/ppermute | solution.py:19
  15.0 10.0 %copy-start = (bf16[1024,256]{1,0:T(8,128)(2,1)S(1)}, bf16[1024,256]{1,0:T(8,128)(2,1)}, u32[]{:S(2)}) copy-start(bf16[1024,256]{1,0:T(8,128)(2,1)} %refs_0_.1) | copy-start | bytes 1572868
  15.0 10.0 %copy-start.1 = (bf16[1024,256]{1,0:T(8,128)(2,1)S(1)}, bf16[1024,256]{1,0:T(8,128)(2,1)}, u32[]{:S(2)}) copy-start(bf16[1024,256]{1,0:T(8,128)(2,1)} %weight.5) | copy-start | bytes 1572868
  15.8 12.5 %collective-permute-start.5 = (bf16[512,256]{1,0:T(8,128)(2,1)S(1)}, bf16[512,256]{1,0:T(8,128)(2,1)S(1)}, u32[]{:S(2)}, u32[]{:S(2)}) collective-permute-start(bf16[512,256]{1,0:T(8,128)(2,1)S(1)} %collective-permute-done.1.near_low), channel_id=1, source_target_pairs={{0,3},{1,2},{2,1},{3,0},{4,7},{5,6},{6,5},{7,4},{8,11},{9,10},{10,... | collective-permute-start | bytes 786440 | tf_op jit(solution)/shard_map/ppermute | solution.py:19
  19.8 8.8 %collective-permute-start.4 = (bf16[512,256]{1,0:T(8,128)(2,1)S(1)}, bf16[512,256]{1,0:T(8,128)(2,1)S(1)}, u32[]{:S(2)}, u32[]{:S(2)}) collective-permute-start(bf16[512,256]{1,0:T(8,128)(2,1)S(1)} %collective-permute-done.2.other_top), channel_id=1, source_target_pairs={{0,1},{1,0},{2,3},{3,2},{4,5},{5,4},{6,7},{7,6},{8,9},{9,8},{10,11... | collective-permute-start | bytes 786440 | tf_op jit(solution)/shard_map/ppermute | solution.py:19
  25.6 14.5 %copy-start.17 = (s32[16,256]{1,0:T(8,128)S(1)}, s32[16,256]{1,0:T(8,128)}, u32[]{:S(2)}) copy-start(s32[16,256]{1,0:T(8,128)} %param.25) | copy-start | bytes 49156
  28.9 14.8 %collective-permute-start.8 = (bf16[1024,256]{1,0:T(8,128)(2,1)S(1)}, bf16[1024,256]{1,0:T(8,128)(2,1)}, u32[]{:S(2)}, u32[]{:S(2)}) collective-permute-start(bf16[1024,256]{1,0:T(8,128)(2,1)S(1)} %last_block.2.refs_0_), channel_id=1, source_target_pairs={{0,4},{4,0},{8,12},{12,8},{16,20},{20,16},{24,28},{28,24},{32,36},... | collective-permute-start | bytes 1572872 | tf_op jit(solution)/shard_map/ppermute | solution.py:19
  30.8 19.5 %collective-permute-start.7 = (bf16[1024,256]{1,0:T(8,128)(2,1)S(1)}, bf16[1024,256]{1,0:T(8,128)(2,1)S(1)}, u32[]{:S(2)}, u32[]{:S(2)}) collective-permute-start(bf16[1024,256]{1,0:T(8,128)(2,1)S(1)} %last_block.2.refs_0_), channel_id=1, source_target_pairs={{8,0},{12,4},{16,8},{20,12},{24,16},{28,20},{32,24},{36,28},{40,32... | collective-permute-start | bytes 1572872 | tf_op jit(solution)/shard_map/ppermute | solution.py:24
  34.1 17.5 %collective-permute-start.6 = (bf16[1024,256]{1,0:T(8,128)(2,1)S(1)}, bf16[1024,256]{1,0:T(8,128)(2,1)S(1)}, u32[]{:S(2)}, u32[]{:S(2)}) collective-permute-start(bf16[1024,256]{1,0:T(8,128)(2,1)S(1)} %last_block.2.refs_0_), channel_id=1, source_target_pairs={{0,8},{4,12},{8,16},{12,20},{16,24},{20,28},{24,32},{28,36},{32,40... | collective-permute-start | bytes 1572872 | tf_op jit(solution)/shard_map/ppermute | solution.py:24
  40.1 42.3 %collective-permute-start.11 = (bf16[1280,256]{1,0:T(8,128)(2,1)}, bf16[1280,256]{1,0:T(8,128)(2,1)S(1)}, u32[]{:S(2)}, u32[]{:S(2)}) collective-permute-start(bf16[1280,256]{1,0:T(8,128)(2,1)} %pad_maximum_fusion.own), channel_id=1, source_target_pairs={{0,2},{1,3},{2,0},{3,1},{4,6},{5,7},{6,4},{7,5},{8,10},{9,11},{10,... | collective-permute-start | bytes 1966088 | tf_op jit(solution)/shard_map/ppermute | solution.py:19
  43.7 38.7 %collective-permute-start.10 = (bf16[1280,256]{1,0:T(8,128)(2,1)}, bf16[1280,256]{1,0:T(8,128)(2,1)S(1)}, u32[]{:S(2)}, u32[]{:S(2)}) collective-permute-start(bf16[1280,256]{1,0:T(8,128)(2,1)} %pad_maximum_fusion.own), channel_id=1, source_target_pairs={{0,3},{1,2},{2,1},{3,0},{4,7},{5,6},{6,5},{7,4},{8,11},{9,10},{10,... | collective-permute-start | bytes 1966088 | tf_op jit(solution)/shard_map/ppermute | solution.py:19
  47.7 34.7 %collective-permute-start.9 = (bf16[1280,256]{1,0:T(8,128)(2,1)}, bf16[1280,256]{1,0:T(8,128)(2,1)S(1)}, u32[]{:S(2)}, u32[]{:S(2)}) collective-permute-start(bf16[1280,256]{1,0:T(8,128)(2,1)} %pad_maximum_fusion.own), channel_id=1, source_target_pairs={{0,1},{1,0},{2,3},{3,2},{4,5},{5,4},{6,7},{7,6},{8,9},{9,8},{10,11... | collective-permute-start | bytes 1966088 | tf_op jit(solution)/shard_map/ppermute | solution.py:19
  51.6 4.4 %copy-start.7 = (f32[16,256]{1,0:T(8,128)S(1)}, f32[16,256]{1,0:T(8,128)}, u32[]{:S(2)}) copy-start(f32[16,256]{1,0:T(8,128)} %slot_ref.3) | copy-start | bytes 49156
  51.6 4.4 %copy-start.8 = (s32[256]{0:T(256)S(1)}, s32[256]{0:T(256)}, u32[]{:S(2)}) copy-start(s32[256]{0:T(256)} %param.27) | copy-start | bytes 3076
  56.0 26.4 %copy-start.6 = (bf16[1280,256]{1,0:T(8,128)(2,1)S(1)}, bf16[1280,256]{1,0:T(8,128)(2,1)}, u32[]{:S(2)}) copy-start(bf16[1280,256]{1,0:T(8,128)(2,1)} %pad_maximum_fusion.own) | copy-start | bytes 1966084
  56.0 26.4 %copy-start.9 = (bf16[1024,256]{1,0:T(8,128)(2,1)S(1)}, bf16[1024,256]{1,0:T(8,128)(2,1)}, u32[]{:S(2)}) copy-start(bf16[1024,256]{1,0:T(8,128)(2,1)} %first.1) | copy-start | bytes 1572868
  56.0 26.4 %copy-start.10 = (bf16[1024,256]{1,0:T(8,128)(2,1)S(1)}, bf16[1024,256]{1,0:T(8,128)(2,1)}, u32[]{:S(2)}) copy-start(bf16[1024,256]{1,0:T(8,128)(2,1)} %second.1) | copy-start | bytes 1572868
  83.7 4.2 %collective-permute-start.12 = (bf16[1536,256]{1,0:T(8,128)(2,1)S(1)}, bf16[1536,256]{1,0:T(8,128)(2,1)S(1)}, u32[]{:S(2)}, u32[]{:S(2)}) collective-permute-start(bf16[1536,256]{1,0:T(8,128)(2,1)S(1)} %get-tuple-element.19.mine), channel_id=1, source_target_pairs={{0,4},{4,0},{8,12},{12,8},{16,20},{20,16},{24,28},{28,24},{32,36},... | collective-permute-start | bytes 2359304 | tf_op jit(solution)/shard_map/ppermute | solution.py:19
  87.9 11.8 %copy-start.13 = (s32[8,256]{1,0:T(8,128)S(1)}, s32[8,256]{1,0:T(8,128)}, u32[]{:S(2)}) copy-start(s32[8,256]{1,0:T(8,128)} %sender_ref.4) | copy-start | bytes 24580
  88.4 12.1 %collective-permute-start.13 = (bf16[256,256]{1,0:T(8,128)(2,1)S(1)}, bf16[256,256]{1,0:T(8,128)(2,1)S(1)}, u32[]{:S(2)}, u32[]{:S(2)}) collective-permute-start(bf16[256,256]{1,0:T(8,128)(2,1)S(1)} %get-tuple-element.22), channel_id=1, source_target_pairs={{8,0},{12,4},{16,8},{20,12},{24,16},{28,20},{32,24},{36,28},{40,32... | collective-permute-start | bytes 393224 | tf_op jit(solution)/shard_map/ppermute | solution.py:24
  90.4 10.1 %collective-permute-start.14 = (bf16[256,256]{1,0:T(8,128)(2,1)S(1)}, bf16[256,256]{1,0:T(8,128)(2,1)S(1)}, u32[]{:S(2)}, u32[]{:S(2)}) collective-permute-start(bf16[256,256]{1,0:T(8,128)(2,1)S(1)} %get-tuple-element.22), channel_id=1, source_target_pairs={{0,8},{4,12},{8,16},{12,20},{16,24},{20,28},{24,32},{28,36},{32,40... | collective-permute-start | bytes 393224 | tf_op jit(solution)/shard_map/ppermute | solution.py:24
  99.6 2.9 %copy-start.14 = (f32[8,256]{1,0:T(8,128)S(1)}, f32[8,256]{1,0:T(8,128)}, u32[]{:S(2)}) copy-start(f32[8,256]{1,0:T(8,128)} %slot_ref.4) | copy-start | bytes 24580
  99.6 2.9 %copy-start.16 = (s32[256]{0:T(256)S(1)}, s32[256]{0:T(256)}, u32[]{:S(2)}) copy-start(s32[256]{0:T(256)} %param.30) | copy-start | bytes 3076
  117.9 19.9 %copy-start.11 = (s32[4,1024]{1,0:T(4,128)S(1)}, s32[4,1024]{1,0:T(4,128)}, u32[]{:S(2)}) copy-start(s32[4,1024]{1,0:T(4,128)} %sender_ref.5) | copy-start | bytes 49156
  117.9 19.9 %copy-start.12 = (f32[4,1024]{1,0:T(4,128)S(1)}, f32[4,1024]{1,0:T(4,128)}, u32[]{:S(2)}) copy-start(f32[4,1024]{1,0:T(4,128)} %slot_ref.5) | copy-start | bytes 49156
  117.9 19.9 %copy-start.15 = (s32[1024]{0:T(1024)S(1)}, s32[1024]{0:T(1024)}, u32[]{:S(2)}) copy-start(s32[1024]{0:T(1024)} %param.33) | copy-start | bytes 12292
  117.9 11.6 %collective-permute-start.16 = (bf16[256,256]{1,0:T(8,128)(2,1)S(1)}, bf16[256,256]{1,0:T(8,128)(2,1)S(1)}, u32[]{:S(2)}, u32[]{:S(2)}) collective-permute-start(bf16[256,256]{1,0:T(8,128)(2,1)S(1)} %get-tuple-element.26), channel_id=1, source_target_pairs={{0,8},{4,12},{8,16},{12,20},{16,24},{20,28},{24,32},{28,36},{32,40... | collective-permute-start | bytes 393224 | tf_op jit(solution)/shard_map/ppermute | solution.py:24
  125.6 10.2 %collective-permute-start.15 = (bf16[256,256]{1,0:T(8,128)(2,1)S(1)}, bf16[256,256]{1,0:T(8,128)(2,1)S(1)}, u32[]{:S(2)}, u32[]{:S(2)}) collective-permute-start(bf16[256,256]{1,0:T(8,128)(2,1)S(1)} %get-tuple-element.26), channel_id=1, source_target_pairs={{8,0},{12,4},{16,8},{20,12},{24,16},{28,20},{32,24},{36,28},{40,32... | collective-permute-start | bytes 393224 | tf_op jit(solution)/shard_map/ppermute | solution.py:24
  142.3 20.6 %copy-start.2 = (bf16[1024,256]{1,0:T(8,128)(2,1)S(1)}, bf16[1024,256]{1,0:T(8,128)(2,1)}, u32[]{:S(2)}) copy-start(bf16[1024,256]{1,0:T(8,128)(2,1)} %weight.7) | copy-start | bytes 1572868
  142.3 11.9 %collective-permute-start.18 = (bf16[512,256]{1,0:T(8,128)(2,1)S(1)}, bf16[512,256]{1,0:T(8,128)(2,1)S(1)}, u32[]{:S(2)}, u32[]{:S(2)}) collective-permute-start(bf16[512,256]{1,0:T(8,128)(2,1)S(1)} %get-tuple-element.30), channel_id=1, source_target_pairs={{0,1},{1,0},{2,3},{3,2},{4,5},{5,4},{6,7},{7,6},{8,9},{9,8},{10,11... | collective-permute-start | bytes 786440 | tf_op jit(solution)/shard_map/ppermute | solution.py:19
  144.9 12.3 %collective-permute-start.19 = (bf16[512,256]{1,0:T(8,128)(2,1)S(1)}, bf16[512,256]{1,0:T(8,128)(2,1)S(1)}, u32[]{:S(2)}, u32[]{:S(2)}) collective-permute-start(bf16[512,256]{1,0:T(8,128)(2,1)S(1)} %get-tuple-element.31), channel_id=1, source_target_pairs={{0,3},{1,2},{2,1},{3,0},{4,7},{5,6},{6,5},{7,4},{8,11},{9,10},{10,... | collective-permute-start | bytes 786440 | tf_op jit(solution)/shard_map/ppermute | solution.py:19
  147.7 15.2 %collective-permute-start.20 = (bf16[512,256]{1,0:T(8,128)(2,1)S(1)}, bf16[512,256]{1,0:T(8,128)(2,1)S(1)}, u32[]{:S(2)}, u32[]{:S(2)}) collective-permute-start(bf16[512,256]{1,0:T(8,128)(2,1)S(1)} %get-tuple-element.30), channel_id=1, source_target_pairs={{0,3},{1,2},{2,1},{3,0},{4,7},{5,6},{6,5},{7,4},{8,11},{9,10},{10,... | collective-permute-start | bytes 786440 | tf_op jit(solution)/shard_map/ppermute | solution.py:19
  152.0 10.8 %collective-permute-start.17 = (bf16[512,256]{1,0:T(8,128)(2,1)S(1)}, bf16[512,256]{1,0:T(8,128)(2,1)S(1)}, u32[]{:S(2)}, u32[]{:S(2)}) collective-permute-start(bf16[512,256]{1,0:T(8,128)(2,1)S(1)} %get-tuple-element.31), channel_id=1, source_target_pairs={{0,1},{1,0},{2,3},{3,2},{4,5},{5,4},{6,7},{7,6},{8,9},{9,8},{10,11... | collective-permute-start | bytes 786440 | tf_op jit(solution)/shard_map/ppermute | solution.py:19
  154.2 13.2 %collective-permute-start.22 = (bf16[512,256]{1,0:T(8,128)(2,1)S(1)}, bf16[512,256]{1,0:T(8,128)(2,1)S(1)}, u32[]{:S(2)}, u32[]{:S(2)}) collective-permute-start(bf16[512,256]{1,0:T(8,128)(2,1)S(1)} %collective-permute-done.18.near_low), channel_id=1, source_target_pairs={{0,3},{1,2},{2,1},{3,0},{4,7},{5,6},{6,5},{7,4},{8,11},{9,10},{10,... | collective-permute-start | bytes 786440 | tf_op jit(solution)/shard_map/ppermute | solution.py:19
  157.3 10.1 %collective-permute-start.21 = (bf16[512,256]{1,0:T(8,128)(2,1)S(1)}, bf16[512,256]{1,0:T(8,128)(2,1)S(1)}, u32[]{:S(2)}, u32[]{:S(2)}) collective-permute-start(bf16[512,256]{1,0:T(8,128)(2,1)S(1)} %collective-permute-done.19.other_top), channel_id=1, source_target_pairs={{0,1},{1,0},{2,3},{3,2},{4,5},{5,4},{6,7},{7,6},{8,9},{9,8},{10,11... | collective-permute-start | bytes 786440 | tf_op jit(solution)/shard_map/ppermute | solution.py:19

commit v7 on v5

--- a/solution.py
+++ b/solution.py
@@ -392,7 +392,7 @@
     mesh_next, projected = mesh_step(
         mesh_next_kernel, mesh_state, (bf16, bf16), core[None], gather_chan(agg), mesh_one, proc_out, mine, other, later
     )
-    agg = aggregate_by_matmul(m2g_index, m2g_weight, m2g_count, grid_state, window_of_pairs(projected), 1)[0]
+    agg = aggregate_by_matmul(m2g_index, m2g_weight, m2g_count, grid_state, window_of_pairs(projected), 1, block=512)[0]
     grid_next, _ = project_by_exchanges(agg, dec_out, base=(grid_state,))
     return grid_next, mesh_next
 

time: 165 us -> 165 us (level)
  no operation moved by 1% of the time
where the time goes in v7:
time: 165 us; the launch traced here: 164 us
  starting transfers between devices  71.8 us (44%)
  blocking collectives  44 us (27%)
  waiting for transfers between devices  23.1 us (14%)
  Pallas kernels  19.2 us (12%)
  local copies, waits for them, and re-layouts  2.8 us (2%)
  other arithmetic  1.97 us (1%)
    ppermute x17, starting transfers between devices, exchange(): return lax.ppermute(shard, axis, [(i, partner(i)) for i in range(n)])  50.7 us
    ppermute x6, starting transfers between devices, shift(): lax.ppermute(shard, 'region', [(i, i + by) for i in range(n) if 0 <= i +...  21.1 us
    all_gather x1, blocking collectives, shards(): full = lax.all_gather(agg[0], 'chan', axis=0)  19 us
    all_to_all x1, blocking collectives, gather_chan(): lax.all_to_all(copies, 'chan', split_axis=0, concat_axis=0, tiled=True)  12.6 us
    all_gather x6, blocking collectives, core_pair(): lax.all_gather(shard, 'region', axis=0, tiled=True, axis_index_groups=gro...  12.3 us
    ppermute x17, waiting for transfers between devices, exchange(): return lax.ppermute(shard, axis, [(i, partner(i)) for i in range(n)])  12.1 us
    ppermute x6, waiting for transfers between devices, shift(): lax.ppermute(shard, 'region', [(i, i + by) for i in range(n) if 0 <= i +...  11 us
    pallas_call x1, Pallas kernels, aggregate_by_rows(): pl.pallas_call(functools.partial(by_rows_kernel, slots, rows, group, size...  7.34 us
  transfers between devices with their start and end apart: 23, of which 9 were waited for; matrix products, arithmetic and copies ran while one was open for 2% of the time, Pallas kernels for 5%

profile of v7, /device:TPU:248, one launch (start us, length us, event | category | flops | bytes accessed | tf_op | source)
XLA Modules:
  0.0 163.9 jit_solution(9931060803698863286)
XLA Ops:
  0.7 1.9 %fusion.6 = (bf16[512,256]{1,0:T(8,128)(2,1)}, bf16[512,256]{1,0:T(8,128)(2,1)}) fusion(bf16[1024,256]{1,0:T(8,128)(2,1)} %refs_0_.1), kind=kLoop, calls=%fused_computation.24 | loop fusion | bytes 1048576 | tf_op jit(solution)/shard_map/slice | solution.py:75
  2.6 3.4 %collective-permute-start.1 = (bf16[512,256]{1,0:T(8,128)(2,1)}, bf16[512,256]{1,0:T(8,128)(2,1)S(1)}, u32[]{:S(2)}, u32[]{:S(2)}) collective-permute-start(bf16[512,256]{1,0:T(8,128)(2,1)} %get-tuple-element.28), channel_id=1, source_target_pairs={{0,1},{1,0},{2,3},{3,2},{4,5},{5,4},{6,7},{7,6},{8,9},{9,8},{10,11... | collective-permute-start | bytes 786440 | tf_op jit(solution)/shard_map/ppermute | solution.py:19
  6.0 4.0 %collective-permute-start.2 = (bf16[512,256]{1,0:T(8,128)(2,1)}, bf16[512,256]{1,0:T(8,128)(2,1)S(1)}, u32[]{:S(2)}, u32[]{:S(2)}) collective-permute-start(bf16[512,256]{1,0:T(8,128)(2,1)} %get-tuple-element.29), channel_id=1, source_target_pairs={{0,3},{1,2},{2,1},{3,0},{4,7},{5,6},{6,5},{7,4},{8,11},{9,10},{10,... | collective-permute-start | bytes 786440 | tf_op jit(solution)/shard_map/ppermute | solution.py:19
  10.0 3.0 %collective-permute-start.3 = (bf16[512,256]{1,0:T(8,128)(2,1)}, bf16[512,256]{1,0:T(8,128)(2,1)S(1)}, u32[]{:S(2)}, u32[]{:S(2)}) collective-permute-start(bf16[512,256]{1,0:T(8,128)(2,1)} %get-tuple-element.28), channel_id=1, source_target_pairs={{0,3},{1,2},{2,1},{3,0},{4,7},{5,6},{6,5},{7,4},{8,11},{9,10},{10,... | collective-permute-start | bytes 786440 | tf_op jit(solution)/shard_map/ppermute | solution.py:19
  13.1 1.9 %collective-permute-start = (bf16[512,256]{1,0:T(8,128)(2,1)}, bf16[512,256]{1,0:T(8,128)(2,1)S(1)}, u32[]{:S(2)}, u32[]{:S(2)}) collective-permute-start(bf16[512,256]{1,0:T(8,128)(2,1)} %get-tuple-element.29), channel_id=1, source_target_pairs={{0,1},{1,0},{2,3},{3,2},{4,5},{5,4},{6,7},{7,6},{8,9},{9,8},{10,11... | collective-permute-start | bytes 786440 | tf_op jit(solution)/shard_map/ppermute | solution.py:19
  15.1 0.7 constant_dynamic-slice_fusion
  15.8 4.0 %collective-permute-start.5 = (bf16[512,256]{1,0:T(8,128)(2,1)S(1)}, bf16[512,256]{1,0:T(8,128)(2,1)S(1)}, u32[]{:S(2)}, u32[]{:S(2)}) collective-permute-start(bf16[512,256]{1,0:T(8,128)(2,1)S(1)} %collective-permute-done.1.near_low), channel_id=1, source_target_pairs={{0,3},{1,2},{2,1},{3,0},{4,7},{5,6},{6,5},{7,4},{8,11},{9,10},{10,... | collective-permute-start | bytes 786440 | tf_op jit(solution)/shard_map/ppermute | solution.py:19
  19.8 3.3 %collective-permute-start.4 = (bf16[512,256]{1,0:T(8,128)(2,1)S(1)}, bf16[512,256]{1,0:T(8,128)(2,1)S(1)}, u32[]{:S(2)}, u32[]{:S(2)}) collective-permute-start(bf16[512,256]{1,0:T(8,128)(2,1)S(1)} %collective-permute-done.2.other_top), channel_id=1, source_target_pairs={{0,1},{1,0},{2,3},{3,2},{4,5},{5,4},{6,7},{7,6},{8,9},{9,8},{10,11... | collective-permute-start | bytes 786440 | tf_op jit(solution)/shard_map/ppermute | solution.py:19
  23.1 1.8 %pad_maximum_fusion.own = bf16[1280,256]{1,0:T(8,128)(2,1)} fusion(bf16[256,256]{1,0:T(8,128)(2,1)S(1)} %copy-done.3, bf16[512,256]{1,0:T(8,128)(2,1)S(1)} %get-tuple-element.34, bf16[512,256]{1,0:T(8,128)(2,1)} %get-tuple-element.35), kind=kLoop, calls=%fused_computation | loop fusion | flops 1966080 | bytes 1310720 | tf_op jit(solution)/shard_map/concatenate | solution.py:377
  25.6 2.7 %collective-permute-done.5.far_low = bf16[512,256]{1,0:T(8,128)(2,1)S(1)} collective-permute-done((bf16[512,256]{1,0:T(8,128)(2,1)S(1)}, bf16[512,256]{1,0:T(8,128)(2,1)S(1)}, u32[]{:S(2)}, u32[]{:S(2)}) %collective-permute-start.5) | collective-permute-done | bytes 262176 | tf_op jit(solution)/shard_map/ppermute | solution.py:19
  28.9 1.9 %collective-permute-start.8 = (bf16[1024,256]{1,0:T(8,128)(2,1)S(1)}, bf16[1024,256]{1,0:T(8,128)(2,1)}, u32[]{:S(2)}, u32[]{:S(2)}) collective-permute-start(bf16[1024,256]{1,0:T(8,128)(2,1)S(1)} %last_block.2.refs_0_), channel_id=1, source_target_pairs={{0,4},{4,0},{8,12},{12,8},{16,20},{20,16},{24,28},{28,24},{32,36},... | collective-permute-start | bytes 1572872 | tf_op jit(solution)/shard_map/ppermute | solution.py:19
  30.8 3.3 %collective-permute-start.7 = (bf16[1024,256]{1,0:T(8,128)(2,1)S(1)}, bf16[1024,256]{1,0:T(8,128)(2,1)S(1)}, u32[]{:S(2)}, u32[]{:S(2)}) collective-permute-start(bf16[1024,256]{1,0:T(8,128)(2,1)S(1)} %last_block.2.refs_0_), channel_id=1, source_target_pairs={{8,0},{12,4},{16,8},{20,12},{24,16},{28,20},{32,24},{36,28},{40,32... | collective-permute-start | bytes 1572872 | tf_op jit(solution)/shard_map/ppermute | solution.py:24
  34.1 5.9 %collective-permute-start.6 = (bf16[1024,256]{1,0:T(8,128)(2,1)S(1)}, bf16[1024,256]{1,0:T(8,128)(2,1)S(1)}, u32[]{:S(2)}, u32[]{:S(2)}) collective-permute-start(bf16[1024,256]{1,0:T(8,128)(2,1)S(1)} %last_block.2.refs_0_), channel_id=1, source_target_pairs={{0,8},{4,12},{8,16},{12,20},{16,24},{20,28},{24,32},{28,36},{32,40... | collective-permute-start | bytes 1572872 | tf_op jit(solution)/shard_map/ppermute | solution.py:24
  40.1 3.6 %collective-permute-start.11 = (bf16[1280,256]{1,0:T(8,128)(2,1)}, bf16[1280,256]{1,0:T(8,128)(2,1)S(1)}, u32[]{:S(2)}, u32[]{:S(2)}) collective-permute-start(bf16[1280,256]{1,0:T(8,128)(2,1)} %pad_maximum_fusion.own), channel_id=1, source_target_pairs={{0,2},{1,3},{2,0},{3,1},{4,6},{5,7},{6,4},{7,5},{8,10},{9,11},{10,... | collective-permute-start | bytes 1966088 | tf_op jit(solution)/shard_map/ppermute | solution.py:19
  43.7 4.0 %collective-permute-start.10 = (bf16[1280,256]{1,0:T(8,128)(2,1)}, bf16[1280,256]{1,0:T(8,128)(2,1)S(1)}, u32[]{:S(2)}, u32[]{:S(2)}) collective-permute-start(bf16[1280,256]{1,0:T(8,128)(2,1)} %pad_maximum_fusion.own), channel_id=1, source_target_pairs={{0,3},{1,2},{2,1},{3,0},{4,7},{5,6},{6,5},{7,4},{8,11},{9,10},{10,... | collective-permute-start | bytes 1966088 | tf_op jit(solution)/shard_map/ppermute | solution.py:19
  47.7 1.9 %collective-permute-start.9 = (bf16[1280,256]{1,0:T(8,128)(2,1)}, bf16[1280,256]{1,0:T(8,128)(2,1)S(1)}, u32[]{:S(2)}, u32[]{:S(2)}) collective-permute-start(bf16[1280,256]{1,0:T(8,128)(2,1)} %pad_maximum_fusion.own), channel_id=1, source_target_pairs={{0,1},{1,0},{2,3},{3,2},{4,5},{5,4},{6,7},{7,6},{8,9},{9,8},{10,11... | collective-permute-start | bytes 1966088 | tf_op jit(solution)/shard_map/ppermute | solution.py:19
  49.7 0.7 collective-permute-done.7.refs_2_
  50.4 1.2 collective-permute-done.6.refs_1_
  51.6 2.2 %all_gather.22.refs_5_ = bf16[1024,256]{1,0:T(8,128)(2,1)S(1)} all-gather(bf16[512,256]{1,0:T(8,128)(2,1)S(1)} %get-tuple-element.24), channel_id=1, replica_groups={{0,4},{8,12},{16,20},{24,28},{32,36},{40,44},{48,52},{56,60},{64,68},{7..., dimensions={0}, use_global_device_ids=true | all-gather | bytes 786432 | tf_op jit(solution)/shard_map/all_gather | solution.py:30
  53.8 2.2 %all_gather.21.refs_4_ = bf16[1024,256]{1,0:T(8,128)(2,1)S(1)} all-gather(bf16[512,256]{1,0:T(8,128)(2,1)S(1)} %get-tuple-element.25), channel_id=1, replica_groups={{0,4},{8,12},{16,20},{24,28},{32,36},{40,44},{48,52},{56,60},{64,68},{7..., dimensions={0}, use_global_device_ids=true | all-gather | bytes 786432 | tf_op jit(solution)/shard_map/all_gather | solution.py:30
  56.0 7.3 %aggregate_by_rows.1 = bf16[1,256,256]{2,1,0:T(8,128)(2,1)S(1)} custom-call(s32[16,256]{1,0:T(8,128)S(1)} %fusion.4.index_ref, f32[16,256]{1,0:T(8,128)S(1)} %copy-done.7, s32[1,256]{1,0:T(1,128)S(1)} %bitcast.12, bf16[256,256]{1,0:T(8,128)(2,1)S(1)} %copy-done.3, bf16[1024,256]{1,0:T(8,128)(2,1)S(1)} %last_block.2.refs_0_, ...), custom_call_target="tpu_custom_call" | custom-call | flops 1 | bytes 1 | tf_op jit(solution)/shard_map/aggregate_by_rows/pallas_call | solution.py:281
  63.4 19.0 %all_gather.23._.full = bf16[4,256,256]{2,1,0:T(8,128)(2,1)S(1)} all-gather(bf16[1,256,256]{2,1,0:T(8,128)(2,1)S(1)} %aggregate_by_rows.1), channel_id=1, replica_groups=mesh['region'=128,'chan'=4] {'chan'}, dimensions={0}, use_global_device_ids=true | all-gather | bytes 655360 | tf_op jit(solution)/shard_map/all_gather | solution.py:385
  82.4 1.3 combine.1
  83.7 1.9 %collective-permute-start.12 = (bf16[1536,256]{1,0:T(8,128)(2,1)S(1)}, bf16[1536,256]{1,0:T(8,128)(2,1)S(1)}, u32[]{:S(2)}, u32[]{:S(2)}) collective-permute-start(bf16[1536,256]{1,0:T(8,128)(2,1)S(1)} %get-tuple-element.17.mine), channel_id=1, source_target_pairs={{0,4},{4,0},{8,12},{12,8},{16,20},{20,16},{24,28},{28,24},{32,36},... | collective-permute-start | bytes 2359304 | tf_op jit(solution)/shard_map/ppermute | solution.py:19
  85.6 2.3 %collective-permute-done.12.other = bf16[1536,256]{1,0:T(8,128)(2,1)S(1)} collective-permute-done((bf16[1536,256]{1,0:T(8,128)(2,1)S(1)}, bf16[1536,256]{1,0:T(8,128)(2,1)S(1)}, u32[]{:S(2)}, u32[]{:S(2)}) %collective-permute-start.12) | collective-permute-done | bytes 786464 | tf_op jit(solution)/shard_map/ppermute | solution.py:19
  88.5 2.3 %collective-permute-start.14 = (bf16[256,256]{1,0:T(8,128)(2,1)S(1)}, bf16[256,256]{1,0:T(8,128)(2,1)S(1)}, u32[]{:S(2)}, u32[]{:S(2)}) collective-permute-start(bf16[256,256]{1,0:T(8,128)(2,1)S(1)} %get-tuple-element.20), channel_id=1, source_target_pairs={{0,8},{4,12},{8,16},{12,20},{16,24},{20,28},{24,32},{28,36},{32,40... | collective-permute-start | bytes 393224 | tf_op jit(solution)/shard_map/ppermute | solution.py:24
  90.8 3.6 %collective-permute-start.13 = (bf16[256,256]{1,0:T(8,128)(2,1)S(1)}, bf16[256,256]{1,0:T(8,128)(2,1)S(1)}, u32[]{:S(2)}, u32[]{:S(2)}) collective-permute-start(bf16[256,256]{1,0:T(8,128)(2,1)S(1)} %get-tuple-element.20), channel_id=1, source_target_pairs={{8,0},{12,4},{16,8},{20,12},{24,16},{28,20},{32,24},{36,28},{40,32... | collective-permute-start | bytes 393224 | tf_op jit(solution)/shard_map/ppermute | solution.py:24
  94.5 2.0 %all_gather.25.refs_1_ = bf16[512,256]{1,0:T(8,128)(2,1)S(1)} all-gather(bf16[256,256]{1,0:T(8,128)(2,1)S(1)} %get-tuple-element.20), channel_id=1, replica_groups={{0,4},{8,12},{16,20},{24,28},{32,36},{40,44},{48,52},{56,60},{64,68},{7..., dimensions={0}, use_global_device_ids=true | all-gather | bytes 393216 | tf_op jit(solution)/shard_map/all_gather | solution.py:30
  96.5 4.8 %collective-permute-done.13 = bf16[256,256]{1,0:T(8,128)(2,1)S(1)} collective-permute-done((bf16[256,256]{1,0:T(8,128)(2,1)S(1)}, bf16[256,256]{1,0:T(8,128)(2,1)S(1)}, u32[]{:S(2)}, u32[]{:S(2)}) %collective-permute-start.13) | collective-permute-done | bytes 131104 | tf_op jit(solution)/shard_map/ppermute | solution.py:24
  101.3 2.0 %all_gather.24.refs_0_ = bf16[512,256]{1,0:T(8,128)(2,1)S(1)} all-gather(bf16[256,256]{1,0:T(8,128)(2,1)S(1)} %get-tuple-element.33), channel_id=1, replica_groups={{0,4},{8,12},{16,20},{24,28},{32,36},{40,44},{48,52},{56,60},{64,68},{7..., dimensions={0}, use_global_device_ids=true | all-gather | bytes 393216 | tf_op jit(solution)/shard_map/all_gather | solution.py:30
  103.3 2.1 %aggregate_by_matmul.2 = bf16[4,256,256]{2,1,0:T(8,128)(2,1)S(1)} custom-call(s32[1]{0:T(128)} %bitcast.1.me_ref, s32[8,256]{1,0:T(8,128)S(1)} %copy-done.13, f32[8,256]{1,0:T(8,128)S(1)} %copy-done.14, s32[1,256]{1,0:T(1,128)S(1)} %bitcast.14, bf16[256,256]{1,0:T(8,128)(2,1)S(1)} %get-tuple-element.19.receiver_ref.mesh_one, ...), custom_call_target="tpu_custom_call" | custom-call | flops 1342177280 | bytes 917504 | tf_op jit(solution)/shard_map/aggregate_by_matmul/pallas_call | solution.py:333
  105.4 12.6 %all_to_all.5.full = bf16[4,256,256]{2,1,0:T(8,128)(2,1)S(1)} all-to-all(bf16[4,256,256]{2,1,0:T(8,128)(2,1)S(1)} %aggregate_by_matmul.2), channel_id=1, replica_groups=mesh['region'=128,'chan'=4] {'chan'}, dimensions={0} | all-to-all | bytes 1048576 | tf_op jit(solution)/shard_map/all_to_all | solution.py:34
  118.0 1.1 mesh_step.3
  119.2 2.0 %collective-permute-start.16 = (bf16[256,256]{1,0:T(8,128)(2,1)S(1)}, bf16[256,256]{1,0:T(8,128)(2,1)S(1)}, u32[]{:S(2)}, u32[]{:S(2)}) collective-permute-start(bf16[256,256]{1,0:T(8,128)(2,1)S(1)} %get-tuple-element.22), channel_id=1, source_target_pairs={{0,8},{4,12},{8,16},{12,20},{16,24},{20,28},{24,32},{28,36},{32,40... | collective-permute-start | bytes 393224 | tf_op jit(solution)/shard_map/ppermute | solution.py:24
  121.2 3.9 %collective-permute-start.15 = (bf16[256,256]{1,0:T(8,128)(2,1)S(1)}, bf16[256,256]{1,0:T(8,128)(2,1)S(1)}, u32[]{:S(2)}, u32[]{:S(2)}) collective-permute-start(bf16[256,256]{1,0:T(8,128)(2,1)S(1)} %get-tuple-element.22), channel_id=1, source_target_pairs={{8,0},{12,4},{16,8},{20,12},{24,16},{28,20},{32,24},{36,28},{40,32... | collective-permute-start | bytes 393224 | tf_op jit(solution)/shard_map/ppermute | solution.py:24
  125.1 2.0 %all_gather.27.refs_1_ = bf16[512,256]{1,0:T(8,128)(2,1)S(1)} all-gather(bf16[256,256]{1,0:T(8,128)(2,1)S(1)} %get-tuple-element.22), channel_id=1, replica_groups={{0,4},{8,12},{16,20},{24,28},{32,36},{40,44},{48,52},{56,60},{64,68},{7..., dimensions={0}, use_global_device_ids=true | all-gather | bytes 393216 | tf_op jit(solution)/shard_map/all_gather | solution.py:30
  127.1 4.3 %collective-permute-done.15 = bf16[256,256]{1,0:T(8,128)(2,1)S(1)} collective-permute-done((bf16[256,256]{1,0:T(8,128)(2,1)S(1)}, bf16[256,256]{1,0:T(8,128)(2,1)S(1)}, u32[]{:S(2)}, u32[]{:S(2)}) %collective-permute-start.15) | collective-permute-done | bytes 131104 | tf_op jit(solution)/shard_map/ppermute | solution.py:24
  131.4 2.0 %all_gather.26.refs_0_ = bf16[512,256]{1,0:T(8,128)(2,1)S(1)} all-gather(bf16[256,256]{1,0:T(8,128)(2,1)S(1)} %get-tuple-element.31), channel_id=1, replica_groups={{0,4},{8,12},{16,20},{24,28},{32,36},{40,44},{48,52},{56,60},{64,68},{7..., dimensions={0}, use_global_device_ids=true | all-gather | bytes 393216 | tf_op jit(solution)/shard_map/all_gather | solution.py:30
  133.4 4.3 %aggregate_by_matmul.3 = bf16[1,1024,256]{2,1,0:T(8,128)(2,1)S(1)} custom-call(s32[1]{0:T(128)} %bitcast.1.me_ref, s32[4,1024]{1,0:T(4,128)S(1)} %copy-done.11, f32[4,1024]{1,0:T(4,128)S(1)} %copy-done.12, s32[1,1024]{1,0:T(1,128)S(1)} %bitcast.13, bf16[1024,256]{1,0:T(8,128)(2,1)S(1)} %copy-done, bf16[512,256]{1,0:T(8,128)(2,1)S(1)} %all_gather.26.refs_0_, ...), custom_call_target="tpu_custom_call" | custom-call | flops 2684354560 | bytes 1703936 | tf_op jit(solution)/shard_map/aggregate_by_matmul/pallas_call | solution.py:333
  137.8 2.6 %collective-permute-start.18 = (bf16[512,256]{1,0:T(8,128)(2,1)S(1)}, bf16[512,256]{1,0:T(8,128)(2,1)S(1)}, u32[]{:S(2)}, u32[]{:S(2)}) collective-permute-start(bf16[512,256]{1,0:T(8,128)(2,1)S(1)} %get-tuple-element.26), channel_id=1, source_target_pairs={{0,1},{1,0},{2,3},{3,2},{4,5},{5,4},{6,7},{7,6},{8,9},{9,8},{10,11... | collective-permute-start | bytes 786440 | tf_op jit(solution)/shard_map/ppermute | solution.py:19
  140.4 2.7 %collective-permute-start.19 = (bf16[512,256]{1,0:T(8,128)(2,1)S(1)}, bf16[512,256]{1,0:T(8,128)(2,1)S(1)}, u32[]{:S(2)}, u32[]{:S(2)}) collective-permute-start(bf16[512,256]{1,0:T(8,128)(2,1)S(1)} %get-tuple-element.27), channel_id=1, source_target_pairs={{0,3},{1,2},{2,1},{3,0},{4,7},{5,6},{6,5},{7,4},{8,11},{9,10},{10,... | collective-permute-start | bytes 786440 | tf_op jit(solution)/shard_map/ppermute | solution.py:19
  143.2 4.3 %collective-permute-start.20 = (bf16[512,256]{1,0:T(8,128)(2,1)S(1)}, bf16[512,256]{1,0:T(8,128)(2,1)S(1)}, u32[]{:S(2)}, u32[]{:S(2)}) collective-permute-start(bf16[512,256]{1,0:T(8,128)(2,1)S(1)} %get-tuple-element.26), channel_id=1, source_target_pairs={{0,3},{1,2},{2,1},{3,0},{4,7},{5,6},{6,5},{7,4},{8,11},{9,10},{10,... | collective-permute-start | bytes 786440 | tf_op jit(solution)/shard_map/ppermute | solution.py:19
  147.5 2.2 %collective-permute-start.17 = (bf16[512,256]{1,0:T(8,128)(2,1)S(1)}, bf16[512,256]{1,0:T(8,128)(2,1)S(1)}, u32[]{:S(2)}, u32[]{:S(2)}) collective-permute-start(bf16[512,256]{1,0:T(8,128)(2,1)S(1)} %get-tuple-element.27), channel_id=1, source_target_pairs={{0,1},{1,0},{2,3},{3,2},{4,5},{5,4},{6,7},{7,6},{8,9},{9,8},{10,11... | collective-permute-start | bytes 786440 | tf_op jit(solution)/shard_map/ppermute | solution.py:19
  149.7 3.1 %collective-permute-start.22 = (bf16[512,256]{1,0:T(8,128)(2,1)S(1)}, bf16[512,256]{1,0:T(8,128)(2,1)S(1)}, u32[]{:S(2)}, u32[]{:S(2)}) collective-permute-start(bf16[512,256]{1,0:T(8,128)(2,1)S(1)} %collective-permute-done.18.near_low), channel_id=1, source_target_pairs={{0,3},{1,2},{2,1},{3,0},{4,7},{5,6},{6,5},{7,4},{8,11},{9,10},{10,... | collective-permute-start | bytes 786440 | tf_op jit(solution)/shard_map/ppermute | solution.py:19
  152.8 2.7 %collective-permute-start.21 = (bf16[512,256]{1,0:T(8,128)(2,1)S(1)}, bf16[512,256]{1,0:T(8,128)(2,1)S(1)}, u32[]{:S(2)}, u32[]{:S(2)}) collective-permute-start(bf16[512,256]{1,0:T(8,128)(2,1)S(1)} %collective-permute-done.19.other_top), channel_id=1, source_target_pairs={{0,1},{1,0},{2,3},{3,2},{4,5},{5,4},{6,7},{7,6},{8,9},{9,8},{10,11... | collective-permute-start | bytes 786440 | tf_op jit(solution)/shard_map/ppermute | solution.py:19
  155.5 2.8 %collective-permute-done.20.other_low = bf16[512,256]{1,0:T(8,128)(2,1)S(1)} collective-permute-done((bf16[512,256]{1,0:T(8,128)(2,1)S(1)}, bf16[512,256]{1,0:T(8,128)(2,1)S(1)}, u32[]{:S(2)}, u32[]{:S(2)}) %collective-permute-start.20) | collective-permute-done | bytes 262176 | tf_op jit(solution)/shard_map/ppermute | solution.py:19
  158.9 3.9 %collective-permute-done.22.far_low = bf16[512,256]{1,0:T(8,128)(2,1)S(1)} collective-permute-done((bf16[512,256]{1,0:T(8,128)(2,1)S(1)}, bf16[512,256]{1,0:T(8,128)(2,1)S(1)}, u32[]{:S(2)}, u32[]{:S(2)}) %collective-permute-start.22) | collective-permute-done | bytes 262176 | tf_op jit(solution)/shard_map/ppermute | solution.py:19
  162.8 1.1 last_block.3
  (60 shorter events, 2.6 us)
Async XLA Ops:
  0.6 14.4 %copy-start.4 = (bf16[1024,256]{1,0:T(8,128)(2,1)S(1)}, bf16[1024,256]{1,0:T(8,128)(2,1)}, u32[]{:S(2)}) copy-start(bf16[1024,256]{1,0:T(8,128)(2,1)} %w_out.3) | copy-start | bytes 1572868
  0.6 14.4 %copy-start.5 = (bf16[1024,256]{1,0:T(8,128)(2,1)S(1)}, bf16[1024,256]{1,0:T(8,128)(2,1)}, u32[]{:S(2)}) copy-start(bf16[1024,256]{1,0:T(8,128)(2,1)} %w_out.2) | copy-start | bytes 1572868
  0.7 22.5 %copy-start.3 = (bf16[256,256]{1,0:T(8,128)(2,1)S(1)}, bf16[256,256]{1,0:T(8,128)(2,1)}, u32[]{:S(2)}) copy-start(bf16[256,256]{1,0:T(8,128)(2,1)} %mesh.1) | copy-start | bytes 393220
  2.6 13.2 %collective-permute-start.1 = (bf16[512,256]{1,0:T(8,128)(2,1)}, bf16[512,256]{1,0:T(8,128)(2,1)S(1)}, u32[]{:S(2)}, u32[]{:S(2)}) collective-permute-start(bf16[512,256]{1,0:T(8,128)(2,1)} %get-tuple-element.28), channel_id=1, source_target_pairs={{0,1},{1,0},{2,3},{3,2},{4,5},{5,4},{6,7},{7,6},{8,9},{9,8},{10,11... | collective-permute-start | bytes 786440 | tf_op jit(solution)/shard_map/ppermute | solution.py:19
  6.0 13.8 %collective-permute-start.2 = (bf16[512,256]{1,0:T(8,128)(2,1)}, bf16[512,256]{1,0:T(8,128)(2,1)S(1)}, u32[]{:S(2)}, u32[]{:S(2)}) collective-permute-start(bf16[512,256]{1,0:T(8,128)(2,1)} %get-tuple-element.29), channel_id=1, source_target_pairs={{0,3},{1,2},{2,1},{3,0},{4,7},{5,6},{6,5},{7,4},{8,11},{9,10},{10,... | collective-permute-start | bytes 786440 | tf_op jit(solution)/shard_map/ppermute | solution.py:19
  10.0 15.0 %collective-permute-start.3 = (bf16[512,256]{1,0:T(8,128)(2,1)}, bf16[512,256]{1,0:T(8,128)(2,1)S(1)}, u32[]{:S(2)}, u32[]{:S(2)}) collective-permute-start(bf16[512,256]{1,0:T(8,128)(2,1)} %get-tuple-element.28), channel_id=1, source_target_pairs={{0,3},{1,2},{2,1},{3,0},{4,7},{5,6},{6,5},{7,4},{8,11},{9,10},{10,... | collective-permute-start | bytes 786440 | tf_op jit(solution)/shard_map/ppermute | solution.py:19
  13.1 11.9 %collective-permute-start = (bf16[512,256]{1,0:T(8,128)(2,1)}, bf16[512,256]{1,0:T(8,128)(2,1)S(1)}, u32[]{:S(2)}, u32[]{:S(2)}) collective-permute-start(bf16[512,256]{1,0:T(8,128)(2,1)} %get-tuple-element.29), channel_id=1, source_target_pairs={{0,1},{1,0},{2,3},{3,2},{4,5},{5,4},{6,7},{7,6},{8,9},{9,8},{10,11... | collective-permute-start | bytes 786440 | tf_op jit(solution)/shard_map/ppermute | solution.py:19
  15.0 10.0 %copy-start = (bf16[1024,256]{1,0:T(8,128)(2,1)S(1)}, bf16[1024,256]{1,0:T(8,128)(2,1)}, u32[]{:S(2)}) copy-start(bf16[1024,256]{1,0:T(8,128)(2,1)} %refs_0_.1) | copy-start | bytes 1572868
  15.0 10.0 %copy-start.1 = (bf16[1024,256]{1,0:T(8,128)(2,1)S(1)}, bf16[1024,256]{1,0:T(8,128)(2,1)}, u32[]{:S(2)}) copy-start(bf16[1024,256]{1,0:T(8,128)(2,1)} %weight.5) | copy-start | bytes 1572868
  15.8 12.5 %collective-permute-start.5 = (bf16[512,256]{1,0:T(8,128)(2,1)S(1)}, bf16[512,256]{1,0:T(8,128)(2,1)S(1)}, u32[]{:S(2)}, u32[]{:S(2)}) collective-permute-start(bf16[512,256]{1,0:T(8,128)(2,1)S(1)} %collective-permute-done.1.near_low), channel_id=1, source_target_pairs={{0,3},{1,2},{2,1},{3,0},{4,7},{5,6},{6,5},{7,4},{8,11},{9,10},{10,... | collective-permute-start | bytes 786440 | tf_op jit(solution)/shard_map/ppermute | solution.py:19
  19.8 8.8 %collective-permute-start.4 = (bf16[512,256]{1,0:T(8,128)(2,1)S(1)}, bf16[512,256]{1,0:T(8,128)(2,1)S(1)}, u32[]{:S(2)}, u32[]{:S(2)}) collective-permute-start(bf16[512,256]{1,0:T(8,128)(2,1)S(1)} %collective-permute-done.2.other_top), channel_id=1, source_target_pairs={{0,1},{1,0},{2,3},{3,2},{4,5},{5,4},{6,7},{7,6},{8,9},{9,8},{10,11... | collective-permute-start | bytes 786440 | tf_op jit(solution)/shard_map/ppermute | solution.py:19
  25.6 14.5 %copy-start.17 = (s32[16,256]{1,0:T(8,128)S(1)}, s32[16,256]{1,0:T(8,128)}, u32[]{:S(2)}) copy-start(s32[16,256]{1,0:T(8,128)} %param.25) | copy-start | bytes 49156
  28.9 14.8 %collective-permute-start.8 = (bf16[1024,256]{1,0:T(8,128)(2,1)S(1)}, bf16[1024,256]{1,0:T(8,128)(2,1)}, u32[]{:S(2)}, u32[]{:S(2)}) collective-permute-start(bf16[1024,256]{1,0:T(8,128)(2,1)S(1)} %last_block.2.refs_0_), channel_id=1, source_target_pairs={{0,4},{4,0},{8,12},{12,8},{16,20},{20,16},{24,28},{28,24},{32,36},... | collective-permute-start | bytes 1572872 | tf_op jit(solution)/shard_map/ppermute | solution.py:19
  30.8 19.5 %collective-permute-start.7 = (bf16[1024,256]{1,0:T(8,128)(2,1)S(1)}, bf16[1024,256]{1,0:T(8,128)(2,1)S(1)}, u32[]{:S(2)}, u32[]{:S(2)}) collective-permute-start(bf16[1024,256]{1,0:T(8,128)(2,1)S(1)} %last_block.2.refs_0_), channel_id=1, source_target_pairs={{8,0},{12,4},{16,8},{20,12},{24,16},{28,20},{32,24},{36,28},{40,32... | collective-permute-start | bytes 1572872 | tf_op jit(solution)/shard_map/ppermute | solution.py:24
  34.1 17.5 %collective-permute-start.6 = (bf16[1024,256]{1,0:T(8,128)(2,1)S(1)}, bf16[1024,256]{1,0:T(8,128)(2,1)S(1)}, u32[]{:S(2)}, u32[]{:S(2)}) collective-permute-start(bf16[1024,256]{1,0:T(8,128)(2,1)S(1)} %last_block.2.refs_0_), channel_id=1, source_target_pairs={{0,8},{4,12},{8,16},{12,20},{16,24},{20,28},{24,32},{28,36},{32,40... | collective-permute-start | bytes 1572872 | tf_op jit(solution)/shard_map/ppermute | solution.py:24
  40.1 42.3 %collective-permute-start.11 = (bf16[1280,256]{1,0:T(8,128)(2,1)}, bf16[1280,256]{1,0:T(8,128)(2,1)S(1)}, u32[]{:S(2)}, u32[]{:S(2)}) collective-permute-start(bf16[1280,256]{1,0:T(8,128)(2,1)} %pad_maximum_fusion.own), channel_id=1, source_target_pairs={{0,2},{1,3},{2,0},{3,1},{4,6},{5,7},{6,4},{7,5},{8,10},{9,11},{10,... | collective-permute-start | bytes 1966088 | tf_op jit(solution)/shard_map/ppermute | solution.py:19
  43.7 38.7 %collective-permute-start.10 = (bf16[1280,256]{1,0:T(8,128)(2,1)}, bf16[1280,256]{1,0:T(8,128)(2,1)S(1)}, u32[]{:S(2)}, u32[]{:S(2)}) collective-permute-start(bf16[1280,256]{1,0:T(8,128)(2,1)} %pad_maximum_fusion.own), channel_id=1, source_target_pairs={{0,3},{1,2},{2,1},{3,0},{4,7},{5,6},{6,5},{7,4},{8,11},{9,10},{10,... | collective-permute-start | bytes 1966088 | tf_op jit(solution)/shard_map/ppermute | solution.py:19
  47.7 34.7 %collective-permute-start.9 = (bf16[1280,256]{1,0:T(8,128)(2,1)}, bf16[1280,256]{1,0:T(8,128)(2,1)S(1)}, u32[]{:S(2)}, u32[]{:S(2)}) collective-permute-start(bf16[1280,256]{1,0:T(8,128)(2,1)} %pad_maximum_fusion.own), channel_id=1, source_target_pairs={{0,1},{1,0},{2,3},{3,2},{4,5},{5,4},{6,7},{7,6},{8,9},{9,8},{10,11... | collective-permute-start | bytes 1966088 | tf_op jit(solution)/shard_map/ppermute | solution.py:19
  51.6 4.4 %copy-start.7 = (f32[16,256]{1,0:T(8,128)S(1)}, f32[16,256]{1,0:T(8,128)}, u32[]{:S(2)}) copy-start(f32[16,256]{1,0:T(8,128)} %slot_ref.3) | copy-start | bytes 49156
  51.6 4.4 %copy-start.8 = (s32[256]{0:T(256)S(1)}, s32[256]{0:T(256)}, u32[]{:S(2)}) copy-start(s32[256]{0:T(256)} %param.27) | copy-start | bytes 3076
  56.0 26.4 %copy-start.6 = (bf16[1280,256]{1,0:T(8,128)(2,1)S(1)}, bf16[1280,256]{1,0:T(8,128)(2,1)}, u32[]{:S(2)}) copy-start(bf16[1280,256]{1,0:T(8,128)(2,1)} %pad_maximum_fusion.own) | copy-start | bytes 1966084
  56.0 26.4 %copy-start.9 = (bf16[1024,256]{1,0:T(8,128)(2,1)S(1)}, bf16[1024,256]{1,0:T(8,128)(2,1)}, u32[]{:S(2)}) copy-start(bf16[1024,256]{1,0:T(8,128)(2,1)} %first.1) | copy-start | bytes 1572868
  56.0 26.4 %copy-start.10 = (bf16[1024,256]{1,0:T(8,128)(2,1)S(1)}, bf16[1024,256]{1,0:T(8,128)(2,1)}, u32[]{:S(2)}) copy-start(bf16[1024,256]{1,0:T(8,128)(2,1)} %second.1) | copy-start | bytes 1572868
  83.7 4.2 %collective-permute-start.12 = (bf16[1536,256]{1,0:T(8,128)(2,1)S(1)}, bf16[1536,256]{1,0:T(8,128)(2,1)S(1)}, u32[]{:S(2)}, u32[]{:S(2)}) collective-permute-start(bf16[1536,256]{1,0:T(8,128)(2,1)S(1)} %get-tuple-element.17.mine), channel_id=1, source_target_pairs={{0,4},{4,0},{8,12},{12,8},{16,20},{20,16},{24,28},{28,24},{32,36},... | collective-permute-start | bytes 2359304 | tf_op jit(solution)/shard_map/ppermute | solution.py:19
  88.4 14.9 %copy-start.13 = (s32[8,256]{1,0:T(8,128)S(1)}, s32[8,256]{1,0:T(8,128)}, u32[]{:S(2)}) copy-start(s32[8,256]{1,0:T(8,128)} %sender_ref.2) | copy-start | bytes 24580
  88.5 14.9 %copy-start.14 = (f32[8,256]{1,0:T(8,128)S(1)}, f32[8,256]{1,0:T(8,128)}, u32[]{:S(2)}) copy-start(f32[8,256]{1,0:T(8,128)} %slot_ref.4) | copy-start | bytes 24580
  88.5 14.9 %copy-start.16 = (s32[256]{0:T(256)S(1)}, s32[256]{0:T(256)}, u32[]{:S(2)}) copy-start(s32[256]{0:T(256)} %param.30) | copy-start | bytes 3076
  88.5 8.0 %collective-permute-start.14 = (bf16[256,256]{1,0:T(8,128)(2,1)S(1)}, bf16[256,256]{1,0:T(8,128)(2,1)S(1)}, u32[]{:S(2)}, u32[]{:S(2)}) collective-permute-start(bf16[256,256]{1,0:T(8,128)(2,1)S(1)} %get-tuple-element.20), channel_id=1, source_target_pairs={{0,8},{4,12},{8,16},{12,20},{16,24},{20,28},{24,32},{28,36},{32,40... | collective-permute-start | bytes 393224 | tf_op jit(solution)/shard_map/ppermute | solution.py:24
  90.8 10.5 %collective-permute-start.13 = (bf16[256,256]{1,0:T(8,128)(2,1)S(1)}, bf16[256,256]{1,0:T(8,128)(2,1)S(1)}, u32[]{:S(2)}, u32[]{:S(2)}) collective-permute-start(bf16[256,256]{1,0:T(8,128)(2,1)S(1)} %get-tuple-element.20), channel_id=1, source_target_pairs={{8,0},{12,4},{16,8},{20,12},{24,16},{28,20},{32,24},{36,28},{40,32... | collective-permute-start | bytes 393224 | tf_op jit(solution)/shard_map/ppermute | solution.py:24
  119.1 14.3 %copy-start.11 = (s32[4,1024]{1,0:T(4,128)S(1)}, s32[4,1024]{1,0:T(4,128)}, u32[]{:S(2)}) copy-start(s32[4,1024]{1,0:T(4,128)} %sender_ref.3) | copy-start | bytes 49156
  119.1 14.3 %copy-start.12 = (f32[4,1024]{1,0:T(4,128)S(1)}, f32[4,1024]{1,0:T(4,128)}, u32[]{:S(2)}) copy-start(f32[4,1024]{1,0:T(4,128)} %slot_ref.5) | copy-start | bytes 49156
  119.1 14.3 %copy-start.15 = (s32[1024]{0:T(1024)S(1)}, s32[1024]{0:T(1024)}, u32[]{:S(2)}) copy-start(s32[1024]{0:T(1024)} %param.33) | copy-start | bytes 12292
  119.2 8.0 %collective-permute-start.16 = (bf16[256,256]{1,0:T(8,128)(2,1)S(1)}, bf16[256,256]{1,0:T(8,128)(2,1)S(1)}, u32[]{:S(2)}, u32[]{:S(2)}) collective-permute-start(bf16[256,256]{1,0:T(8,128)(2,1)S(1)} %get-tuple-element.22), channel_id=1, source_target_pairs={{0,8},{4,12},{8,16},{12,20},{16,24},{20,28},{24,32},{28,36},{32,40... | collective-permute-start | bytes 393224 | tf_op jit(solution)/shard_map/ppermute | solution.py:24
  121.2 10.2 %collective-permute-start.15 = (bf16[256,256]{1,0:T(8,128)(2,1)S(1)}, bf16[256,256]{1,0:T(8,128)(2,1)S(1)}, u32[]{:S(2)}, u32[]{:S(2)}) collective-permute-start(bf16[256,256]{1,0:T(8,128)(2,1)S(1)} %get-tuple-element.22), channel_id=1, source_target_pairs={{8,0},{12,4},{16,8},{20,12},{24,16},{28,20},{32,24},{36,28},{40,32... | collective-permute-start | bytes 393224 | tf_op jit(solution)/shard_map/ppermute | solution.py:24
  137.8 20.6 %copy-start.2 = (bf16[1024,256]{1,0:T(8,128)(2,1)S(1)}, bf16[1024,256]{1,0:T(8,128)(2,1)}, u32[]{:S(2)}) copy-start(bf16[1024,256]{1,0:T(8,128)(2,1)} %weight.7) | copy-start | bytes 1572868
  137.8 11.9 %collective-permute-start.18 = (bf16[512,256]{1,0:T(8,128)(2,1)S(1)}, bf16[512,256]{1,0:T(8,128)(2,1)S(1)}, u32[]{:S(2)}, u32[]{:S(2)}) collective-permute-start(bf16[512,256]{1,0:T(8,128)(2,1)S(1)} %get-tuple-element.26), channel_id=1, source_target_pairs={{0,1},{1,0},{2,3},{3,2},{4,5},{5,4},{6,7},{7,6},{8,9},{9,8},{10,11... | collective-permute-start | bytes 786440 | tf_op jit(solution)/shard_map/ppermute | solution.py:19
  140.4 12.3 %collective-permute-start.19 = (bf16[512,256]{1,0:T(8,128)(2,1)S(1)}, bf16[512,256]{1,0:T(8,128)(2,1)S(1)}, u32[]{:S(2)}, u32[]{:S(2)}) collective-permute-start(bf16[512,256]{1,0:T(8,128)(2,1)S(1)} %get-tuple-element.27), channel_id=1, source_target_pairs={{0,3},{1,2},{2,1},{3,0},{4,7},{5,6},{6,5},{7,4},{8,11},{9,10},{10,... | collective-permute-start | bytes 786440 | tf_op jit(solution)/shard_map/ppermute | solution.py:19
  143.2 15.2 %collective-permute-start.20 = (bf16[512,256]{1,0:T(8,128)(2,1)S(1)}, bf16[512,256]{1,0:T(8,128)(2,1)S(1)}, u32[]{:S(2)}, u32[]{:S(2)}) collective-permute-start(bf16[512,256]{1,0:T(8,128)(2,1)S(1)} %get-tuple-element.26), channel_id=1, source_target_pairs={{0,3},{1,2},{2,1},{3,0},{4,7},{5,6},{6,5},{7,4},{8,11},{9,10},{10,... | collective-permute-start | bytes 786440 | tf_op jit(solution)/shard_map/ppermute | solution.py:19
  147.5 10.8 %collective-permute-start.17 = (bf16[512,256]{1,0:T(8,128)(2,1)S(1)}, bf16[512,256]{1,0:T(8,128)(2,1)S(1)}, u32[]{:S(2)}, u32[]{:S(2)}) collective-permute-start(bf16[512,256]{1,0:T(8,128)(2,1)S(1)} %get-tuple-element.27), channel_id=1, source_target_pairs={{0,1},{1,0},{2,3},{3,2},{4,5},{5,4},{6,7},{7,6},{8,9},{9,8},{10,11... | collective-permute-start | bytes 786440 | tf_op jit(solution)/shard_map/ppermute | solution.py:19
  149.7 13.2 %collective-permute-start.22 = (bf16[512,256]{1,0:T(8,128)(2,1)S(1)}, bf16[512,256]{1,0:T(8,128)(2,1)S(1)}, u32[]{:S(2)}, u32[]{:S(2)}) collective-permute-start(bf16[512,256]{1,0:T(8,128)(2,1)S(1)} %collective-permute-done.18.near_low), channel_id=1, source_target_pairs={{0,3},{1,2},{2,1},{3,0},{4,7},{5,6},{6,5},{7,4},{8,11},{9,10},{10,... | collective-permute-start | bytes 786440 | tf_op jit(solution)/shard_map/ppermute | solution.py:19
  152.8 10.1 %collective-permute-start.21 = (bf16[512,256]{1,0:T(8,128)(2,1)S(1)}, bf16[512,256]{1,0:T(8,128)(2,1)S(1)}, u32[]{:S(2)}, u32[]{:S(2)}) collective-permute-start(bf16[512,256]{1,0:T(8,128)(2,1)S(1)} %collective-permute-done.19.other_top), channel_id=1, source_target_pairs={{0,1},{1,0},{2,3},{3,2},{4,5},{5,4},{6,7},{7,6},{8,9},{9,8},{10,11... | collective-permute-start | bytes 786440 | tf_op jit(solution)/shard_map/ppermute | solution.py:19
